TPU v7x, 128 devices: a whole 4x4x4 slice. The times are simulated.
128 devices in a mesh: group: 4 (over y_lo, core), span: 32 (over x, z, y_hi).
Axes of the slice: x: 4, y: 4 (y_hi: 2, y_lo: 2; y = y_hi * 2 + y_lo), z: 4, core: 2. Of those that a mesh axis runs over, the one named last changes fastest.
Arguments:
- tokens: bfloat16 [16384, 1024], P(('group', 'span')), may hold values from -32 to 32
- query_weight: bfloat16 [1024, 1024], replicated, may hold values from -0.1875 to 0.1875
- key_weight: bfloat16 [1024, 1024], replicated, may hold values from -0.1875 to 0.1875
- value_weight: bfloat16 [1024, 1024], replicated, may hold values from -0.1875 to 0.1875
- log_decay: float32 [16, 16384], P(None, ('group', 'span')), may hold values from -0.6 to 0
- neighbour_blocks: int32 [128, 4], P(('group', 'span')), may hold values from 0 to 127, as said below
- cotangent: bfloat16 [16384, 1024], P(('group', 'span')), may hold values from -6 to 6
Outputs:
- layer_out: bfloat16 [16384, 1024], P(('group', 'span'))
- tokens_grad: bfloat16 [16384, 1024], P(('group', 'span'))
- query_grad: bfloat16 [1024, 1024], replicated
- key_grad: bfloat16 [1024, 1024], replicated
- value_grad: bfloat16 [1024, 1024], replicated
Inputs may be any that keep to these rules, and one draw needn't show every extreme that they name: `neighbour_blocks`: row b is [b, b - 1, b - 1, b - 1]; any entry that would fall before block 0 is block 0.
All inputs are finite; a program needn't handle non-finite values.
Results may differ from a plain program's by a relative error of at most 0.0077.
Values may be sent and summed in bfloat16 or wider, within the bound.
No kernel may reach another device: no remote copies, remote signals or barrier semaphores. Data moves between devices by JAX's collectives and lax.ppermute only.
A program may use at most 192 MiB of HBM per device.

v0:
```python
import math

import jax
import jax.numpy as jnp
from jax import lax
from jax.sharding import PartitionSpec as P

BLK = 128
NB = 4


def prefix(part, axis, combine, identity, reverse):
    count = lax.axis_size(axis)
    place = lax.axis_index(axis)
    ahead = count - 1 - place if reverse else place
    gathered = jax.tree.map(lambda a: lax.all_gather(a, axis), part)
    state = jax.tree.map(lambda a, e: jnp.zeros_like(a) + jnp.asarray(e, a.dtype), part, identity)

    def one(hop, state):
        source = count - 1 - hop if reverse else hop
        return combine(
            state, jax.tree.map(lambda a: lax.dynamic_index_in_dim(a, source, 0, False), gathered)
        )

    return lax.fori_loop(0, ahead, one, state)


def shifted(block, axis, distance):
    devices = range(lax.axis_size(axis))
    route = [(i - distance, i) for i in devices if i - distance in devices]
    return lax.ppermute(block, axis, route)


def project(inputs, weight):
    return jnp.dot(inputs, weight, preferred_element_type=jnp.float32).astype(jnp.bfloat16)


def back_project(grad_kv, key_weight, value_weight, feat_width):
    key_part = jnp.einsum(
        "tc,dc->td", grad_kv[:, :feat_width], key_weight, preferred_element_type=jnp.float32
    )
    return key_part + jnp.einsum(
        "tc,dc->td", grad_kv[:, feat_width:], value_weight, preferred_element_type=jnp.float32
    )


def join_carry(earlier, later):
    return (earlier[0] + later[0], jnp.exp(later[0])[:, None] * earlier[1] + later[1])


def carry_across(seg_total, seg_state, reverse):
    identity_pair = (jnp.zeros_like(seg_total), jnp.zeros_like(seg_state))
    result = prefix((seg_total, seg_state), ("group", "span"), join_carry, identity_pair, reverse)
    return result[1]


def shards(tokens, query_weight, key_weight, value_weight, log_decay, neighbour_blocks, cotangent):
    row_count, feat_width = tokens.shape
    head_count = log_decay.shape[0]
    head_size = feat_width // head_count
    blocks = row_count // BLK
    lin_scale = 1.0 / (head_size * math.sqrt(row_count))
    soft_scale = 1.0 / math.sqrt(head_size)
    devices = lax.axis_size(("group", "span"))
    position = lax.axis_index(("group", "span"))
    query = project(tokens, query_weight)
    keyval = jnp.concatenate([project(tokens, key_weight), project(tokens, value_weight)], axis=1)
    running = jnp.cumsum(log_decay, axis=1)
    seg_total = running[:, -1]
    growth = jnp.exp(running).T[:, :, None]
    fading = jnp.exp(seg_total[:, None] - running).T[:, :, None]
    q_heads = query.reshape(row_count, head_count, head_size)
    k_heads = keyval[:, :feat_width].reshape(row_count, head_count, head_size)
    v_heads = keyval[:, feat_width:].reshape(row_count, head_count, head_size)
    g_heads = cotangent.reshape(row_count, head_count, head_size)
    weighted = (v_heads * fading).astype(jnp.bfloat16)
    local_state = jnp.einsum(
        "shd,she->hde", k_heads, weighted, preferred_element_type=jnp.float32
    ).reshape(head_count, head_size * head_size)
    scaled_grad = (g_heads * growth).astype(jnp.bfloat16)
    head_grad = lin_scale * jnp.einsum(
        "thd,the->hde", q_heads, scaled_grad, preferred_element_type=jnp.float32
    )
    head_grad = head_grad.reshape(head_count, head_size * head_size)
    state_in = carry_across(seg_total, local_state, False).reshape(head_count, head_size, head_size)
    later = carry_across(seg_total, head_grad, True).reshape(head_count, head_size, head_size)
    prev_keyval = shifted(keyval, ("group", "span"), 1)
    places = jnp.arange(row_count, dtype=jnp.int32)
    is_lower = places[:, None] >= places[None, :]
    decay_mat = jnp.where(
        is_lower[None], jnp.exp(jnp.minimum(running[:, :, None] - running[:, None, :], 0.0)), 0.0
    )
    intra_mat = (
        jnp.einsum("thd,shd->hts", q_heads, k_heads, preferred_element_type=jnp.float32) * decay_mat
    ).astype(jnp.bfloat16)
    state_bf = state_in.astype(jnp.bfloat16)
    linear_out = jnp.einsum("hts,she->the", intra_mat, v_heads, preferred_element_type=jnp.float32)
    linear_out = linear_out + growth * jnp.einsum(
        "thd,hde->the", q_heads, state_bf, preferred_element_type=jnp.float32
    )
    extended = jnp.concatenate([prev_keyval, keyval], axis=0).reshape(
        2 * blocks, BLK, 2 * feat_width
    )
    local_ids = neighbour_blocks - (position - 1) * blocks
    picked = jnp.take(extended, local_ids, axis=0).reshape(blocks, NB * BLK, 2 * feat_width)
    near_key = picked[:, :, :feat_width].reshape(blocks, NB * BLK, head_count, head_size)
    near_val = picked[:, :, feat_width:].reshape(blocks, NB * BLK, head_count, head_size)
    q_blocks = q_heads.reshape(blocks, BLK, head_count, head_size)
    g_blocks = g_heads.reshape(blocks, BLK, head_count, head_size)
    logits = (
        jnp.einsum("bthd,bshd->bhts", q_blocks, near_key, preferred_element_type=jnp.float32)
        * soft_scale
    )
    row_peak = jnp.max(logits, axis=-1, keepdims=True)
    exp_terms = jnp.exp(logits - row_peak)
    soft_probs = exp_terms / jnp.sum(exp_terms, axis=-1, keepdims=True)
    probs_bf = soft_probs.astype(jnp.bfloat16)
    near_out = jnp.einsum(
        "bhts,bshd->bthd", probs_bf, near_val, preferred_element_type=jnp.float32
    ).reshape(row_count, head_count, head_size)
    layer_out = (
        (lin_scale * linear_out + near_out).reshape(row_count, feat_width).astype(jnp.bfloat16)
    )
    prob_grad = jnp.einsum(
        "bthd,bshd->bhts", g_blocks, near_val, preferred_element_type=jnp.float32
    )
    inner_sum = jnp.sum(soft_probs * prob_grad, axis=-1, keepdims=True)
    dlogit = (soft_probs * (prob_grad - inner_sum) * soft_scale).astype(jnp.bfloat16)
    dq_near = jnp.einsum(
        "bhts,bshd->bthd", dlogit, near_key, preferred_element_type=jnp.float32
    ).reshape(row_count, head_count, head_size)
    dk_near = jnp.einsum(
        "bhts,bthd->bshd", dlogit, q_blocks, preferred_element_type=jnp.float32
    ).reshape(blocks * NB, BLK, feat_width)
    dv_near = jnp.einsum(
        "bhts,bthd->bshd", probs_bf, g_blocks, preferred_element_type=jnp.float32
    ).reshape(blocks * NB, BLK, feat_width)
    dpicked = jnp.concatenate([dk_near, dv_near], axis=-1)
    onehot = (
        local_ids.reshape(-1)[:, None] == jnp.arange(2 * blocks, dtype=jnp.int32)[None, :]
    ).astype(jnp.float32)
    ext_grad = jnp.einsum("nm,ntc->mtc", onehot, dpicked, precision=lax.Precision.HIGHEST).reshape(
        2 * row_count, 2 * feat_width
    )
    back_mat = (
        jnp.einsum("thd,shd->hts", g_heads, v_heads, preferred_element_type=jnp.float32) * decay_mat
    ).astype(jnp.bfloat16)
    later_bf = later.astype(jnp.bfloat16)
    dq_lin = jnp.einsum("hts,shd->thd", back_mat, k_heads, preferred_element_type=jnp.float32)
    dq_lin = lin_scale * (
        dq_lin
        + growth * jnp.einsum("the,hde->thd", g_heads, state_bf, preferred_element_type=jnp.float32)
    )
    dk_lin = lin_scale * jnp.einsum(
        "hts,thd->shd", back_mat, q_heads, preferred_element_type=jnp.float32
    )
    dk_lin = dk_lin + fading * jnp.einsum(
        "she,hde->shd", v_heads, later_bf, preferred_element_type=jnp.float32
    )
    dv_lin = lin_scale * jnp.einsum(
        "hts,the->she", intra_mat, g_heads, preferred_element_type=jnp.float32
    )
    dv_lin = dv_lin + fading * jnp.einsum(
        "shd,hde->she", k_heads, later_bf, preferred_element_type=jnp.float32
    )
    query_delta = (dq_lin + dq_near).reshape(row_count, feat_width).astype(jnp.bfloat16)
    lin_kv = jnp.concatenate(
        [dk_lin.reshape(row_count, feat_width), dv_lin.reshape(row_count, feat_width)], axis=1
    )
    own_grad = (lin_kv + ext_grad[row_count:]).astype(jnp.bfloat16)
    prev_grad = ext_grad[:row_count].astype(jnp.bfloat16)
    query_part = jnp.einsum("td,tc->dc", tokens, query_delta, preferred_element_type=jnp.float32)
    kv_part = jnp.einsum("td,tc->dc", tokens, own_grad, preferred_element_type=jnp.float32)
    tokens_back = jnp.einsum(
        "tc,dc->td", query_delta, query_weight, preferred_element_type=jnp.float32
    )
    tokens_back = tokens_back + back_project(own_grad, key_weight, value_weight, feat_width)
    next_grad = shifted(prev_grad, ("group", "span"), -1)
    kv_part = kv_part + jnp.einsum(
        "td,tc->dc", tokens, next_grad, preferred_element_type=jnp.float32
    )
    tokens_back = tokens_back + back_project(next_grad, key_weight, value_weight, feat_width)
    grad_norm = 1.0 / math.sqrt(row_count * devices)
    key_part = kv_part[:, :feat_width]
    value_part = kv_part[:, feat_width:]
    summed = lax.psum((query_part, key_part, value_part), ("group", "span"))
    weight_grads = tuple(((part_sum * grad_norm).astype(jnp.bfloat16) for part_sum in summed))
    return (
        layer_out,
        tokens_back.astype(jnp.bfloat16),
        weight_grads[0],
        weight_grads[1],
        weight_grads[2],
    )


def solution(mesh):
    return jax.shard_map(
        shards,
        mesh=mesh,
        in_specs=(
            P(("group", "span"), None),
            P(),
            P(),
            P(),
            P(None, ("group", "span")),
            P(("group", "span"), None),
            P(("group", "span"), None),
        ),
        out_specs=(P(("group", "span"), None), P(("group", "span"), None), P(), P(), P()),
        check_vma=False,
    )
```

profile of v0, /device:TPU:1, one launch (start us, length us, event | category | flops | bytes accessed | tf_op | source)
XLA Modules:
  0.0 1195.2 jit_solution(11433108022394367070)
XLA Ops:
  9.8 2.2 convolution_convert_fusion.1
  14.6 2.8 convolution_convert_fusion
  19.7 1.9 all_gather_reshape.6
  21.7 1.9 pad_maximum_fusion
  23.5 5.6 collective-permute-start
  32.6 72.9 %all-reduce = f32[2048]{0:T(1024)S(1)} all-reduce(f32[2048]{0:T(1024)S(1)} %dynamic-update-slice), channel_id=2, replica_groups=mesh['group'=4,'span'=32] {'group','span'}, use_global_device_ids=true, to_apply=%add | all-reduce | flops 2048 | bytes 16384
  105.6 2.3 convolution_bitcast_fusion.6
  107.9 2.1 fusion.35
  111.4 2.0 gather_fusion
  113.4 3.9 copy.61
  117.3 1.9 broadcast_select_fusion
  119.2 1.5 fusion.65
  120.7 4.6 fusion.66
  125.3 4.1 convolution_bitcast_fusion.1
  129.4 2.9 reshape.204
  132.3 3.9 copy.69
  136.2 4.0 fusion.67
  140.2 19.0 %fusion.16 = f32[1,512,16,64]{1,3,2,0:T(8,128)} fusion(bf16[128,16,64]{0,2,1:T(8,128)(2,1)S(1)} %bitcast.223, f32[16,512,128]{1,2,0:T(8,128)} %fusion.67, f32[16,128,512]{2,1,0:T(8,128)} %get-tuple-element.182, f32[16,128]{1,0:T(8,128)S(1)} %get-tuple-element.181), kind=kOutput, calls=%fused_computation.30 | convolution fusion | flops 141560320 | bytes 10756096 | tf_op jit(solution)/shard_map/bhts,bthd->bshd/dot_general | solution.py:132
  159.2 2.9 reshape.203
  162.1 4.1 copy.68
  166.1 6.8 fusion.2
  173.9 2.1 slice.55
  177.1 5.9 collective-permute-start.1
  183.0 201.1 %all-gather.6.cloned.1.call-done = f32[128,16,4096]{2,1,0:T(8,128)} async-done(((f32[1,16,4096]{2,1,0:T(8,128)}), f32[128,16,4096]{2,1,0:T(8,128)}) %all-gather.6.cloned.1.call-update) | async-done | bytes 33554448 | tf_op jit(solution)/shard_map/all_gather | solution.py:16
  384.1 105.3 %while.27 = (s32[]{:T(128)}, f32[16,4096]{1,0:T(8,128)S(1)}, s32[]{:T(128)}, f32[128,16]{1,0:T(8,128)S(1)}, f32[128,16,4096]{2,1,0:T(8,128)}, /*index=5*/s32[]{:T(128)}, s32[]{:T(128)}, s32[]{:T(128)}, s32[]{:T(128)}) while((s32[]{:T(128)}, f32[16,4096]{1,0:T(8,128)S(1)}, s32[]{:T(128)}, f32[128,16]{1,0:T(8,128)S(1)}, ...), condition=%wide.region_7.8_spmd, body=%wide.region_6.7_spmd.sunk | while | flops 131078 | bytes 786779 | solution.py:25
  490.3 2.1 fusion.30
  492.4 2.1 copy.66
  494.5 2.2 fusion.32
  496.7 2.1 copy.67
  498.7 237.8 %all-gather.4.cloned.1.call-done = f32[128,16,4096]{2,1,0:T(8,128)} async-done(((f32[1,16,4096]{2,1,0:T(8,128)}), f32[128,16,4096]{2,1,0:T(8,128)}) %all-gather.4.cloned.1.call-update) | async-done | bytes 33554448 | tf_op jit(solution)/shard_map/all_gather | solution.py:16
  736.5 57.2 %while.26 = (s32[]{:T(128)}, f32[16,4096]{1,0:T(8,128)S(1)}, s32[]{:T(128)}, f32[128,16]{1,0:T(8,128)}, f32[128,16,4096]{2,1,0:T(8,128)}, /*index=5*/s32[]{:T(128)}, s32[]{:T(128)}, s32[]{:T(128)}) while((s32[]{:T(128)}, f32[16,4096]{1,0:T(8,128)S(1)}, s32[]{:T(128)}, f32[128,16]{1,0:T(8,128)}, f32[128,16,4096]{2,1,0:T(8,128)}, ...), condition=%wide.region_2.3_spmd, body=%wide.region_1.2_spmd.sunk | while | flops 131077 | bytes 786759 | solution.py:25
  794.0 2.1 fusion.28
  796.1 18.5 %fusion.38 = bf16[128,16,64]{0,2,1:T(8,128)(2,1)} fusion(f32[128,16,64]{0,2,1:T(8,128)} %fusion.28, bf16[512,16,64]{0,2,1:T(8,128)(2,1)} %bitcast.242, f32[16,512,128]{1,2,0:T(8,128)} %fusion.67, f32[16,128,512]{2,1,0:T(8,128)} %get-tuple-element.182, f32[16,128]{1,0:T(8,128)S(1)} %copy-done.19), kind=kOutput, calls=%fused_computation.67 | convolution fusion | flops 141822464 | bytes 10231808 | tf_op jit(solution)/shard_map/bhts,bshd->bthd/dot_general | solution.py:129
  814.6 1.9 fusion.40
  816.5 3.6 convolution_bitcast_fusion
  821.4 2.3 add_bitcast_fusion
  823.7 4.1 fusion.64
  828.7 1.6 convolution_bitcast_fusion.9
  830.4 2.7 fusion.46
  835.1 2.6 fusion.68
  837.7 2.4 fusion.50
  841.0 2.5 fusion.39
  843.5 322.3 %all-reduce.4.cloned.1.call-done = (f32[1024,1024]{0,1:T(8,128)}, f32[1024,1024]{0,1:T(8,128)}, f32[1024,1024]{0,1:T(8,128)}) async-done(((f32[1024,1024]{0,1:T(8,128)}, f32[1024,1024]{0,1:T(8,128)}, f32[1024,1024]{0,1:T(8,128)}), (f32[1024,1024]{0,1:T(8,128)}, f32[1024,1024]{0,1:T(8,128)}, f32[1024,1024]{0,1:T(8,128)})) %all-reduce.4.cloned.1.call-update) | async-done | bytes 12582928 | tf_op jit(solution)/shard_map/psum | solution.py:186
  1165.8 4.1 multiply_convert_fusion.2
  1169.9 3.9 copy.71
  1173.8 6.7 multiply_convert_fusion
  1180.5 3.9 copy.73
  1184.5 3.9 copy.72
  (340 shorter events, 179.2 us)
Async XLA Ops:
  7.2 6.3 copy-start
  7.2 6.3 copy-start.2
  7.2 376.9 %all-gather.6.cloned.1.call-start = ((), (), s32[]{:S(2)}) async-start(), calls=%async_computation.1 | async-start | bytes 33816576 | tf_op jit(solution)/shard_map/all_gather | solution.py:16
  9.8 98.2 %copy-start.5 = (bf16[128,1024]{0,1:T(8,128)(2,1)}, bf16[128,1024]{0,1:T(8,128)(2,1)S(1)}, u32[]{:S(2)}) copy-start(bf16[128,1024]{0,1:T(8,128)(2,1)S(1)} %copy.62) | copy-start | bytes 786436
  12.2 19.0 %copy-start.3 = (bf16[128,1024]{0,1:T(8,128)(2,1)}, bf16[128,1024]{0,1:T(8,128)(2,1)S(1)}, u32[]{:S(2)}) copy-start(bf16[128,1024]{0,1:T(8,128)(2,1)S(1)} %copy.58) | copy-start | bytes 786436
  13.4 15.8 %copy-start.20 = (s32[1,4]{1,0:T(1,128)S(1)}, s32[1,4]{1,0:T(1,128)}, u32[]{:S(2)}) copy-start(s32[1,4]{1,0:T(1,128)} %param.16) | copy-start | bytes 52
  13.4 723.1 %all-gather.4.cloned.1.call-start = ((), (), s32[]{:S(2)}) async-start(), calls=%async_computation | async-start | bytes 33816576 | tf_op jit(solution)/shard_map/all_gather | solution.py:16
  13.9 0.7 copy-start.12
  14.6 16.0 %copy-start.8 = (bf16[128,1024]{0,1:T(8,128)(2,1)}, bf16[128,1024]{0,1:T(8,128)(2,1)S(1)}, u32[]{:S(2)}) copy-start(bf16[128,1024]{0,1:T(8,128)(2,1)S(1)} %copy.57) | copy-start | bytes 786436
  18.6 87.0 %copy-start.11 = (bf16[128,1024]{0,1:T(8,128)(2,1)}, bf16[128,1024]{0,1:T(8,128)(2,1)S(1)}, u32[]{:S(2)}) copy-start(bf16[128,1024]{0,1:T(8,128)(2,1)S(1)} %copy.59) | copy-start | bytes 786436
  21.6 1144.2 %all-reduce.4.cloned.1.call-start = ((), (), s32[]{:S(2)}) async-start(), calls=%async_computation.2 | async-start | bytes 25165824 | tf_op jit(solution)/shard_map/psum | solution.py:186
  23.5 86.5 %collective-permute-start = (bf16[128,2048]{1,0:T(8,128)(2,1)}, bf16[128,2048]{1,0:T(8,128)(2,1)}, u32[]{:S(2)}, u32[]{:S(2)}) collective-permute-start(bf16[128,2048]{1,0:T(8,128)(2,1)} %pad_maximum_fusion), channel_id=1, source_target_pairs={{0,1},{1,2},{2,3},{3,4},{4,5},{5,6},{6,7},{7,8},{8,9},{9,10},{10,1... | collective-permute-start | bytes 1572872 | tf_op jit(solution)/shard_map/ppermute | solution.py:31
  31.2 1.1 copy-start.14
  117.3 3.4 copy-start.4
  119.2 6.2 copy-start.6
  125.3 14.8 %copy-start.18 = (f32[16,128]{1,0:T(8,128)}, f32[16,128]{1,0:T(8,128)S(1)}, u32[]{:S(2)}) copy-start(f32[16,128]{1,0:T(8,128)S(1)} %get-tuple-element.181) | copy-start | bytes 24580
  173.9 316.4 %copy-start.9 = (bf16[128,1024]{0,1:T(8,128)(2,1)S(1)}, bf16[128,1024]{0,1:T(8,128)(2,1)}, u32[]{:S(2)}) copy-start(bf16[128,1024]{0,1:T(8,128)(2,1)} %copy-done.8) | copy-start | bytes 786436
  177.1 644.3 %collective-permute-start.1 = (bf16[128,2048]{1,0:T(8,128)(2,1)}, bf16[128,2048]{1,0:T(8,128)(2,1)}, u32[]{:S(2)}, u32[]{:S(2)}) collective-permute-start(bf16[128,2048]{1,0:T(8,128)(2,1)} %bitcast.208), channel_id=1, source_target_pairs={{1,0},{2,1},{3,2},{4,3},{5,4},{6,5},{7,6},{8,7},{9,8},{10,9},{11,1... | collective-permute-start | bytes 1572872 | tf_op jit(solution)/shard_map/ppermute | solution.py:31
  489.4 0.6 copy-start.17
  496.7 299.4 %copy-start.19 = (f32[16,128]{1,0:T(8,128)S(1)}, f32[16,128]{1,0:T(8,128)}, u32[]{:S(2)}) copy-start(f32[16,128]{1,0:T(8,128)} %copy-done.18) | copy-start | bytes 24580
  827.8 0.9 copy-start.10
  828.7 4.6 copy-start.7
  828.7 4.6 copy-start.13
  833.3 1.8 copy-start.16
  835.1 5.9 copy-start.1
  835.1 5.9 copy-start.15
Sparse Core Ops, SparseCore 0:
  13.5 370.5 all-gather.5
  385.8 350.6 all-gather.3
  827.9 337.8 all-reduce.3
where the time goes:
time: 1210 us; the launch traced here: 1200 us
  waiting for transfers between devices  761 us (63%)
  other arithmetic  154 us (13%)
  matrix products  98.5 us (8%)
  local copies, waits for them, and re-layouts  78.4 us (6%)
  blocking collectives  72.9 us (6%)
  between operations  14.4 us (1%)
    all_gather x2, waiting for transfers between devices, prefix(): gathered = jax.tree.map(lambda a: lax.all_gather(a, axis), part)  439 us
    psum x1, waiting for transfers between devices, shards(): summed = lax.psum((query_part, key_part, value_part), ('group', 'span'))  322 us
    add x127, other arithmetic, join_carry(): jnp.exp(later[0])[:, None] * earlier[1] + later[1]  135 us
    unnamed x1, blocking collectives  72.9 us
  transfers between devices with their start and end apart: 5, of which 3 were waited for; matrix products, arithmetic and copies ran while one was open for 25% of the time, Pallas kernels for 0%

commit v1 on v0

v1 whole, which is shorter than its diff:
```python
import functools
import math

import jax
import jax.numpy as jnp
from jax import lax
from jax.experimental import pallas as pl
from jax.experimental.pallas import tpu as pltpu
from jax.sharding import Mesh
from jax.sharding import PartitionSpec as P

BF = jnp.bfloat16
F32 = jnp.float32
AX = ("yl", "c", "x", "z", "yh")
NEAR8 = ("z", "yh")
FAR16 = ("yl", "c", "x")
PLANE = ("yl", "x", "z", "yh")
SEG = 128
PAIR = 128
DH = 64
DEVS = 128
VMEM = pltpu.VMEM
HIGH = lax.Precision.HIGHEST


def dot(a, b, ca, cb, precision=None):
    return lax.dot_general(
        a, b, (((ca,), (cb,)), ((), ())), precision=precision, preferred_element_type=F32
    )


def iota(shape, axis):
    return lax.broadcasted_iota(jnp.int32, shape, axis)


def params(mib):
    return pltpu.CompilerParams(vmem_limit_bytes=mib << 20)


def cost(flops, moved, trans=0):
    return pl.CostEstimate(flops=flops, bytes_accessed=moved, transcendentals=trans)


def project_kernel(lin_scale, tok, tok_col, wq, wk, wv, decay, cot, q_out, kv_out, run_out, runt_out, tokt_out, msg):
    step = pl.program_id(0)
    x = tok[...]
    q = dot(x, wq[...], 1, 0).astype(BF)
    k = dot(x, wk[...], 1, 0).astype(BF)
    v = dot(x, wv[...], 1, 0).astype(BF)
    q_out[...] = q
    kv_out[0] = k
    kv_out[1] = v
    tokt_out[...] = tok_col[...].T
    ld = decay[...]
    heads = ld.shape[0]
    lower = (iota((SEG, SEG), 0) >= iota((SEG, SEG), 1)).astype(F32)
    runt = dot(lower, ld, 1, 1, HIGH)
    runt_out[...] = runt

    @pl.when(step == 0)
    def _():
        run_out[...] = dot(ld, lower, 1, 1, HIGH)

    head_of = iota((SEG, PAIR), 1) // DH
    head_id = iota((SEG, heads), 1)
    rows = iota((8, PAIR), 0)
    for half in range(2):
        cols = slice(half * PAIR, (half + 1) * PAIR)
        first = (step * 2 + half) * 2
        c0 = jnp.sum(jnp.where(head_id == first, runt, 0.0), axis=1, keepdims=True)
        c1 = jnp.sum(jnp.where(head_id == first + 1, runt, 0.0), axis=1, keepdims=True)
        run = jnp.where(head_of == 0, c0, c1)
        total = run[SEG - 1 : SEG, :]
        weighted = (v[:, cols].astype(F32) * jnp.exp(total - run)).astype(BF)
        scaled = (cot[:, cols].astype(F32) * jnp.exp(run)).astype(BF)
        full_s = dot(k[:, cols], weighted, 0, 0)
        full_g = dot(q[:, cols], scaled, 0, 0) * lin_scale
        high = total.astype(BF).astype(F32)
        mid = (total - high).astype(BF).astype(F32)
        low = total - high - mid
        tail = jnp.where(rows == 0, high, jnp.where(rows == 1, mid, jnp.where(rows == 2, low, 0.0)))
        tail = jnp.broadcast_to(tail[None], (8, 8, PAIR))
        lanes = iota((DH, PAIR), 1) < DH
        for part, full in ((0, full_s), (1, full_g)):
            own = jnp.where(lanes, full[:DH], full[DH:]).reshape(8, 8, PAIR)
            both = jnp.concatenate([own, tail], axis=1).reshape(PAIR, PAIR)
            msg[part, half * PAIR : (half + 1) * PAIR, :] = both.astype(BF)


def project(tokens, wq, wk, wv, log_decay, cot, lin_scale):
    rows, width = tokens.shape
    heads = log_decay.shape[0]
    steps = width // 256
    col = pl.BlockSpec((rows, 256), lambda i: (0, i))
    weight = pl.BlockSpec((width, 256), lambda i: (0, i))
    return pl.pallas_call(
        functools.partial(project_kernel, lin_scale),
        grid=(steps,),
        in_specs=[
            pl.BlockSpec((rows, width), lambda i: (0, 0)),
            col,
            weight,
            weight,
            weight,
            pl.BlockSpec((heads, rows), lambda i: (0, 0)),
            col,
        ],
        out_specs=[
            col,
            pl.BlockSpec((2, rows, 256), lambda i: (0, 0, i)),
            pl.BlockSpec((heads, rows), lambda i: (0, 0)),
            pl.BlockSpec((rows, heads), lambda i: (0, 0)),
            pl.BlockSpec((256, rows), lambda i: (i, 0)),
            pl.BlockSpec((2, 2 * PAIR, PAIR), lambda i: (0, i, 0)),
        ],
        out_shape=[
            jax.ShapeDtypeStruct((rows, width), BF),
            jax.ShapeDtypeStruct((2, rows, width), BF),
            jax.ShapeDtypeStruct((heads, rows), F32),
            jax.ShapeDtypeStruct((rows, heads), F32),
            jax.ShapeDtypeStruct((width, rows), BF),
            jax.ShapeDtypeStruct((2, width, PAIR), BF),
        ],
        compiler_params=params(40),
        cost_estimate=cost(6 * rows * width * width, 6 * width * width + 12 * rows * width),
        name="project",
    )(tokens, tokens, wq, wk, wv, log_decay, cot)


def scan_kernel(place, got, out, xs, decays, states):
    both = got[...].astype(F32)
    xs[...] = both[:, :8, :]
    total = both[:, 8:9, :] + both[:, 9:10, :] + both[:, 10:11, :]
    decays[...] = jnp.broadcast_to(jnp.exp(total), decays.shape)
    backward = place[0] >= DEVS // 2

    def one(i, state):
        at = jnp.where(backward, DEVS - 1 - i, i)
        states[at] = state
        return decays[at] * state + xs[at]

    lax.fori_loop(0, DEVS, one, jnp.zeros((8, PAIR), F32), unroll=8)
    out[...] = states[...].reshape(DEVS * 8, PAIR).astype(BF)


def scan(place, got):
    whole = pl.BlockSpec(memory_space=VMEM)
    return pl.pallas_call(
        scan_kernel,
        in_specs=[pl.BlockSpec(memory_space=pltpu.SMEM), whole],
        out_specs=whole,
        out_shape=jax.ShapeDtypeStruct((DEVS * 8, PAIR), BF),
        scratch_shapes=[VMEM((DEVS, 8, PAIR), F32)] * 3,
        compiler_params=params(24),
        cost_estimate=cost(2 * DEVS * 8 * PAIR, 4 * DEVS * 16 * PAIR),
        name="scan",
    )(place, got)


def near_kernel(lin_scale, place, blocks, q_ref, kv, pkv, cot, run_rows, runt, out, dq_out, own, prev):
    pair = pl.program_id(0)
    soft_scale = 1.0 / math.sqrt(DH)
    n_own = jnp.int32(0)
    n_prev = jnp.int32(0)
    for j in range(blocks.shape[1]):
        n_own += (blocks[0, j] == place[0]).astype(jnp.int32)
        n_prev += (blocks[0, j] == place[0] - 1).astype(jnp.int32)
    is_own = iota((1, 2 * SEG), 1) < SEG
    times = jnp.where(is_own, n_own, n_prev)
    bias = jnp.where(times > 0, 0.0, -1e30)
    times = times.astype(F32)
    q = q_ref[...]
    g = cot[...]
    kk = jnp.concatenate([kv[0], pkv[0]], axis=0)
    vv = jnp.concatenate([kv[1], pkv[1]], axis=0)
    head_of = iota((SEG, PAIR), 1) // DH
    head_of2 = iota((2 * SEG, PAIR), 1) // DH
    lower = iota((SEG, SEG), 0) >= iota((SEG, SEG), 1)
    head_id = iota(runt.shape, 1)
    zero = jnp.zeros((), BF)
    res = []
    for i in range(2):
        mine = head_of == i
        col = jnp.sum(jnp.where(head_id == pair * 2 + i, runt[...], 0.0), axis=1, keepdims=True)
        row = run_rows[0, i : i + 1, :]
        dec = jnp.where(lower, jnp.exp(jnp.minimum(col - row, 0.0)), 0.0) * lin_scale
        scores = dot(jnp.where(mine, q, zero), kk, 1, 1)
        pgrad = dot(jnp.where(mine, g, zero), vv, 1, 1)
        logits = scores * soft_scale + bias
        peak = jnp.max(logits, axis=1, keepdims=True)
        terms = jnp.exp(logits - peak) * times
        probs = terms * (1.0 / jnp.sum(terms, axis=1, keepdims=True))
        inner = jnp.sum(probs * pgrad, axis=1, keepdims=True)
        dlog = probs * (pgrad - inner) * soft_scale
        a = jnp.concatenate(
            [probs[:, :SEG] + scores[:, :SEG] * dec, probs[:, SEG:]], axis=1
        ).astype(BF)
        b = jnp.concatenate([dlog[:, :SEG] + pgrad[:, :SEG] * dec, dlog[:, SEG:]], axis=1).astype(BF)
        res.append((dot(a, vv, 1, 0), dot(b, kk, 1, 0), dot(b, q, 0, 0), dot(a, g, 0, 0)))
    out[...] = jnp.where(head_of == 0, res[0][0], res[1][0])
    dq_out[...] = jnp.where(head_of == 0, res[0][1], res[1][1])
    for part in range(2):
        both = jnp.where(head_of2 == 0, res[0][2 + part], res[1][2 + part])
        own[part] = both[:SEG]
        prev[part] = both[SEG:].astype(BF)


def near(place, blocks, q, kv, pkv, cot, run, runt, lin_scale):
    rows, width = q.shape
    heads = run.shape[0]
    smem = pl.BlockSpec(memory_space=pltpu.SMEM)
    col = pl.BlockSpec((rows, PAIR), lambda i: (0, i))
    two = pl.BlockSpec((2, rows, PAIR), lambda i: (0, 0, i))
    return pl.pallas_call(
        functools.partial(near_kernel, lin_scale),
        grid=(width // PAIR,),
        in_specs=[
            smem,
            smem,
            col,
            two,
            two,
            col,
            pl.BlockSpec((1, 2, rows), lambda i: (i, 0, 0)),
            pl.BlockSpec((rows, heads), lambda i: (0, 0)),
        ],
        out_specs=[col, col, two, two],
        out_shape=[
            jax.ShapeDtypeStruct((rows, width), F32),
            jax.ShapeDtypeStruct((rows, width), F32),
            jax.ShapeDtypeStruct((2, rows, width), F32),
            jax.ShapeDtypeStruct((2, rows, width), BF),
        ],
        compiler_params=params(32),
        cost_estimate=cost(4000 * 1000 * 1000, 16 * 1000 * 1000, heads * 3 * SEG * SEG),
        name="near",
    )(place, blocks, q, kv, pkv, cot, run.reshape(heads // 2, 2, rows), runt)


def join_kernel(lin_scale, near_out, dq_in, own, nxt, q, kv, cot, runt, states, layer, delta):
    pair = pl.program_id(0)
    head_of = iota((SEG, PAIR), 1) // DH
    head_id = iota(runt.shape, 1)
    c0 = jnp.sum(jnp.where(head_id == pair * 2, runt[...], 0.0), axis=1, keepdims=True)
    c1 = jnp.sum(jnp.where(head_id == pair * 2 + 1, runt[...], 0.0), axis=1, keepdims=True)
    run = jnp.where(head_of == 0, c0, c1)
    growth = jnp.exp(run) * lin_scale
    fading = jnp.exp(run[SEG - 1 : SEG, :] - run)
    diag = iota((PAIR, PAIR), 0) // DH == iota((PAIR, PAIR), 1) // DH
    zero = jnp.zeros((), BF)

    def blocks(part):
        one = states[part, 0]
        return jnp.where(diag, jnp.concatenate([one, one], axis=0), zero)

    before, after = blocks(0), blocks(1)
    layer[...] = (near_out[...] + growth * dot(q[...], before, 1, 0)).astype(BF)
    delta[0, :, :PAIR] = (dq_in[...] + growth * dot(cot[...], before, 1, 1)).astype(BF)
    dk = own[0] + fading * dot(kv[1], after, 1, 1)
    dv = own[1] + fading * dot(kv[0], after, 1, 0)
    delta[0, :, PAIR : 2 * PAIR] = (dk + nxt[0].astype(F32)).astype(BF)
    delta[0, :, 2 * PAIR :] = (dv + nxt[1].astype(F32)).astype(BF)


def join(near_out, dq, own, nxt, q, kv, cot, runt, states, lin_scale):
    rows, width = q.shape
    heads = runt.shape[1]
    pairs = width // PAIR
    col = pl.BlockSpec((rows, PAIR), lambda i: (0, i))
    two = pl.BlockSpec((2, rows, PAIR), lambda i: (0, 0, i))
    return pl.pallas_call(
        functools.partial(join_kernel, lin_scale),
        grid=(pairs,),
        in_specs=[
            col,
            col,
            two,
            two,
            col,
            two,
            col,
            pl.BlockSpec((rows, heads), lambda i: (0, 0)),
            pl.BlockSpec((2, 1, DH, PAIR), lambda i: (0, i, 0, 0)),
        ],
        out_specs=[col, pl.BlockSpec((1, rows, 3 * PAIR), lambda i: (i, 0, 0))],
        out_shape=[
            jax.ShapeDtypeStruct((rows, width), BF),
            jax.ShapeDtypeStruct((pairs, rows, 3 * PAIR), BF),
        ],
        compiler_params=params(32),
        cost_estimate=cost(8 * rows * PAIR * PAIR * pairs, 24 * rows * width),
        name="join",
    )(near_out, dq, own, nxt, q, kv, cot, runt, states)


def back_kernel(delta, wq, wk, wv, out, total):
    step = pl.program_id(0)

    @pl.when(step == 0)
    def _():
        total[...] = jnp.zeros_like(total)

    acc = total[...]
    for part, w in enumerate((wq, wk, wv)):
        for half in range(2):
            acc += dot(
                delta[half, :, part * PAIR : (part + 1) * PAIR],
                w[:, half * PAIR : (half + 1) * PAIR],
                1,
                1,
            )
    total[...] = acc

    @pl.when(step == pl.num_programs(0) - 1)
    def _():
        out[...] = acc.astype(BF)


def back(delta, wq, wk, wv):
    pairs, rows, _ = delta.shape
    width = wq.shape[0]
    weight = pl.BlockSpec((width, 2 * PAIR), lambda i: (0, i))
    return pl.pallas_call(
        back_kernel,
        grid=(pairs // 2,),
        in_specs=[pl.BlockSpec((2, rows, 3 * PAIR), lambda i: (i, 0, 0)), weight, weight, weight],
        out_specs=pl.BlockSpec((rows, width), lambda i: (0, 0)),
        out_shape=jax.ShapeDtypeStruct((rows, width), BF),
        scratch_shapes=[VMEM((rows, width), F32)],
        compiler_params=params(32),
        cost_estimate=cost(6 * rows * width * width, 6 * width * width + 8 * rows * width),
        name="back",
    )(delta, wq, wk, wv)


def outer_kernel(tokt, delta, out):
    acc = dot(tokt[0], delta[0], 1, 0)
    for i in range(1, delta.shape[0]):
        acc += dot(tokt[i], delta[i], 1, 0)
    out[...] = acc.astype(BF)


def outer(tokt, delta):
    near_count, rows, cols = delta.shape
    width = tokt.shape[1]
    return pl.pallas_call(
        outer_kernel,
        grid=(4,),
        in_specs=[
            pl.BlockSpec((near_count, width // 4, rows), lambda i: (0, i, 0)),
            pl.BlockSpec((near_count, rows, cols), lambda i: (0, 0, 0)),
        ],
        out_specs=pl.BlockSpec((width // 4, cols), lambda i: (i, 0)),
        out_shape=jax.ShapeDtypeStruct((width, cols), BF),
        compiler_params=params(32),
        cost_estimate=cost(
            2 * near_count * rows * cols * width, 2 * near_count * rows * (width + cols)
        ),
        name="outer",
    )(tokt, delta)


def place_kernel(core, mine, other, gq, gk, gv):
    del core
    step = pl.program_id(0)

    def put(src):
        for j in range(8):
            for part, o in enumerate((gq, gk, gv)):
                o[:, j * PAIR : (j + 1) * PAIR] = src[0, j, :, part * PAIR : (part + 1) * PAIR]

    @pl.when(step < 8)
    def _():
        put(mine)

    @pl.when(step >= 8)
    def _():
        put(other)


def place_all(core, mine, other):
    blocks, near_count, rows, cols = mine.shape
    width = 2 * blocks * rows

    def where(i, core):
        half = i // 8
        piece = i % 8
        c = jnp.where(half == 0, core[0], 1 - core[0])
        return ((piece // 4) * 8 + c * 4 + piece % 4, 0)

    grad = pl.BlockSpec((rows, width), where)
    return pl.pallas_call(
        place_kernel,
        grid_spec=pltpu.PrefetchScalarGridSpec(
            num_scalar_prefetch=1,
            grid=(16,),
            in_specs=[
                pl.BlockSpec(
                    (1, near_count, rows, cols), lambda i, core: (jnp.minimum(i, 7), 0, 0, 0)
                ),
                pl.BlockSpec(
                    (1, near_count, rows, cols), lambda i, core: (jnp.maximum(i - 8, 0), 0, 0, 0)
                ),
            ],
            out_specs=[grad, grad, grad],
        ),
        out_shape=[jax.ShapeDtypeStruct((width, width), BF)] * 3,
        compiler_params=params(32),
        cost_estimate=cost(0, 12 * width * width),
        name="place",
    )(core, mine, other)


def shards(tokens, wq, wk, wv, log_decay, neighbour_blocks, cot):
    rows, width = tokens.shape
    lin_scale = 1.0 / (DH * math.sqrt(rows))
    place = lax.axis_index(AX).astype(jnp.int32).reshape(1)
    core = lax.axis_index("c").astype(jnp.int32).reshape(1)

    q, kv, run, runt, tokt, msg = project(tokens, wq, wk, wv, log_decay, cot, lin_scale)
    got = lax.all_to_all(msg.reshape(DEVS, 16, PAIR), AX, 0, 0)
    pkv = lax.ppermute(kv, AX, [(i, i + 1) for i in range(DEVS - 1)])
    tokt8 = lax.all_gather(tokt, NEAR8)
    near_out, dq, own, prev = near(
        place, neighbour_blocks, q, kv, pkv, cot, run, runt, lin_scale
    )
    states = scan(place, got)
    nxt = lax.ppermute(prev, AX, [(i + 1, i) for i in range(DEVS - 1)])
    states = lax.all_to_all(states.reshape(DEVS, 8, PAIR), AX, 0, 0)
    states = states.reshape(2, width // PAIR, DH, PAIR)
    layer, delta = join(near_out, dq, own, nxt, q, kv, cot, runt, states, lin_scale)

    delta8 = lax.all_to_all(delta, NEAR8, 0, 0)
    partial = outer(tokt8, delta8)
    parts = lax.all_to_all(partial.reshape(16, width // 16, 3 * PAIR), FAR16, 0, 0)
    grad_norm = 1.0 / math.sqrt(rows * DEVS)
    piece = (jnp.sum(parts.astype(F32), axis=0) * grad_norm).astype(BF)
    plane = lax.all_to_all(jnp.broadcast_to(piece[None], (DEVS // 2, *piece.shape)), PLANE, 0, 0)
    other = lax.ppermute(plane, "c", [(0, 1), (1, 0)])
    tokens_grad = back(delta, wq, wk, wv)
    shape = (8, 8, *piece.shape)
    gq, gk, gv = place_all(core, plane.reshape(shape), other.reshape(shape))
    return layer, tokens_grad, gq, gk, gv


def solution(mesh):
    chips = Mesh(mesh.devices.reshape(2, 2, 4, 4, 2), AX)
    tok = P(AX, None)
    return jax.shard_map(
        shards,
        mesh=chips,
        in_specs=(tok, P(), P(), P(), P(None, AX), tok, tok),
        out_specs=(tok, tok, P(), P(), P()),
        check_vma=False,
    )
```

time: 1210 us -> 207 us (0.17); the launches traced: 1200 us -> 206 us
  waiting for transfers between devices: 761 us -> 10.3 us
  other arithmetic: 154 us -> 0.12 us
  matrix products: 98.5 us -> 0 us
  local copies, waits for them, and re-layouts: 78.4 us -> 13.1 us
  Pallas kernels: 0 us -> 35.2 us
  blocking collectives: 72.9 us -> 103 us
  starting transfers between devices: 11.7 us -> 30 us
    all_gather x2 -> x1, waiting for transfers between devices: 439 us -> 0.01 us  [shards(): tokt8 = lax.all_gather(tokt, NEAR8)]
    psum x1 -> x0, waiting for transfers between devices: 322 us -> none  [shards(): summed = lax.psum((query_part, key_part, value_part), ('group', 'span'))]
    add x127 -> x0, other arithmetic: 135 us -> none  [join_carry(): jnp.exp(later[0])[:, None] * earlier[1] + later[1]]
    all_to_all x0 -> x4, blocking collectives: none -> 103 us  [the longest x1 44.9 us: shards(): lax.all_to_all(jnp.broadcast_to(piece[None], (DEVS // 2, *piece.shape)),...]
    dot_general x29 -> x0, matrix products: 93.9 us -> none  [the longest x1 19 us: shards(): jnp.einsum('bhts,bthd->bshd', dlogit, q_blocks, preferred_element_type=jn...]
    unnamed x1 -> x0, blocking collectives: 72.9 us -> none
    pallas_call x0 -> x7, Pallas kernels: none -> 35.2 us  [the longest x1 10.9 us: near(): pl.pallas_call(functools.partial(near_kernel, lin_scale), grid=(width //...]
    exp x127 -> x0, local copies, waits for them, and re-layouts: 23.5 us -> none  [join_carry(): jnp.exp(later[0])[:, None] * earlier[1] + later[1]]
  transfers between devices with their start and end apart: 5 -> 5, of which waited for: 3 -> 2; matrix products, arithmetic and copies ran while one was open for 25% -> 0% of each run, Pallas kernels for 0% -> 10%
where the time goes in v1:
time: 207 us; the launch traced here: 206 us
  blocking collectives  103 us (50%)
  Pallas kernels  35.2 us (17%)
  starting transfers between devices  30 us (14%)
  between operations  14.2 us (7%)
  local copies, waits for them, and re-layouts  13.1 us (6%)
  waiting for transfers between devices  10.3 us (5%)
    all_to_all x1, blocking collectives, shards(): lax.all_to_all(jnp.broadcast_to(piece[None], (DEVS // 2, *piece.shape)),...  44.9 us
    all_to_all x1, blocking collectives, shards(): states = lax.all_to_all(states.reshape(DEVS, 8, PAIR), AX, 0, 0)  21.6 us
    all_to_all x1, blocking collectives, shards(): lax.all_to_all(partial.reshape(16, width // 16, 3 * PAIR), FAR16, 0, 0)  19.3 us
    all_to_all x1, blocking collectives, shards(): delta8 = lax.all_to_all(delta, NEAR8, 0, 0)  16.9 us
    unnamed x32, local copies, waits for them, and re-layouts  12.6 us
    ppermute x1, starting transfers between devices, shards(): nxt = lax.ppermute(prev, AX, [(i + 1, i) for i in range(DEVS - 1)])  12.4 us
    pallas_call x1, Pallas kernels, near(): pl.pallas_call(functools.partial(near_kernel, lin_scale), grid=(width //...  10.9 us
    all_to_all x1, starting transfers between devices, shards(): got = lax.all_to_all(msg.reshape(DEVS, 16, PAIR), AX, 0, 0)  9.72 us
  transfers between devices with their start and end apart: 5, of which 2 were waited for; matrix products, arithmetic and copies ran while one was open for 0% of the time, Pallas kernels for 10%

profile of v1, /device:TPU:1, one launch (start us, length us, event | category | flops | bytes accessed | tf_op | source)
XLA Modules:
  0.0 205.6 jit_solution(9456340681228039671)
XLA Ops:
  7.2 0.0 all-gather.3.cloned.1.call-start
  7.2 0.0 copy-start
  7.2 1.6 copy-done
  8.8 0.0 copy-start.2
  8.8 1.6 copy-done.2
  10.4 0.0 copy-start.4
  10.4 1.6 copy-done.4
  12.0 0.9 copy-done.7
  12.9 0.0 copy-start.8
  12.9 0.9 copy-done.8
  13.9 0.0 copy-start.12
  13.9 0.7 copy-done.12
  14.6 0.0 copy-start.9
  14.6 4.9 %project.1 = (bf16[128,1024]{1,0:T(8,128)(2,1)S(1)}, bf16[2,128,1024]{2,1,0:T(8,128)(2,1)S(1)}, f32[16,128]{1,0:T(8,128)S(1)}, f32[128,16]{1,0:T(8,128)S(1)}, bf...) custom-call(bf16[128,1024]{1,0:T(8,128)(2,1)S(1)} %copy-done.7, bf16[128,1024]{1,0:T(8,128)(2,1)S(1)} %copy-done.7, ...), custom_call_target="tpu_custom_call" | custom-call | flops 805306368 | bytes 7864320 | tf_op jit(solution)/shard_map/project/pallas_call | solution.py:96
  19.5 0.0 all-gather.3.cloned.1.call-update
  19.6 5.6 %collective-permute-start = (bf16[2,128,1024]{2,1,0:T(8,128)(2,1)S(1)}, bf16[2,128,1024]{2,1,0:T(8,128)(2,1)S(1)}, u32[]{:S(2)}, u32[]{:S(2)}) collective-permute-start(bf16[2,128,1024]{2,1,0:T(8,128)(2,1)S(1)} %get-tuple-element.21.kv), channel_id=1, source_target_pairs={{0,1},{1,2},{2,3},{3,4},{4,5},{5,6},{6,7},{7,8},{8,9},{9,10},{10,1... | collective-permute-start | bytes 1572872 | tf_op jit(solution)/shard_map/ppermute | solution.py:422
  25.2 9.7 %all-to-all-start = ((bf16[128,16,128]{2,1,0:T(8,128)(2,1)}), bf16[128,16,128]{2,1,0:T(8,128)(2,1)S(1)}, u32[]{:S(2)}, u32[]{:S(2)}) async-start(bf16[128,16,128]{2,1,0:T(8,128)(2,1)} %bitcast.2), calls=%async_computation | async-start | bytes 1048576 | tf_op jit(solution)/shard_map/all_to_all | solution.py:421
  35.0 8.9 %collective-permute-done.pkv = bf16[2,128,1024]{2,1,0:T(8,128)(2,1)S(1)} collective-permute-done((bf16[2,128,1024]{2,1,0:T(8,128)(2,1)S(1)}, bf16[2,128,1024]{2,1,0:T(8,128)(2,1)S(1)}, u32[]{:S(2)}, u32[]{:S(2)}) %collective-permute-start) | collective-permute-done | bytes 524320 | tf_op jit(solution)/shard_map/ppermute | solution.py:422
  43.9 0.8 copy-done.13
  44.7 0.0 copy-done.9
  44.7 0.0 copy-done.15
  44.7 1.0 copy-done.14
  45.7 10.9 %near.1 = (f32[128,1024]{1,0:T(8,128)S(1)}, f32[128,1024]{1,0:T(8,128)S(1)}, f32[2,128,1024]{2,1,0:T(8,128)S(1)}, bf16[2,128,1024]{2,1,0:T(8,128)(2,1)}) custom-call(s32[1]{0:T(128)} %bitcast.place, s32[1,4]{1,0:T(1,128)S(1)} %copy-done.15, bf16[128,1024]{1,0:T(8,128)(2,1)S(1)} %get-tuple-element.20.q_ref.q, bf16[2,128,1024]{2,1,0:T(8,128)(2,1)S(1)} %get-tuple-element.21.kv, ...), custom_call_target="tpu_custom_call" | custom-call | flops 4000000000 | bytes 16000000 | tf_op jit(solution)/shard_map/near/pallas_call | solution.py:214
  56.6 0.8 copy-done.10
  57.4 12.4 %collective-permute-start.1 = (bf16[2,128,1024]{2,1,0:T(8,128)(2,1)}, bf16[2,128,1024]{2,1,0:T(8,128)(2,1)}, u32[]{:S(2)}, u32[]{:S(2)}) collective-permute-start(bf16[2,128,1024]{2,1,0:T(8,128)(2,1)} %get-tuple-element.27), channel_id=1, source_target_pairs={{1,0},{2,1},{3,2},{4,3},{5,4},{6,5},{7,6},{8,7},{9,8},{10,9},{11,1... | collective-permute-start | bytes 1572872 | tf_op jit(solution)/shard_map/ppermute | solution.py:428
  69.8 0.0 all-to-all-done.got
  69.8 0.5 scan.1
  70.4 21.6 %all_to_all.25 = bf16[128,8,128]{2,1,0:T(8,128)(2,1)S(1)} all-to-all(bf16[128,8,128]{2,1,0:T(8,128)(2,1)S(1)} %bitcast.14), channel_id=1, replica_groups=mesh['yl'=2,'c'=2,'x'=4,'z'=4,'yh'=2] {'yl','c','x','z','yh'}, dimensions={0} | all-to-all | bytes 524288 | tf_op jit(solution)/shard_map/all_to_all | solution.py:429
  92.0 0.0 collective-permute-done.1.nxt
  92.0 1.0 copy-done.11
  93.0 5.5 %join.1 = (bf16[128,1024]{1,0:T(8,128)(2,1)}, bf16[8,128,384]{2,1,0:T(8,128)(2,1)S(1)}) custom-call(f32[128,1024]{1,0:T(8,128)S(1)} %get-tuple-element.24.near_out, f32[128,1024]{1,0:T(8,128)S(1)} %copy-done.11, f32[2,128,1024]{2,1,0:T(8,128)S(1)} %get-tuple-element.26.own, bf16[2,128,1024]{2,1,0:T(8,128)(2,1)} %collective-permute-done.1.nxt, ...), custom_call_target="tpu_custom_call" | custom-call | flops 134217728 | bytes 3145728 | tf_op jit(solution)/shard_map/join/pallas_call | solution.py:271
  98.6 16.9 %all_to_all.26.delta = bf16[8,128,384]{2,1,0:T(8,128)(2,1)S(1)} all-to-all(bf16[8,128,384]{2,1,0:T(8,128)(2,1)S(1)} %get-tuple-element.30.delta), channel_id=1, replica_groups=mesh['yl'=2,'c'=2,'x'=4,'z'=4,'yh'=2] {'z','yh'}, dimensions={0} | all-to-all | bytes 1572864 | tf_op jit(solution)/shard_map/all_to_all | solution.py:433
  115.5 1.6 copy-done.6
  117.1 2.4 %outer.1 = bf16[1024,384]{1,0:T(8,128)(2,1)S(1)} custom-call(bf16[8,1024,128]{2,1,0:T(8,128)(2,1)S(1)} %bitcast.13, bf16[8,128,384]{2,1,0:T(8,128)(2,1)S(1)} %all_to_all.26.delta), custom_call_target="tpu_custom_call" | custom-call | flops 805306368 | bytes 2883584 | tf_op jit(solution)/shard_map/outer/pallas_call | solution.py:346
  119.5 19.3 %all_to_all.27 = bf16[16,64,384]{2,1,0:T(8,128)(2,1)S(1)} all-to-all(bf16[16,64,384]{2,1,0:T(8,128)(2,1)S(1)} %bitcast.11), channel_id=1, replica_groups=mesh['yl'=2,'c'=2,'x'=4,'z'=4,'yh'=2] {'yl','c','x'}, dimensions={0} | all-to-all | bytes 1572864 | tf_op jit(solution)/shard_map/all_to_all | solution.py:435
  138.8 0.1 convert_reduce_fusion
  138.9 0.5 broadcast_in_dim.2
  139.4 0.0 copy-start.1
  139.4 0.0 copy-start.3
  139.4 0.0 copy-start.5
  139.5 44.9 %all_to_all.28 = bf16[64,64,384]{2,1,0:T(8,128)(2,1)S(1)} all-to-all(bf16[64,64,384]{2,1,0:T(8,128)(2,1)S(1)} %broadcast_in_dim.2), channel_id=1, replica_groups=mesh['yl'=2,'c'=2,'x'=4,'z'=4,'yh'=2] {'yl','x','z','yh'}, dimensions={0} | all-to-all | bytes 6291456 | tf_op jit(solution)/shard_map/all_to_all | solution.py:438
  184.3 2.1 %collective-permute-start.2 = (bf16[64,64,384]{2,1,0:T(8,128)(2,1)S(1)}, bf16[64,64,384]{2,1,0:T(8,128)(2,1)S(1)}, u32[]{:S(2)}, u32[]{:S(2)}) collective-permute-start(bf16[64,64,384]{2,1,0:T(8,128)(2,1)S(1)} %all_to_all.28), channel_id=1, source_target_pairs={{0,32},{32,0},{1,33},{33,1},{2,34},{34,2},{3,35},{35,3},{4,36},{36... | collective-permute-start | bytes 9437192 | tf_op jit(solution)/shard_map/ppermute | solution.py:439
  186.5 0.0 copy-done.1
  186.5 0.0 copy-done.3
  186.5 0.0 copy-done.5
  186.5 3.9 %back.1 = bf16[128,1024]{1,0:T(8,128)(2,1)} custom-call(bf16[8,128,384]{2,1,0:T(8,128)(2,1)S(1)} %get-tuple-element.30.delta, bf16[1024,1024]{1,0:T(8,128)(2,1)S(1)} %copy-done.1, bf16[1024,1024]{1,0:T(8,128)(2,1)S(1)} %copy-done.3, bf16[1024,1024]{1,0:T(8,128)(2,1)S(1)} %copy-done.5), custom_call_target="tpu_custom_call" | custom-call | flops 805306368 | bytes 7340032 | tf_op jit(solution)/shard_map/back/pallas_call | solution.py:323
  190.4 1.3 collective-permute-done.2
  191.7 7.0 %place.1 = (bf16[1024,1024]{1,0:T(8,128)(2,1)}, bf16[1024,1024]{1,0:T(8,128)(2,1)}, bf16[1024,1024]{1,0:T(8,128)(2,1)}) custom-call(s32[1]{0:T(128)} %bitcast.5.core, bf16[8,8,64,384]{3,2,1,0:T(8,128)(2,1)S(1)} %bitcast.10, bf16[8,8,64,384]{3,2,1,0:T(8,128)(2,1)S(1)} %bitcast.12), custom_call_target="tpu_custom_call" | custom-call | bytes 12582912 | tf_op jit(solution)/shard_map/place/pallas_call | solution.py:392
  (9 shorter events, 0.0 us)
Async XLA Ops:
  7.2 108.3 %all-gather.3.cloned.1.call-start = ((), (), s32[]{:S(2)}) async-start(), calls=%async_computation.5 | async-start | bytes 2359296 | tf_op jit(solution)/shard_map/all_gather | solution.py:423
  7.2 1.6 copy-start
  8.8 1.6 copy-start.2
  10.4 1.6 copy-start.4
  12.0 0.9 copy-start.7
  12.9 0.9 copy-start.8
  13.9 0.7 copy-start.12
  14.6 30.1 %copy-start.9 = (bf16[128,1024]{1,0:T(8,128)(2,1)S(1)}, bf16[128,1024]{1,0:T(8,128)(2,1)}, u32[]{:S(2)}) copy-start(bf16[128,1024]{1,0:T(8,128)(2,1)} %cot.5) | copy-start | bytes 786436
  14.6 30.1 %copy-start.15 = (s32[1,4]{1,0:T(1,128)S(1)}, s32[1,4]{1,0:T(1,128)}, u32[]{:S(2)}) copy-start(s32[1,4]{1,0:T(1,128)} %blocks.1) | copy-start | bytes 52
  19.6 24.3 %collective-permute-start = (bf16[2,128,1024]{2,1,0:T(8,128)(2,1)S(1)}, bf16[2,128,1024]{2,1,0:T(8,128)(2,1)S(1)}, u32[]{:S(2)}, u32[]{:S(2)}) collective-permute-start(bf16[2,128,1024]{2,1,0:T(8,128)(2,1)S(1)} %get-tuple-element.21.kv), channel_id=1, source_target_pairs={{0,1},{1,2},{2,3},{3,4},{4,5},{5,6},{6,7},{7,8},{8,9},{9,10},{10,1... | collective-permute-start | bytes 1572872 | tf_op jit(solution)/shard_map/ppermute | solution.py:422
  25.2 44.6 %all-to-all-start = ((bf16[128,16,128]{2,1,0:T(8,128)(2,1)}), bf16[128,16,128]{2,1,0:T(8,128)(2,1)S(1)}, u32[]{:S(2)}, u32[]{:S(2)}) async-start(bf16[128,16,128]{2,1,0:T(8,128)(2,1)} %bitcast.2), calls=%async_computation | async-start | bytes 1048576 | tf_op jit(solution)/shard_map/all_to_all | solution.py:421
  43.9 0.8 copy-start.13
  44.7 1.0 copy-start.14
  56.6 0.8 copy-start.10
  57.4 34.6 %collective-permute-start.1 = (bf16[2,128,1024]{2,1,0:T(8,128)(2,1)}, bf16[2,128,1024]{2,1,0:T(8,128)(2,1)}, u32[]{:S(2)}, u32[]{:S(2)}) collective-permute-start(bf16[2,128,1024]{2,1,0:T(8,128)(2,1)} %get-tuple-element.27), channel_id=1, source_target_pairs={{1,0},{2,1},{3,2},{4,3},{5,4},{6,5},{7,6},{8,7},{9,8},{10,9},{11,1... | collective-permute-start | bytes 1572872 | tf_op jit(solution)/shard_map/ppermute | solution.py:428
  92.0 1.0 copy-start.11
  115.5 1.6 copy-start.6
  139.4 47.0 %copy-start.1 = (bf16[1024,1024]{1,0:T(8,128)(2,1)S(1)}, bf16[1024,1024]{1,0:T(8,128)(2,1)}, u32[]{:S(2)}) copy-start(bf16[1024,1024]{1,0:T(8,128)(2,1)} %wq.3) | copy-start | bytes 6291460
  139.4 47.0 %copy-start.3 = (bf16[1024,1024]{1,0:T(8,128)(2,1)S(1)}, bf16[1024,1024]{1,0:T(8,128)(2,1)}, u32[]{:S(2)}) copy-start(bf16[1024,1024]{1,0:T(8,128)(2,1)} %wk.3) | copy-start | bytes 6291460
  139.4 47.0 %copy-start.5 = (bf16[1024,1024]{1,0:T(8,128)(2,1)S(1)}, bf16[1024,1024]{1,0:T(8,128)(2,1)}, u32[]{:S(2)}) copy-start(bf16[1024,1024]{1,0:T(8,128)(2,1)} %wv.3) | copy-start | bytes 6291460
  184.3 7.4 %collective-permute-start.2 = (bf16[64,64,384]{2,1,0:T(8,128)(2,1)S(1)}, bf16[64,64,384]{2,1,0:T(8,128)(2,1)S(1)}, u32[]{:S(2)}, u32[]{:S(2)}) collective-permute-start(bf16[64,64,384]{2,1,0:T(8,128)(2,1)S(1)} %all_to_all.28), channel_id=1, source_target_pairs={{0,32},{32,0},{1,33},{33,1},{2,34},{34,2},{3,35},{35,3},{4,36},{36... | collective-permute-start | bytes 9437192 | tf_op jit(solution)/shard_map/ppermute | solution.py:439
Sparse Core Ops, SparseCore 0:
  19.7 76.2 all-gather.2

commit v2 on v1

--- a/solution.py
+++ b/solution.py
@@ -12,9 +12,9 @@
 BF = jnp.bfloat16
 F32 = jnp.float32
 AX = ("yl", "c", "x", "z", "yh")
-NEAR8 = ("z", "yh")
-FAR16 = ("yl", "c", "x")
-PLANE = ("yl", "x", "z", "yh")
+NEAR8 = ("c", "x")
+FAR16 = ("yl", "z", "yh")
+PLANE = ("x", "yl", "z", "yh")
 SEG = 128
 PAIR = 128
 DH = 64
@@ -41,16 +41,19 @@
     return pl.CostEstimate(flops=flops, bytes_accessed=moved, transcendentals=trans)
 
 
-def project_kernel(lin_scale, tok, tok_col, wq, wk, wv, decay, cot, q_out, kv_out, run_out, runt_out, tokt_out, msg):
+def project_kernel(lin_scale, tok, ptok, wq, wk, wv, decay, cot, q_out, kv_out, pkv_out, run_out, runt_out, msg):
     step = pl.program_id(0)
     x = tok[...]
+    both = jnp.concatenate([x, ptok[...]], axis=0)
     q = dot(x, wq[...], 1, 0).astype(BF)
-    k = dot(x, wk[...], 1, 0).astype(BF)
-    v = dot(x, wv[...], 1, 0).astype(BF)
+    kk = dot(both, wk[...], 1, 0).astype(BF)
+    vv = dot(both, wv[...], 1, 0).astype(BF)
+    k, v = kk[:SEG], vv[:SEG]
     q_out[...] = q
     kv_out[0] = k
     kv_out[1] = v
-    tokt_out[...] = tok_col[...].T
+    pkv_out[0] = kk[SEG:]
+    pkv_out[1] = vv[SEG:]
     ld = decay[...]
     heads = ld.shape[0]
     lower = (iota((SEG, SEG), 0) >= iota((SEG, SEG), 1)).astype(F32)
@@ -87,7 +90,7 @@
             msg[part, half * PAIR : (half + 1) * PAIR, :] = both.astype(BF)
 
 
-def project(tokens, wq, wk, wv, log_decay, cot, lin_scale):
+def project(tokens, prev_tokens, wq, wk, wv, log_decay, cot, lin_scale):
     rows, width = tokens.shape
     heads = log_decay.shape[0]
     steps = width // 256
@@ -98,7 +101,7 @@
         grid=(steps,),
         in_specs=[
             pl.BlockSpec((rows, width), lambda i: (0, 0)),
-            col,
+            pl.BlockSpec((rows, width), lambda i: (0, 0)),
             weight,
             weight,
             weight,
@@ -108,23 +111,40 @@
         out_specs=[
             col,
             pl.BlockSpec((2, rows, 256), lambda i: (0, 0, i)),
+            pl.BlockSpec((2, rows, 256), lambda i: (0, 0, i)),
             pl.BlockSpec((heads, rows), lambda i: (0, 0)),
             pl.BlockSpec((rows, heads), lambda i: (0, 0)),
-            pl.BlockSpec((256, rows), lambda i: (i, 0)),
             pl.BlockSpec((2, 2 * PAIR, PAIR), lambda i: (0, i, 0)),
         ],
         out_shape=[
             jax.ShapeDtypeStruct((rows, width), BF),
             jax.ShapeDtypeStruct((2, rows, width), BF),
+            jax.ShapeDtypeStruct((2, rows, width), BF),
             jax.ShapeDtypeStruct((heads, rows), F32),
             jax.ShapeDtypeStruct((rows, heads), F32),
-            jax.ShapeDtypeStruct((width, rows), BF),
             jax.ShapeDtypeStruct((2, width, PAIR), BF),
         ],
-        compiler_params=params(40),
-        cost_estimate=cost(6 * rows * width * width, 6 * width * width + 12 * rows * width),
+        compiler_params=params(58),
+        cost_estimate=cost(10 * rows * width * width, 6 * width * width + 12 * rows * width),
         name="project",
-    )(tokens, tokens, wq, wk, wv, log_decay, cot)
+    )(tokens, prev_tokens, wq, wk, wv, log_decay, cot)
+
+
+def flip_kernel(tok, out):
+    out[...] = tok[...].T
+
+
+def flip(tokens):
+    rows, width = tokens.shape
+    return pl.pallas_call(
+        flip_kernel,
+        in_specs=[pl.BlockSpec(memory_space=VMEM)],
+        out_specs=pl.BlockSpec(memory_space=VMEM),
+        out_shape=jax.ShapeDtypeStruct((width, rows), BF),
+        compiler_params=params(16),
+        cost_estimate=cost(0, 4 * rows * width),
+        name="flip",
+    )(tokens)
 
 
 def scan_kernel(place, got, out, xs, decays, states):
@@ -352,7 +372,7 @@
         ],
         out_specs=pl.BlockSpec((width // 4, cols), lambda i: (i, 0)),
         out_shape=jax.ShapeDtypeStruct((width, cols), BF),
-        compiler_params=params(32),
+        compiler_params=params(58),
         cost_estimate=cost(
             2 * near_count * rows * cols * width, 2 * near_count * rows * (width + cols)
         ),
@@ -360,55 +380,37 @@
     )(tokt, delta)
 
 
-def place_kernel(core, mine, other, gq, gk, gv):
-    del core
-    step = pl.program_id(0)
-
-    def put(src):
-        for j in range(8):
-            for part, o in enumerate((gq, gk, gv)):
-                o[:, j * PAIR : (j + 1) * PAIR] = src[0, j, :, part * PAIR : (part + 1) * PAIR]
-
-    @pl.when(step < 8)
-    def _():
-        put(mine)
-
-    @pl.when(step >= 8)
-    def _():
-        put(other)
-
-
-def place_all(core, mine, other):
-    blocks, near_count, rows, cols = mine.shape
-    width = 2 * blocks * rows
-
-    def where(i, core):
-        half = i // 8
-        piece = i % 8
-        c = jnp.where(half == 0, core[0], 1 - core[0])
-        return ((piece // 4) * 8 + c * 4 + piece % 4, 0)
-
-    grad = pl.BlockSpec((rows, width), where)
+def place_kernel(side, pieces, *rest):
+    del side
+    for x in range(pieces.shape[0]):
+        for r in range(pieces.shape[1]):
+            rows = slice(r * pieces.shape[2], (r + 1) * pieces.shape[2])
+            for part, o in enumerate(rest[-3:]):
+                o[rows, x * PAIR : (x + 1) * PAIR] = pieces[x, r, :, part * PAIR : (part + 1) * PAIR]
+
+
+def place_half(side, pieces, grads=()):
+    near_count, blocks, rows, cols = pieces.shape
+    width = blocks * rows
+    out = jax.ShapeDtypeStruct((width, width), BF)
     return pl.pallas_call(
         place_kernel,
         grid_spec=pltpu.PrefetchScalarGridSpec(
             num_scalar_prefetch=1,
-            grid=(16,),
-            in_specs=[
-                pl.BlockSpec(
-                    (1, near_count, rows, cols), lambda i, core: (jnp.minimum(i, 7), 0, 0, 0)
-                ),
-                pl.BlockSpec(
-                    (1, near_count, rows, cols), lambda i, core: (jnp.maximum(i - 8, 0), 0, 0, 0)
-                ),
-            ],
-            out_specs=[grad, grad, grad],
+            grid=(blocks // 2,),
+            in_specs=[pl.BlockSpec((near_count, 2, rows, cols), lambda i, side: (0, i, 0, 0))]
+            + [pl.BlockSpec(memory_space=pl.ANY)] * len(grads),
+            out_specs=[
+                pl.BlockSpec((2 * rows, near_count * PAIR), lambda i, side: (i, side[0]))
+            ]
+            * 3,
         ),
-        out_shape=[jax.ShapeDtypeStruct((width, width), BF)] * 3,
-        compiler_params=params(32),
-        cost_estimate=cost(0, 12 * width * width),
+        out_shape=[out] * 3,
+        input_output_aliases={2 + i: i for i in range(len(grads))},
+        compiler_params=params(24),
+        cost_estimate=cost(0, 6 * width * width),
         name="place",
-    )(core, mine, other)
+    )(side, pieces, *grads)
 
 
 def shards(tokens, wq, wk, wv, log_decay, neighbour_blocks, cot):
@@ -417,10 +419,12 @@
     place = lax.axis_index(AX).astype(jnp.int32).reshape(1)
     core = lax.axis_index("c").astype(jnp.int32).reshape(1)
 
-    q, kv, run, runt, tokt, msg = project(tokens, wq, wk, wv, log_decay, cot, lin_scale)
+    prev_tokens = lax.ppermute(tokens, AX, [(i, i + 1) for i in range(DEVS - 1)])
+    tokt8 = lax.all_gather(flip(tokens), NEAR8)
+    q, kv, pkv, run, runt, msg = project(
+        tokens, prev_tokens, wq, wk, wv, log_decay, cot, lin_scale
+    )
     got = lax.all_to_all(msg.reshape(DEVS, 16, PAIR), AX, 0, 0)
-    pkv = lax.ppermute(kv, AX, [(i, i + 1) for i in range(DEVS - 1)])
-    tokt8 = lax.all_gather(tokt, NEAR8)
     near_out, dq, own, prev = near(
         place, neighbour_blocks, q, kv, pkv, cot, run, runt, lin_scale
     )
@@ -438,8 +442,9 @@
     plane = lax.all_to_all(jnp.broadcast_to(piece[None], (DEVS // 2, *piece.shape)), PLANE, 0, 0)
     other = lax.ppermute(plane, "c", [(0, 1), (1, 0)])
     tokens_grad = back(delta, wq, wk, wv)
-    shape = (8, 8, *piece.shape)
-    gq, gk, gv = place_all(core, plane.reshape(shape), other.reshape(shape))
+    shape = (4, 16, *piece.shape)
+    grads = place_half(core, plane.reshape(shape))
+    gq, gk, gv = place_half(1 - core, other.reshape(shape), grads)
     return layer, tokens_grad, gq, gk, gv
 
 

time: 207 us -> 197 us (0.952)
  blocking collectives: 103 us -> 80.3 us
  waiting for transfers between devices: 10.3 us -> 22.8 us
  Pallas kernels: 35.2 us -> 41.4 us
  local copies, waits for them, and re-layouts: 13.1 us -> 9.54 us
    all_to_all x1 -> x0, blocking collectives: 21.6 us -> none  [shards(): states = lax.all_to_all(states.reshape(DEVS, 8, PAIR), AX, 0, 0)]
    all_to_all x0 -> x1, waiting for transfers between devices: none -> 6.5 us  [shards(): states = lax.all_to_all(states.reshape(DEVS, 8, PAIR), AX, 0, 0)]
    all_to_all x1, starting transfers between devices: 9.72 us -> 5.02 us  [shards(): got = lax.all_to_all(msg.reshape(DEVS, 16, PAIR), AX, 0, 0)]
    ppermute x1, waiting for transfers between devices: 0.01 us -> 3.88 us  [shards(): nxt = lax.ppermute(prev, AX, [(i + 1, i) for i in range(DEVS - 1)])]
    unnamed x32 -> x34, local copies, waits for them, and re-layouts: 12.6 us -> 9.05 us
    all_to_all x0 -> x1, starting transfers between devices: none -> 3.55 us  [shards(): states = lax.all_to_all(states.reshape(DEVS, 8, PAIR), AX, 0, 0)]
    ppermute x1, waiting for transfers between devices: 8.93 us -> 12.4 us  [shards(): lax.ppermute(tokens, AX, [(i, i + 1) for i in range(DEVS - 1)])]
    pallas_call x1, Pallas kernels: 2.4 us -> 4.83 us  [outer(): pl.pallas_call(outer_kernel, grid=(4,), in_specs=[pl.BlockSpec((near_coun...]
  transfers between devices with their start and end apart: 5 -> 6, of which waited for: 2 -> 3; matrix products, arithmetic and copies ran while one was open for 0% -> 0% of each run, Pallas kernels for 10% -> 16%
where the time goes in v2:
time: 197 us; the launch traced here: 196 us
  blocking collectives  80.3 us (41%)
  Pallas kernels  41.4 us (21%)
  starting transfers between devices  28 us (14%)
  waiting for transfers between devices  22.8 us (12%)
  between operations  14.2 us (7%)
  local copies, waits for them, and re-layouts  9.54 us (5%)
    all_to_all x1, blocking collectives, shards(): lax.all_to_all(jnp.broadcast_to(piece[None], (DEVS // 2, *piece.shape)),...  43.2 us
    all_to_all x1, blocking collectives, shards(): lax.all_to_all(partial.reshape(16, width // 16, 3 * PAIR), FAR16, 0, 0)  20.2 us
    all_to_all x1, blocking collectives, shards(): delta8 = lax.all_to_all(delta, NEAR8, 0, 0)  16.9 us
    ppermute x1, waiting for transfers between devices, shards(): lax.ppermute(tokens, AX, [(i, i + 1) for i in range(DEVS - 1)])  12.4 us
    pallas_call x1, Pallas kernels, near(): pl.pallas_call(functools.partial(near_kernel, lin_scale), grid=(width //...  10.9 us
    ppermute x1, starting transfers between devices, shards(): nxt = lax.ppermute(prev, AX, [(i + 1, i) for i in range(DEVS - 1)])  10.1 us
    unnamed x34, local copies, waits for them, and re-layouts  9.05 us
    pallas_call x2, Pallas kernels, place_half(): pl.pallas_call(place_kernel, grid_spec=pltpu.PrefetchScalarGridSpec(num_s...  7.21 us
  transfers between devices with their start and end apart: 6, of which 3 were waited for; matrix products, arithmetic and copies ran while one was open for 0% of the time, Pallas kernels for 16%

profile of v2, /device:TPU:1, one launch (start us, length us, event | category | flops | bytes accessed | tf_op | source)
XLA Modules:
  0.0 196.3 jit_solution(8613106791233760553)
XLA Ops:
  7.2 0.0 all-gather.3.cloned.1.call-start
  7.2 0.0 copy-start.3
  7.2 0.9 copy-done.3
  8.2 0.8 flip.1
  9.0 0.0 all-gather.3.cloned.1.call-update
  9.0 5.7 %collective-permute-start = (bf16[128,1024]{1,0:T(8,128)(2,1)}, bf16[128,1024]{1,0:T(8,128)(2,1)S(1)}, u32[]{:S(2)}, u32[]{:S(2)}) collective-permute-start(bf16[128,1024]{1,0:T(8,128)(2,1)} %tok.3), channel_id=1, source_target_pairs={{0,1},{1,2},{2,3},{3,4},{4,5},{5,6},{6,7},{7,8},{8,9},{9,10},{10,1... | collective-permute-start | bytes 786440 | tf_op jit(solution)/shard_map/ppermute | solution.py:422
  14.7 0.0 copy-start.4
  14.7 0.0 copy-start.15
  14.7 12.4 %collective-permute-done.ptok = bf16[128,1024]{1,0:T(8,128)(2,1)S(1)} collective-permute-done((bf16[128,1024]{1,0:T(8,128)(2,1)}, bf16[128,1024]{1,0:T(8,128)(2,1)S(1)}, u32[]{:S(2)}, u32[]{:S(2)}) %collective-permute-start) | collective-permute-done | bytes 262176 | tf_op jit(solution)/shard_map/ppermute | solution.py:422
  27.1 0.7 copy-done.16
  27.8 6.9 %project.1 = (bf16[128,1024]{1,0:T(8,128)(2,1)}, bf16[2,128,1024]{2,1,0:T(8,128)(2,1)}, bf16[2,128,1024]{2,1,0:T(8,128)(2,1)}, f32[16,128]{1,0:T(8,128)}, f32[12...) custom-call(bf16[128,1024]{1,0:T(8,128)(2,1)} %tok.3, bf16[128,1024]{1,0:T(8,128)(2,1)} %copy-done.16, bf16[1024,1024]{1,0:T(8,128)(2,1)} %wq.3, ...), custom_call_target="tpu_custom_call" | custom-call | flops 1342177280 | bytes 7864320 | tf_op jit(solution)/shard_map/project/pallas_call | solution.py:99
  34.7 5.0 %all-to-all-start = ((bf16[128,16,128]{2,1,0:T(8,128)(2,1)}), bf16[128,16,128]{2,1,0:T(8,128)(2,1)S(1)}, u32[]{:S(2)}, u32[]{:S(2)}) async-start(bf16[128,16,128]{2,1,0:T(8,128)(2,1)} %bitcast.16), calls=%async_computation | async-start | bytes 1048576 | tf_op jit(solution)/shard_map/all_to_all | solution.py:427
  39.8 0.0 copy-done.4
  39.8 0.0 copy-done.15
  39.8 0.0 copy-start.5
  39.8 1.0 copy-done.5
  40.8 0.9 copy-done.9
  41.8 0.8 copy-done.11
  42.6 1.0 copy-done.13
  43.7 0.7 copy-done.14
  44.4 10.9 %near.1 = (f32[128,1024]{1,0:T(8,128)S(1)}, f32[128,1024]{1,0:T(8,128)S(1)}, f32[2,128,1024]{2,1,0:T(8,128)S(1)}, bf16[2,128,1024]{2,1,0:T(8,128)(2,1)}) custom-call(s32[1]{0:T(128)} %bitcast.place, s32[1,4]{1,0:T(1,128)S(1)} %copy-done.15, bf16[128,1024]{1,0:T(8,128)(2,1)S(1)} %copy-done.9, bf16[2,128,1024]{2,1,0:T(8,128)(2,1)S(1)} %copy-done.5, ...), custom_call_target="tpu_custom_call" | custom-call | flops 4000000000 | bytes 16000000 | tf_op jit(solution)/shard_map/near/pallas_call | solution.py:234
  55.3 0.8 copy-done.7
  56.1 10.1 %collective-permute-start.1 = (bf16[2,128,1024]{2,1,0:T(8,128)(2,1)}, bf16[2,128,1024]{2,1,0:T(8,128)(2,1)}, u32[]{:S(2)}, u32[]{:S(2)}) collective-permute-start(bf16[2,128,1024]{2,1,0:T(8,128)(2,1)} %get-tuple-element.31), channel_id=1, source_target_pairs={{1,0},{2,1},{3,2},{4,3},{5,4},{6,5},{7,6},{8,7},{9,8},{10,9},{11,1... | collective-permute-start | bytes 1572872 | tf_op jit(solution)/shard_map/ppermute | solution.py:432
  66.2 0.0 all-to-all-done.got
  66.2 1.2 scan.1
  67.4 3.5 %all-to-all-start.1 = ((bf16[128,8,128]{2,1,0:T(8,128)(2,1)}), bf16[128,8,128]{2,1,0:T(8,128)(2,1)S(1)}, u32[]{:S(2)}, u32[]{:S(2)}) async-start(bf16[128,8,128]{2,1,0:T(8,128)(2,1)} %bitcast.3), calls=%async_computation.1 | async-start | bytes 524288 | tf_op jit(solution)/shard_map/all_to_all | solution.py:433
  71.0 3.9 %collective-permute-done.1.nxt = bf16[2,128,1024]{2,1,0:T(8,128)(2,1)} collective-permute-done((bf16[2,128,1024]{2,1,0:T(8,128)(2,1)}, bf16[2,128,1024]{2,1,0:T(8,128)(2,1)}, u32[]{:S(2)}, u32[]{:S(2)}) %collective-permute-start.1) | collective-permute-done | bytes 524320 | tf_op jit(solution)/shard_map/ppermute | solution.py:432
  74.9 6.5 %all-to-all-done.1 = bf16[128,8,128]{2,1,0:T(8,128)(2,1)S(1)} async-done(((bf16[128,8,128]{2,1,0:T(8,128)(2,1)}), bf16[128,8,128]{2,1,0:T(8,128)(2,1)S(1)}, u32[]{:S(2)}, u32[]{:S(2)}) %all-to-all-start.1) | async-done | bytes 262176 | tf_op jit(solution)/shard_map/all_to_all | solution.py:433
  81.4 0.0 copy-done.6
  81.4 0.0 copy-done.12
  81.4 1.0 copy-done.8
  82.4 0.9 copy-done.10
  83.4 5.5 %join.1 = (bf16[128,1024]{1,0:T(8,128)(2,1)}, bf16[8,128,384]{2,1,0:T(8,128)(2,1)S(1)}) custom-call(f32[128,1024]{1,0:T(8,128)S(1)} %get-tuple-element.28.near_out, f32[128,1024]{1,0:T(8,128)S(1)} %copy-done.8, f32[2,128,1024]{2,1,0:T(8,128)S(1)} %get-tuple-element.30.own, bf16[2,128,1024]{2,1,0:T(8,128)(2,1)} %collective-permute-done.1.nxt, ...), custom_call_target="tpu_custom_call" | custom-call | flops 134217728 | bytes 3145728 | tf_op jit(solution)/shard_map/join/pallas_call | solution.py:291
  88.9 16.9 %all_to_all.25.delta = bf16[8,128,384]{2,1,0:T(8,128)(2,1)} all-to-all(bf16[8,128,384]{2,1,0:T(8,128)(2,1)S(1)} %get-tuple-element.34.delta), channel_id=1, replica_groups=mesh['yl'=2,'c'=2,'x'=4,'z'=4,'yh'=2] {'c','x'}, dimensions={0} | all-to-all | bytes 1572864 | tf_op jit(solution)/shard_map/all_to_all | solution.py:437
  105.8 4.8 %outer.1 = bf16[1024,384]{1,0:T(8,128)(2,1)} custom-call(bf16[8,1024,128]{2,1,0:T(8,128)(2,1)} %bitcast.15, bf16[8,128,384]{2,1,0:T(8,128)(2,1)} %all_to_all.25.delta), custom_call_target="tpu_custom_call" | custom-call | flops 805306368 | bytes 2883584 | tf_op jit(solution)/shard_map/outer/pallas_call | solution.py:366
  110.7 20.2 %all_to_all.26 = bf16[16,64,384]{2,1,0:T(8,128)(2,1)S(1)} all-to-all(bf16[16,64,384]{2,1,0:T(8,128)(2,1)} %bitcast.14), channel_id=1, replica_groups=mesh['yl'=2,'c'=2,'x'=4,'z'=4,'yh'=2] {'yl','z','yh'}, dimensions={0} | all-to-all | bytes 1572864 | tf_op jit(solution)/shard_map/all_to_all | solution.py:439
  130.9 0.1 convert_reduce_fusion
  131.0 0.5 broadcast_in_dim.2
  131.5 0.0 copy-start
  131.5 0.0 copy-start.1
  131.5 0.0 copy-start.2
  131.5 43.2 %all_to_all.27 = bf16[64,64,384]{2,1,0:T(8,128)(2,1)S(1)} all-to-all(bf16[64,64,384]{2,1,0:T(8,128)(2,1)S(1)} %broadcast_in_dim.2), channel_id=1, replica_groups=mesh['yl'=2,'c'=2,'x'=4,'z'=4,'yh'=2] {'x','yl','z','yh'}, dimensions={0} | all-to-all | bytes 6291456 | tf_op jit(solution)/shard_map/all_to_all | solution.py:442
  174.7 3.6 %collective-permute-start.2 = (bf16[64,64,384]{2,1,0:T(8,128)(2,1)S(1)}, bf16[64,64,384]{2,1,0:T(8,128)(2,1)S(1)}, u32[]{:S(2)}, u32[]{:S(2)}) collective-permute-start(bf16[64,64,384]{2,1,0:T(8,128)(2,1)S(1)} %all_to_all.27), channel_id=1, source_target_pairs={{0,32},{32,0},{1,33},{33,1},{2,34},{34,2},{3,35},{35,3},{4,36},{36... | collective-permute-start | bytes 9437192 | tf_op jit(solution)/shard_map/ppermute | solution.py:443
  178.3 0.0 copy-done
  178.3 3.9 %back.1 = bf16[128,1024]{1,0:T(8,128)(2,1)} custom-call(bf16[8,128,384]{2,1,0:T(8,128)(2,1)S(1)} %get-tuple-element.34.delta, bf16[1024,1024]{1,0:T(8,128)(2,1)S(1)} %copy-done, bf16[1024,1024]{1,0:T(8,128)(2,1)S(1)} %copy-done.1, bf16[1024,1024]{1,0:T(8,128)(2,1)S(1)} %copy-done.2), custom_call_target="tpu_custom_call" | custom-call | flops 805306368 | bytes 7340032 | tf_op jit(solution)/shard_map/back/pallas_call | solution.py:343
  182.2 3.6 %place.2 = (bf16[1024,1024]{1,0:T(8,128)(2,1)}, bf16[1024,1024]{1,0:T(8,128)(2,1)}, bf16[1024,1024]{1,0:T(8,128)(2,1)}) custom-call(s32[1]{0:T(128)} %bitcast.5.side, bf16[4,16,64,384]{3,2,1,0:T(8,128)(2,1)S(1)} %bitcast.10), custom_call_target="tpu_custom_call" | custom-call | bytes 6291456 | tf_op jit(solution)/shard_map/place/pallas_call | solution.py:396
  185.8 0.0 collective-permute-done.2
  185.8 3.6 %place.3 = (bf16[1024,1024]{1,0:T(8,128)(2,1)}, bf16[1024,1024]{1,0:T(8,128)(2,1)}, bf16[1024,1024]{1,0:T(8,128)(2,1)}) custom-call(s32[1]{0:T(128)S(6)} %sub.3.side, bf16[4,16,64,384]{3,2,1,0:T(8,128)(2,1)S(1)} %bitcast.11, bf16[1024,1024]{1,0:T(8,128)(2,1)} %get-tuple-element.35.rest_0_, ...), custom_call_target="tpu_custom_call", output_to_operand_aliasing={{0}: (2, {}), {1}: (3, {}), {2}: (4, {})} | custom-call | bytes 6291456 | tf_op jit(solution)/shard_map/place/pallas_call | solution.py:396
  (14 shorter events, 0.0 us)
Async XLA Ops:
  7.2 98.7 %all-gather.3.cloned.1.call-start = ((), (), s32[]{:S(2)}) async-start(), calls=%async_computation.5 | async-start | bytes 2359296 | tf_op jit(solution)/shard_map/all_gather | solution.py:423
  7.2 1.0 copy-start.3
  9.0 18.1 %collective-permute-start = (bf16[128,1024]{1,0:T(8,128)(2,1)}, bf16[128,1024]{1,0:T(8,128)(2,1)S(1)}, u32[]{:S(2)}, u32[]{:S(2)}) collective-permute-start(bf16[128,1024]{1,0:T(8,128)(2,1)} %tok.3), channel_id=1, source_target_pairs={{0,1},{1,2},{2,3},{3,4},{4,5},{5,6},{6,7},{7,8},{8,9},{9,10},{10,1... | collective-permute-start | bytes 786440 | tf_op jit(solution)/shard_map/ppermute | solution.py:422
  14.7 25.1 %copy-start.4 = (bf16[128,1024]{1,0:T(8,128)(2,1)S(1)}, bf16[128,1024]{1,0:T(8,128)(2,1)}, u32[]{:S(2)}) copy-start(bf16[128,1024]{1,0:T(8,128)(2,1)} %cot.5) | copy-start | bytes 786436
  14.7 25.1 %copy-start.15 = (s32[1,4]{1,0:T(1,128)S(1)}, s32[1,4]{1,0:T(1,128)}, u32[]{:S(2)}) copy-start(s32[1,4]{1,0:T(1,128)} %blocks.1) | copy-start | bytes 52
  27.1 0.7 copy-start.16
  34.7 31.4 %all-to-all-start = ((bf16[128,16,128]{2,1,0:T(8,128)(2,1)}), bf16[128,16,128]{2,1,0:T(8,128)(2,1)S(1)}, u32[]{:S(2)}, u32[]{:S(2)}) async-start(bf16[128,16,128]{2,1,0:T(8,128)(2,1)} %bitcast.16), calls=%async_computation | async-start | bytes 1048576 | tf_op jit(solution)/shard_map/all_to_all | solution.py:427
  39.8 1.0 copy-start.5
  40.8 0.9 copy-start.9
  41.8 0.8 copy-start.11
  42.6 1.0 copy-start.13
  43.7 0.7 copy-start.14
  44.4 37.0 %copy-start.6 = (bf16[2,128,1024]{2,1,0:T(8,128)(2,1)S(1)}, bf16[2,128,1024]{2,1,0:T(8,128)(2,1)}, u32[]{:S(2)}) copy-start(bf16[2,128,1024]{2,1,0:T(8,128)(2,1)} %get-tuple-element.24.kv) | copy-start | bytes 1572868
  44.4 37.0 %copy-start.12 = (f32[128,16]{1,0:T(8,128)S(1)}, f32[128,16]{1,0:T(8,128)}, u32[]{:S(2)}) copy-start(f32[128,16]{1,0:T(8,128)} %get-tuple-element.27.runt) | copy-start | bytes 24580
  55.3 0.8 copy-start.7
  56.1 18.8 %collective-permute-start.1 = (bf16[2,128,1024]{2,1,0:T(8,128)(2,1)}, bf16[2,128,1024]{2,1,0:T(8,128)(2,1)}, u32[]{:S(2)}, u32[]{:S(2)}) collective-permute-start(bf16[2,128,1024]{2,1,0:T(8,128)(2,1)} %get-tuple-element.31), channel_id=1, source_target_pairs={{1,0},{2,1},{3,2},{4,3},{5,4},{6,5},{7,6},{8,7},{9,8},{10,9},{11,1... | collective-permute-start | bytes 1572872 | tf_op jit(solution)/shard_map/ppermute | solution.py:432
  67.4 13.9 %all-to-all-start.1 = ((bf16[128,8,128]{2,1,0:T(8,128)(2,1)}), bf16[128,8,128]{2,1,0:T(8,128)(2,1)S(1)}, u32[]{:S(2)}, u32[]{:S(2)}) async-start(bf16[128,8,128]{2,1,0:T(8,128)(2,1)} %bitcast.3), calls=%async_computation.1 | async-start | bytes 524288 | tf_op jit(solution)/shard_map/all_to_all | solution.py:433
  81.4 1.0 copy-start.8
  82.4 0.9 copy-start.10
  131.5 46.8 %copy-start = (bf16[1024,1024]{1,0:T(8,128)(2,1)S(1)}, bf16[1024,1024]{1,0:T(8,128)(2,1)}, u32[]{:S(2)}) copy-start(bf16[1024,1024]{1,0:T(8,128)(2,1)} %wq.3) | copy-start | bytes 6291460
  131.5 46.8 %copy-start.1 = (bf16[1024,1024]{1,0:T(8,128)(2,1)S(1)}, bf16[1024,1024]{1,0:T(8,128)(2,1)}, u32[]{:S(2)}) copy-start(bf16[1024,1024]{1,0:T(8,128)(2,1)} %wk.3) | copy-start | bytes 6291460
  131.5 46.8 %copy-start.2 = (bf16[1024,1024]{1,0:T(8,128)(2,1)S(1)}, bf16[1024,1024]{1,0:T(8,128)(2,1)}, u32[]{:S(2)}) copy-start(bf16[1024,1024]{1,0:T(8,128)(2,1)} %wv.3) | copy-start | bytes 6291460
  174.7 11.2 %collective-permute-start.2 = (bf16[64,64,384]{2,1,0:T(8,128)(2,1)S(1)}, bf16[64,64,384]{2,1,0:T(8,128)(2,1)S(1)}, u32[]{:S(2)}, u32[]{:S(2)}) collective-permute-start(bf16[64,64,384]{2,1,0:T(8,128)(2,1)S(1)} %all_to_all.27), channel_id=1, source_target_pairs={{0,32},{32,0},{1,33},{33,1},{2,34},{34,2},{3,35},{35,3},{4,36},{36... | collective-permute-start | bytes 9437192 | tf_op jit(solution)/shard_map/ppermute | solution.py:443
Sparse Core Ops, SparseCore 0:
  9.7 28.7 all-gather.2

commit v3 on v2

v3 whole, which is shorter than its diff:
```python
import functools
import math

import jax
import jax.numpy as jnp
from jax import lax
from jax.experimental import pallas as pl
from jax.experimental.pallas import tpu as pltpu
from jax.sharding import Mesh
from jax.sharding import PartitionSpec as P

BF = jnp.bfloat16
F32 = jnp.float32
AX = ("yl", "c", "x", "z", "yh")
NEAR8 = ("c", "x")
FAR16 = ("yl", "z", "yh")
PLANE = ("x", "yl", "z", "yh")
SEG = 128
PAIR = 128
DH = 64
DEVS = 128
VMEM = pltpu.VMEM
HIGH = lax.Precision.HIGHEST


def dot(a, b, ca, cb, precision=None):
    return lax.dot_general(
        a, b, (((ca,), (cb,)), ((), ())), precision=precision, preferred_element_type=F32
    )


def iota(shape, axis):
    return lax.broadcasted_iota(jnp.int32, shape, axis)


def params(mib):
    return pltpu.CompilerParams(vmem_limit_bytes=mib << 20)


def cost(flops, moved, trans=0):
    return pl.CostEstimate(flops=flops, bytes_accessed=moved, transcendentals=trans)


CHUNK = 256


def project_kernel(lin_scale, tok, ptok, wq, wk, wv, decay, cot, q_out, kv_out, pkv_out, run_out, runt_out, msg, held, sems):
    width = tok.shape[1]
    chunks = width // CHUNK
    copies = []
    for step in range(chunks):
        for part, w in enumerate((wq, wk, wv)):
            copy = pltpu.make_async_copy(
                w.at[:, pl.ds(step * CHUNK, CHUNK)], held.at[part, step], sems.at[part, step]
            )
            copy.start()
            copies.append(copy)
    x = tok[...]
    both = jnp.concatenate([x, ptok[...]], axis=0)
    ld = decay[...]
    heads = ld.shape[0]
    lower = (iota((SEG, SEG), 0) >= iota((SEG, SEG), 1)).astype(F32)
    runt = dot(lower, ld, 1, 1, HIGH)
    run = dot(ld, lower, 1, 1, HIGH)
    group = heads // chunks
    for step in range(chunks):
        runt_out[step] = runt[:, step * group : (step + 1) * group]
        run_out[step] = run[step * group : (step + 1) * group, :]
    head_of = iota((SEG, PAIR), 1) // DH
    rows = iota((8, PAIR), 0)
    lanes = iota((DH, PAIR), 1) < DH
    for step in range(chunks):
        for part in range(3):
            copies[step * 3 + part].wait()
        at = slice(step * CHUNK, (step + 1) * CHUNK)
        q = dot(x, held[0, step], 1, 0).astype(BF)
        kk = dot(both, held[1, step], 1, 0).astype(BF)
        vv = dot(both, held[2, step], 1, 0).astype(BF)
        k, v = kk[:SEG], vv[:SEG]
        q_out[:, at] = q
        kv_out[0, :, at] = k
        kv_out[1, :, at] = v
        pkv_out[0, :, at] = kk[SEG:]
        pkv_out[1, :, at] = vv[SEG:]
        for half in range(CHUNK // PAIR):
            cols = slice(half * PAIR, (half + 1) * PAIR)
            pair = step * (CHUNK // PAIR) + half
            run = jnp.where(
                head_of == 0, runt[:, 2 * pair : 2 * pair + 1], runt[:, 2 * pair + 1 : 2 * pair + 2]
            )
            total = run[SEG - 1 : SEG, :]
            grads = cot[:, pair * PAIR : (pair + 1) * PAIR].astype(F32)
            weighted = (v[:, cols].astype(F32) * jnp.exp(total - run)).astype(BF)
            scaled = (grads * jnp.exp(run)).astype(BF)
            full_s = dot(k[:, cols], weighted, 0, 0)
            full_g = dot(q[:, cols], scaled, 0, 0) * lin_scale
            high = total.astype(BF).astype(F32)
            mid = (total - high).astype(BF).astype(F32)
            low = total - high - mid
            tail = jnp.where(
                rows == 0, high, jnp.where(rows == 1, mid, jnp.where(rows == 2, low, 0.0))
            )
            tail = jnp.broadcast_to(tail[None], (8, 8, PAIR))
            for part, full in ((0, full_s), (1, full_g)):
                own = jnp.where(lanes, full[:DH], full[DH:]).reshape(8, 8, PAIR)
                sent = jnp.concatenate([own, tail], axis=1).reshape(PAIR, PAIR)
                msg[part, pair * PAIR : (pair + 1) * PAIR, :] = sent.astype(BF)


def project(tokens, prev_tokens, wq, wk, wv, log_decay, cot, lin_scale):
    rows, width = tokens.shape
    heads = log_decay.shape[0]
    vmem = pl.BlockSpec(memory_space=VMEM)
    hbm = pl.BlockSpec(memory_space=pltpu.HBM)
    return pl.pallas_call(
        functools.partial(project_kernel, lin_scale),
        in_specs=[vmem, vmem, hbm, hbm, hbm, vmem, vmem],
        out_specs=[vmem] * 6,
        out_shape=[
            jax.ShapeDtypeStruct((rows, width), BF),
            jax.ShapeDtypeStruct((2, rows, width), BF),
            jax.ShapeDtypeStruct((2, rows, width), BF),
            jax.ShapeDtypeStruct((width // CHUNK, heads * CHUNK // width, rows), F32),
            jax.ShapeDtypeStruct((width // CHUNK, rows, heads * CHUNK // width), F32),
            jax.ShapeDtypeStruct((2, width, PAIR), BF),
        ],
        scratch_shapes=[
            VMEM((3, width // CHUNK, width, CHUNK), BF),
            pltpu.SemaphoreType.DMA((3, width // CHUNK)),
        ],
        compiler_params=params(58),
        cost_estimate=cost(10 * rows * width * width, 6 * width * width + 12 * rows * width),
        name="project",
    )(tokens, prev_tokens, wq, wk, wv, log_decay, cot)


def flip_kernel(tok, after, out):
    del after
    out[...] = tok[...].T


def flip(tokens, after):
    rows, width = tokens.shape
    return pl.pallas_call(
        flip_kernel,
        in_specs=[pl.BlockSpec(memory_space=VMEM), pl.BlockSpec(memory_space=pl.ANY)],
        out_specs=pl.BlockSpec(memory_space=VMEM),
        out_shape=jax.ShapeDtypeStruct((width, rows), BF),
        compiler_params=params(16),
        cost_estimate=cost(0, 4 * rows * width),
        name="flip",
    )(tokens, after)


def scan_kernel(place, got, after, out, xs, decays, states):
    del after
    both = got[...].astype(F32)
    xs[...] = both[:, :8, :]
    total = both[:, 8:9, :] + both[:, 9:10, :] + both[:, 10:11, :]
    decays[...] = jnp.broadcast_to(jnp.exp(total), decays.shape)
    backward = place[0] >= DEVS // 2

    def one(i, state):
        at = jnp.where(backward, DEVS - 1 - i, i)
        states[at] = state
        return decays[at] * state + xs[at]

    lax.fori_loop(0, DEVS, one, jnp.zeros((8, PAIR), F32), unroll=8)
    out[...] = states[...].reshape(DEVS * 8, PAIR).astype(BF)


def scan(place, got, after):
    whole = pl.BlockSpec(memory_space=VMEM)
    return pl.pallas_call(
        scan_kernel,
        in_specs=[
            pl.BlockSpec(memory_space=pltpu.SMEM),
            whole,
            pl.BlockSpec(memory_space=pl.ANY),
        ],
        out_specs=whole,
        out_shape=jax.ShapeDtypeStruct((DEVS * 8, PAIR), BF),
        scratch_shapes=[VMEM((DEVS, 8, PAIR), F32)] * 3,
        compiler_params=params(24),
        cost_estimate=cost(2 * DEVS * 8 * PAIR, 4 * DEVS * 16 * PAIR),
        name="scan",
    )(place, got, after)


def near_kernel(lin_scale, place, blocks, q_ref, kv, pkv, cot, run, runt, out, dq_out, own, prev):
    soft_scale = 1.0 / math.sqrt(DH)
    n_own = jnp.int32(0)
    n_prev = jnp.int32(0)
    for j in range(blocks.shape[1]):
        n_own += (blocks[0, j] == place[0]).astype(jnp.int32)
        n_prev += (blocks[0, j] == place[0] - 1).astype(jnp.int32)
    is_own = iota((1, 2 * SEG), 1) < SEG
    times = jnp.where(is_own, n_own, n_prev)
    bias = jnp.where(times > 0, 0.0, -1e30)
    times = times.astype(F32)
    head_of = iota((SEG, PAIR), 1) // DH
    head_of2 = iota((2 * SEG, PAIR), 1) // DH
    lower = iota((SEG, SEG), 0) >= iota((SEG, SEG), 1)
    zero = jnp.zeros((), BF)
    for pair in range(q_ref.shape[1] // PAIR):
        at = slice(pair * PAIR, (pair + 1) * PAIR)
        q = q_ref[:, at]
        g = cot[:, at]
        kk = jnp.concatenate([kv[0, :, at], pkv[0, :, at]], axis=0)
        vv = jnp.concatenate([kv[1, :, at], pkv[1, :, at]], axis=0)
        res = []
        for i in range(2):
            head = pair * 2 + i
            mine = head_of == i
            col = runt[0, :, head : head + 1]
            row = run[0, head : head + 1, :]
            dec = jnp.where(lower, jnp.exp(jnp.minimum(col - row, 0.0)), 0.0) * lin_scale
            scores = dot(jnp.where(mine, q, zero), kk, 1, 1)
            pgrad = dot(jnp.where(mine, g, zero), vv, 1, 1)
            logits = scores * soft_scale + bias
            peak = jnp.max(logits, axis=1, keepdims=True)
            terms = jnp.exp(logits - peak) * times
            probs = terms * (1.0 / jnp.sum(terms, axis=1, keepdims=True))
            inner = jnp.sum(probs * pgrad, axis=1, keepdims=True)
            dlog = probs * (pgrad - inner) * soft_scale
            a = jnp.concatenate(
                [probs[:, :SEG] + scores[:, :SEG] * dec, probs[:, SEG:]], axis=1
            ).astype(BF)
            b = jnp.concatenate(
                [dlog[:, :SEG] + pgrad[:, :SEG] * dec, dlog[:, SEG:]], axis=1
            ).astype(BF)
            res.append((dot(a, vv, 1, 0), dot(b, kk, 1, 0), dot(b, q, 0, 0), dot(a, g, 0, 0)))
        out[:, at] = jnp.where(head_of == 0, res[0][0], res[1][0])
        dq_out[:, at] = jnp.where(head_of == 0, res[0][1], res[1][1])
        for part in range(2):
            sums = jnp.where(head_of2 == 0, res[0][2 + part], res[1][2 + part])
            own[part, :, at] = sums[:SEG]
            prev[part, :, at] = sums[SEG:].astype(BF)


def near(place, blocks, q, kv, pkv, cot, run, runt, lin_scale):
    rows, width = q.shape
    heads = run.shape[1]
    smem = pl.BlockSpec(memory_space=pltpu.SMEM)
    col = pl.BlockSpec((rows, CHUNK), lambda i: (0, i))
    two = pl.BlockSpec((2, rows, CHUNK), lambda i: (0, 0, i))
    return pl.pallas_call(
        functools.partial(near_kernel, lin_scale),
        grid=(width // CHUNK,),
        in_specs=[
            smem,
            smem,
            col,
            two,
            two,
            col,
            pl.BlockSpec((1, heads, rows), lambda i: (i, 0, 0)),
            pl.BlockSpec((1, rows, heads), lambda i: (i, 0, 0)),
        ],
        out_specs=[col, col, two, two],
        out_shape=[
            jax.ShapeDtypeStruct((rows, width), F32),
            jax.ShapeDtypeStruct((rows, width), F32),
            jax.ShapeDtypeStruct((2, rows, width), F32),
            jax.ShapeDtypeStruct((2, rows, width), BF),
        ],
        compiler_params=params(58),
        cost_estimate=cost(4000 * 1000 * 1000, 16 * 1000 * 1000, 1000 * 1000),
        name="near",
    )(place, blocks, q, kv, pkv, cot, run, runt)


def join_kernel(lin_scale, near_out, dq_in, own, nxt, q, kv, cot, runt, states, after, layer, delta):
    del after
    head_of = iota((SEG, PAIR), 1) // DH
    diag = iota((PAIR, PAIR), 0) // DH == iota((PAIR, PAIR), 1) // DH
    zero = jnp.zeros((), BF)
    for pair in range(q.shape[1] // PAIR):
        at = slice(pair * PAIR, (pair + 1) * PAIR)
        run = jnp.where(
            head_of == 0,
            runt[0, :, 2 * pair : 2 * pair + 1],
            runt[0, :, 2 * pair + 1 : 2 * pair + 2],
        )
        growth = jnp.exp(run) * lin_scale
        fading = jnp.exp(run[SEG - 1 : SEG, :] - run)
        before, after = (
            jnp.where(diag, jnp.concatenate([states[part, pair]] * 2, axis=0), zero)
            for part in range(2)
        )
        layer[:, at] = (near_out[:, at] + growth * dot(q[:, at], before, 1, 0)).astype(BF)
        dq = dq_in[:, at] + growth * dot(cot[:, at], before, 1, 1)
        dk = own[0, :, at] + fading * dot(kv[1, :, at], after, 1, 1) + nxt[0, :, at].astype(F32)
        dv = own[1, :, at] + fading * dot(kv[0, :, at], after, 1, 0) + nxt[1, :, at].astype(F32)
        delta[pair, :, :PAIR] = dq.astype(BF)
        delta[pair, :, PAIR : 2 * PAIR] = dk.astype(BF)
        delta[pair, :, 2 * PAIR :] = dv.astype(BF)


def join(near_out, dq, own, nxt, q, kv, cot, runt, states, after, lin_scale):
    rows, width = q.shape
    pairs = width // PAIR
    col = pl.BlockSpec((rows, CHUNK), lambda i: (0, i))
    two = pl.BlockSpec((2, rows, CHUNK), lambda i: (0, 0, i))
    return pl.pallas_call(
        functools.partial(join_kernel, lin_scale),
        grid=(width // CHUNK,),
        in_specs=[
            col,
            col,
            two,
            two,
            col,
            two,
            col,
            pl.BlockSpec((1, rows, runt.shape[2]), lambda i: (i, 0, 0)),
            pl.BlockSpec((2, CHUNK // PAIR, DH, PAIR), lambda i: (0, i, 0, 0)),
            pl.BlockSpec(memory_space=pl.ANY),
        ],
        out_specs=[col, pl.BlockSpec((CHUNK // PAIR, rows, 3 * PAIR), lambda i: (i, 0, 0))],
        out_shape=[
            jax.ShapeDtypeStruct((rows, width), BF),
            jax.ShapeDtypeStruct((pairs, rows, 3 * PAIR), BF),
        ],
        compiler_params=params(58),
        cost_estimate=cost(8 * rows * PAIR * PAIR * pairs, 24 * rows * width),
        name="join",
    )(near_out, dq, own, nxt, q, kv, cot, runt, states, after)


def back_kernel(delta, wq, wk, wv, out, total):
    step = pl.program_id(0)

    @pl.when(step == 0)
    def _():
        total[...] = jnp.zeros_like(total)

    acc = total[...]
    for part, w in enumerate((wq, wk, wv)):
        for half in range(2):
            acc += dot(
                delta[half, :, part * PAIR : (part + 1) * PAIR],
                w[:, half * PAIR : (half + 1) * PAIR],
                1,
                1,
            )
    total[...] = acc

    @pl.when(step == pl.num_programs(0) - 1)
    def _():
        out[...] = acc.astype(BF)


def back(delta, wq, wk, wv):
    pairs, rows, _ = delta.shape
    width = wq.shape[0]
    weight = pl.BlockSpec((width, 2 * PAIR), lambda i: (0, i))
    return pl.pallas_call(
        back_kernel,
        grid=(pairs // 2,),
        in_specs=[pl.BlockSpec((2, rows, 3 * PAIR), lambda i: (i, 0, 0)), weight, weight, weight],
        out_specs=pl.BlockSpec((rows, width), lambda i: (0, 0)),
        out_shape=jax.ShapeDtypeStruct((rows, width), BF),
        scratch_shapes=[VMEM((rows, width), F32)],
        compiler_params=params(58),
        cost_estimate=cost(6 * rows * width * width, 6 * width * width + 8 * rows * width),
        name="back",
    )(delta, wq, wk, wv)


def outer_kernel(tokt, delta, after, out):
    del after
    near_count, rows, cols = delta.shape
    left = jnp.concatenate([tokt[i] for i in range(near_count)], axis=1)
    out[...] = dot(left, delta[...].reshape(near_count * rows, cols), 1, 0).astype(BF)


def outer(tokt, delta, after):
    near_count, rows, cols = delta.shape
    width = tokt.shape[1]
    return pl.pallas_call(
        outer_kernel,
        grid=(4,),
        in_specs=[
            pl.BlockSpec((near_count, width // 4, rows), lambda i: (0, i, 0)),
            pl.BlockSpec((near_count, rows, cols), lambda i: (0, 0, 0)),
            pl.BlockSpec(memory_space=pl.ANY),
        ],
        out_specs=pl.BlockSpec((width // 4, cols), lambda i: (i, 0)),
        out_shape=jax.ShapeDtypeStruct((width, cols), BF),
        compiler_params=params(58),
        cost_estimate=cost(
            2 * near_count * rows * cols * width, 2 * near_count * rows * (width + cols)
        ),
        name="outer",
    )(tokt, delta, after)


def place_kernel(side, pieces, *rest):
    del side
    for x in range(pieces.shape[0]):
        for r in range(pieces.shape[1]):
            rows = slice(r * pieces.shape[2], (r + 1) * pieces.shape[2])
            for part, o in enumerate(rest[-3:]):
                o[rows, x * PAIR : (x + 1) * PAIR] = pieces[x, r, :, part * PAIR : (part + 1) * PAIR]


def place_half(side, pieces, grads=()):
    near_count, blocks, rows, cols = pieces.shape
    width = blocks * rows
    out = jax.ShapeDtypeStruct((width, width), BF)
    return pl.pallas_call(
        place_kernel,
        grid_spec=pltpu.PrefetchScalarGridSpec(
            num_scalar_prefetch=1,
            grid=(blocks // 4,),
            in_specs=[pl.BlockSpec((near_count, 4, rows, cols), lambda i, side: (0, i, 0, 0))]
            + [pl.BlockSpec(memory_space=pl.ANY)] * len(grads),
            out_specs=[
                pl.BlockSpec((4 * rows, near_count * PAIR), lambda i, side: (i, side[0]))
            ]
            * 3,
        ),
        out_shape=[out] * 3,
        input_output_aliases={2 + i: i for i in range(len(grads))},
        compiler_params=params(24),
        cost_estimate=cost(0, 6 * width * width),
        name="place",
    )(side, pieces, *grads)


def shards(tokens, wq, wk, wv, log_decay, neighbour_blocks, cot):
    rows, width = tokens.shape
    lin_scale = 1.0 / (DH * math.sqrt(rows))
    place = lax.axis_index(AX).astype(jnp.int32).reshape(1)
    core = lax.axis_index("c").astype(jnp.int32).reshape(1)

    prev_tokens = lax.ppermute(tokens, AX, [(i, i + 1) for i in range(DEVS - 1)])
    q, kv, pkv, run, runt, msg = project(
        tokens, prev_tokens, wq, wk, wv, log_decay, cot, lin_scale
    )
    got = lax.all_to_all(msg.reshape(DEVS, 16, PAIR), AX, 0, 0)
    near_out, dq, own, prev = near(
        place, neighbour_blocks, q, kv, pkv, cot, run, runt, lin_scale
    )
    states = scan(place, got, prev)
    tokt = flip(tokens, states)
    tokt8 = lax.all_to_all(jnp.broadcast_to(tokt[None], (8, *tokt.shape)), NEAR8, 0, 0)
    nxt = lax.ppermute(prev, AX, [(i + 1, i) for i in range(DEVS - 1)])
    states = lax.all_to_all(states.reshape(DEVS, 8, PAIR), AX, 0, 0)
    states = states.reshape(2, width // PAIR, DH, PAIR)
    layer, delta = join(near_out, dq, own, nxt, q, kv, cot, runt, states, tokt8, lin_scale)

    delta8 = lax.all_to_all(delta, NEAR8, 0, 0)
    tokens_grad = back(delta, wq, wk, wv)
    partial = outer(tokt8, delta8, tokens_grad)
    parts = lax.all_to_all(partial.reshape(16, width // 16, 3 * PAIR), FAR16, 0, 0)
    grad_norm = 1.0 / math.sqrt(rows * DEVS)
    piece = (jnp.sum(parts.astype(F32), axis=0) * grad_norm).astype(BF)
    plane = lax.all_to_all(jnp.broadcast_to(piece[None], (DEVS // 2, *piece.shape)), PLANE, 0, 0)
    other = lax.ppermute(plane, "c", [(0, 1), (1, 0)])
    shape = (4, 16, *piece.shape)
    grads = place_half(core, plane.reshape(shape))
    gq, gk, gv = place_half(1 - core, other.reshape(shape), grads)
    return layer, tokens_grad, gq, gk, gv


def solution(mesh):
    chips = Mesh(mesh.devices.reshape(2, 2, 4, 4, 2), AX)
    tok = P(AX, None)
    return jax.shard_map(
        shards,
        mesh=chips,
        in_specs=(tok, P(), P(), P(), P(None, AX), tok, tok),
        out_specs=(tok, tok, P(), P(), P()),
        check_vma=False,
    )
```

time: 197 us -> 211 us (1.071)
  waiting for transfers between devices: 22.8 us -> 58.8 us
  blocking collectives: 80.3 us -> 64.1 us
  starting transfers between devices: 28 us -> 41.9 us
  between operations: 14.2 us -> 0.74 us
  local copies, waits for them, and re-layouts: 9.54 us -> 6.21 us
  Pallas kernels: 41.4 us -> 38.1 us
    ppermute x1, waiting for transfers between devices: 3.88 us -> 23.6 us  [shards(): nxt = lax.ppermute(prev, AX, [(i + 1, i) for i in range(DEVS - 1)])]
    all_to_all x1 -> x0, blocking collectives: 16.9 us -> none  [shards(): delta8 = lax.all_to_all(delta, NEAR8, 0, 0)]
    all_to_all x0 -> x2, starting transfers between devices: none -> 15 us  [the longest x1 10.1 us: shards(): delta8 = lax.all_to_all(delta, NEAR8, 0, 0)]
    all_to_all x0 -> x2, waiting for transfers between devices: none -> 6.67 us  [the longest x1 6.67 us: shards(): delta8 = lax.all_to_all(delta, NEAR8, 0, 0)]
    unnamed x34 -> x16, local copies, waits for them, and re-layouts: 9.05 us -> 4.12 us
    ppermute x1, starting transfers between devices: 10.1 us -> 5.57 us  [shards(): nxt = lax.ppermute(prev, AX, [(i + 1, i) for i in range(DEVS - 1)])]
    all_to_all x1, waiting for transfers between devices: 6.5 us -> 10.6 us  [shards(): states = lax.all_to_all(states.reshape(DEVS, 8, PAIR), AX, 0, 0)]
    all_to_all x1, starting transfers between devices: 3.55 us -> 7 us  [shards(): states = lax.all_to_all(states.reshape(DEVS, 8, PAIR), AX, 0, 0)]
  transfers between devices with their start and end apart: 6 -> 7, of which waited for: 3 -> 6; matrix products, arithmetic and copies ran while one was open for 0% -> 0% of each run, Pallas kernels for 16% -> 9%
where the time goes in v3:
time: 211 us; the launch traced here: 210 us
  blocking collectives  64.1 us (30%)
  waiting for transfers between devices  58.8 us (28%)
  starting transfers between devices  41.9 us (20%)
  Pallas kernels  38.1 us (18%)
  local copies, waits for them, and re-layouts  6.21 us (3%)
    all_to_all x1, blocking collectives, shards(): lax.all_to_all(jnp.broadcast_to(piece[None], (DEVS // 2, *piece.shape)),...  43 us
    ppermute x1, waiting for transfers between devices, shards(): nxt = lax.ppermute(prev, AX, [(i + 1, i) for i in range(DEVS - 1)])  23.6 us
    all_to_all x1, blocking collectives, shards(): lax.all_to_all(partial.reshape(16, width // 16, 3 * PAIR), FAR16, 0, 0)  21.1 us
    ppermute x1, waiting for transfers between devices, shards(): lax.ppermute(tokens, AX, [(i, i + 1) for i in range(DEVS - 1)])  12.4 us
    pallas_call x1, Pallas kernels, near(): pl.pallas_call(functools.partial(near_kernel, lin_scale), grid=(width //...  10.7 us
    all_to_all x1, waiting for transfers between devices, shards(): states = lax.all_to_all(states.reshape(DEVS, 8, PAIR), AX, 0, 0)  10.6 us
    all_to_all x1, starting transfers between devices, shards(): delta8 = lax.all_to_all(delta, NEAR8, 0, 0)  10.1 us
    all_to_all x1, starting transfers between devices, shards(): states = lax.all_to_all(states.reshape(DEVS, 8, PAIR), AX, 0, 0)  7 us
  transfers between devices with their start and end apart: 7, of which 6 were waited for; matrix products, arithmetic and copies ran while one was open for 0% of the time, Pallas kernels for 9%

profile of v3, /device:TPU:1, one launch (start us, length us, event | category | flops | bytes accessed | tf_op | source)
XLA Modules:
  0.0 209.9 jit_solution(16880777253145658336)
XLA Ops:
  0.6 5.7 %collective-permute-start = (bf16[128,1024]{1,0:T(8,128)(2,1)}, bf16[128,1024]{1,0:T(8,128)(2,1)S(1)}, u32[]{:S(2)}, u32[]{:S(2)}) collective-permute-start(bf16[128,1024]{1,0:T(8,128)(2,1)} %tok.3), channel_id=1, source_target_pairs={{0,1},{1,2},{2,3},{3,4},{4,5},{5,6},{6,7},{7,8},{8,9},{9,10},{10,1... | collective-permute-start | bytes 786440 | tf_op jit(solution)/shard_map/ppermute | solution.py:438
  6.3 12.4 %collective-permute-done.ptok = bf16[128,1024]{1,0:T(8,128)(2,1)S(1)} collective-permute-done((bf16[128,1024]{1,0:T(8,128)(2,1)}, bf16[128,1024]{1,0:T(8,128)(2,1)S(1)}, u32[]{:S(2)}, u32[]{:S(2)}) %collective-permute-start) | collective-permute-done | bytes 262176 | tf_op jit(solution)/shard_map/ppermute | solution.py:438
  18.7 0.0 copy-start.7
  18.7 0.7 copy-done.7
  19.4 6.5 %project.1 = (bf16[128,1024]{1,0:T(8,128)(2,1)}, bf16[2,128,1024]{2,1,0:T(8,128)(2,1)}, bf16[2,128,1024]{2,1,0:T(8,128)(2,1)}, f32[4,4,128]{2,1,0:T(4,128)}, f32...) custom-call(bf16[128,1024]{1,0:T(8,128)(2,1)} %tok.3, bf16[128,1024]{1,0:T(8,128)(2,1)} %copy-done.7, ...), custom_call_target="tpu_custom_call" | custom-call | flops 1342177280 | bytes 7864320 | tf_op jit(solution)/shard_map/project/pallas_call | solution.py:115
  26.0 5.1 %all-to-all-start = ((bf16[128,16,128]{2,1,0:T(8,128)(2,1)}), bf16[128,16,128]{2,1,0:T(8,128)(2,1)S(1)}, u32[]{:S(2)}, u32[]{:S(2)}) async-start(bf16[128,16,128]{2,1,0:T(8,128)(2,1)} %bitcast.12), calls=%async_computation | async-start | bytes 1048576 | tf_op jit(solution)/shard_map/all_to_all | solution.py:442
  31.0 0.0 copy-start
  31.1 10.7 %near.1 = (f32[128,1024]{1,0:T(8,128)}, f32[128,1024]{1,0:T(8,128)}, f32[2,128,1024]{2,1,0:T(8,128)}, bf16[2,128,1024]{2,1,0:T(8,128)(2,1)}) custom-call(s32[1]{0:T(128)} %bitcast.place, s32[1,4]{1,0:T(1,128)} %blocks.1, bf16[128,1024]{1,0:T(8,128)(2,1)} %get-tuple-element.23.q_ref.q, bf16[2,128,1024]{2,1,0:T(8,128)(2,1)} %get-tuple-element.24.kv, ...), custom_call_target="tpu_custom_call" | custom-call | flops 4000000000 | bytes 16000000 | tf_op jit(solution)/shard_map/near/pallas_call | solution.py:247
  41.7 2.8 %all-to-all-done.got = bf16[128,16,128]{2,1,0:T(8,128)(2,1)S(1)} async-done(((bf16[128,16,128]{2,1,0:T(8,128)(2,1)}), bf16[128,16,128]{2,1,0:T(8,128)(2,1)S(1)}, u32[]{:S(2)}, u32[]{:S(2)}) %all-to-all-start) | async-done | bytes 524320 | tf_op jit(solution)/shard_map/all_to_all | solution.py:442
  44.5 0.0 copy-start.1
  44.5 1.0 copy-done.1
  45.5 1.2 scan.1.after
  46.8 7.0 %all-to-all-start.1 = ((bf16[128,8,128]{2,1,0:T(8,128)(2,1)}), bf16[128,8,128]{2,1,0:T(8,128)(2,1)S(1)}, u32[]{:S(2)}, u32[]{:S(2)}) async-start(bf16[128,8,128]{2,1,0:T(8,128)(2,1)} %bitcast.2), calls=%async_computation.1 | async-start | bytes 524288 | tf_op jit(solution)/shard_map/all_to_all | solution.py:450
  53.8 0.0 copy-done
  53.8 0.1 flip.1
  53.9 10.6 %all-to-all-done.1 = bf16[128,8,128]{2,1,0:T(8,128)(2,1)S(1)} async-done(((bf16[128,8,128]{2,1,0:T(8,128)(2,1)}), bf16[128,8,128]{2,1,0:T(8,128)(2,1)S(1)}, u32[]{:S(2)}, u32[]{:S(2)}) %all-to-all-start.1) | async-done | bytes 262176 | tf_op jit(solution)/shard_map/all_to_all | solution.py:450
  64.5 0.0 copy-start.5
  64.5 1.6 broadcast_in_dim.4
  66.1 0.0 copy-start.2
  66.1 0.0 copy-done.5
  66.1 4.8 %all-to-all-start.2 = ((bf16[8,1024,128]{2,1,0:T(8,128)(2,1)}), bf16[8,1024,128]{2,1,0:T(8,128)(2,1)S(1)}, u32[]{:S(2)}, u32[]{:S(2)}) async-start(bf16[8,1024,128]{2,1,0:T(8,128)(2,1)} %broadcast_in_dim.4), calls=%async_computation.2 | async-start | bytes 4194304 | tf_op jit(solution)/shard_map/all_to_all | solution.py:448
  71.0 0.0 copy-done.2
  71.0 5.6 %collective-permute-start.1 = (bf16[2,128,1024]{2,1,0:T(8,128)(2,1)S(1)}, bf16[2,128,1024]{2,1,0:T(8,128)(2,1)S(1)}, u32[]{:S(2)}, u32[]{:S(2)}) collective-permute-start(bf16[2,128,1024]{2,1,0:T(8,128)(2,1)S(1)} %copy-done.2), channel_id=1, source_target_pairs={{1,0},{2,1},{3,2},{4,3},{5,4},{6,5},{7,6},{8,7},{9,8},{10,9},{11,1... | collective-permute-start | bytes 1572872 | tf_op jit(solution)/shard_map/ppermute | solution.py:449
  76.5 23.6 %collective-permute-done.1.nxt = bf16[2,128,1024]{2,1,0:T(8,128)(2,1)S(1)} collective-permute-done((bf16[2,128,1024]{2,1,0:T(8,128)(2,1)S(1)}, bf16[2,128,1024]{2,1,0:T(8,128)(2,1)S(1)}, u32[]{:S(2)}, u32[]{:S(2)}) %collective-permute-start.1) | collective-permute-done | bytes 524320 | tf_op jit(solution)/shard_map/ppermute | solution.py:449
  100.1 0.0 copy-start.6
  100.1 0.0 all-to-all-done.2.after.tokt
  100.1 0.0 copy-start.3
  100.1 0.8 copy-done.6
  100.9 0.7 copy-done.3
  101.6 4.3 %join.1 = (bf16[128,1024]{1,0:T(8,128)(2,1)}, bf16[8,128,384]{2,1,0:T(8,128)(2,1)}) custom-call(f32[128,1024]{1,0:T(8,128)} %get-tuple-element.28.near_out, f32[128,1024]{1,0:T(8,128)} %get-tuple-element.29.dq_in, f32[2,128,1024]{2,1,0:T(8,128)} %get-tuple-element.30.own, bf16[2,128,1024]{2,1,0:T(8,128)(2,1)} %copy-done.6, ...), custom_call_target="tpu_custom_call" | custom-call | flops 134217728 | bytes 3145728 | tf_op jit(solution)/shard_map/join/pallas_call | solution.py:305
  105.9 10.1 %all-to-all-start.3 = ((bf16[8,128,384]{2,1,0:T(8,128)(2,1)}), bf16[8,128,384]{2,1,0:T(8,128)(2,1)S(1)}, u32[]{:S(2)}, u32[]{:S(2)}) async-start(bf16[8,128,384]{2,1,0:T(8,128)(2,1)} %get-tuple-element.34.delta), calls=%async_computation.3 | async-start | bytes 1572864 | tf_op jit(solution)/shard_map/all_to_all | solution.py:454
  116.0 5.5 %back.1.after = bf16[128,1024]{1,0:T(8,128)(2,1)} custom-call(bf16[8,128,384]{2,1,0:T(8,128)(2,1)} %get-tuple-element.34.delta, bf16[1024,1024]{1,0:T(8,128)(2,1)} %wq.3, bf16[1024,1024]{1,0:T(8,128)(2,1)} %wk.3, bf16[1024,1024]{1,0:T(8,128)(2,1)} %wv.3), custom_call_target="tpu_custom_call" | custom-call | flops 805306368 | bytes 7340032 | tf_op jit(solution)/shard_map/back/pallas_call | solution.py:358
  121.5 6.7 %all-to-all-done.3.delta = bf16[8,128,384]{2,1,0:T(8,128)(2,1)S(1)} async-done(((bf16[8,128,384]{2,1,0:T(8,128)(2,1)}), bf16[8,128,384]{2,1,0:T(8,128)(2,1)S(1)}, u32[]{:S(2)}, u32[]{:S(2)}) %all-to-all-start.3) | async-done | bytes 786464 | tf_op jit(solution)/shard_map/all_to_all | solution.py:454
  128.2 0.0 copy-start.4
  128.2 0.9 copy-done.4
  129.1 4.6 %outer.1 = bf16[1024,384]{1,0:T(8,128)(2,1)} custom-call(bf16[8,1024,128]{2,1,0:T(8,128)(2,1)} %copy-done.3, bf16[8,128,384]{2,1,0:T(8,128)(2,1)} %copy-done.4, bf16[128,1024]{1,0:T(8,128)(2,1)} %back.1.after), custom_call_target="tpu_custom_call" | custom-call | flops 805306368 | bytes 2883584 | tf_op jit(solution)/shard_map/outer/pallas_call | solution.py:381
  133.7 21.1 %all_to_all.30 = bf16[16,64,384]{2,1,0:T(8,128)(2,1)S(1)} all-to-all(bf16[16,64,384]{2,1,0:T(8,128)(2,1)} %bitcast.10), channel_id=1, replica_groups=mesh['yl'=2,'c'=2,'x'=4,'z'=4,'yh'=2] {'yl','z','yh'}, dimensions={0} | all-to-all | bytes 1572864 | tf_op jit(solution)/shard_map/all_to_all | solution.py:457
  154.8 0.1 convert_reduce_fusion
  154.9 0.5 broadcast_in_dim.5
  155.4 43.0 %all_to_all.31 = bf16[64,64,384]{2,1,0:T(8,128)(2,1)S(1)} all-to-all(bf16[64,64,384]{2,1,0:T(8,128)(2,1)S(1)} %broadcast_in_dim.5), channel_id=1, replica_groups=mesh['yl'=2,'c'=2,'x'=4,'z'=4,'yh'=2] {'x','yl','z','yh'}, dimensions={0} | all-to-all | bytes 6291456 | tf_op jit(solution)/shard_map/all_to_all | solution.py:460
  198.4 3.6 %collective-permute-start.2 = (bf16[64,64,384]{2,1,0:T(8,128)(2,1)S(1)}, bf16[64,64,384]{2,1,0:T(8,128)(2,1)S(1)}, u32[]{:S(2)}, u32[]{:S(2)}) collective-permute-start(bf16[64,64,384]{2,1,0:T(8,128)(2,1)S(1)} %all_to_all.31), channel_id=1, source_target_pairs={{0,32},{32,0},{1,33},{33,1},{2,34},{34,2},{3,35},{35,3},{4,36},{36... | collective-permute-start | bytes 9437192 | tf_op jit(solution)/shard_map/ppermute | solution.py:461
  202.0 2.6 %place.2 = (bf16[1024,1024]{1,0:T(8,128)(2,1)}, bf16[1024,1024]{1,0:T(8,128)(2,1)}, bf16[1024,1024]{1,0:T(8,128)(2,1)}) custom-call(s32[1]{0:T(128)} %bitcast.4.side, bf16[4,16,64,384]{3,2,1,0:T(8,128)(2,1)S(1)} %bitcast.8), custom_call_target="tpu_custom_call" | custom-call | bytes 6291456 | tf_op jit(solution)/shard_map/place/pallas_call | solution.py:412
  204.6 2.7 %collective-permute-done.2 = bf16[64,64,384]{2,1,0:T(8,128)(2,1)S(1)} collective-permute-done((bf16[64,64,384]{2,1,0:T(8,128)(2,1)S(1)}, bf16[64,64,384]{2,1,0:T(8,128)(2,1)S(1)}, u32[]{:S(2)}, u32[]{:S(2)}) %collective-permute-start.2) | collective-permute-done | bytes 3145760 | tf_op jit(solution)/shard_map/ppermute | solution.py:461
  207.3 2.6 %place.3 = (bf16[1024,1024]{1,0:T(8,128)(2,1)}, bf16[1024,1024]{1,0:T(8,128)(2,1)}, bf16[1024,1024]{1,0:T(8,128)(2,1)}) custom-call(s32[1]{0:T(128)S(6)} %sub.3.side, bf16[4,16,64,384]{3,2,1,0:T(8,128)(2,1)S(1)} %bitcast.9, bf16[1024,1024]{1,0:T(8,128)(2,1)} %get-tuple-element.35.rest_0_, ...), custom_call_target="tpu_custom_call", output_to_operand_aliasing={{0}: (2, {}), {1}: (3, {}), {2}: (4, {})} | custom-call | bytes 6291456 | tf_op jit(solution)/shard_map/place/pallas_call | solution.py:412
  (1 shorter events, 0.0 us)
Async XLA Ops:
  0.6 18.1 %collective-permute-start = (bf16[128,1024]{1,0:T(8,128)(2,1)}, bf16[128,1024]{1,0:T(8,128)(2,1)S(1)}, u32[]{:S(2)}, u32[]{:S(2)}) collective-permute-start(bf16[128,1024]{1,0:T(8,128)(2,1)} %tok.3), channel_id=1, source_target_pairs={{0,1},{1,2},{2,3},{3,4},{4,5},{5,6},{6,7},{7,8},{8,9},{9,10},{10,1... | collective-permute-start | bytes 786440 | tf_op jit(solution)/shard_map/ppermute | solution.py:438
  18.7 0.7 copy-start.7
  26.0 18.5 %all-to-all-start = ((bf16[128,16,128]{2,1,0:T(8,128)(2,1)}), bf16[128,16,128]{2,1,0:T(8,128)(2,1)S(1)}, u32[]{:S(2)}, u32[]{:S(2)}) async-start(bf16[128,16,128]{2,1,0:T(8,128)(2,1)} %bitcast.12), calls=%async_computation | async-start | bytes 1048576 | tf_op jit(solution)/shard_map/all_to_all | solution.py:442
  31.0 22.7 %copy-start = (bf16[128,1024]{1,0:T(8,128)(2,1)S(1)}, bf16[128,1024]{1,0:T(8,128)(2,1)}, u32[]{:S(2)}) copy-start(bf16[128,1024]{1,0:T(8,128)(2,1)} %tok.3) | copy-start | bytes 786436
  44.5 1.0 copy-start.1
  46.8 17.7 %all-to-all-start.1 = ((bf16[128,8,128]{2,1,0:T(8,128)(2,1)}), bf16[128,8,128]{2,1,0:T(8,128)(2,1)S(1)}, u32[]{:S(2)}, u32[]{:S(2)}) async-start(bf16[128,8,128]{2,1,0:T(8,128)(2,1)} %bitcast.2), calls=%async_computation.1 | async-start | bytes 524288 | tf_op jit(solution)/shard_map/all_to_all | solution.py:450
  64.5 1.6 copy-start.5
  66.1 4.9 %copy-start.2 = (bf16[2,128,1024]{2,1,0:T(8,128)(2,1)S(1)}, bf16[2,128,1024]{2,1,0:T(8,128)(2,1)}, u32[]{:S(2)}) copy-start(bf16[2,128,1024]{2,1,0:T(8,128)(2,1)} %get-tuple-element.31.after) | copy-start | bytes 1572868
  66.1 34.0 %all-to-all-start.2 = ((bf16[8,1024,128]{2,1,0:T(8,128)(2,1)}), bf16[8,1024,128]{2,1,0:T(8,128)(2,1)S(1)}, u32[]{:S(2)}, u32[]{:S(2)}) async-start(bf16[8,1024,128]{2,1,0:T(8,128)(2,1)} %broadcast_in_dim.4), calls=%async_computation.2 | async-start | bytes 4194304 | tf_op jit(solution)/shard_map/all_to_all | solution.py:448
  71.0 29.1 %collective-permute-start.1 = (bf16[2,128,1024]{2,1,0:T(8,128)(2,1)S(1)}, bf16[2,128,1024]{2,1,0:T(8,128)(2,1)S(1)}, u32[]{:S(2)}, u32[]{:S(2)}) collective-permute-start(bf16[2,128,1024]{2,1,0:T(8,128)(2,1)S(1)} %copy-done.2), channel_id=1, source_target_pairs={{1,0},{2,1},{3,2},{4,3},{5,4},{6,5},{7,6},{8,7},{9,8},{10,9},{11,1... | collective-permute-start | bytes 1572872 | tf_op jit(solution)/shard_map/ppermute | solution.py:449
  100.1 0.8 copy-start.6
  100.1 1.5 copy-start.3
  105.9 22.3 %all-to-all-start.3 = ((bf16[8,128,384]{2,1,0:T(8,128)(2,1)}), bf16[8,128,384]{2,1,0:T(8,128)(2,1)S(1)}, u32[]{:S(2)}, u32[]{:S(2)}) async-start(bf16[8,128,384]{2,1,0:T(8,128)(2,1)} %get-tuple-element.34.delta), calls=%async_computation.3 | async-start | bytes 1572864 | tf_op jit(solution)/shard_map/all_to_all | solution.py:454
  128.2 0.9 copy-start.4
  198.4 8.9 %collective-permute-start.2 = (bf16[64,64,384]{2,1,0:T(8,128)(2,1)S(1)}, bf16[64,64,384]{2,1,0:T(8,128)(2,1)S(1)}, u32[]{:S(2)}, u32[]{:S(2)}) collective-permute-start(bf16[64,64,384]{2,1,0:T(8,128)(2,1)S(1)} %all_to_all.31), channel_id=1, source_target_pairs={{0,32},{32,0},{1,33},{33,1},{2,34},{34,2},{3,35},{35,3},{4,36},{36... | collective-permute-start | bytes 9437192 | tf_op jit(solution)/shard_map/ppermute | solution.py:461

commit v4 on v3

--- a/solution.py
+++ b/solution.py
@@ -44,7 +44,7 @@
 CHUNK = 256
 
 
-def project_kernel(lin_scale, tok, ptok, wq, wk, wv, decay, cot, q_out, kv_out, pkv_out, run_out, runt_out, msg, held, sems):
+def project_kernel(lin_scale, tok, wq, wk, wv, decay, cot, q_out, kv_out, run_out, runt_out, msg, held, sems):
     width = tok.shape[1]
     chunks = width // CHUNK
     copies = []
@@ -56,7 +56,6 @@
             copy.start()
             copies.append(copy)
     x = tok[...]
-    both = jnp.concatenate([x, ptok[...]], axis=0)
     ld = decay[...]
     heads = ld.shape[0]
     lower = (iota((SEG, SEG), 0) >= iota((SEG, SEG), 1)).astype(F32)
@@ -74,14 +73,11 @@
             copies[step * 3 + part].wait()
         at = slice(step * CHUNK, (step + 1) * CHUNK)
         q = dot(x, held[0, step], 1, 0).astype(BF)
-        kk = dot(both, held[1, step], 1, 0).astype(BF)
-        vv = dot(both, held[2, step], 1, 0).astype(BF)
-        k, v = kk[:SEG], vv[:SEG]
+        k = dot(x, held[1, step], 1, 0).astype(BF)
+        v = dot(x, held[2, step], 1, 0).astype(BF)
         q_out[:, at] = q
         kv_out[0, :, at] = k
         kv_out[1, :, at] = v
-        pkv_out[0, :, at] = kk[SEG:]
-        pkv_out[1, :, at] = vv[SEG:]
         for half in range(CHUNK // PAIR):
             cols = slice(half * PAIR, (half + 1) * PAIR)
             pair = step * (CHUNK // PAIR) + half
@@ -107,18 +103,17 @@
                 msg[part, pair * PAIR : (pair + 1) * PAIR, :] = sent.astype(BF)
 
 
-def project(tokens, prev_tokens, wq, wk, wv, log_decay, cot, lin_scale):
+def project(tokens, wq, wk, wv, log_decay, cot, lin_scale):
     rows, width = tokens.shape
     heads = log_decay.shape[0]
     vmem = pl.BlockSpec(memory_space=VMEM)
     hbm = pl.BlockSpec(memory_space=pltpu.HBM)
     return pl.pallas_call(
         functools.partial(project_kernel, lin_scale),
-        in_specs=[vmem, vmem, hbm, hbm, hbm, vmem, vmem],
-        out_specs=[vmem] * 6,
+        in_specs=[vmem, hbm, hbm, hbm, vmem, vmem],
+        out_specs=[vmem] * 5,
         out_shape=[
             jax.ShapeDtypeStruct((rows, width), BF),
-            jax.ShapeDtypeStruct((2, rows, width), BF),
             jax.ShapeDtypeStruct((2, rows, width), BF),
             jax.ShapeDtypeStruct((width // CHUNK, heads * CHUNK // width, rows), F32),
             jax.ShapeDtypeStruct((width // CHUNK, rows, heads * CHUNK // width), F32),
@@ -129,9 +124,9 @@
             pltpu.SemaphoreType.DMA((3, width // CHUNK)),
         ],
         compiler_params=params(58),
-        cost_estimate=cost(10 * rows * width * width, 6 * width * width + 12 * rows * width),
+        cost_estimate=cost(6 * rows * width * width, 6 * width * width + 12 * rows * width),
         name="project",
-    )(tokens, prev_tokens, wq, wk, wv, log_decay, cot)
+    )(tokens, wq, wk, wv, log_decay, cot)
 
 
 def flip_kernel(tok, after, out):
@@ -150,6 +145,26 @@
         cost_estimate=cost(0, 4 * rows * width),
         name="flip",
     )(tokens, after)
+
+
+def stack_kernel(*refs):
+    out = refs[-1]
+    for i in range(out.shape[0]):
+        out[i] = refs[i][...]
+
+
+def stack(parts, after):
+    shape = parts[0].shape
+    whole = pl.BlockSpec(memory_space=VMEM)
+    return pl.pallas_call(
+        stack_kernel,
+        in_specs=[whole] * len(parts) + [pl.BlockSpec(memory_space=pl.ANY)],
+        out_specs=whole,
+        out_shape=jax.ShapeDtypeStruct((len(parts), *shape), BF),
+        compiler_params=params(16),
+        cost_estimate=cost(0, 4 * len(parts) * shape[0] * shape[1]),
+        name="stack",
+    )(*parts, after)
 
 
 def scan_kernel(place, got, after, out, xs, decays, states):
@@ -270,8 +285,8 @@
     )(place, blocks, q, kv, pkv, cot, run, runt)
 
 
-def join_kernel(lin_scale, near_out, dq_in, own, nxt, q, kv, cot, runt, states, after, layer, delta):
-    del after
+def join_kernel(lin_scale, near_out, dq_in, own, nxt, q, kv, cot, runt, states, *rest):
+    layer, delta = rest[-2:]
     head_of = iota((SEG, PAIR), 1) // DH
     diag = iota((PAIR, PAIR), 0) // DH == iota((PAIR, PAIR), 1) // DH
     zero = jnp.zeros((), BF)
@@ -315,8 +330,8 @@
             col,
             pl.BlockSpec((1, rows, runt.shape[2]), lambda i: (i, 0, 0)),
             pl.BlockSpec((2, CHUNK // PAIR, DH, PAIR), lambda i: (0, i, 0, 0)),
-            pl.BlockSpec(memory_space=pl.ANY),
-        ],
+        ]
+        + [pl.BlockSpec(memory_space=pl.ANY)] * len(after),
         out_specs=[col, pl.BlockSpec((CHUNK // PAIR, rows, 3 * PAIR), lambda i: (i, 0, 0))],
         out_shape=[
             jax.ShapeDtypeStruct((rows, width), BF),
@@ -325,7 +340,7 @@
         compiler_params=params(58),
         cost_estimate=cost(8 * rows * PAIR * PAIR * pairs, 24 * rows * width),
         name="join",
-    )(near_out, dq, own, nxt, q, kv, cot, runt, states, after)
+    )(near_out, dq, own, nxt, q, kv, cot, runt, states, *after)
 
 
 def back_kernel(delta, wq, wk, wv, out, total):
@@ -368,21 +383,31 @@
     )(delta, wq, wk, wv)
 
 
-def outer_kernel(tokt, delta, after, out):
+def outer_kernel(core, at_x, mine, theirs, delta, after, out):
     del after
+    near_x = mine.shape[0]
+    left, right = [], []
+    for tokt, c in ((mine, core[0]), (theirs, 1 - core[0])):
+        for i in range(near_x):
+            left.append(tokt[i])
+            right.append(delta[c * near_x + lax.rem(at_x[0] + near_x - i, near_x)])
+    left = jnp.concatenate(left, axis=1)
+    out[...] = dot(left, jnp.concatenate(right, axis=0), 1, 0).astype(BF)
+
+
+def outer(core, at_x, mine, theirs, delta, after):
     near_count, rows, cols = delta.shape
-    left = jnp.concatenate([tokt[i] for i in range(near_count)], axis=1)
-    out[...] = dot(left, delta[...].reshape(near_count * rows, cols), 1, 0).astype(BF)
-
-
-def outer(tokt, delta, after):
-    near_count, rows, cols = delta.shape
-    width = tokt.shape[1]
+    width = mine.shape[1]
+    smem = pl.BlockSpec(memory_space=pltpu.SMEM)
+    tok = pl.BlockSpec((near_count // 2, width // 4, rows), lambda i: (0, i, 0))
     return pl.pallas_call(
         outer_kernel,
         grid=(4,),
         in_specs=[
-            pl.BlockSpec((near_count, width // 4, rows), lambda i: (0, i, 0)),
+            smem,
+            smem,
+            tok,
+            tok,
             pl.BlockSpec((near_count, rows, cols), lambda i: (0, 0, 0)),
             pl.BlockSpec(memory_space=pl.ANY),
         ],
@@ -393,7 +418,7 @@
             2 * near_count * rows * cols * width, 2 * near_count * rows * (width + cols)
         ),
         name="outer",
-    )(tokt, delta, after)
+    )(core, at_x, mine, theirs, delta, after)
 
 
 def place_kernel(side, pieces, *rest):
@@ -435,30 +460,32 @@
     place = lax.axis_index(AX).astype(jnp.int32).reshape(1)
     core = lax.axis_index("c").astype(jnp.int32).reshape(1)
 
-    prev_tokens = lax.ppermute(tokens, AX, [(i, i + 1) for i in range(DEVS - 1)])
-    q, kv, pkv, run, runt, msg = project(
-        tokens, prev_tokens, wq, wk, wv, log_decay, cot, lin_scale
-    )
+    at_x = lax.axis_index("x").astype(jnp.int32).reshape(1)
+    swap = [(0, 1), (1, 0)]
+    q, kv, run, runt, msg = project(tokens, wq, wk, wv, log_decay, cot, lin_scale)
+    pkv = lax.ppermute(kv, AX, [(i, i + 1) for i in range(DEVS - 1)])
     got = lax.all_to_all(msg.reshape(DEVS, 16, PAIR), AX, 0, 0)
     near_out, dq, own, prev = near(
         place, neighbour_blocks, q, kv, pkv, cot, run, runt, lin_scale
     )
+    nxt = lax.ppermute(prev, AX, [(i + 1, i) for i in range(DEVS - 1)])
     states = scan(place, got, prev)
-    tokt = flip(tokens, states)
-    tokt8 = lax.all_to_all(jnp.broadcast_to(tokt[None], (8, *tokt.shape)), NEAR8, 0, 0)
-    nxt = lax.ppermute(prev, AX, [(i + 1, i) for i in range(DEVS - 1)])
+    tokt = flip(tokens, prev)
+    around = [lax.ppermute(tokt, "x", [(i, (i + d) % 4) for i in range(4)]) for d in (1, 2, 3)]
     states = lax.all_to_all(states.reshape(DEVS, 8, PAIR), AX, 0, 0)
     states = states.reshape(2, width // PAIR, DH, PAIR)
-    layer, delta = join(near_out, dq, own, nxt, q, kv, cot, runt, states, tokt8, lin_scale)
+    layer, delta = join(near_out, dq, own, nxt, q, kv, cot, runt, states, [], lin_scale)
 
     delta8 = lax.all_to_all(delta, NEAR8, 0, 0)
+    mine = stack([tokt, *around], delta)
+    theirs = lax.ppermute(mine, "c", swap)
     tokens_grad = back(delta, wq, wk, wv)
-    partial = outer(tokt8, delta8, tokens_grad)
+    partial = outer(core, at_x, mine, theirs, delta8, tokens_grad)
     parts = lax.all_to_all(partial.reshape(16, width // 16, 3 * PAIR), FAR16, 0, 0)
     grad_norm = 1.0 / math.sqrt(rows * DEVS)
     piece = (jnp.sum(parts.astype(F32), axis=0) * grad_norm).astype(BF)
     plane = lax.all_to_all(jnp.broadcast_to(piece[None], (DEVS // 2, *piece.shape)), PLANE, 0, 0)
-    other = lax.ppermute(plane, "c", [(0, 1), (1, 0)])
+    other = lax.ppermute(plane, "c", swap)
     shape = (4, 16, *piece.shape)
     grads = place_half(core, plane.reshape(shape))
     gq, gk, gv = place_half(1 - core, other.reshape(shape), grads)

time: 211 us -> 174 us (0.82)
  waiting for transfers between devices: 58.8 us -> 27.6 us
    ppermute x1, waiting for transfers between devices: 23.6 us -> 0.01 us  [shards(): nxt = lax.ppermute(prev, AX, [(i + 1, i) for i in range(DEVS - 1)])]
    all_to_all x1, starting transfers between devices: 10.1 us -> 3.53 us  [shards(): delta8 = lax.all_to_all(delta, NEAR8, 0, 0)]
    all_to_all x1 -> x0, starting transfers between devices: 4.85 us -> none  [shards(): lax.all_to_all(jnp.broadcast_to(tokt[None], (8, *tokt.shape)), NEAR8, 0, 0)]
    all_to_all x1, starting transfers between devices: 5.06 us -> 9.71 us  [shards(): got = lax.all_to_all(msg.reshape(DEVS, 16, PAIR), AX, 0, 0)]
    ppermute x2 -> x6, starting transfers between devices: 9.29 us -> 13.6 us  [the longest x1 5.65 us: shards(): pkv = lax.ppermute(kv, AX, [(i, i + 1) for i in range(DEVS - 1)])]
    ppermute x1, starting transfers between devices: 5.57 us -> 9.48 us  [shards(): nxt = lax.ppermute(prev, AX, [(i + 1, i) for i in range(DEVS - 1)])]
    all_to_all x1, waiting for transfers between devices: 10.6 us -> 6.78 us  [shards(): states = lax.all_to_all(states.reshape(DEVS, 8, PAIR), AX, 0, 0)]
    all_to_all x1, starting transfers between devices: 7 us -> 3.66 us  [shards(): states = lax.all_to_all(states.reshape(DEVS, 8, PAIR), AX, 0, 0)]
  transfers between devices with their start and end apart: 7 -> 10, of which waited for: 6 -> 5; matrix products, arithmetic and copies ran while one was open for 0% -> 0% of each run, Pallas kernels for 9% -> 14%
where the time goes in v4:
time: 174 us
  blocking collectives  63.3 us (36%)
  starting transfers between devices  40 us (23%)
  Pallas kernels  37.5 us (22%)
  waiting for transfers between devices  27.6 us (16%)
  local copies, waits for them, and re-layouts  4.46 us (3%)
    all_to_all x1, blocking collectives, shards(): lax.all_to_all(jnp.broadcast_to(piece[None], (DEVS // 2, *piece.shape)),...  43 us
    all_to_all x1, blocking collectives, shards(): lax.all_to_all(partial.reshape(16, width // 16, 3 * PAIR), FAR16, 0, 0)  20.2 us
    pallas_call x1, Pallas kernels, near(): pl.pallas_call(functools.partial(near_kernel, lin_scale), grid=(width //...  10.6 us
    all_to_all x1, starting transfers between devices, shards(): got = lax.all_to_all(msg.reshape(DEVS, 16, PAIR), AX, 0, 0)  9.71 us
    ppermute x1, starting transfers between devices, shards(): nxt = lax.ppermute(prev, AX, [(i + 1, i) for i in range(DEVS - 1)])  9.48 us
    ppermute x1, waiting for transfers between devices, shards(): pkv = lax.ppermute(kv, AX, [(i, i + 1) for i in range(DEVS - 1)])  9.18 us
    all_to_all x1, waiting for transfers between devices, shards(): states = lax.all_to_all(states.reshape(DEVS, 8, PAIR), AX, 0, 0)  6.78 us
    all_to_all x1, waiting for transfers between devices, shards(): delta8 = lax.all_to_all(delta, NEAR8, 0, 0)  6.67 us
  transfers between devices with their start and end apart: 10, of which 5 were waited for; matrix products, arithmetic and copies ran while one was open for 0% of the time, Pallas kernels for 14%

profile of v4, /device:TPU:1, one launch (start us, length us, event | category | flops | bytes accessed | tf_op | source)
XLA Modules:
  0.0 173.7 jit_solution(7558698270757972552)
XLA Ops:
  0.6 5.9 %project.1 = (bf16[128,1024]{1,0:T(8,128)(2,1)}, bf16[2,128,1024]{2,1,0:T(8,128)(2,1)}, f32[4,4,128]{2,1,0:T(4,128)}, f32[4,128,4]{2,1,0:T(8,128)}, bf16[2,1024,128]{2,1,0:T(8,128)(2,1)}) custom-call(bf16[128,1024]{1,0:T(8,128)(2,1)} %tok.3, bf16[1024,1024]{1,0:T(8,128)(2,1)} %wq.3, bf16[1024,1024]{1,0:T(8,128)(2,1)} %wk.3, bf16[1024,1024]{1,0:T(8,128)(2,1)} %wv.3, ...), custom_call_target="tpu_custom_call" | custom-call | flops 805306368 | bytes 7864320 | tf_op jit(solution)/shard_map/project/pallas_call | solution.py:111
  6.5 5.7 %collective-permute-start = (bf16[2,128,1024]{2,1,0:T(8,128)(2,1)}, bf16[2,128,1024]{2,1,0:T(8,128)(2,1)S(1)}, u32[]{:S(2)}, u32[]{:S(2)}) collective-permute-start(bf16[2,128,1024]{2,1,0:T(8,128)(2,1)} %get-tuple-element.23.kv), channel_id=1, source_target_pairs={{0,1},{1,2},{2,3},{3,4},{4,5},{5,6},{6,7},{7,8},{8,9},{9,10},{10,1... | collective-permute-start | bytes 1572872 | tf_op jit(solution)/shard_map/ppermute | solution.py:466
  12.2 9.7 %all-to-all-start = ((bf16[128,16,128]{2,1,0:T(8,128)(2,1)}), bf16[128,16,128]{2,1,0:T(8,128)(2,1)S(1)}, u32[]{:S(2)}, u32[]{:S(2)}) async-start(bf16[128,16,128]{2,1,0:T(8,128)(2,1)} %bitcast.13), calls=%async_computation | async-start | bytes 1048576 | tf_op jit(solution)/shard_map/all_to_all | solution.py:467
  21.9 9.2 %collective-permute-done.pkv = bf16[2,128,1024]{2,1,0:T(8,128)(2,1)S(1)} collective-permute-done((bf16[2,128,1024]{2,1,0:T(8,128)(2,1)}, bf16[2,128,1024]{2,1,0:T(8,128)(2,1)S(1)}, u32[]{:S(2)}, u32[]{:S(2)}) %collective-permute-start) | collective-permute-done | bytes 524320 | tf_op jit(solution)/shard_map/ppermute | solution.py:466
  31.1 0.0 copy-start.8
  31.1 0.8 copy-done.8
  31.9 0.0 copy-start.3
  31.9 10.6 %near.1 = (f32[128,1024]{1,0:T(8,128)}, f32[128,1024]{1,0:T(8,128)}, f32[2,128,1024]{2,1,0:T(8,128)}, bf16[2,128,1024]{2,1,0:T(8,128)(2,1)}) custom-call(s32[1]{0:T(128)} %bitcast.place, s32[1,4]{1,0:T(1,128)} %blocks.1, bf16[128,1024]{1,0:T(8,128)(2,1)} %get-tuple-element.22.q_ref.q, bf16[2,128,1024]{2,1,0:T(8,128)(2,1)} %get-tuple-element.23.kv, ...), custom_call_target="tpu_custom_call" | custom-call | flops 4000000000 | bytes 16000000 | tf_op jit(solution)/shard_map/near/pallas_call | solution.py:262
  42.6 9.5 %collective-permute-start.1 = (bf16[2,128,1024]{2,1,0:T(8,128)(2,1)}, bf16[2,128,1024]{2,1,0:T(8,128)(2,1)S(1)}, u32[]{:S(2)}, u32[]{:S(2)}) collective-permute-start(bf16[2,128,1024]{2,1,0:T(8,128)(2,1)} %get-tuple-element.29.after), channel_id=1, source_target_pairs={{1,0},{2,1},{3,2},{4,3},{5,4},{6,5},{7,6},{8,7},{9,8},{10,9},{11,1... | collective-permute-start | bytes 1572872 | tf_op jit(solution)/shard_map/ppermute | solution.py:471
  52.1 0.0 all-to-all-done.got
  52.1 0.0 copy-start.1
  52.1 1.0 copy-done.1
  53.1 0.0 copy-start.2
  53.1 1.2 scan.1
  54.3 3.7 %all-to-all-start.1 = ((bf16[128,8,128]{2,1,0:T(8,128)(2,1)}), bf16[128,8,128]{2,1,0:T(8,128)(2,1)S(1)}, u32[]{:S(2)}, u32[]{:S(2)}) async-start(bf16[128,8,128]{2,1,0:T(8,128)(2,1)} %bitcast.2), calls=%async_computation.1 | async-start | bytes 524288 | tf_op jit(solution)/shard_map/all_to_all | solution.py:475
  58.0 0.0 copy-done.3
  58.0 0.0 copy-done.2
  58.0 0.1 flip.1.refs_0_
  58.2 2.7 %collective-permute-start.4 = (bf16[1024,128]{1,0:T(8,128)(2,1)S(1)}, bf16[1024,128]{1,0:T(8,128)(2,1)S(1)}, u32[]{:S(2)}, u32[]{:S(2)}) collective-permute-start(bf16[1024,128]{1,0:T(8,128)(2,1)S(1)} %flip.1.refs_0_), channel_id=1, source_target_pairs={{0,24},{8,0},{16,8},{24,16},{1,25},{9,1},{17,9},{25,17},{2,26},{10... | collective-permute-start | bytes 786440 | tf_op jit(solution)/shard_map/ppermute | solution.py:474
  60.8 0.6 collective-permute-start.3
  61.4 0.6 collective-permute-start.2
  62.0 6.8 %all-to-all-done.1 = bf16[128,8,128]{2,1,0:T(8,128)(2,1)S(1)} async-done(((bf16[128,8,128]{2,1,0:T(8,128)(2,1)}), bf16[128,8,128]{2,1,0:T(8,128)(2,1)S(1)}, u32[]{:S(2)}, u32[]{:S(2)}) %all-to-all-start.1) | async-done | bytes 262176 | tf_op jit(solution)/shard_map/all_to_all | solution.py:475
  68.8 0.0 collective-permute-done.1.nxt
  68.8 0.7 copy-done.6
  69.5 0.2 copy-done.7
  69.6 4.3 %join.1 = (bf16[128,1024]{1,0:T(8,128)(2,1)}, bf16[8,128,384]{2,1,0:T(8,128)(2,1)}) custom-call(f32[128,1024]{1,0:T(8,128)} %get-tuple-element.26.near_out, f32[128,1024]{1,0:T(8,128)} %get-tuple-element.27.dq_in, f32[2,128,1024]{2,1,0:T(8,128)} %get-tuple-element.28.own, bf16[2,128,1024]{2,1,0:T(8,128)(2,1)} %copy-done.7, ...), custom_call_target="tpu_custom_call" | custom-call | flops 134217728 | bytes 3145728 | tf_op jit(solution)/shard_map/join/pallas_call | solution.py:320
  74.0 0.0 collective-permute-done.4.refs_3_
  74.0 0.0 collective-permute-done.3.refs_2_
  74.0 2.2 %collective-permute-done.2.refs_1_ = bf16[1024,128]{1,0:T(8,128)(2,1)S(1)} collective-permute-done((bf16[1024,128]{1,0:T(8,128)(2,1)S(1)}, bf16[1024,128]{1,0:T(8,128)(2,1)S(1)}, u32[]{:S(2)}, u32[]{:S(2)}) %collective-permute-start.2) | collective-permute-done | bytes 262176 | tf_op jit(solution)/shard_map/ppermute | solution.py:474
  76.2 0.1 stack.1.mine
  76.3 0.0 copy-start
  76.3 0.5 collective-permute-start.5
  76.8 3.5 %all-to-all-start.2 = ((bf16[8,128,384]{2,1,0:T(8,128)(2,1)}), bf16[8,128,384]{2,1,0:T(8,128)(2,1)S(1)}, u32[]{:S(2)}, u32[]{:S(2)}) async-start(bf16[8,128,384]{2,1,0:T(8,128)(2,1)} %get-tuple-element.32.delta.refs_4_), calls=%async_computation.2 | async-start | bytes 1572864 | tf_op jit(solution)/shard_map/all_to_all | solution.py:479
  80.4 5.5 %back.1.after = bf16[128,1024]{1,0:T(8,128)(2,1)} custom-call(bf16[8,128,384]{2,1,0:T(8,128)(2,1)} %get-tuple-element.32.delta.refs_4_, bf16[1024,1024]{1,0:T(8,128)(2,1)} %wq.3, bf16[1024,1024]{1,0:T(8,128)(2,1)} %wk.3, bf16[1024,1024]{1,0:T(8,128)(2,1)} %wv.3), custom_call_target="tpu_custom_call" | custom-call | flops 805306368 | bytes 7340032 | tf_op jit(solution)/shard_map/back/pallas_call | solution.py:373
  85.9 0.0 copy-done
  85.9 6.7 %all-to-all-done.2.delta = bf16[8,128,384]{2,1,0:T(8,128)(2,1)S(1)} async-done(((bf16[8,128,384]{2,1,0:T(8,128)(2,1)}), bf16[8,128,384]{2,1,0:T(8,128)(2,1)S(1)}, u32[]{:S(2)}, u32[]{:S(2)}) %all-to-all-start.2) | async-done | bytes 786464 | tf_op jit(solution)/shard_map/all_to_all | solution.py:479
  92.5 0.0 collective-permute-done.5.theirs
  92.5 0.9 copy-done.4
  93.4 0.3 copy-done.5
  93.8 4.6 %outer.1 = bf16[1024,384]{1,0:T(8,128)(2,1)} custom-call(s32[1]{0:T(128)} %bitcast.4.core.side, s32[1]{0:T(128)} %bitcast.5.at_x, bf16[4,1024,128]{2,1,0:T(8,128)(2,1)} %copy-done, bf16[4,1024,128]{2,1,0:T(8,128)(2,1)} %copy-done.5, bf16[8,128,384]{2,1,0:T(8,128)(2,1)} %copy-done.4, bf16[128,1024]{1,0:T(8,128)(2,1)} %back.1.after), custom_call_target="tpu_custom_call" | custom-call | flops 805306368 | bytes 2883584 | tf_op jit(solution)/shard_map/outer/pallas_call | solution.py:403
  98.4 20.2 %all_to_all.25 = bf16[16,64,384]{2,1,0:T(8,128)(2,1)S(1)} all-to-all(bf16[16,64,384]{2,1,0:T(8,128)(2,1)} %bitcast.11), channel_id=1, replica_groups=mesh['yl'=2,'c'=2,'x'=4,'z'=4,'yh'=2] {'yl','z','yh'}, dimensions={0} | all-to-all | bytes 1572864 | tf_op jit(solution)/shard_map/all_to_all | solution.py:484
  118.6 0.1 convert_reduce_fusion
  118.7 0.5 broadcast_in_dim.2
  119.2 43.0 %all_to_all.26 = bf16[64,64,384]{2,1,0:T(8,128)(2,1)S(1)} all-to-all(bf16[64,64,384]{2,1,0:T(8,128)(2,1)S(1)} %broadcast_in_dim.2), channel_id=1, replica_groups=mesh['yl'=2,'c'=2,'x'=4,'z'=4,'yh'=2] {'x','yl','z','yh'}, dimensions={0} | all-to-all | bytes 6291456 | tf_op jit(solution)/shard_map/all_to_all | solution.py:487
  162.2 3.6 %collective-permute-start.6 = (bf16[64,64,384]{2,1,0:T(8,128)(2,1)S(1)}, bf16[64,64,384]{2,1,0:T(8,128)(2,1)S(1)}, u32[]{:S(2)}, u32[]{:S(2)}) collective-permute-start(bf16[64,64,384]{2,1,0:T(8,128)(2,1)S(1)} %all_to_all.26), channel_id=1, source_target_pairs={{0,32},{32,0},{1,33},{33,1},{2,34},{34,2},{3,35},{35,3},{4,36},{36... | collective-permute-start | bytes 9437192 | tf_op jit(solution)/shard_map/ppermute | solution.py:488
  165.9 2.6 %place.2 = (bf16[1024,1024]{1,0:T(8,128)(2,1)}, bf16[1024,1024]{1,0:T(8,128)(2,1)}, bf16[1024,1024]{1,0:T(8,128)(2,1)}) custom-call(s32[1]{0:T(128)} %bitcast.4.core.side, bf16[4,16,64,384]{3,2,1,0:T(8,128)(2,1)S(1)} %bitcast.9), custom_call_target="tpu_custom_call" | custom-call | bytes 6291456 | tf_op jit(solution)/shard_map/place/pallas_call | solution.py:437
  168.4 2.7 %collective-permute-done.6 = bf16[64,64,384]{2,1,0:T(8,128)(2,1)S(1)} collective-permute-done((bf16[64,64,384]{2,1,0:T(8,128)(2,1)S(1)}, bf16[64,64,384]{2,1,0:T(8,128)(2,1)S(1)}, u32[]{:S(2)}, u32[]{:S(2)}) %collective-permute-start.6) | collective-permute-done | bytes 3145760 | tf_op jit(solution)/shard_map/ppermute | solution.py:488
  171.2 2.6 %place.3 = (bf16[1024,1024]{1,0:T(8,128)(2,1)}, bf16[1024,1024]{1,0:T(8,128)(2,1)}, bf16[1024,1024]{1,0:T(8,128)(2,1)}) custom-call(s32[1]{0:T(128)S(6)} %sub.3.side, bf16[4,16,64,384]{3,2,1,0:T(8,128)(2,1)S(1)} %bitcast.10, bf16[1024,1024]{1,0:T(8,128)(2,1)} %get-tuple-element.33.rest_0_, ...), custom_call_target="tpu_custom_call", output_to_operand_aliasing={{0}: (2, {}), {1}: (3, {}), {2}: (4, {})} | custom-call | bytes 6291456 | tf_op jit(solution)/shard_map/place/pallas_call | solution.py:437
  (5 shorter events, 0.0 us)
Async XLA Ops:
  6.5 24.6 %collective-permute-start = (bf16[2,128,1024]{2,1,0:T(8,128)(2,1)}, bf16[2,128,1024]{2,1,0:T(8,128)(2,1)S(1)}, u32[]{:S(2)}, u32[]{:S(2)}) collective-permute-start(bf16[2,128,1024]{2,1,0:T(8,128)(2,1)} %get-tuple-element.23.kv), channel_id=1, source_target_pairs={{0,1},{1,2},{2,3},{3,4},{4,5},{5,6},{6,7},{7,8},{8,9},{9,10},{10,1... | collective-permute-start | bytes 1572872 | tf_op jit(solution)/shard_map/ppermute | solution.py:466
  12.2 39.9 %all-to-all-start = ((bf16[128,16,128]{2,1,0:T(8,128)(2,1)}), bf16[128,16,128]{2,1,0:T(8,128)(2,1)S(1)}, u32[]{:S(2)}, u32[]{:S(2)}) async-start(bf16[128,16,128]{2,1,0:T(8,128)(2,1)} %bitcast.13), calls=%async_computation | async-start | bytes 1048576 | tf_op jit(solution)/shard_map/all_to_all | solution.py:467
  31.1 0.8 copy-start.8
  31.9 26.1 %copy-start.3 = (bf16[128,1024]{1,0:T(8,128)(2,1)S(1)}, bf16[128,1024]{1,0:T(8,128)(2,1)}, u32[]{:S(2)}) copy-start(bf16[128,1024]{1,0:T(8,128)(2,1)} %tok.3) | copy-start | bytes 786436
  42.6 26.2 %collective-permute-start.1 = (bf16[2,128,1024]{2,1,0:T(8,128)(2,1)}, bf16[2,128,1024]{2,1,0:T(8,128)(2,1)S(1)}, u32[]{:S(2)}, u32[]{:S(2)}) collective-permute-start(bf16[2,128,1024]{2,1,0:T(8,128)(2,1)} %get-tuple-element.29.after), channel_id=1, source_target_pairs={{1,0},{2,1},{3,2},{4,3},{5,4},{6,5},{7,6},{8,7},{9,8},{10,9},{11,1... | collective-permute-start | bytes 1572872 | tf_op jit(solution)/shard_map/ppermute | solution.py:471
  52.1 1.0 copy-start.1
  53.1 4.9 %copy-start.2 = (bf16[2,128,1024]{2,1,0:T(8,128)(2,1)S(1)}, bf16[2,128,1024]{2,1,0:T(8,128)(2,1)}, u32[]{:S(2)}) copy-start(bf16[2,128,1024]{2,1,0:T(8,128)(2,1)} %get-tuple-element.29.after) | copy-start | bytes 1572868
  54.3 14.4 %all-to-all-start.1 = ((bf16[128,8,128]{2,1,0:T(8,128)(2,1)}), bf16[128,8,128]{2,1,0:T(8,128)(2,1)S(1)}, u32[]{:S(2)}, u32[]{:S(2)}) async-start(bf16[128,8,128]{2,1,0:T(8,128)(2,1)} %bitcast.2), calls=%async_computation.1 | async-start | bytes 524288 | tf_op jit(solution)/shard_map/all_to_all | solution.py:475
  58.2 15.8 %collective-permute-start.4 = (bf16[1024,128]{1,0:T(8,128)(2,1)S(1)}, bf16[1024,128]{1,0:T(8,128)(2,1)S(1)}, u32[]{:S(2)}, u32[]{:S(2)}) collective-permute-start(bf16[1024,128]{1,0:T(8,128)(2,1)S(1)} %flip.1.refs_0_), channel_id=1, source_target_pairs={{0,24},{8,0},{16,8},{24,16},{1,25},{9,1},{17,9},{25,17},{2,26},{10... | collective-permute-start | bytes 786440 | tf_op jit(solution)/shard_map/ppermute | solution.py:474
  60.8 13.2 %collective-permute-start.3 = (bf16[1024,128]{1,0:T(8,128)(2,1)S(1)}, bf16[1024,128]{1,0:T(8,128)(2,1)S(1)}, u32[]{:S(2)}, u32[]{:S(2)}) collective-permute-start(bf16[1024,128]{1,0:T(8,128)(2,1)S(1)} %flip.1.refs_0_), channel_id=1, source_target_pairs={{0,16},{8,24},{16,0},{24,8},{1,17},{9,25},{17,1},{25,9},{2,18},{10... | collective-permute-start | bytes 786440 | tf_op jit(solution)/shard_map/ppermute | solution.py:474
  61.4 14.8 %collective-permute-start.2 = (bf16[1024,128]{1,0:T(8,128)(2,1)S(1)}, bf16[1024,128]{1,0:T(8,128)(2,1)S(1)}, u32[]{:S(2)}, u32[]{:S(2)}) collective-permute-start(bf16[1024,128]{1,0:T(8,128)(2,1)S(1)} %flip.1.refs_0_), channel_id=1, source_target_pairs={{0,8},{8,16},{16,24},{24,0},{1,9},{9,17},{17,25},{25,1},{2,10},{10... | collective-permute-start | bytes 786440 | tf_op jit(solution)/shard_map/ppermute | solution.py:474
  68.8 0.7 copy-start.6
  68.8 0.9 copy-start.7
  76.3 9.6 %copy-start = (bf16[4,1024,128]{2,1,0:T(8,128)(2,1)}, bf16[4,1024,128]{2,1,0:T(8,128)(2,1)S(1)}, u32[]{:S(2)}) copy-start(bf16[4,1024,128]{2,1,0:T(8,128)(2,1)S(1)} %stack.1.mine) | copy-start | bytes 3145732
  76.3 16.2 %collective-permute-start.5 = (bf16[4,1024,128]{2,1,0:T(8,128)(2,1)S(1)}, bf16[4,1024,128]{2,1,0:T(8,128)(2,1)S(1)}, u32[]{:S(2)}, u32[]{:S(2)}) collective-permute-start(bf16[4,1024,128]{2,1,0:T(8,128)(2,1)S(1)} %stack.1.mine), channel_id=1, source_target_pairs={{0,32},{32,0},{1,33},{33,1},{2,34},{34,2},{3,35},{35,3},{4,36},{36... | collective-permute-start | bytes 3145736 | tf_op jit(solution)/shard_map/ppermute | solution.py:481
  76.8 15.7 %all-to-all-start.2 = ((bf16[8,128,384]{2,1,0:T(8,128)(2,1)}), bf16[8,128,384]{2,1,0:T(8,128)(2,1)S(1)}, u32[]{:S(2)}, u32[]{:S(2)}) async-start(bf16[8,128,384]{2,1,0:T(8,128)(2,1)} %get-tuple-element.32.delta.refs_4_), calls=%async_computation.2 | async-start | bytes 1572864 | tf_op jit(solution)/shard_map/all_to_all | solution.py:479
  92.5 0.9 copy-start.4
  92.5 1.2 copy-start.5
  162.2 8.9 %collective-permute-start.6 = (bf16[64,64,384]{2,1,0:T(8,128)(2,1)S(1)}, bf16[64,64,384]{2,1,0:T(8,128)(2,1)S(1)}, u32[]{:S(2)}, u32[]{:S(2)}) collective-permute-start(bf16[64,64,384]{2,1,0:T(8,128)(2,1)S(1)} %all_to_all.26), channel_id=1, source_target_pairs={{0,32},{32,0},{1,33},{33,1},{2,34},{34,2},{3,35},{35,3},{4,36},{36... | collective-permute-start | bytes 9437192 | tf_op jit(solution)/shard_map/ppermute | solution.py:488

commit v5 on v4

--- a/solution.py
+++ b/solution.py
@@ -42,54 +42,65 @@
 
 
 CHUNK = 256
+WIDE = 512
+
+
+def pair_lanes(columns, pair):
+    shape = (columns.shape[0], PAIR)
+    return jnp.where(
+        iota(shape, 1) < DH,
+        columns[:, 2 * pair : 2 * pair + 1],
+        columns[:, 2 * pair + 1 : 2 * pair + 2],
+    )
 
 
 def project_kernel(lin_scale, tok, wq, wk, wv, decay, cot, q_out, kv_out, run_out, runt_out, msg, held, sems):
     width = tok.shape[1]
-    chunks = width // CHUNK
+    wide = held.shape[3]
     copies = []
-    for step in range(chunks):
+    for step in range(width // wide):
         for part, w in enumerate((wq, wk, wv)):
             copy = pltpu.make_async_copy(
-                w.at[:, pl.ds(step * CHUNK, CHUNK)], held.at[part, step], sems.at[part, step]
+                w.at[:, pl.ds(step * wide, wide)], held.at[part, step], sems.at[part, step]
             )
             copy.start()
             copies.append(copy)
     x = tok[...]
     ld = decay[...]
-    heads = ld.shape[0]
     lower = (iota((SEG, SEG), 0) >= iota((SEG, SEG), 1)).astype(F32)
     runt = dot(lower, ld, 1, 1, HIGH)
     run = dot(ld, lower, 1, 1, HIGH)
-    group = heads // chunks
-    for step in range(chunks):
+    group = ld.shape[0] // run_out.shape[0]
+    for step in range(run_out.shape[0]):
         runt_out[step] = runt[:, step * group : (step + 1) * group]
         run_out[step] = run[step * group : (step + 1) * group, :]
-    head_of = iota((SEG, PAIR), 1) // DH
     rows = iota((8, PAIR), 0)
-    lanes = iota((DH, PAIR), 1) < DH
-    for step in range(chunks):
+    first = iota((DH, PAIR), 1) < DH
+    for step in range(width // wide):
         for part in range(3):
             copies[step * 3 + part].wait()
-        at = slice(step * CHUNK, (step + 1) * CHUNK)
+        at = slice(step * wide, (step + 1) * wide)
         q = dot(x, held[0, step], 1, 0).astype(BF)
         k = dot(x, held[1, step], 1, 0).astype(BF)
         v = dot(x, held[2, step], 1, 0).astype(BF)
         q_out[:, at] = q
         kv_out[0, :, at] = k
         kv_out[1, :, at] = v
-        for half in range(CHUNK // PAIR):
-            cols = slice(half * PAIR, (half + 1) * PAIR)
-            pair = step * (CHUNK // PAIR) + half
-            run = jnp.where(
-                head_of == 0, runt[:, 2 * pair : 2 * pair + 1], runt[:, 2 * pair + 1 : 2 * pair + 2]
+        here = []
+        for part in range(wide // PAIR):
+            cols = slice(part * PAIR, (part + 1) * PAIR)
+            pair = step * (wide // PAIR) + part
+            lanes = pair_lanes(runt, pair)
+            total = lanes[SEG - 1 : SEG, :]
+            g = cot[:, pair * PAIR : (pair + 1) * PAIR].astype(F32)
+            weighted = (v[:, cols].astype(F32) * jnp.exp(total - lanes)).astype(BF)
+            scaled = (g * jnp.exp(lanes)).astype(BF)
+            states = (
+                dot(k[:, cols], weighted, 0, 0),
+                dot(q[:, cols], scaled, 0, 0) * lin_scale,
             )
-            total = run[SEG - 1 : SEG, :]
-            grads = cot[:, pair * PAIR : (pair + 1) * PAIR].astype(F32)
-            weighted = (v[:, cols].astype(F32) * jnp.exp(total - run)).astype(BF)
-            scaled = (grads * jnp.exp(run)).astype(BF)
-            full_s = dot(k[:, cols], weighted, 0, 0)
-            full_g = dot(q[:, cols], scaled, 0, 0) * lin_scale
+            here.append((pair, total, states))
+        for pair, total, states in here:
             high = total.astype(BF).astype(F32)
             mid = (total - high).astype(BF).astype(F32)
             low = total - high - mid
@@ -97,8 +108,8 @@
                 rows == 0, high, jnp.where(rows == 1, mid, jnp.where(rows == 2, low, 0.0))
             )
             tail = jnp.broadcast_to(tail[None], (8, 8, PAIR))
-            for part, full in ((0, full_s), (1, full_g)):
-                own = jnp.where(lanes, full[:DH], full[DH:]).reshape(8, 8, PAIR)
+            for part, full in enumerate(states):
+                own = jnp.where(first, full[:DH], full[DH:]).reshape(8, 8, PAIR)
                 sent = jnp.concatenate([own, tail], axis=1).reshape(PAIR, PAIR)
                 msg[part, pair * PAIR : (pair + 1) * PAIR, :] = sent.astype(BF)
 
@@ -106,6 +117,8 @@
 def project(tokens, wq, wk, wv, log_decay, cot, lin_scale):
     rows, width = tokens.shape
     heads = log_decay.shape[0]
+    chunks = width // CHUNK
+    wide = WIDE
     vmem = pl.BlockSpec(memory_space=VMEM)
     hbm = pl.BlockSpec(memory_space=pltpu.HBM)
     return pl.pallas_call(
@@ -115,18 +128,49 @@
         out_shape=[
             jax.ShapeDtypeStruct((rows, width), BF),
             jax.ShapeDtypeStruct((2, rows, width), BF),
-            jax.ShapeDtypeStruct((width // CHUNK, heads * CHUNK // width, rows), F32),
-            jax.ShapeDtypeStruct((width // CHUNK, rows, heads * CHUNK // width), F32),
+            jax.ShapeDtypeStruct((chunks, heads // chunks, rows), F32),
+            jax.ShapeDtypeStruct((chunks, rows, heads // chunks), F32),
             jax.ShapeDtypeStruct((2, width, PAIR), BF),
         ],
         scratch_shapes=[
-            VMEM((3, width // CHUNK, width, CHUNK), BF),
-            pltpu.SemaphoreType.DMA((3, width // CHUNK)),
+            VMEM((3, width // wide, width, wide), BF),
+            pltpu.SemaphoreType.DMA((3, width // wide)),
         ],
         compiler_params=params(58),
         cost_estimate=cost(6 * rows * width * width, 6 * width * width + 12 * rows * width),
         name="project",
     )(tokens, wq, wk, wv, log_decay, cot)
+
+
+def prior_kernel(tok, wk, wv, after, out, held, sems):
+    del after
+    copies = [
+        pltpu.make_async_copy(w, held.at[part], sems.at[part]) for part, w in enumerate((wk, wv))
+    ]
+    for copy in copies:
+        copy.start()
+    for part in range(2):
+        copies[part].wait()
+        out[part] = dot(tok[...], held[part], 1, 0).astype(BF)
+
+
+def prior(tokens, wk, wv, after):
+    rows, width = tokens.shape
+    vmem = pl.BlockSpec(memory_space=VMEM)
+    hbm = pl.BlockSpec(memory_space=pltpu.HBM)
+    return pl.pallas_call(
+        prior_kernel,
+        in_specs=[vmem, hbm, hbm, hbm],
+        out_specs=vmem,
+        out_shape=jax.ShapeDtypeStruct((2, rows, width), BF),
+        scratch_shapes=[
+            VMEM((2, width, width), BF),
+            pltpu.SemaphoreType.DMA((2,)),
+        ],
+        compiler_params=params(58),
+        cost_estimate=cost(4 * rows * width * width, 4 * width * width + 6 * rows * width),
+        name="prior",
+    )(tokens, wk, wv, after)
 
 
 def flip_kernel(tok, after, out):
@@ -202,7 +246,8 @@
     )(place, got, after)
 
 
-def near_kernel(lin_scale, place, blocks, q_ref, kv, pkv, cot, run, runt, out, dq_out, own, prev):
+def near_kernel(lin_scale, place, blocks, q_ref, kv, pkv, cot, run, runt, out, dq_out, own, prev, mark):
+    mark[...] = jnp.zeros_like(mark)
     soft_scale = 1.0 / math.sqrt(DH)
     n_own = jnp.int32(0)
     n_prev = jnp.int32(0)
@@ -217,38 +262,54 @@
     head_of2 = iota((2 * SEG, PAIR), 1) // DH
     lower = iota((SEG, SEG), 0) >= iota((SEG, SEG), 1)
     zero = jnp.zeros((), BF)
-    for pair in range(q_ref.shape[1] // PAIR):
+    pairs = q_ref.shape[1] // PAIR
+    work = []
+    for pair in range(pairs):
         at = slice(pair * PAIR, (pair + 1) * PAIR)
         q = q_ref[:, at]
         g = cot[:, at]
         kk = jnp.concatenate([kv[0, :, at], pkv[0, :, at]], axis=0)
         vv = jnp.concatenate([kv[1, :, at], pkv[1, :, at]], axis=0)
+        for i in range(2):
+            mine = head_of == i
+            work.append(
+                (
+                    dot(jnp.where(mine, q, zero), kk, 1, 1),
+                    dot(jnp.where(mine, g, zero), vv, 1, 1),
+                )
+            )
+    mats = []
+    for head in range(2 * pairs):
+        scores, pgrad = work[head]
+        col = runt[0, :, head : head + 1]
+        row = run[0, head : head + 1, :]
+        dec = jnp.where(lower, jnp.exp(jnp.minimum(col - row, 0.0)), 0.0) * lin_scale
+        logits = scores * soft_scale + bias
+        peak = jnp.max(logits, axis=1, keepdims=True)
+        terms = jnp.exp(logits - peak) * times
+        probs = terms * (1.0 / jnp.sum(terms, axis=1, keepdims=True))
+        inner = jnp.sum(probs * pgrad, axis=1, keepdims=True)
+        dlog = probs * (pgrad - inner) * soft_scale
+        a = jnp.concatenate([probs[:, :SEG] + scores[:, :SEG] * dec, probs[:, SEG:]], axis=1)
+        b = jnp.concatenate([dlog[:, :SEG] + pgrad[:, :SEG] * dec, dlog[:, SEG:]], axis=1)
+        mats.append((a.astype(BF), b.astype(BF)))
+    for pair in range(pairs):
+        at = slice(pair * PAIR, (pair + 1) * PAIR)
+        q = q_ref[:, at]
+        g = cot[:, at]
+        kk = jnp.concatenate([kv[0, :, at], pkv[0, :, at]], axis=0)
+        vv = jnp.concatenate([kv[1, :, at], pkv[1, :, at]], axis=0)
+        qt = q.T
+        gt = g.T
         res = []
         for i in range(2):
-            head = pair * 2 + i
-            mine = head_of == i
-            col = runt[0, :, head : head + 1]
-            row = run[0, head : head + 1, :]
-            dec = jnp.where(lower, jnp.exp(jnp.minimum(col - row, 0.0)), 0.0) * lin_scale
-            scores = dot(jnp.where(mine, q, zero), kk, 1, 1)
-            pgrad = dot(jnp.where(mine, g, zero), vv, 1, 1)
-            logits = scores * soft_scale + bias
-            peak = jnp.max(logits, axis=1, keepdims=True)
-            terms = jnp.exp(logits - peak) * times
-            probs = terms * (1.0 / jnp.sum(terms, axis=1, keepdims=True))
-            inner = jnp.sum(probs * pgrad, axis=1, keepdims=True)
-            dlog = probs * (pgrad - inner) * soft_scale
-            a = jnp.concatenate(
-                [probs[:, :SEG] + scores[:, :SEG] * dec, probs[:, SEG:]], axis=1
-            ).astype(BF)
-            b = jnp.concatenate(
-                [dlog[:, :SEG] + pgrad[:, :SEG] * dec, dlog[:, SEG:]], axis=1
-            ).astype(BF)
-            res.append((dot(a, vv, 1, 0), dot(b, kk, 1, 0), dot(b, q, 0, 0), dot(a, g, 0, 0)))
+            a, b = mats[2 * pair + i]
+            half = slice(i * DH, (i + 1) * DH)
+            res.append((dot(a, vv, 1, 0), dot(b, kk, 1, 0), dot(qt[half], b, 1, 0), dot(gt[half], a, 1, 0)))
         out[:, at] = jnp.where(head_of == 0, res[0][0], res[1][0])
         dq_out[:, at] = jnp.where(head_of == 0, res[0][1], res[1][1])
         for part in range(2):
-            sums = jnp.where(head_of2 == 0, res[0][2 + part], res[1][2 + part])
+            sums = jnp.concatenate([res[0][2 + part], res[1][2 + part]], axis=0).T
             own[part, :, at] = sums[:SEG]
             prev[part, :, at] = sums[SEG:].astype(BF)
 
@@ -272,12 +333,13 @@
             pl.BlockSpec((1, heads, rows), lambda i: (i, 0, 0)),
             pl.BlockSpec((1, rows, heads), lambda i: (i, 0, 0)),
         ],
-        out_specs=[col, col, two, two],
+        out_specs=[col, col, two, two, pl.BlockSpec((8, PAIR), lambda i: (0, 0))],
         out_shape=[
             jax.ShapeDtypeStruct((rows, width), F32),
             jax.ShapeDtypeStruct((rows, width), F32),
             jax.ShapeDtypeStruct((2, rows, width), F32),
             jax.ShapeDtypeStruct((2, rows, width), BF),
+            jax.ShapeDtypeStruct((8, PAIR), F32),
         ],
         compiler_params=params(58),
         cost_estimate=cost(4000 * 1000 * 1000, 16 * 1000 * 1000, 1000 * 1000),
@@ -290,23 +352,36 @@
     head_of = iota((SEG, PAIR), 1) // DH
     diag = iota((PAIR, PAIR), 0) // DH == iota((PAIR, PAIR), 1) // DH
     zero = jnp.zeros((), BF)
-    for pair in range(q.shape[1] // PAIR):
+    pairs = q.shape[1] // PAIR
+    work = []
+    for pair in range(pairs):
         at = slice(pair * PAIR, (pair + 1) * PAIR)
-        run = jnp.where(
-            head_of == 0,
-            runt[0, :, 2 * pair : 2 * pair + 1],
-            runt[0, :, 2 * pair + 1 : 2 * pair + 2],
-        )
-        growth = jnp.exp(run) * lin_scale
-        fading = jnp.exp(run[SEG - 1 : SEG, :] - run)
         before, after = (
             jnp.where(diag, jnp.concatenate([states[part, pair]] * 2, axis=0), zero)
             for part in range(2)
         )
-        layer[:, at] = (near_out[:, at] + growth * dot(q[:, at], before, 1, 0)).astype(BF)
-        dq = dq_in[:, at] + growth * dot(cot[:, at], before, 1, 1)
-        dk = own[0, :, at] + fading * dot(kv[1, :, at], after, 1, 1) + nxt[0, :, at].astype(F32)
-        dv = own[1, :, at] + fading * dot(kv[0, :, at], after, 1, 0) + nxt[1, :, at].astype(F32)
+        work.append(
+            (
+                dot(q[:, at], before, 1, 0),
+                dot(cot[:, at], before, 1, 1),
+                dot(kv[1, :, at], after, 1, 1),
+                dot(kv[0, :, at], after, 1, 0),
+            )
+        )
+    for pair in range(pairs):
+        at = slice(pair * PAIR, (pair + 1) * PAIR)
+        run = jnp.where(
+            head_of == 0,
+            runt[pair // 2, :, 2 * (pair % 2) : 2 * (pair % 2) + 1],
+            runt[pair // 2, :, 2 * (pair % 2) + 1 : 2 * (pair % 2) + 2],
+        )
+        growth = jnp.exp(run) * lin_scale
+        fading = jnp.exp(run[SEG - 1 : SEG, :] - run)
+        from_q, from_g, from_v, from_k = work[pair]
+        layer[:, at] = (near_out[:, at] + growth * from_q).astype(BF)
+        dq = dq_in[:, at] + growth * from_g
+        dk = own[0, :, at] + fading * from_v + nxt[0, :, at].astype(F32)
+        dv = own[1, :, at] + fading * from_k + nxt[1, :, at].astype(F32)
         delta[pair, :, :PAIR] = dq.astype(BF)
         delta[pair, :, PAIR : 2 * PAIR] = dk.astype(BF)
         delta[pair, :, 2 * PAIR :] = dv.astype(BF)
@@ -315,11 +390,12 @@
 def join(near_out, dq, own, nxt, q, kv, cot, runt, states, after, lin_scale):
     rows, width = q.shape
     pairs = width // PAIR
-    col = pl.BlockSpec((rows, CHUNK), lambda i: (0, i))
-    two = pl.BlockSpec((2, rows, CHUNK), lambda i: (0, 0, i))
+    wide = 2 * CHUNK
+    col = pl.BlockSpec((rows, wide), lambda i: (0, i))
+    two = pl.BlockSpec((2, rows, wide), lambda i: (0, 0, i))
     return pl.pallas_call(
         functools.partial(join_kernel, lin_scale),
-        grid=(width // CHUNK,),
+        grid=(width // wide,),
         in_specs=[
             col,
             col,
@@ -328,11 +404,11 @@
             col,
             two,
             col,
-            pl.BlockSpec((1, rows, runt.shape[2]), lambda i: (i, 0, 0)),
-            pl.BlockSpec((2, CHUNK // PAIR, DH, PAIR), lambda i: (0, i, 0, 0)),
+            pl.BlockSpec((2, rows, runt.shape[2]), lambda i: (i, 0, 0)),
+            pl.BlockSpec((2, wide // PAIR, DH, PAIR), lambda i: (0, i, 0, 0)),
         ]
         + [pl.BlockSpec(memory_space=pl.ANY)] * len(after),
-        out_specs=[col, pl.BlockSpec((CHUNK // PAIR, rows, 3 * PAIR), lambda i: (i, 0, 0))],
+        out_specs=[col, pl.BlockSpec((wide // PAIR, rows, 3 * PAIR), lambda i: (i, 0, 0))],
         out_shape=[
             jax.ShapeDtypeStruct((rows, width), BF),
             jax.ShapeDtypeStruct((pairs, rows, 3 * PAIR), BF),
@@ -399,10 +475,10 @@
     near_count, rows, cols = delta.shape
     width = mine.shape[1]
     smem = pl.BlockSpec(memory_space=pltpu.SMEM)
-    tok = pl.BlockSpec((near_count // 2, width // 4, rows), lambda i: (0, i, 0))
+    tok = pl.BlockSpec((near_count // 2, width // 2, rows), lambda i: (0, i, 0))
     return pl.pallas_call(
         outer_kernel,
-        grid=(4,),
+        grid=(2,),
         in_specs=[
             smem,
             smem,
@@ -411,7 +487,7 @@
             pl.BlockSpec((near_count, rows, cols), lambda i: (0, 0, 0)),
             pl.BlockSpec(memory_space=pl.ANY),
         ],
-        out_specs=pl.BlockSpec((width // 4, cols), lambda i: (i, 0)),
+        out_specs=pl.BlockSpec((width // 2, cols), lambda i: (i, 0)),
         out_shape=jax.ShapeDtypeStruct((width, cols), BF),
         compiler_params=params(58),
         cost_estimate=cost(
@@ -462,15 +538,16 @@
 
     at_x = lax.axis_index("x").astype(jnp.int32).reshape(1)
     swap = [(0, 1), (1, 0)]
+    prev_tokens = lax.ppermute(tokens, AX, [(i, i + 1) for i in range(DEVS - 1)])
     q, kv, run, runt, msg = project(tokens, wq, wk, wv, log_decay, cot, lin_scale)
-    pkv = lax.ppermute(kv, AX, [(i, i + 1) for i in range(DEVS - 1)])
     got = lax.all_to_all(msg.reshape(DEVS, 16, PAIR), AX, 0, 0)
-    near_out, dq, own, prev = near(
+    pkv = prior(prev_tokens, wk, wv, runt)
+    near_out, dq, own, prev, mark = near(
         place, neighbour_blocks, q, kv, pkv, cot, run, runt, lin_scale
     )
     nxt = lax.ppermute(prev, AX, [(i + 1, i) for i in range(DEVS - 1)])
-    states = scan(place, got, prev)
-    tokt = flip(tokens, prev)
+    states = scan(place, got, mark)
+    tokt = flip(tokens, mark)
     around = [lax.ppermute(tokt, "x", [(i, (i + d) % 4) for i in range(4)]) for d in (1, 2, 3)]
     states = lax.all_to_all(states.reshape(DEVS, 8, PAIR), AX, 0, 0)
     states = states.reshape(2, width // PAIR, DH, PAIR)

time: 174 us -> 166 us (0.954)
  waiting for transfers between devices: 27.6 us -> 19.4 us
  starting transfers between devices: 40 us -> 43.5 us
  Pallas kernels: 37.5 us -> 35.2 us
  blocking collectives: 63.3 us -> 61.3 us
    ppermute x1, waiting for transfers between devices: 9.18 us -> 0.01 us  [shards(): lax.ppermute(tokens, AX, [(i, i + 1) for i in range(DEVS - 1)])]
    pallas_call x1, Pallas kernels: 10.6 us -> 6.21 us  [near(): pl.pallas_call(functools.partial(near_kernel, lin_scale), grid=(width //...]
    all_to_all x1, starting transfers between devices: 3.53 us -> 7.66 us  [shards(): delta8 = lax.all_to_all(delta, NEAR8, 0, 0)]
    pallas_call x1 -> x2, Pallas kernels: 4.59 us -> 8.09 us  [the longest x1 4.45 us: prior(): pl.pallas_call(prior_kernel, in_specs=[vmem, hbm, hbm, hbm], out_specs=vm...]
    all_to_all x1, blocking collectives: 20.2 us -> 16.9 us  [shards(): lax.all_to_all(partial.reshape(16, width // 16, 3 * PAIR), FAR16, 0, 0)]
  transfers between devices with their start and end apart: 10 -> 10, of which waited for: 5 -> 5; matrix products, arithmetic and copies ran while one was open for 0% -> 0% of each run, Pallas kernels for 14% -> 18%
where the time goes in v5:
time: 166 us; the launch traced here: 165 us
  blocking collectives  61.3 us (37%)
  starting transfers between devices  43.5 us (26%)
  Pallas kernels  35.2 us (21%)
  waiting for transfers between devices  19.4 us (12%)
  local copies, waits for them, and re-layouts  4.67 us (3%)
    all_to_all x1, blocking collectives, shards(): lax.all_to_all(jnp.broadcast_to(piece[None], (DEVS // 2, *piece.shape)),...  44.4 us
    all_to_all x1, blocking collectives, shards(): lax.all_to_all(partial.reshape(16, width // 16, 3 * PAIR), FAR16, 0, 0)  16.9 us
    ppermute x1, starting transfers between devices, shards(): nxt = lax.ppermute(prev, AX, [(i + 1, i) for i in range(DEVS - 1)])  10.1 us
    all_to_all x1, starting transfers between devices, shards(): got = lax.all_to_all(msg.reshape(DEVS, 16, PAIR), AX, 0, 0)  9.71 us
    all_to_all x1, starting transfers between devices, shards(): delta8 = lax.all_to_all(delta, NEAR8, 0, 0)  7.66 us
    all_to_all x1, waiting for transfers between devices, shards(): delta8 = lax.all_to_all(delta, NEAR8, 0, 0)  6.67 us
    pallas_call x1, Pallas kernels, near(): pl.pallas_call(functools.partial(near_kernel, lin_scale), grid=(width //...  6.21 us
    all_to_all x1, waiting for transfers between devices, shards(): states = lax.all_to_all(states.reshape(DEVS, 8, PAIR), AX, 0, 0)  6.1 us
  transfers between devices with their start and end apart: 10, of which 5 were waited for; matrix products, arithmetic and copies ran while one was open for 0% of the time, Pallas kernels for 18%

profile of v5, /device:TPU:1, one launch (start us, length us, event | category | flops | bytes accessed | tf_op | source)
XLA Modules:
  0.0 164.9 jit_solution(15285450032083159623)
XLA Ops:
  0.6 5.7 %collective-permute-start = (bf16[128,1024]{1,0:T(8,128)(2,1)}, bf16[128,1024]{1,0:T(8,128)(2,1)S(1)}, u32[]{:S(2)}, u32[]{:S(2)}) collective-permute-start(bf16[128,1024]{1,0:T(8,128)(2,1)} %tok.3), channel_id=1, source_target_pairs={{0,1},{1,2},{2,3},{3,4},{4,5},{5,6},{6,7},{7,8},{8,9},{9,10},{10,1... | collective-permute-start | bytes 786440 | tf_op jit(solution)/shard_map/ppermute | solution.py:541
  6.3 5.6 %project.1 = (bf16[128,1024]{1,0:T(8,128)(2,1)}, bf16[2,128,1024]{2,1,0:T(8,128)(2,1)}, f32[4,4,128]{2,1,0:T(4,128)}, f32[4,128,4]{2,1,0:T(8,128)}, bf16[2,1024,128]{2,1,0:T(8,128)(2,1)}) custom-call(bf16[128,1024]{1,0:T(8,128)(2,1)} %tok.3, bf16[1024,1024]{1,0:T(8,128)(2,1)} %wq.3, bf16[1024,1024]{1,0:T(8,128)(2,1)} %wk.5, bf16[1024,1024]{1,0:T(8,128)(2,1)} %wv.5, ...), custom_call_target="tpu_custom_call" | custom-call | flops 805306368 | bytes 7864320 | tf_op jit(solution)/shard_map/project/pallas_call | solution.py:124
  11.9 9.7 %all-to-all-start = ((bf16[128,16,128]{2,1,0:T(8,128)(2,1)}), bf16[128,16,128]{2,1,0:T(8,128)(2,1)S(1)}, u32[]{:S(2)}, u32[]{:S(2)}) async-start(bf16[128,16,128]{2,1,0:T(8,128)(2,1)} %bitcast.13), calls=%async_computation | async-start | bytes 1048576 | tf_op jit(solution)/shard_map/all_to_all | solution.py:543
  21.6 0.0 collective-permute-done.tok
  21.6 0.0 copy-start.8
  21.6 0.7 copy-done.8
  22.3 4.4 %prior.1.pkv = bf16[2,128,1024]{2,1,0:T(8,128)(2,1)} custom-call(bf16[128,1024]{1,0:T(8,128)(2,1)} %copy-done.8, bf16[1024,1024]{1,0:T(8,128)(2,1)} %wk.5, bf16[1024,1024]{1,0:T(8,128)(2,1)} %wv.5, f32[4,128,4]{2,1,0:T(8,128)} %get-tuple-element.25.after.runt), custom_call_target="tpu_custom_call" | custom-call | flops 536870912 | bytes 4980736 | tf_op jit(solution)/shard_map/prior/pallas_call | solution.py:161
  26.8 0.0 copy-start.1
  26.8 6.2 %near.1 = (f32[128,1024]{1,0:T(8,128)}, f32[128,1024]{1,0:T(8,128)}, f32[2,128,1024]{2,1,0:T(8,128)}, bf16[2,128,1024]{2,1,0:T(8,128)(2,1)}, f32[8,128]{1,0:T(8,128)}) custom-call(s32[1]{0:T(128)} %bitcast.place, s32[1,4]{1,0:T(1,128)} %blocks.1, bf16[128,1024]{1,0:T(8,128)(2,1)} %get-tuple-element.23.q_ref.q, bf16[2,128,1024]{2,1,0:T(8,128)(2,1)} %get-tuple-element.24.kv, ...), custom_call_target="tpu_custom_call" | custom-call | flops 4000000000 | bytes 16000000 | tf_op jit(solution)/shard_map/near/pallas_call | solution.py:323
  33.0 10.1 %collective-permute-start.1 = (bf16[2,128,1024]{2,1,0:T(8,128)(2,1)}, bf16[2,128,1024]{2,1,0:T(8,128)(2,1)S(1)}, u32[]{:S(2)}, u32[]{:S(2)}) collective-permute-start(bf16[2,128,1024]{2,1,0:T(8,128)(2,1)} %get-tuple-element.30), channel_id=1, source_target_pairs={{1,0},{2,1},{3,2},{4,3},{5,4},{6,5},{7,6},{8,7},{9,8},{10,9},{11,1... | collective-permute-start | bytes 1572872 | tf_op jit(solution)/shard_map/ppermute | solution.py:548
  43.1 0.0 all-to-all-done.got
  43.1 0.0 copy-start.2
  43.1 0.7 copy-done.2
  43.8 1.2 scan.1
  45.0 3.5 %all-to-all-start.1 = ((bf16[128,8,128]{2,1,0:T(8,128)(2,1)}), bf16[128,8,128]{2,1,0:T(8,128)(2,1)S(1)}, u32[]{:S(2)}, u32[]{:S(2)}) async-start(bf16[128,8,128]{2,1,0:T(8,128)(2,1)} %bitcast.2), calls=%async_computation.1 | async-start | bytes 524288 | tf_op jit(solution)/shard_map/all_to_all | solution.py:552
  48.6 0.0 copy-done.1
  48.6 0.0 copy-start.3
  48.6 0.7 copy-done.3
  49.3 0.1 flip.1.refs_0_
  49.4 1.8 %collective-permute-start.4 = (bf16[1024,128]{1,0:T(8,128)(2,1)S(1)}, bf16[1024,128]{1,0:T(8,128)(2,1)S(1)}, u32[]{:S(2)}, u32[]{:S(2)}) collective-permute-start(bf16[1024,128]{1,0:T(8,128)(2,1)S(1)} %flip.1.refs_0_), channel_id=1, source_target_pairs={{0,24},{8,0},{16,8},{24,16},{1,25},{9,1},{17,9},{25,17},{2,26},{10... | collective-permute-start | bytes 786440 | tf_op jit(solution)/shard_map/ppermute | solution.py:551
  51.2 0.6 collective-permute-start.3
  51.8 0.6 collective-permute-start.2
  52.4 6.1 %all-to-all-done.1 = bf16[128,8,128]{2,1,0:T(8,128)(2,1)S(1)} async-done(((bf16[128,8,128]{2,1,0:T(8,128)(2,1)}), bf16[128,8,128]{2,1,0:T(8,128)(2,1)S(1)}, u32[]{:S(2)}, u32[]{:S(2)}) %all-to-all-start.1) | async-done | bytes 262176 | tf_op jit(solution)/shard_map/all_to_all | solution.py:552
  58.5 0.0 collective-permute-done.1.nxt
  58.5 0.7 copy-done.6
  59.2 0.2 copy-done.7
  59.4 3.3 %join.1 = (bf16[128,1024]{1,0:T(8,128)(2,1)}, bf16[8,128,384]{2,1,0:T(8,128)(2,1)}) custom-call(f32[128,1024]{1,0:T(8,128)} %get-tuple-element.27.near_out, f32[128,1024]{1,0:T(8,128)} %get-tuple-element.28.dq_in, f32[2,128,1024]{2,1,0:T(8,128)} %get-tuple-element.29.own, bf16[2,128,1024]{2,1,0:T(8,128)(2,1)} %copy-done.7, ...), custom_call_target="tpu_custom_call" | custom-call | flops 134217728 | bytes 3145728 | tf_op jit(solution)/shard_map/join/pallas_call | solution.py:396
  62.6 0.9 collective-permute-done.4.refs_3_
  63.5 0.0 collective-permute-done.3.refs_2_
  63.5 3.1 %collective-permute-done.2.refs_1_ = bf16[1024,128]{1,0:T(8,128)(2,1)S(1)} collective-permute-done((bf16[1024,128]{1,0:T(8,128)(2,1)S(1)}, bf16[1024,128]{1,0:T(8,128)(2,1)S(1)}, u32[]{:S(2)}, u32[]{:S(2)}) %collective-permute-start.2) | collective-permute-done | bytes 262176 | tf_op jit(solution)/shard_map/ppermute | solution.py:551
  66.6 0.1 stack.1.mine
  66.6 0.0 copy-start
  66.6 0.6 collective-permute-start.5
  67.2 7.7 %all-to-all-start.2 = ((bf16[8,128,384]{2,1,0:T(8,128)(2,1)}), bf16[8,128,384]{2,1,0:T(8,128)(2,1)S(1)}, u32[]{:S(2)}, u32[]{:S(2)}) async-start(bf16[8,128,384]{2,1,0:T(8,128)(2,1)} %get-tuple-element.34.delta.refs_4_), calls=%async_computation.2 | async-start | bytes 1572864 | tf_op jit(solution)/shard_map/all_to_all | solution.py:556
  74.9 5.5 %back.1.after = bf16[128,1024]{1,0:T(8,128)(2,1)} custom-call(bf16[8,128,384]{2,1,0:T(8,128)(2,1)} %get-tuple-element.34.delta.refs_4_, bf16[1024,1024]{1,0:T(8,128)(2,1)} %wq.3, bf16[1024,1024]{1,0:T(8,128)(2,1)} %wk.5, bf16[1024,1024]{1,0:T(8,128)(2,1)} %wv.5), custom_call_target="tpu_custom_call" | custom-call | flops 805306368 | bytes 7340032 | tf_op jit(solution)/shard_map/back/pallas_call | solution.py:449
  80.4 6.7 %all-to-all-done.2.delta = bf16[8,128,384]{2,1,0:T(8,128)(2,1)S(1)} async-done(((bf16[8,128,384]{2,1,0:T(8,128)(2,1)}), bf16[8,128,384]{2,1,0:T(8,128)(2,1)S(1)}, u32[]{:S(2)}, u32[]{:S(2)}) %all-to-all-start.2) | async-done | bytes 786464 | tf_op jit(solution)/shard_map/all_to_all | solution.py:556
  87.0 0.0 collective-permute-done.5.theirs
  87.1 0.9 copy-done.4
  87.9 0.3 copy-done.5
  88.3 3.6 %outer.1 = bf16[1024,384]{1,0:T(8,128)(2,1)} custom-call(s32[1]{0:T(128)} %bitcast.4.core.side, s32[1]{0:T(128)} %bitcast.5.at_x, bf16[4,1024,128]{2,1,0:T(8,128)(2,1)} %copy-done, bf16[4,1024,128]{2,1,0:T(8,128)(2,1)} %copy-done.5, bf16[8,128,384]{2,1,0:T(8,128)(2,1)} %copy-done.4, bf16[128,1024]{1,0:T(8,128)(2,1)} %back.1.after), custom_call_target="tpu_custom_call" | custom-call | flops 805306368 | bytes 2883584 | tf_op jit(solution)/shard_map/outer/pallas_call | solution.py:479
  91.9 16.9 %all_to_all.25 = bf16[16,64,384]{2,1,0:T(8,128)(2,1)S(1)} all-to-all(bf16[16,64,384]{2,1,0:T(8,128)(2,1)} %bitcast.11), channel_id=1, replica_groups=mesh['yl'=2,'c'=2,'x'=4,'z'=4,'yh'=2] {'yl','z','yh'}, dimensions={0} | all-to-all | bytes 1572864 | tf_op jit(solution)/shard_map/all_to_all | solution.py:561
  108.8 0.1 convert_reduce_fusion
  109.0 0.5 broadcast_in_dim.2
  109.5 44.4 %all_to_all.26 = bf16[64,64,384]{2,1,0:T(8,128)(2,1)S(1)} all-to-all(bf16[64,64,384]{2,1,0:T(8,128)(2,1)S(1)} %broadcast_in_dim.2), channel_id=1, replica_groups=mesh['yl'=2,'c'=2,'x'=4,'z'=4,'yh'=2] {'x','yl','z','yh'}, dimensions={0} | all-to-all | bytes 6291456 | tf_op jit(solution)/shard_map/all_to_all | solution.py:564
  153.8 3.3 %collective-permute-start.6 = (bf16[64,64,384]{2,1,0:T(8,128)(2,1)S(1)}, bf16[64,64,384]{2,1,0:T(8,128)(2,1)S(1)}, u32[]{:S(2)}, u32[]{:S(2)}) collective-permute-start(bf16[64,64,384]{2,1,0:T(8,128)(2,1)S(1)} %all_to_all.26), channel_id=1, source_target_pairs={{0,32},{32,0},{1,33},{33,1},{2,34},{34,2},{3,35},{35,3},{4,36},{36... | collective-permute-start | bytes 9437192 | tf_op jit(solution)/shard_map/ppermute | solution.py:565
  157.1 2.6 %place.2 = (bf16[1024,1024]{1,0:T(8,128)(2,1)}, bf16[1024,1024]{1,0:T(8,128)(2,1)}, bf16[1024,1024]{1,0:T(8,128)(2,1)}) custom-call(s32[1]{0:T(128)} %bitcast.4.core.side, bf16[4,16,64,384]{3,2,1,0:T(8,128)(2,1)S(1)} %bitcast.9), custom_call_target="tpu_custom_call" | custom-call | bytes 6291456 | tf_op jit(solution)/shard_map/place/pallas_call | solution.py:513
  159.6 2.7 %collective-permute-done.6 = bf16[64,64,384]{2,1,0:T(8,128)(2,1)S(1)} collective-permute-done((bf16[64,64,384]{2,1,0:T(8,128)(2,1)S(1)}, bf16[64,64,384]{2,1,0:T(8,128)(2,1)S(1)}, u32[]{:S(2)}, u32[]{:S(2)}) %collective-permute-start.6) | collective-permute-done | bytes 3145760 | tf_op jit(solution)/shard_map/ppermute | solution.py:565
  162.4 2.6 %place.3 = (bf16[1024,1024]{1,0:T(8,128)(2,1)}, bf16[1024,1024]{1,0:T(8,128)(2,1)}, bf16[1024,1024]{1,0:T(8,128)(2,1)}) custom-call(s32[1]{0:T(128)S(6)} %sub.3.side, bf16[4,16,64,384]{3,2,1,0:T(8,128)(2,1)S(1)} %bitcast.10, bf16[1024,1024]{1,0:T(8,128)(2,1)} %get-tuple-element.35.rest_0_, ...), custom_call_target="tpu_custom_call", output_to_operand_aliasing={{0}: (2, {}), {1}: (3, {}), {2}: (4, {})} | custom-call | bytes 6291456 | tf_op jit(solution)/shard_map/place/pallas_call | solution.py:513
  (6 shorter events, 0.0 us)
Async XLA Ops:
  0.6 21.0 %collective-permute-start = (bf16[128,1024]{1,0:T(8,128)(2,1)}, bf16[128,1024]{1,0:T(8,128)(2,1)S(1)}, u32[]{:S(2)}, u32[]{:S(2)}) collective-permute-start(bf16[128,1024]{1,0:T(8,128)(2,1)} %tok.3), channel_id=1, source_target_pairs={{0,1},{1,2},{2,3},{3,4},{4,5},{5,6},{6,7},{7,8},{8,9},{9,10},{10,1... | collective-permute-start | bytes 786440 | tf_op jit(solution)/shard_map/ppermute | solution.py:541
  11.9 31.2 %all-to-all-start = ((bf16[128,16,128]{2,1,0:T(8,128)(2,1)}), bf16[128,16,128]{2,1,0:T(8,128)(2,1)S(1)}, u32[]{:S(2)}, u32[]{:S(2)}) async-start(bf16[128,16,128]{2,1,0:T(8,128)(2,1)} %bitcast.13), calls=%async_computation | async-start | bytes 1048576 | tf_op jit(solution)/shard_map/all_to_all | solution.py:543
  21.6 0.7 copy-start.8
  26.8 21.8 %copy-start.1 = (bf16[128,1024]{1,0:T(8,128)(2,1)S(1)}, bf16[128,1024]{1,0:T(8,128)(2,1)}, u32[]{:S(2)}) copy-start(bf16[128,1024]{1,0:T(8,128)(2,1)} %tok.3) | copy-start | bytes 786436
  33.0 25.5 %collective-permute-start.1 = (bf16[2,128,1024]{2,1,0:T(8,128)(2,1)}, bf16[2,128,1024]{2,1,0:T(8,128)(2,1)S(1)}, u32[]{:S(2)}, u32[]{:S(2)}) collective-permute-start(bf16[2,128,1024]{2,1,0:T(8,128)(2,1)} %get-tuple-element.30), channel_id=1, source_target_pairs={{1,0},{2,1},{3,2},{4,3},{5,4},{6,5},{7,6},{8,7},{9,8},{10,9},{11,1... | collective-permute-start | bytes 1572872 | tf_op jit(solution)/shard_map/ppermute | solution.py:548
  43.1 0.7 copy-start.2
  45.0 13.4 %all-to-all-start.1 = ((bf16[128,8,128]{2,1,0:T(8,128)(2,1)}), bf16[128,8,128]{2,1,0:T(8,128)(2,1)S(1)}, u32[]{:S(2)}, u32[]{:S(2)}) async-start(bf16[128,8,128]{2,1,0:T(8,128)(2,1)} %bitcast.2), calls=%async_computation.1 | async-start | bytes 524288 | tf_op jit(solution)/shard_map/all_to_all | solution.py:552
  48.6 0.7 copy-start.3
  49.4 14.1 %collective-permute-start.4 = (bf16[1024,128]{1,0:T(8,128)(2,1)S(1)}, bf16[1024,128]{1,0:T(8,128)(2,1)S(1)}, u32[]{:S(2)}, u32[]{:S(2)}) collective-permute-start(bf16[1024,128]{1,0:T(8,128)(2,1)S(1)} %flip.1.refs_0_), channel_id=1, source_target_pairs={{0,24},{8,0},{16,8},{24,16},{1,25},{9,1},{17,9},{25,17},{2,26},{10... | collective-permute-start | bytes 786440 | tf_op jit(solution)/shard_map/ppermute | solution.py:551
  51.2 12.3 %collective-permute-start.3 = (bf16[1024,128]{1,0:T(8,128)(2,1)S(1)}, bf16[1024,128]{1,0:T(8,128)(2,1)S(1)}, u32[]{:S(2)}, u32[]{:S(2)}) collective-permute-start(bf16[1024,128]{1,0:T(8,128)(2,1)S(1)} %flip.1.refs_0_), channel_id=1, source_target_pairs={{0,16},{8,24},{16,0},{24,8},{1,17},{9,25},{17,1},{25,9},{2,18},{10... | collective-permute-start | bytes 786440 | tf_op jit(solution)/shard_map/ppermute | solution.py:551
  51.8 14.8 %collective-permute-start.2 = (bf16[1024,128]{1,0:T(8,128)(2,1)S(1)}, bf16[1024,128]{1,0:T(8,128)(2,1)S(1)}, u32[]{:S(2)}, u32[]{:S(2)}) collective-permute-start(bf16[1024,128]{1,0:T(8,128)(2,1)S(1)} %flip.1.refs_0_), channel_id=1, source_target_pairs={{0,8},{8,16},{16,24},{24,0},{1,9},{9,17},{17,25},{25,1},{2,10},{10... | collective-permute-start | bytes 786440 | tf_op jit(solution)/shard_map/ppermute | solution.py:551
  58.5 0.7 copy-start.6
  58.5 0.9 copy-start.7
  66.6 13.8 %copy-start = (bf16[4,1024,128]{2,1,0:T(8,128)(2,1)}, bf16[4,1024,128]{2,1,0:T(8,128)(2,1)S(1)}, u32[]{:S(2)}) copy-start(bf16[4,1024,128]{2,1,0:T(8,128)(2,1)S(1)} %stack.1.mine) | copy-start | bytes 3145732
  66.6 20.4 %collective-permute-start.5 = (bf16[4,1024,128]{2,1,0:T(8,128)(2,1)S(1)}, bf16[4,1024,128]{2,1,0:T(8,128)(2,1)S(1)}, u32[]{:S(2)}, u32[]{:S(2)}) collective-permute-start(bf16[4,1024,128]{2,1,0:T(8,128)(2,1)S(1)} %stack.1.mine), channel_id=1, source_target_pairs={{0,32},{32,0},{1,33},{33,1},{2,34},{34,2},{3,35},{35,3},{4,36},{36... | collective-permute-start | bytes 3145736 | tf_op jit(solution)/shard_map/ppermute | solution.py:558
  67.2 19.8 %all-to-all-start.2 = ((bf16[8,128,384]{2,1,0:T(8,128)(2,1)}), bf16[8,128,384]{2,1,0:T(8,128)(2,1)S(1)}, u32[]{:S(2)}, u32[]{:S(2)}) async-start(bf16[8,128,384]{2,1,0:T(8,128)(2,1)} %get-tuple-element.34.delta.refs_4_), calls=%async_computation.2 | async-start | bytes 1572864 | tf_op jit(solution)/shard_map/all_to_all | solution.py:556
  87.0 0.9 copy-start.4
  87.1 1.2 copy-start.5
  153.8 8.5 %collective-permute-start.6 = (bf16[64,64,384]{2,1,0:T(8,128)(2,1)S(1)}, bf16[64,64,384]{2,1,0:T(8,128)(2,1)S(1)}, u32[]{:S(2)}, u32[]{:S(2)}) collective-permute-start(bf16[64,64,384]{2,1,0:T(8,128)(2,1)S(1)} %all_to_all.26), channel_id=1, source_target_pairs={{0,32},{32,0},{1,33},{33,1},{2,34},{34,2},{3,35},{35,3},{4,36},{36... | collective-permute-start | bytes 9437192 | tf_op jit(solution)/shard_map/ppermute | solution.py:565

commit v6 on v5

--- a/solution.py
+++ b/solution.py
@@ -206,7 +206,7 @@
         out_specs=whole,
         out_shape=jax.ShapeDtypeStruct((len(parts), *shape), BF),
         compiler_params=params(16),
-        cost_estimate=cost(0, 4 * len(parts) * shape[0] * shape[1]),
+        cost_estimate=cost(0, 4 * len(parts) * math.prod(shape)),
         name="stack",
     )(*parts, after)
 
@@ -497,37 +497,133 @@
     )(core, at_x, mine, theirs, delta, after)
 
 
-def place_kernel(side, pieces, *rest):
-    del side
-    for x in range(pieces.shape[0]):
-        for r in range(pieces.shape[1]):
-            rows = slice(r * pieces.shape[2], (r + 1) * pieces.shape[2])
-            for part, o in enumerate(rest[-3:]):
-                o[rows, x * PAIR : (x + 1) * PAIR] = pieces[x, r, :, part * PAIR : (part + 1) * PAIR]
-
-
-def place_half(side, pieces, grads=()):
-    near_count, blocks, rows, cols = pieces.shape
-    width = blocks * rows
-    out = jax.ShapeDtypeStruct((width, width), BF)
-    return pl.pallas_call(
-        place_kernel,
-        grid_spec=pltpu.PrefetchScalarGridSpec(
-            num_scalar_prefetch=1,
-            grid=(blocks // 4,),
-            in_specs=[pl.BlockSpec((near_count, 4, rows, cols), lambda i, side: (0, i, 0, 0))]
-            + [pl.BlockSpec(memory_space=pl.ANY)] * len(grads),
-            out_specs=[
-                pl.BlockSpec((4 * rows, near_count * PAIR), lambda i, side: (i, side[0]))
-            ]
-            * 3,
-        ),
-        out_shape=[out] * 3,
-        input_output_aliases={2 + i: i for i in range(len(grads))},
-        compiler_params=params(24),
-        cost_estimate=cost(0, 6 * width * width),
+def device(yl, c, x, z, yh):
+    return (((yl * 2 + c) * 4 + x) * 4 + z) * 2 + yh
+
+
+def gather_groups():
+    zero = [
+        [device(yl, 0, x, z, yh) for yl in range(2) for z in range(4) for yh in range(2)]
+        for x in range(4)
+    ]
+    one = [
+        [device(yl, 1, x, z, yh) for x in range(4) for yl in range(2) for yh in range(2)]
+        for z in range(4)
+    ]
+    return zero + one
+
+
+def ring(array, by):
+    route = []
+    for yl in range(2):
+        for x in range(4):
+            for z in range(4):
+                for yh in range(2):
+                    route.append((device(yl, 0, x, z, yh), device(yl, 0, (x + by) % 4, z, yh)))
+                    route.append((device(yl, 1, x, z, yh), device(yl, 1, x, (z + by) % 4, yh)))
+    return lax.ppermute(array, AX, route)
+
+
+def place_kernel(pieces, side, at_x, at_z, own, other, *refs):
+    grads, mark, sems = refs[-5:-2], refs[-2], refs[-1]
+    mark[...] = jnp.zeros_like(mark)
+
+    def put(zero, one):
+        copies = []
+
+        def start(src, dst):
+            copy = pltpu.make_async_copy(src, dst, sems.at[len(copies)])
+            copy.start()
+            copies.append(copy)
+
+        rows = zero.shape[1]
+        for place, by in enumerate(pieces):
+            x = lax.rem(at_x[0] + by + 4, 4)
+            z = lax.rem(at_z[0] + by + 4, 4)
+            for part, grad in enumerate(grads):
+                lanes = pl.ds(part * PAIR, PAIR)
+                for i in range(8):
+                    start(
+                        zero.at[place * 8 + i, :, lanes],
+                        grad.at[pl.ds(i * rows, rows), pl.ds(pl.multiple_of(x * PAIR, PAIR), PAIR)],
+                    )
+                    to = pl.multiple_of(((i % 2) * 4 + z) * rows, rows)
+                    start(
+                        one.at[place * 8 + i, :, lanes],
+                        grad.at[pl.ds(to, rows), pl.ds((4 + i // 2) * PAIR, PAIR)],
+                    )
+        for copy in copies:
+            copy.wait()
+
+    @pl.when(side[0] == 0)
+    def _():
+        put(own, other)
+
+    @pl.when(side[0] == 1)
+    def _():
+        put(other, own)
+
+
+def place_tiles(where, pieces, own, other, grads, width):
+    hbm = pl.BlockSpec(memory_space=pl.ANY)
+    smem = pl.BlockSpec(memory_space=pltpu.SMEM)
+    return pl.pallas_call(
+        functools.partial(place_kernel, pieces),
+        in_specs=[smem] * 3 + [hbm] * (2 + len(grads)),
+        out_specs=[hbm] * 3 + [pl.BlockSpec(memory_space=VMEM)],
+        out_shape=[jax.ShapeDtypeStruct((width, width), BF)] * 3
+        + [jax.ShapeDtypeStruct((8, PAIR), F32)],
+        scratch_shapes=[pltpu.SemaphoreType.DMA((6 * own.shape[0],))],
+        input_output_aliases={5 + i: i for i in range(len(grads))},
+        compiler_params=params(16),
+        cost_estimate=cost(0, 8 * own.size),
         name="place",
-    )(side, pieces, *grads)
+    )(*where, own, other, *grads)
+
+
+def halves_kernel(behind, ahead, after, first, second, both):
+    del after
+    half = first.shape[0]
+    first[...] = behind[:half]
+    second[...] = ahead[half:]
+    both[: 2 * half] = behind[...]
+    both[2 * half :] = ahead[...]
+
+
+def halves(behind, ahead, after):
+    pairs, *rest = behind.shape
+    whole = pl.BlockSpec(memory_space=VMEM)
+    return pl.pallas_call(
+        halves_kernel,
+        in_specs=[whole, whole, pl.BlockSpec(memory_space=pl.ANY)],
+        out_specs=[whole] * 3,
+        out_shape=[jax.ShapeDtypeStruct((n, *rest), BF) for n in (pairs // 2, pairs // 2, 2 * pairs)],
+        compiler_params=params(16),
+        cost_estimate=cost(0, 12 * behind.size),
+        name="halves",
+    )(behind, ahead, after)
+
+
+def gather_tiles(piece, where, width):
+    swap = [(0, 1), (1, 0)]
+
+    def swapped(array):
+        return lax.ppermute(array, "c", swap)
+
+    rows, cols = piece.shape
+    here = lax.all_to_all(
+        jnp.broadcast_to(piece[None], (16, rows, cols)), AX, 0, 0, axis_index_groups=gather_groups()
+    ).reshape(8, 2 * rows, cols)
+    behind = ring(here, 1)
+    ahead = ring(here, -1)
+    *grads, mark = place_tiles(where, (0,), here, swapped(here), (), width)
+    half_a, half_b, both = halves(behind, ahead, mark)
+    far_a = ring(half_a, 1)
+    far_b = ring(half_b, -1)
+    *grads, mark = place_tiles(where, (-1, 1), both, swapped(both), grads, width)
+    far = stack([far_a, far_b], mark).reshape(here.shape)
+    *grads, _ = place_tiles(where, (2,), far, swapped(far), grads, width)
+    return grads
 
 
 def shards(tokens, wq, wk, wv, log_decay, neighbour_blocks, cot):
@@ -561,11 +657,8 @@
     parts = lax.all_to_all(partial.reshape(16, width // 16, 3 * PAIR), FAR16, 0, 0)
     grad_norm = 1.0 / math.sqrt(rows * DEVS)
     piece = (jnp.sum(parts.astype(F32), axis=0) * grad_norm).astype(BF)
-    plane = lax.all_to_all(jnp.broadcast_to(piece[None], (DEVS // 2, *piece.shape)), PLANE, 0, 0)
-    other = lax.ppermute(plane, "c", swap)
-    shape = (4, 16, *piece.shape)
-    grads = place_half(core, plane.reshape(shape))
-    gq, gk, gv = place_half(1 - core, other.reshape(shape), grads)
+    at_z = lax.axis_index("z").astype(jnp.int32).reshape(1)
+    gq, gk, gv = gather_tiles(piece, (core, at_x, at_z), width)
     return layer, tokens_grad, gq, gk, gv
 
 

time: 166 us -> 156 us (0.940)
  blocking collectives: 61.3 us -> 31.4 us
  waiting for transfers between devices: 19.4 us -> 32.4 us
  starting transfers between devices: 43.5 us -> 50.2 us
    all_to_all x1, blocking collectives: 44.4 us -> 14.5 us  [gather_tiles(): lax.all_to_all(jnp.broadcast_to(piece[None], (16, rows, cols)), AX, 0, 0,...]
    ppermute x1 -> x7, waiting for transfers between devices: 2.73 us -> 15.7 us  [the longest x4 13.4 us: ring(): return lax.ppermute(array, AX, route)]
    ppermute x1 -> x7, starting transfers between devices: 3.25 us -> 9.99 us  [the longest x3 5.37 us: swapped(): return lax.ppermute(array, 'c', swap)]
    pallas_call x2 -> x4, Pallas kernels: 5.11 us -> 6.33 us  [the longest x3 6.13 us: place_tiles(): pl.pallas_call(functools.partial(place_kernel, pieces), in_specs=[smem] *...]
  transfers between devices with their start and end apart: 10 -> 16, of which waited for: 5 -> 9; matrix products, arithmetic and copies ran while one was open for 0% -> 0% of each run, Pallas kernels for 18% -> 20%
where the time goes in v6:
time: 156 us
  starting transfers between devices  50.2 us (32%)
  Pallas kernels  36.5 us (23%)
  waiting for transfers between devices  32.4 us (21%)
  blocking collectives  31.4 us (20%)
  local copies, waits for them, and re-layouts  4.27 us (3%)
    all_to_all x1, blocking collectives, shards(): lax.all_to_all(partial.reshape(16, width // 16, 3 * PAIR), FAR16, 0, 0)  16.9 us
    all_to_all x1, blocking collectives, gather_tiles(): lax.all_to_all(jnp.broadcast_to(piece[None], (16, rows, cols)), AX, 0, 0,...  14.5 us
    ppermute x4, waiting for transfers between devices, ring(): return lax.ppermute(array, AX, route)  13.4 us
    ppermute x1, starting transfers between devices, shards(): nxt = lax.ppermute(prev, AX, [(i + 1, i) for i in range(DEVS - 1)])  10.1 us
    all_to_all x1, starting transfers between devices, shards(): got = lax.all_to_all(msg.reshape(DEVS, 16, PAIR), AX, 0, 0)  9.71 us
    all_to_all x1, starting transfers between devices, shards(): delta8 = lax.all_to_all(delta, NEAR8, 0, 0)  7.64 us
    all_to_all x1, waiting for transfers between devices, shards(): delta8 = lax.all_to_all(delta, NEAR8, 0, 0)  6.67 us
    pallas_call x1, Pallas kernels, near(): pl.pallas_call(functools.partial(near_kernel, lin_scale), grid=(width //...  6.21 us
  transfers between devices with their start and end apart: 16, of which 9 were waited for; matrix products, arithmetic and copies ran while one was open for 0% of the time, Pallas kernels for 20%

profile of v6, /device:TPU:1, one launch (start us, length us, event | category | flops | bytes accessed | tf_op | source)
XLA Modules:
  0.0 155.7 jit_solution(14332543195080718888)
XLA Ops:
  0.6 5.7 %collective-permute-start = (bf16[128,1024]{1,0:T(8,128)(2,1)}, bf16[128,1024]{1,0:T(8,128)(2,1)S(1)}, u32[]{:S(2)}, u32[]{:S(2)}) collective-permute-start(bf16[128,1024]{1,0:T(8,128)(2,1)} %tok.3), channel_id=1, source_target_pairs={{0,1},{1,2},{2,3},{3,4},{4,5},{5,6},{6,7},{7,8},{8,9},{9,10},{10,1... | collective-permute-start | bytes 786440 | tf_op jit(solution)/shard_map/ppermute | solution.py:637
  6.3 5.6 %project.1 = (bf16[128,1024]{1,0:T(8,128)(2,1)}, bf16[2,128,1024]{2,1,0:T(8,128)(2,1)}, f32[4,4,128]{2,1,0:T(4,128)}, f32[4,128,4]{2,1,0:T(8,128)}, bf16[2,1024,128]{2,1,0:T(8,128)(2,1)}) custom-call(bf16[128,1024]{1,0:T(8,128)(2,1)} %tok.3, bf16[1024,1024]{1,0:T(8,128)(2,1)} %wq.3, bf16[1024,1024]{1,0:T(8,128)(2,1)} %wk.5, bf16[1024,1024]{1,0:T(8,128)(2,1)} %wv.5, ...), custom_call_target="tpu_custom_call" | custom-call | flops 805306368 | bytes 7864320 | tf_op jit(solution)/shard_map/project/pallas_call | solution.py:124
  11.9 9.7 %all-to-all-start = ((bf16[128,16,128]{2,1,0:T(8,128)(2,1)}), bf16[128,16,128]{2,1,0:T(8,128)(2,1)S(1)}, u32[]{:S(2)}, u32[]{:S(2)}) async-start(bf16[128,16,128]{2,1,0:T(8,128)(2,1)} %bitcast.18), calls=%async_computation | async-start | bytes 1048576 | tf_op jit(solution)/shard_map/all_to_all | solution.py:639
  21.6 0.7 copy-done.8
  22.3 4.4 %prior.1.pkv = bf16[2,128,1024]{2,1,0:T(8,128)(2,1)} custom-call(bf16[128,1024]{1,0:T(8,128)(2,1)} %copy-done.8, bf16[1024,1024]{1,0:T(8,128)(2,1)} %wk.5, bf16[1024,1024]{1,0:T(8,128)(2,1)} %wv.5, f32[4,128,4]{2,1,0:T(8,128)} %get-tuple-element.33.after.runt), custom_call_target="tpu_custom_call" | custom-call | flops 536870912 | bytes 4980736 | tf_op jit(solution)/shard_map/prior/pallas_call | solution.py:161
  26.8 6.2 %near.1 = (f32[128,1024]{1,0:T(8,128)}, f32[128,1024]{1,0:T(8,128)}, f32[2,128,1024]{2,1,0:T(8,128)}, bf16[2,128,1024]{2,1,0:T(8,128)(2,1)}, f32[8,128]{1,0:T(8,128)}) custom-call(s32[1]{0:T(128)} %bitcast.place, s32[1,4]{1,0:T(1,128)} %blocks.1, bf16[128,1024]{1,0:T(8,128)(2,1)} %get-tuple-element.31.q_ref.q, bf16[2,128,1024]{2,1,0:T(8,128)(2,1)} %get-tuple-element.32.kv, ...), custom_call_target="tpu_custom_call" | custom-call | flops 4000000000 | bytes 16000000 | tf_op jit(solution)/shard_map/near/pallas_call | solution.py:323
  33.0 10.1 %collective-permute-start.1 = (bf16[2,128,1024]{2,1,0:T(8,128)(2,1)}, bf16[2,128,1024]{2,1,0:T(8,128)(2,1)S(1)}, u32[]{:S(2)}, u32[]{:S(2)}) collective-permute-start(bf16[2,128,1024]{2,1,0:T(8,128)(2,1)} %get-tuple-element.38), channel_id=1, source_target_pairs={{1,0},{2,1},{3,2},{4,3},{5,4},{6,5},{7,6},{8,7},{9,8},{10,9},{11,1... | collective-permute-start | bytes 1572872 | tf_op jit(solution)/shard_map/ppermute | solution.py:644
  43.1 0.7 copy-done.2
  43.8 1.2 scan.1
  45.0 3.5 %all-to-all-start.1 = ((bf16[128,8,128]{2,1,0:T(8,128)(2,1)}), bf16[128,8,128]{2,1,0:T(8,128)(2,1)S(1)}, u32[]{:S(2)}, u32[]{:S(2)}) async-start(bf16[128,8,128]{2,1,0:T(8,128)(2,1)} %bitcast.2), calls=%async_computation.1 | async-start | bytes 524288 | tf_op jit(solution)/shard_map/all_to_all | solution.py:648
  48.6 0.7 copy-done.3
  49.3 0.1 flip.1.refs_0_
  49.4 1.8 %collective-permute-start.4 = (bf16[1024,128]{1,0:T(8,128)(2,1)S(1)}, bf16[1024,128]{1,0:T(8,128)(2,1)S(1)}, u32[]{:S(2)}, u32[]{:S(2)}) collective-permute-start(bf16[1024,128]{1,0:T(8,128)(2,1)S(1)} %flip.1.refs_0_), channel_id=1, source_target_pairs={{0,24},{8,0},{16,8},{24,16},{1,25},{9,1},{17,9},{25,17},{2,26},{10... | collective-permute-start | bytes 786440 | tf_op jit(solution)/shard_map/ppermute | solution.py:647
  51.2 0.6 collective-permute-start.3
  51.8 0.6 collective-permute-start.2
  52.4 6.1 %all-to-all-done.1 = bf16[128,8,128]{2,1,0:T(8,128)(2,1)S(1)} async-done(((bf16[128,8,128]{2,1,0:T(8,128)(2,1)}), bf16[128,8,128]{2,1,0:T(8,128)(2,1)S(1)}, u32[]{:S(2)}, u32[]{:S(2)}) %all-to-all-start.1) | async-done | bytes 262176 | tf_op jit(solution)/shard_map/all_to_all | solution.py:648
  58.5 0.7 copy-done.6
  59.2 0.2 copy-done.7
  59.4 3.3 %join.1 = (bf16[128,1024]{1,0:T(8,128)(2,1)}, bf16[8,128,384]{2,1,0:T(8,128)(2,1)}) custom-call(f32[128,1024]{1,0:T(8,128)} %get-tuple-element.35.near_out, f32[128,1024]{1,0:T(8,128)} %get-tuple-element.36.dq_in, f32[2,128,1024]{2,1,0:T(8,128)} %get-tuple-element.37.own, bf16[2,128,1024]{2,1,0:T(8,128)(2,1)} %copy-done.7, ...), custom_call_target="tpu_custom_call" | custom-call | flops 134217728 | bytes 3145728 | tf_op jit(solution)/shard_map/join/pallas_call | solution.py:396
  62.6 0.8 collective-permute-done.4.refs_3_
  63.4 3.1 %collective-permute-done.2.refs_1_ = bf16[1024,128]{1,0:T(8,128)(2,1)S(1)} collective-permute-done((bf16[1024,128]{1,0:T(8,128)(2,1)S(1)}, bf16[1024,128]{1,0:T(8,128)(2,1)S(1)}, u32[]{:S(2)}, u32[]{:S(2)}) %collective-permute-start.2) | collective-permute-done | bytes 262176 | tf_op jit(solution)/shard_map/ppermute | solution.py:647
  66.5 0.1 stack.2.mine
  66.6 0.6 collective-permute-start.5
  67.2 7.6 %all-to-all-start.2 = ((bf16[8,128,384]{2,1,0:T(8,128)(2,1)}), bf16[8,128,384]{2,1,0:T(8,128)(2,1)S(1)}, u32[]{:S(2)}, u32[]{:S(2)}) async-start(bf16[8,128,384]{2,1,0:T(8,128)(2,1)} %get-tuple-element.42.delta.refs_4_), calls=%async_computation.2 | async-start | bytes 1572864 | tf_op jit(solution)/shard_map/all_to_all | solution.py:652
  74.8 5.5 %back.1.after = bf16[128,1024]{1,0:T(8,128)(2,1)} custom-call(bf16[8,128,384]{2,1,0:T(8,128)(2,1)} %get-tuple-element.42.delta.refs_4_, bf16[1024,1024]{1,0:T(8,128)(2,1)} %wq.3, bf16[1024,1024]{1,0:T(8,128)(2,1)} %wk.5, bf16[1024,1024]{1,0:T(8,128)(2,1)} %wv.5), custom_call_target="tpu_custom_call" | custom-call | flops 805306368 | bytes 7340032 | tf_op jit(solution)/shard_map/back/pallas_call | solution.py:449
  80.4 6.7 %all-to-all-done.2.delta = bf16[8,128,384]{2,1,0:T(8,128)(2,1)S(1)} async-done(((bf16[8,128,384]{2,1,0:T(8,128)(2,1)}), bf16[8,128,384]{2,1,0:T(8,128)(2,1)S(1)}, u32[]{:S(2)}, u32[]{:S(2)}) %all-to-all-start.2) | async-done | bytes 786464 | tf_op jit(solution)/shard_map/all_to_all | solution.py:652
  87.0 0.9 copy-done.4
  87.9 0.3 copy-done.5
  88.3 3.7 %outer.1 = bf16[1024,384]{1,0:T(8,128)(2,1)} custom-call(s32[1]{0:T(128)} %bitcast.4.core.side, s32[1]{0:T(128)} %bitcast.5.at_x, bf16[4,1024,128]{2,1,0:T(8,128)(2,1)} %copy-done, bf16[4,1024,128]{2,1,0:T(8,128)(2,1)} %copy-done.5, bf16[8,128,384]{2,1,0:T(8,128)(2,1)} %copy-done.4, bf16[128,1024]{1,0:T(8,128)(2,1)} %back.1.after), custom_call_target="tpu_custom_call" | custom-call | flops 805306368 | bytes 2883584 | tf_op jit(solution)/shard_map/outer/pallas_call | solution.py:479
  91.9 16.9 %all_to_all.25 = bf16[16,64,384]{2,1,0:T(8,128)(2,1)S(1)} all-to-all(bf16[16,64,384]{2,1,0:T(8,128)(2,1)} %bitcast.16), channel_id=1, replica_groups=mesh['yl'=2,'c'=2,'x'=4,'z'=4,'yh'=2] {'yl','z','yh'}, dimensions={0} | all-to-all | bytes 1572864 | tf_op jit(solution)/shard_map/all_to_all | solution.py:657
  108.8 0.1 convert_reduce_fusion
  109.0 0.1 broadcast_in_dim.2
  109.1 14.5 %all_to_all.26 = bf16[16,64,384]{2,1,0:T(8,128)(2,1)S(1)} all-to-all(bf16[16,64,384]{2,1,0:T(8,128)(2,1)S(1)} %broadcast_in_dim.2), channel_id=1, replica_groups={{0,1,2,3,4,5,6,7,64,65,66,67,68,69,70,71},{8,9,10,11,12,13,14,15,72,73,..., dimensions={0} | all-to-all | bytes 1572864 | tf_op jit(solution)/shard_map/all_to_all | solution.py:614
  123.6 3.8 %collective-permute-start.8 = (bf16[8,128,384]{2,1,0:T(8,128)(2,1)S(1)}, bf16[8,128,384]{2,1,0:T(8,128)(2,1)S(1)}, u32[]{:S(2)}, u32[]{:S(2)}) collective-permute-start(bf16[8,128,384]{2,1,0:T(8,128)(2,1)S(1)} %bitcast.12), channel_id=1, source_target_pairs={{0,32},{32,0},{1,33},{33,1},{2,34},{34,2},{3,35},{35,3},{4,36},{36... | collective-permute-start | bytes 2359304 | tf_op jit(solution)/shard_map/ppermute | solution.py:611
  127.3 1.9 %collective-permute-start.7 = (bf16[8,128,384]{2,1,0:T(8,128)(2,1)S(1)}, bf16[8,128,384]{2,1,0:T(8,128)(2,1)S(1)}, u32[]{:S(2)}, u32[]{:S(2)}) collective-permute-start(bf16[8,128,384]{2,1,0:T(8,128)(2,1)S(1)} %bitcast.13), channel_id=1, source_target_pairs={{0,24},{32,38},{1,25},{33,39},{2,26},{34,32},{3,27},{35,33},{4,28}... | collective-permute-start | bytes 2359304 | tf_op jit(solution)/shard_map/ppermute | solution.py:524
  129.3 1.5 place.3
  130.8 7.6 %collective-permute-done.7.ahead = bf16[8,128,384]{2,1,0:T(8,128)(2,1)S(1)} collective-permute-done((bf16[8,128,384]{2,1,0:T(8,128)(2,1)S(1)}, bf16[8,128,384]{2,1,0:T(8,128)(2,1)S(1)}, u32[]{:S(2)}, u32[]{:S(2)}) %collective-permute-start.7) | collective-permute-done | bytes 786464 | tf_op jit(solution)/shard_map/ppermute | solution.py:524
  138.5 3.1 %collective-permute-done.6.behind = bf16[8,128,384]{2,1,0:T(8,128)(2,1)S(1)} collective-permute-done((bf16[8,128,384]{2,1,0:T(8,128)(2,1)S(1)}, bf16[8,128,384]{2,1,0:T(8,128)(2,1)S(1)}, u32[]{:S(2)}, u32[]{:S(2)}) %collective-permute-start.6) | collective-permute-done | bytes 786464 | tf_op jit(solution)/shard_map/ppermute | solution.py:524
  141.6 0.2 halves.1
  141.8 0.6 collective-permute-start.11
  142.4 0.6 collective-permute-start.9
  143.0 2.1 %collective-permute-start.10 = (bf16[4,128,384]{2,1,0:T(8,128)(2,1)S(1)}, bf16[4,128,384]{2,1,0:T(8,128)(2,1)S(1)}, u32[]{:S(2)}, u32[]{:S(2)}) collective-permute-start(bf16[4,128,384]{2,1,0:T(8,128)(2,1)S(1)} %get-tuple-element.45), channel_id=1, source_target_pairs={{0,24},{32,38},{1,25},{33,39},{2,26},{34,32},{3,27},{35,33},{4,28}... | collective-permute-start | bytes 1179656 | tf_op jit(solution)/shard_map/ppermute | solution.py:524
  145.1 0.4 collective-permute-done.11.other
  145.4 2.5 %place.4 = (bf16[1024,1024]{1,0:T(8,128)(2,1)}, bf16[1024,1024]{1,0:T(8,128)(2,1)}, bf16[1024,1024]{1,0:T(8,128)(2,1)}, f32[8,128]{1,0:T(8,128)S(1)}) custom-call(s32[1]{0:T(128)} %bitcast.4.core.side, s32[1]{0:T(128)} %bitcast.5.at_x, s32[1]{0:T(128)} %bitcast.6.at_z, ...), custom_call_target="tpu_custom_call", output_to_operand_aliasing={{0}: (5, {}), {1}: (6, {}), {2}: (7, {})} | custom-call | bytes 6291456 | tf_op jit(solution)/shard_map/place/pallas_call | solution.py:570
  147.9 2.6 %collective-permute-done.9.refs_0_ = bf16[4,128,384]{2,1,0:T(8,128)(2,1)S(1)} collective-permute-done((bf16[4,128,384]{2,1,0:T(8,128)(2,1)S(1)}, bf16[4,128,384]{2,1,0:T(8,128)(2,1)S(1)}, u32[]{:S(2)}, u32[]{:S(2)}) %collective-permute-start.9) | collective-permute-done | bytes 393248 | tf_op jit(solution)/shard_map/ppermute | solution.py:524
  150.6 1.0 collective-permute-start.12
  151.6 1.9 %collective-permute-done.12.other = bf16[8,128,384]{2,1,0:T(8,128)(2,1)S(1)} collective-permute-done((bf16[8,128,384]{2,1,0:T(8,128)(2,1)S(1)}, bf16[8,128,384]{2,1,0:T(8,128)(2,1)S(1)}, u32[]{:S(2)}, u32[]{:S(2)}) %collective-permute-start.12) | collective-permute-done | bytes 786464 | tf_op jit(solution)/shard_map/ppermute | solution.py:611
  153.5 2.1 %place.5 = (bf16[1024,1024]{1,0:T(8,128)(2,1)}, bf16[1024,1024]{1,0:T(8,128)(2,1)}, bf16[1024,1024]{1,0:T(8,128)(2,1)}, f32[8,128]{1,0:T(8,128)}) custom-call(s32[1]{0:T(128)} %bitcast.4.core.side, s32[1]{0:T(128)} %bitcast.5.at_x, s32[1]{0:T(128)} %bitcast.6.at_z, ...), custom_call_target="tpu_custom_call", output_to_operand_aliasing={{0}: (5, {}), {1}: (6, {}), {2}: (7, {})} | custom-call | bytes 3145728 | tf_op jit(solution)/shard_map/place/pallas_call | solution.py:570
  (21 shorter events, 0.1 us)
Async XLA Ops:
  0.6 21.0 %collective-permute-start = (bf16[128,1024]{1,0:T(8,128)(2,1)}, bf16[128,1024]{1,0:T(8,128)(2,1)S(1)}, u32[]{:S(2)}, u32[]{:S(2)}) collective-permute-start(bf16[128,1024]{1,0:T(8,128)(2,1)} %tok.3), channel_id=1, source_target_pairs={{0,1},{1,2},{2,3},{3,4},{4,5},{5,6},{6,7},{7,8},{8,9},{9,10},{10,1... | collective-permute-start | bytes 786440 | tf_op jit(solution)/shard_map/ppermute | solution.py:637
  11.9 31.2 %all-to-all-start = ((bf16[128,16,128]{2,1,0:T(8,128)(2,1)}), bf16[128,16,128]{2,1,0:T(8,128)(2,1)S(1)}, u32[]{:S(2)}, u32[]{:S(2)}) async-start(bf16[128,16,128]{2,1,0:T(8,128)(2,1)} %bitcast.18), calls=%async_computation | async-start | bytes 1048576 | tf_op jit(solution)/shard_map/all_to_all | solution.py:639
  21.6 0.7 copy-start.8
  26.8 21.8 %copy-start.1 = (bf16[128,1024]{1,0:T(8,128)(2,1)S(1)}, bf16[128,1024]{1,0:T(8,128)(2,1)}, u32[]{:S(2)}) copy-start(bf16[128,1024]{1,0:T(8,128)(2,1)} %tok.3) | copy-start | bytes 786436
  33.0 25.5 %collective-permute-start.1 = (bf16[2,128,1024]{2,1,0:T(8,128)(2,1)}, bf16[2,128,1024]{2,1,0:T(8,128)(2,1)S(1)}, u32[]{:S(2)}, u32[]{:S(2)}) collective-permute-start(bf16[2,128,1024]{2,1,0:T(8,128)(2,1)} %get-tuple-element.38), channel_id=1, source_target_pairs={{1,0},{2,1},{3,2},{4,3},{5,4},{6,5},{7,6},{8,7},{9,8},{10,9},{11,1... | collective-permute-start | bytes 1572872 | tf_op jit(solution)/shard_map/ppermute | solution.py:644
  43.1 0.7 copy-start.2
  45.0 13.4 %all-to-all-start.1 = ((bf16[128,8,128]{2,1,0:T(8,128)(2,1)}), bf16[128,8,128]{2,1,0:T(8,128)(2,1)S(1)}, u32[]{:S(2)}, u32[]{:S(2)}) async-start(bf16[128,8,128]{2,1,0:T(8,128)(2,1)} %bitcast.2), calls=%async_computation.1 | async-start | bytes 524288 | tf_op jit(solution)/shard_map/all_to_all | solution.py:648
  48.6 0.7 copy-start.3
  49.4 14.0 %collective-permute-start.4 = (bf16[1024,128]{1,0:T(8,128)(2,1)S(1)}, bf16[1024,128]{1,0:T(8,128)(2,1)S(1)}, u32[]{:S(2)}, u32[]{:S(2)}) collective-permute-start(bf16[1024,128]{1,0:T(8,128)(2,1)S(1)} %flip.1.refs_0_), channel_id=1, source_target_pairs={{0,24},{8,0},{16,8},{24,16},{1,25},{9,1},{17,9},{25,17},{2,26},{10... | collective-permute-start | bytes 786440 | tf_op jit(solution)/shard_map/ppermute | solution.py:647
  51.2 12.3 %collective-permute-start.3 = (bf16[1024,128]{1,0:T(8,128)(2,1)S(1)}, bf16[1024,128]{1,0:T(8,128)(2,1)S(1)}, u32[]{:S(2)}, u32[]{:S(2)}) collective-permute-start(bf16[1024,128]{1,0:T(8,128)(2,1)S(1)} %flip.1.refs_0_), channel_id=1, source_target_pairs={{0,16},{8,24},{16,0},{24,8},{1,17},{9,25},{17,1},{25,9},{2,18},{10... | collective-permute-start | bytes 786440 | tf_op jit(solution)/shard_map/ppermute | solution.py:647
  51.8 14.8 %collective-permute-start.2 = (bf16[1024,128]{1,0:T(8,128)(2,1)S(1)}, bf16[1024,128]{1,0:T(8,128)(2,1)S(1)}, u32[]{:S(2)}, u32[]{:S(2)}) collective-permute-start(bf16[1024,128]{1,0:T(8,128)(2,1)S(1)} %flip.1.refs_0_), channel_id=1, source_target_pairs={{0,8},{8,16},{16,24},{24,0},{1,9},{9,17},{17,25},{25,1},{2,10},{10... | collective-permute-start | bytes 786440 | tf_op jit(solution)/shard_map/ppermute | solution.py:647
  58.5 0.7 copy-start.6
  58.5 0.9 copy-start.7
  66.6 13.7 %copy-start = (bf16[4,1024,128]{2,1,0:T(8,128)(2,1)}, bf16[4,1024,128]{2,1,0:T(8,128)(2,1)S(1)}, u32[]{:S(2)}) copy-start(bf16[4,1024,128]{2,1,0:T(8,128)(2,1)S(1)} %stack.2.mine) | copy-start | bytes 3145732
  66.6 20.4 %collective-permute-start.5 = (bf16[4,1024,128]{2,1,0:T(8,128)(2,1)S(1)}, bf16[4,1024,128]{2,1,0:T(8,128)(2,1)S(1)}, u32[]{:S(2)}, u32[]{:S(2)}) collective-permute-start(bf16[4,1024,128]{2,1,0:T(8,128)(2,1)S(1)} %stack.2.mine), channel_id=1, source_target_pairs={{0,32},{32,0},{1,33},{33,1},{2,34},{34,2},{3,35},{35,3},{4,36},{36... | collective-permute-start | bytes 3145736 | tf_op jit(solution)/shard_map/ppermute | solution.py:654
  67.2 19.8 %all-to-all-start.2 = ((bf16[8,128,384]{2,1,0:T(8,128)(2,1)}), bf16[8,128,384]{2,1,0:T(8,128)(2,1)S(1)}, u32[]{:S(2)}, u32[]{:S(2)}) async-start(bf16[8,128,384]{2,1,0:T(8,128)(2,1)} %get-tuple-element.42.delta.refs_4_), calls=%async_computation.2 | async-start | bytes 1572864 | tf_op jit(solution)/shard_map/all_to_all | solution.py:652
  87.0 0.9 copy-start.4
  87.0 1.2 copy-start.5
  123.6 5.7 %collective-permute-start.8 = (bf16[8,128,384]{2,1,0:T(8,128)(2,1)S(1)}, bf16[8,128,384]{2,1,0:T(8,128)(2,1)S(1)}, u32[]{:S(2)}, u32[]{:S(2)}) collective-permute-start(bf16[8,128,384]{2,1,0:T(8,128)(2,1)S(1)} %bitcast.12), channel_id=1, source_target_pairs={{0,32},{32,0},{1,33},{33,1},{2,34},{34,2},{3,35},{35,3},{4,36},{36... | collective-permute-start | bytes 2359304 | tf_op jit(solution)/shard_map/ppermute | solution.py:611
  127.3 11.1 %collective-permute-start.7 = (bf16[8,128,384]{2,1,0:T(8,128)(2,1)S(1)}, bf16[8,128,384]{2,1,0:T(8,128)(2,1)S(1)}, u32[]{:S(2)}, u32[]{:S(2)}) collective-permute-start(bf16[8,128,384]{2,1,0:T(8,128)(2,1)S(1)} %bitcast.13), channel_id=1, source_target_pairs={{0,24},{32,38},{1,25},{33,39},{2,26},{34,32},{3,27},{35,33},{4,28}... | collective-permute-start | bytes 2359304 | tf_op jit(solution)/shard_map/ppermute | solution.py:524
  129.3 12.3 %collective-permute-start.6 = (bf16[8,128,384]{2,1,0:T(8,128)(2,1)S(1)}, bf16[8,128,384]{2,1,0:T(8,128)(2,1)S(1)}, u32[]{:S(2)}, u32[]{:S(2)}) collective-permute-start(bf16[8,128,384]{2,1,0:T(8,128)(2,1)S(1)} %bitcast.14), channel_id=1, source_target_pairs={{0,8},{32,34},{1,9},{33,35},{2,10},{34,36},{3,11},{35,37},{4,12},{... | collective-permute-start | bytes 2359304 | tf_op jit(solution)/shard_map/ppermute | solution.py:524
  141.8 3.6 %collective-permute-start.11 = (bf16[16,128,384]{2,1,0:T(8,128)(2,1)S(1)}, bf16[16,128,384]{2,1,0:T(8,128)(2,1)S(1)}, u32[]{:S(2)}, u32[]{:S(2)}) collective-permute-start(bf16[16,128,384]{2,1,0:T(8,128)(2,1)S(1)} %get-tuple-element.46.own), channel_id=1, source_target_pairs={{0,32},{32,0},{1,33},{33,1},{2,34},{34,2},{3,35},{35,3},{4,36},{36... | collective-permute-start | bytes 4718600 | tf_op jit(solution)/shard_map/ppermute | solution.py:611
  142.4 8.1 %collective-permute-start.9 = (bf16[4,128,384]{2,1,0:T(8,128)(2,1)S(1)}, bf16[4,128,384]{2,1,0:T(8,128)(2,1)S(1)}, u32[]{:S(2)}, u32[]{:S(2)}) collective-permute-start(bf16[4,128,384]{2,1,0:T(8,128)(2,1)S(1)} %get-tuple-element.44), channel_id=1, source_target_pairs={{0,8},{32,34},{1,9},{33,35},{2,10},{34,36},{3,11},{35,37},{4,12},{... | collective-permute-start | bytes 1179656 | tf_op jit(solution)/shard_map/ppermute | solution.py:524
  143.0 7.5 %collective-permute-start.10 = (bf16[4,128,384]{2,1,0:T(8,128)(2,1)S(1)}, bf16[4,128,384]{2,1,0:T(8,128)(2,1)S(1)}, u32[]{:S(2)}, u32[]{:S(2)}) collective-permute-start(bf16[4,128,384]{2,1,0:T(8,128)(2,1)S(1)} %get-tuple-element.45), channel_id=1, source_target_pairs={{0,24},{32,38},{1,25},{33,39},{2,26},{34,32},{3,27},{35,33},{4,28}... | collective-permute-start | bytes 1179656 | tf_op jit(solution)/shard_map/ppermute | solution.py:524
  150.6 2.9 %collective-permute-start.12 = (bf16[8,128,384]{2,1,0:T(8,128)(2,1)S(1)}, bf16[8,128,384]{2,1,0:T(8,128)(2,1)S(1)}, u32[]{:S(2)}, u32[]{:S(2)}) collective-permute-start(bf16[8,128,384]{2,1,0:T(8,128)(2,1)S(1)} %bitcast.10), channel_id=1, source_target_pairs={{0,32},{32,0},{1,33},{33,1},{2,34},{34,2},{3,35},{35,3},{4,36},{36... | collective-permute-start | bytes 2359304 | tf_op jit(solution)/shard_map/ppermute | solution.py:611

commit v7 on v6

--- a/solution.py
+++ b/solution.py
@@ -19,6 +19,12 @@
 PAIR = 128
 DH = 64
 DEVS = 128
+SPAN = ("x", "z", "yh")
+GROUP = ("yl", "c")
+PLACES = 32
+GROUPS = 4
+SLICE = 32
+SENT = SLICE + 16
 VMEM = pltpu.VMEM
 HIGH = lax.Precision.HIGHEST
 
@@ -74,7 +80,7 @@
     for step in range(run_out.shape[0]):
         runt_out[step] = runt[:, step * group : (step + 1) * group]
         run_out[step] = run[step * group : (step + 1) * group, :]
-    rows = iota((8, PAIR), 0)
+    rows = iota((SENT - SLICE, PAIR), 0)
     first = iota((DH, PAIR), 1) < DH
     for step in range(width // wide):
         for part in range(3):
@@ -107,11 +113,10 @@
             tail = jnp.where(
                 rows == 0, high, jnp.where(rows == 1, mid, jnp.where(rows == 2, low, 0.0))
             )
-            tail = jnp.broadcast_to(tail[None], (8, 8, PAIR))
             for part, full in enumerate(states):
-                own = jnp.where(first, full[:DH], full[DH:]).reshape(8, 8, PAIR)
-                sent = jnp.concatenate([own, tail], axis=1).reshape(PAIR, PAIR)
-                msg[part, pair * PAIR : (pair + 1) * PAIR, :] = sent.astype(BF)
+                own = jnp.where(first, full[:DH], full[DH:])
+                sent = jnp.concatenate([own[:SLICE], tail, own[SLICE:], tail], axis=0)
+                msg[part, pair * 2 * SENT : (pair + 1) * 2 * SENT, :] = sent.astype(BF)
 
 
 def project(tokens, wq, wk, wv, log_decay, cot, lin_scale):
@@ -130,7 +135,7 @@
             jax.ShapeDtypeStruct((2, rows, width), BF),
             jax.ShapeDtypeStruct((chunks, heads // chunks, rows), F32),
             jax.ShapeDtypeStruct((chunks, rows, heads // chunks), F32),
-            jax.ShapeDtypeStruct((2, width, PAIR), BF),
+            jax.ShapeDtypeStruct((2, width // PAIR * 2 * SENT, PAIR), BF),
         ],
         scratch_shapes=[
             VMEM((3, width // wide, width, wide), BF),
@@ -211,39 +216,83 @@
     )(*parts, after)
 
 
-def scan_kernel(place, got, after, out, xs, decays, states):
+def unpack(got, xs, decays):
+    both = got[...].astype(F32)
+    xs[...] = both[:, :SLICE, :]
+    total = both[:, SLICE : SLICE + 1, :] + both[:, SLICE + 1 : SLICE + 2, :]
+    total += both[:, SLICE + 2 : SLICE + 3, :]
+    decays[...] = jnp.exp(total)
+    return total
+
+
+def along(backward, i):
+    return jnp.where(backward, PLACES - 1 - i, i)
+
+
+def total_kernel(at_span, got, after, out, xs, decays):
     del after
-    both = got[...].astype(F32)
-    xs[...] = both[:, :8, :]
-    total = both[:, 8:9, :] + both[:, 9:10, :] + both[:, 10:11, :]
-    decays[...] = jnp.broadcast_to(jnp.exp(total), decays.shape)
-    backward = place[0] >= DEVS // 2
-
-    def one(i, state):
-        at = jnp.where(backward, DEVS - 1 - i, i)
+    total = unpack(got, xs, decays)
+    backward = at_span[0] >= PLACES // 2
+    state = jnp.zeros((SLICE, PAIR), F32)
+    for i in range(PLACES):
+        at = along(backward, i)
+        state = decays[at] * state + xs[at]
+    out[:SLICE] = state
+    out[SLICE:] = jnp.broadcast_to(jnp.sum(total, axis=0), (8, PAIR))
+
+
+def scan_kernel(at_span, at_group, got, one, two, three, out, xs, decays, states):
+    unpack(got, xs, decays)
+    backward = at_span[0] >= PLACES // 2
+    group = at_group[0]
+    state = jnp.zeros((SLICE, PAIR), F32)
+    for near_by, front, back in ((3, three, one), (2, two, two), (1, one, three)):
+        there = jnp.where(backward, group + near_by < GROUPS, group >= near_by)
+        that = jnp.where(backward, back[...], front[...])
+        joined = jnp.exp(that[SLICE : SLICE + 1]) * state + that[:SLICE]
+        state = jnp.where(there, joined, state)
+    for i in range(PLACES):
+        at = along(backward, i)
         states[at] = state
-        return decays[at] * state + xs[at]
-
-    lax.fori_loop(0, DEVS, one, jnp.zeros((8, PAIR), F32), unroll=8)
-    out[...] = states[...].reshape(DEVS * 8, PAIR).astype(BF)
-
-
-def scan(place, got, after):
+        state = decays[at] * state + xs[at]
+    out[...] = states[...].reshape(PLACES * SLICE, PAIR).astype(BF)
+
+
+def group_total(at_span, got, after):
     whole = pl.BlockSpec(memory_space=VMEM)
     return pl.pallas_call(
-        scan_kernel,
+        total_kernel,
         in_specs=[
             pl.BlockSpec(memory_space=pltpu.SMEM),
             whole,
             pl.BlockSpec(memory_space=pl.ANY),
         ],
         out_specs=whole,
-        out_shape=jax.ShapeDtypeStruct((DEVS * 8, PAIR), BF),
-        scratch_shapes=[VMEM((DEVS, 8, PAIR), F32)] * 3,
+        out_shape=jax.ShapeDtypeStruct((SLICE + 8, PAIR), F32),
+        scratch_shapes=[VMEM((PLACES, SLICE, PAIR), F32), VMEM((PLACES, 1, PAIR), F32)],
         compiler_params=params(24),
-        cost_estimate=cost(2 * DEVS * 8 * PAIR, 4 * DEVS * 16 * PAIR),
+        cost_estimate=cost(2 * PLACES * SLICE * PAIR, 4 * PLACES * SENT * PAIR),
+        name="group_total",
+    )(at_span, got, after)
+
+
+def scan(at_span, at_group, got, others):
+    whole = pl.BlockSpec(memory_space=VMEM)
+    smem = pl.BlockSpec(memory_space=pltpu.SMEM)
+    return pl.pallas_call(
+        scan_kernel,
+        in_specs=[smem, smem] + [whole] * 4,
+        out_specs=whole,
+        out_shape=jax.ShapeDtypeStruct((PLACES * SLICE, PAIR), BF),
+        scratch_shapes=[
+            VMEM((PLACES, SLICE, PAIR), F32),
+            VMEM((PLACES, 1, PAIR), F32),
+            VMEM((PLACES, SLICE, PAIR), F32),
+        ],
+        compiler_params=params(24),
+        cost_estimate=cost(2 * PLACES * SLICE * PAIR, 4 * PLACES * SENT * PAIR),
         name="scan",
-    )(place, got, after)
+    )(at_span, at_group, got, *others)
 
 
 def near_kernel(lin_scale, place, blocks, q_ref, kv, pkv, cot, run, runt, out, dq_out, own, prev, mark):
@@ -636,16 +685,23 @@
     swap = [(0, 1), (1, 0)]
     prev_tokens = lax.ppermute(tokens, AX, [(i, i + 1) for i in range(DEVS - 1)])
     q, kv, run, runt, msg = project(tokens, wq, wk, wv, log_decay, cot, lin_scale)
-    got = lax.all_to_all(msg.reshape(DEVS, 16, PAIR), AX, 0, 0)
+    got = lax.all_to_all(msg.reshape(PLACES, SENT, PAIR), SPAN, 0, 0)
     pkv = prior(prev_tokens, wk, wv, runt)
     near_out, dq, own, prev, mark = near(
         place, neighbour_blocks, q, kv, pkv, cot, run, runt, lin_scale
     )
     nxt = lax.ppermute(prev, AX, [(i + 1, i) for i in range(DEVS - 1)])
-    states = scan(place, got, mark)
+    at_span = lax.axis_index(SPAN).astype(jnp.int32).reshape(1)
+    at_group = lax.axis_index(GROUP).astype(jnp.int32).reshape(1)
+    total = group_total(at_span, got, mark)
+    others = [
+        lax.ppermute(total, GROUP, [(i, (i + d) % GROUPS) for i in range(GROUPS)])
+        for d in range(1, GROUPS)
+    ]
+    states = scan(at_span, at_group, got, others)
     tokt = flip(tokens, mark)
     around = [lax.ppermute(tokt, "x", [(i, (i + d) % 4) for i in range(4)]) for d in (1, 2, 3)]
-    states = lax.all_to_all(states.reshape(DEVS, 8, PAIR), AX, 0, 0)
+    states = lax.all_to_all(states.reshape(PLACES, SLICE, PAIR), SPAN, 0, 0)
     states = states.reshape(2, width // PAIR, DH, PAIR)
     layer, delta = join(near_out, dq, own, nxt, q, kv, cot, runt, states, [], lin_scale)
 

time: 156 us -> 166 us (1.064)
  waiting for transfers between devices: 32.4 us -> 39.7 us
  blocking collectives: 31.4 us -> 33.3 us
    ppermute x0 -> x3, waiting for transfers between devices: none -> 7.53 us  [shards(): lax.ppermute(total, GROUP, [(i, (i + d) % GROUPS) for i in range(GROUPS)])]
    all_to_all x1, starting transfers between devices: 7.64 us -> 3.53 us  [shards(): delta8 = lax.all_to_all(delta, NEAR8, 0, 0)]
    ppermute x0 -> x3, starting transfers between devices: none -> 3.39 us  [shards(): lax.ppermute(total, GROUP, [(i, (i + d) % GROUPS) for i in range(GROUPS)])]
    all_to_all x1, blocking collectives: 16.9 us -> 19.7 us  [shards(): lax.all_to_all(partial.reshape(16, width // 16, 3 * PAIR), FAR16, 0, 0)]
  transfers between devices with their start and end apart: 16 -> 19, of which waited for: 9 -> 9; matrix products, arithmetic and copies ran while one was open for 0% -> 0% of each run, Pallas kernels for 20% -> 18%
where the time goes in v7:
time: 166 us; the launch traced here: 165 us
  starting transfers between devices  50.6 us (30%)
  waiting for transfers between devices  39.7 us (24%)
  Pallas kernels  36.2 us (22%)
  blocking collectives  33.3 us (20%)
  local copies, waits for them, and re-layouts  4.24 us (3%)
    all_to_all x1, blocking collectives, shards(): lax.all_to_all(partial.reshape(16, width // 16, 3 * PAIR), FAR16, 0, 0)  19.7 us
    all_to_all x1, blocking collectives, gather_tiles(): lax.all_to_all(jnp.broadcast_to(piece[None], (16, rows, cols)), AX, 0, 0,...  13.5 us
    ppermute x4, waiting for transfers between devices, ring(): return lax.ppermute(array, AX, route)  13.1 us
    ppermute x1, starting transfers between devices, shards(): nxt = lax.ppermute(prev, AX, [(i + 1, i) for i in range(DEVS - 1)])  10.3 us
    all_to_all x1, starting transfers between devices, shards(): got = lax.all_to_all(msg.reshape(PLACES, SENT, PAIR), SPAN, 0, 0)  8.57 us
    ppermute x3, waiting for transfers between devices, shards(): lax.ppermute(total, GROUP, [(i, (i + d) % GROUPS) for i in range(GROUPS)])  7.53 us
    all_to_all x1, waiting for transfers between devices, shards(): delta8 = lax.all_to_all(delta, NEAR8, 0, 0)  6.66 us
    pallas_call x1, Pallas kernels, near(): pl.pallas_call(functools.partial(near_kernel, lin_scale), grid=(width //...  6.21 us
  transfers between devices with their start and end apart: 19, of which 9 were waited for; matrix products, arithmetic and copies ran while one was open for 0% of the time, Pallas kernels for 18%

profile of v7, /device:TPU:1, one launch (start us, length us, event | category | flops | bytes accessed | tf_op | source)
XLA Modules:
  0.0 165.0 jit_solution(9498544233870987635)
XLA Ops:
  0.6 5.7 %collective-permute-start = (bf16[128,1024]{1,0:T(8,128)(2,1)}, bf16[128,1024]{1,0:T(8,128)(2,1)S(1)}, u32[]{:S(2)}, u32[]{:S(2)}) collective-permute-start(bf16[128,1024]{1,0:T(8,128)(2,1)} %tok.3), channel_id=1, source_target_pairs={{0,1},{1,2},{2,3},{3,4},{4,5},{5,6},{6,7},{7,8},{8,9},{9,10},{10,1... | collective-permute-start | bytes 786440 | tf_op jit(solution)/shard_map/ppermute | solution.py:686
  6.3 5.5 %project.1 = (bf16[128,1024]{1,0:T(8,128)(2,1)}, bf16[2,128,1024]{2,1,0:T(8,128)(2,1)}, f32[4,4,128]{2,1,0:T(4,128)}, f32[4,128,4]{2,1,0:T(8,128)}, bf16[2,768,128]{2,1,0:T(8,128)(2,1)}) custom-call(bf16[128,1024]{1,0:T(8,128)(2,1)} %tok.3, bf16[1024,1024]{1,0:T(8,128)(2,1)} %wq.3, bf16[1024,1024]{1,0:T(8,128)(2,1)} %wk.5, bf16[1024,1024]{1,0:T(8,128)(2,1)} %wv.5, ...), custom_call_target="tpu_custom_call" | custom-call | flops 805306368 | bytes 7864320 | tf_op jit(solution)/shard_map/project/pallas_call | solution.py:129
  11.8 8.6 %all-to-all-start = ((bf16[32,48,128]{2,1,0:T(8,128)(2,1)}), bf16[32,48,128]{2,1,0:T(8,128)(2,1)S(1)}, u32[]{:S(2)}, u32[]{:S(2)}) async-start(bf16[32,48,128]{2,1,0:T(8,128)(2,1)} %bitcast.20), calls=%async_computation | async-start | bytes 786432 | tf_op jit(solution)/shard_map/all_to_all | solution.py:688
  20.4 0.7 copy-done.8
  21.1 4.4 %prior.1.pkv = bf16[2,128,1024]{2,1,0:T(8,128)(2,1)} custom-call(bf16[128,1024]{1,0:T(8,128)(2,1)} %copy-done.8, bf16[1024,1024]{1,0:T(8,128)(2,1)} %wk.5, bf16[1024,1024]{1,0:T(8,128)(2,1)} %wv.5, f32[4,128,4]{2,1,0:T(8,128)} %get-tuple-element.33.after.runt), custom_call_target="tpu_custom_call" | custom-call | flops 536870912 | bytes 4980736 | tf_op jit(solution)/shard_map/prior/pallas_call | solution.py:166
  25.6 6.2 %near.1 = (f32[128,1024]{1,0:T(8,128)}, f32[128,1024]{1,0:T(8,128)}, f32[2,128,1024]{2,1,0:T(8,128)}, bf16[2,128,1024]{2,1,0:T(8,128)(2,1)}, f32[8,128]{1,0:T(8,128)}) custom-call(s32[1]{0:T(128)} %bitcast.place, s32[1,4]{1,0:T(1,128)} %blocks.1, bf16[128,1024]{1,0:T(8,128)(2,1)} %get-tuple-element.31.q_ref.q, bf16[2,128,1024]{2,1,0:T(8,128)(2,1)} %get-tuple-element.32.kv, ...), custom_call_target="tpu_custom_call" | custom-call | flops 4000000000 | bytes 16000000 | tf_op jit(solution)/shard_map/near/pallas_call | solution.py:372
  31.8 10.3 %collective-permute-start.1 = (bf16[2,128,1024]{2,1,0:T(8,128)(2,1)}, bf16[2,128,1024]{2,1,0:T(8,128)(2,1)S(1)}, u32[]{:S(2)}, u32[]{:S(2)}) collective-permute-start(bf16[2,128,1024]{2,1,0:T(8,128)(2,1)} %get-tuple-element.38), channel_id=1, source_target_pairs={{1,0},{2,1},{3,2},{4,3},{5,4},{6,5},{7,6},{8,7},{9,8},{10,9},{11,1... | collective-permute-start | bytes 1572872 | tf_op jit(solution)/shard_map/ppermute | solution.py:693
  42.2 0.7 copy-done.2
  42.8 0.1 group_total.1
  43.0 1.4 collective-permute-start.3
  44.4 1.9 %collective-permute-start.2 = (f32[40,128]{1,0:T(8,128)S(1)}, f32[40,128]{1,0:T(8,128)S(1)}, u32[]{:S(2)}, u32[]{:S(2)}) collective-permute-start(f32[40,128]{1,0:T(8,128)S(1)} %group_total.1), channel_id=1, source_target_pairs={{0,32},{32,64},{64,96},{96,0},{1,33},{33,65},{65,97},{97,1},{2,34}... | collective-permute-start | bytes 61448 | tf_op jit(solution)/shard_map/ppermute | solution.py:698
  46.4 7.5 %collective-permute-done.4.three = f32[40,128]{1,0:T(8,128)S(1)} collective-permute-done((f32[40,128]{1,0:T(8,128)S(1)}, f32[40,128]{1,0:T(8,128)S(1)}, u32[]{:S(2)}, u32[]{:S(2)}) %collective-permute-start.4) | collective-permute-done | bytes 20512 | tf_op jit(solution)/shard_map/ppermute | solution.py:698
  53.9 0.9 scan.1
  54.8 4.5 %all-to-all-start.1 = ((bf16[32,32,128]{2,1,0:T(8,128)(2,1)}), bf16[32,32,128]{2,1,0:T(8,128)(2,1)S(1)}, u32[]{:S(2)}, u32[]{:S(2)}) async-start(bf16[32,32,128]{2,1,0:T(8,128)(2,1)} %bitcast.4), calls=%async_computation.1 | async-start | bytes 524288 | tf_op jit(solution)/shard_map/all_to_all | solution.py:704
  59.4 0.7 copy-done.3
  60.0 0.1 flip.1.refs_0_
  60.1 2.6 %collective-permute-start.7 = (bf16[1024,128]{1,0:T(8,128)(2,1)S(1)}, bf16[1024,128]{1,0:T(8,128)(2,1)S(1)}, u32[]{:S(2)}, u32[]{:S(2)}) collective-permute-start(bf16[1024,128]{1,0:T(8,128)(2,1)S(1)} %flip.1.refs_0_), channel_id=1, source_target_pairs={{0,24},{8,0},{16,8},{24,16},{1,25},{9,1},{17,9},{25,17},{2,26},{10... | collective-permute-start | bytes 786440 | tf_op jit(solution)/shard_map/ppermute | solution.py:703
  62.7 0.5 collective-permute-start.6
  63.2 0.6 collective-permute-start.5
  63.8 5.0 %all-to-all-done.1 = bf16[32,32,128]{2,1,0:T(8,128)(2,1)S(1)} async-done(((bf16[32,32,128]{2,1,0:T(8,128)(2,1)}), bf16[32,32,128]{2,1,0:T(8,128)(2,1)S(1)}, u32[]{:S(2)}, u32[]{:S(2)}) %all-to-all-start.1) | async-done | bytes 262176 | tf_op jit(solution)/shard_map/all_to_all | solution.py:704
  68.9 0.7 copy-done.6
  69.6 0.2 copy-done.7
  69.7 3.3 %join.1 = (bf16[128,1024]{1,0:T(8,128)(2,1)}, bf16[8,128,384]{2,1,0:T(8,128)(2,1)}) custom-call(f32[128,1024]{1,0:T(8,128)} %get-tuple-element.35.near_out, f32[128,1024]{1,0:T(8,128)} %get-tuple-element.36.dq_in, f32[2,128,1024]{2,1,0:T(8,128)} %get-tuple-element.37.own, bf16[2,128,1024]{2,1,0:T(8,128)(2,1)} %copy-done.7, ...), custom_call_target="tpu_custom_call" | custom-call | flops 134217728 | bytes 3145728 | tf_op jit(solution)/shard_map/join/pallas_call | solution.py:445
  73.0 5.1 %collective-permute-done.5.refs_1_ = bf16[1024,128]{1,0:T(8,128)(2,1)S(1)} collective-permute-done((bf16[1024,128]{1,0:T(8,128)(2,1)S(1)}, bf16[1024,128]{1,0:T(8,128)(2,1)S(1)}, u32[]{:S(2)}, u32[]{:S(2)}) %collective-permute-start.5) | collective-permute-done | bytes 262176 | tf_op jit(solution)/shard_map/ppermute | solution.py:703
  78.2 0.5 collective-permute-start.8
  78.7 3.5 %all-to-all-start.2 = ((bf16[8,128,384]{2,1,0:T(8,128)(2,1)}), bf16[8,128,384]{2,1,0:T(8,128)(2,1)S(1)}, u32[]{:S(2)}, u32[]{:S(2)}) async-start(bf16[8,128,384]{2,1,0:T(8,128)(2,1)} %get-tuple-element.42.delta.refs_4_), calls=%async_computation.2 | async-start | bytes 1572864 | tf_op jit(solution)/shard_map/all_to_all | solution.py:708
  82.2 5.5 %back.1.after = bf16[128,1024]{1,0:T(8,128)(2,1)} custom-call(bf16[8,128,384]{2,1,0:T(8,128)(2,1)} %get-tuple-element.42.delta.refs_4_, bf16[1024,1024]{1,0:T(8,128)(2,1)} %wq.3, bf16[1024,1024]{1,0:T(8,128)(2,1)} %wk.5, bf16[1024,1024]{1,0:T(8,128)(2,1)} %wv.5), custom_call_target="tpu_custom_call" | custom-call | flops 805306368 | bytes 7340032 | tf_op jit(solution)/shard_map/back/pallas_call | solution.py:498
  87.7 6.7 %all-to-all-done.2.delta = bf16[8,128,384]{2,1,0:T(8,128)(2,1)S(1)} async-done(((bf16[8,128,384]{2,1,0:T(8,128)(2,1)}), bf16[8,128,384]{2,1,0:T(8,128)(2,1)S(1)}, u32[]{:S(2)}, u32[]{:S(2)}) %all-to-all-start.2) | async-done | bytes 786464 | tf_op jit(solution)/shard_map/all_to_all | solution.py:708
  94.4 0.9 copy-done.4
  95.3 0.3 copy-done.5
  95.6 3.7 %outer.1 = bf16[1024,384]{1,0:T(8,128)(2,1)} custom-call(s32[1]{0:T(128)} %bitcast.6.core.side, s32[1]{0:T(128)} %bitcast.7.at_x, bf16[4,1024,128]{2,1,0:T(8,128)(2,1)} %copy-done, bf16[4,1024,128]{2,1,0:T(8,128)(2,1)} %copy-done.5, bf16[8,128,384]{2,1,0:T(8,128)(2,1)} %copy-done.4, bf16[128,1024]{1,0:T(8,128)(2,1)} %back.1.after), custom_call_target="tpu_custom_call" | custom-call | flops 805306368 | bytes 2883584 | tf_op jit(solution)/shard_map/outer/pallas_call | solution.py:528
  99.3 19.7 %all_to_all.25 = bf16[16,64,384]{2,1,0:T(8,128)(2,1)S(1)} all-to-all(bf16[16,64,384]{2,1,0:T(8,128)(2,1)} %bitcast.18), channel_id=1, replica_groups=mesh['yl'=2,'c'=2,'x'=4,'z'=4,'yh'=2] {'yl','z','yh'}, dimensions={0} | all-to-all | bytes 1572864 | tf_op jit(solution)/shard_map/all_to_all | solution.py:713
  119.2 13.5 %all_to_all.26 = bf16[16,64,384]{2,1,0:T(8,128)(2,1)S(1)} all-to-all(bf16[16,64,384]{2,1,0:T(8,128)(2,1)S(1)} %broadcast_in_dim.2), channel_id=1, replica_groups={{0,1,2,3,4,5,6,7,64,65,66,67,68,69,70,71},{8,9,10,11,12,13,14,15,72,73,..., dimensions={0} | all-to-all | bytes 1572864 | tf_op jit(solution)/shard_map/all_to_all | solution.py:663
  132.8 4.1 %collective-permute-start.11 = (bf16[8,128,384]{2,1,0:T(8,128)(2,1)S(1)}, bf16[8,128,384]{2,1,0:T(8,128)(2,1)S(1)}, u32[]{:S(2)}, u32[]{:S(2)}) collective-permute-start(bf16[8,128,384]{2,1,0:T(8,128)(2,1)S(1)} %bitcast.14), channel_id=1, source_target_pairs={{0,32},{32,0},{1,33},{33,1},{2,34},{34,2},{3,35},{35,3},{4,36},{36... | collective-permute-start | bytes 2359304 | tf_op jit(solution)/shard_map/ppermute | solution.py:660
  136.9 2.1 %collective-permute-start.10 = (bf16[8,128,384]{2,1,0:T(8,128)(2,1)S(1)}, bf16[8,128,384]{2,1,0:T(8,128)(2,1)S(1)}, u32[]{:S(2)}, u32[]{:S(2)}) collective-permute-start(bf16[8,128,384]{2,1,0:T(8,128)(2,1)S(1)} %bitcast.15), channel_id=1, source_target_pairs={{0,24},{32,38},{1,25},{33,39},{2,26},{34,32},{3,27},{35,33},{4,28}... | collective-permute-start | bytes 2359304 | tf_op jit(solution)/shard_map/ppermute | solution.py:573
  139.0 1.5 place.3
  140.5 7.5 %collective-permute-done.10.ahead = bf16[8,128,384]{2,1,0:T(8,128)(2,1)S(1)} collective-permute-done((bf16[8,128,384]{2,1,0:T(8,128)(2,1)S(1)}, bf16[8,128,384]{2,1,0:T(8,128)(2,1)S(1)}, u32[]{:S(2)}, u32[]{:S(2)}) %collective-permute-start.10) | collective-permute-done | bytes 786464 | tf_op jit(solution)/shard_map/ppermute | solution.py:573
  148.0 3.0 %collective-permute-done.9.behind = bf16[8,128,384]{2,1,0:T(8,128)(2,1)S(1)} collective-permute-done((bf16[8,128,384]{2,1,0:T(8,128)(2,1)S(1)}, bf16[8,128,384]{2,1,0:T(8,128)(2,1)S(1)}, u32[]{:S(2)}, u32[]{:S(2)}) %collective-permute-start.9) | collective-permute-done | bytes 786464 | tf_op jit(solution)/shard_map/ppermute | solution.py:573
  151.0 0.2 halves.1
  151.2 0.4 collective-permute-start.14
  151.7 0.6 collective-permute-start.12
  152.3 2.1 %collective-permute-start.13 = (bf16[4,128,384]{2,1,0:T(8,128)(2,1)S(1)}, bf16[4,128,384]{2,1,0:T(8,128)(2,1)S(1)}, u32[]{:S(2)}, u32[]{:S(2)}) collective-permute-start(bf16[4,128,384]{2,1,0:T(8,128)(2,1)S(1)} %get-tuple-element.45), channel_id=1, source_target_pairs={{0,24},{32,38},{1,25},{33,39},{2,26},{34,32},{3,27},{35,33},{4,28}... | collective-permute-start | bytes 1179656 | tf_op jit(solution)/shard_map/ppermute | solution.py:573
  154.3 0.4 collective-permute-done.14.other
  154.7 2.5 %place.4 = (bf16[1024,1024]{1,0:T(8,128)(2,1)}, bf16[1024,1024]{1,0:T(8,128)(2,1)}, bf16[1024,1024]{1,0:T(8,128)(2,1)}, f32[8,128]{1,0:T(8,128)S(1)}) custom-call(s32[1]{0:T(128)} %bitcast.6.core.side, s32[1]{0:T(128)} %bitcast.7.at_x, s32[1]{0:T(128)} %bitcast.8.at_z, ...), custom_call_target="tpu_custom_call", output_to_operand_aliasing={{0}: (5, {}), {1}: (6, {}), {2}: (7, {})} | custom-call | bytes 6291456 | tf_op jit(solution)/shard_map/place/pallas_call | solution.py:619
  157.2 2.6 %collective-permute-done.12.refs_0_ = bf16[4,128,384]{2,1,0:T(8,128)(2,1)S(1)} collective-permute-done((bf16[4,128,384]{2,1,0:T(8,128)(2,1)S(1)}, bf16[4,128,384]{2,1,0:T(8,128)(2,1)S(1)}, u32[]{:S(2)}, u32[]{:S(2)}) %collective-permute-start.12) | collective-permute-done | bytes 393248 | tf_op jit(solution)/shard_map/ppermute | solution.py:573
  159.9 1.1 collective-permute-start.15
  160.9 1.9 %collective-permute-done.15.other = bf16[8,128,384]{2,1,0:T(8,128)(2,1)S(1)} collective-permute-done((bf16[8,128,384]{2,1,0:T(8,128)(2,1)S(1)}, bf16[8,128,384]{2,1,0:T(8,128)(2,1)S(1)}, u32[]{:S(2)}, u32[]{:S(2)}) %collective-permute-start.15) | collective-permute-done | bytes 786464 | tf_op jit(solution)/shard_map/ppermute | solution.py:660
  162.9 2.1 %place.5 = (bf16[1024,1024]{1,0:T(8,128)(2,1)}, bf16[1024,1024]{1,0:T(8,128)(2,1)}, bf16[1024,1024]{1,0:T(8,128)(2,1)}, f32[8,128]{1,0:T(8,128)}) custom-call(s32[1]{0:T(128)} %bitcast.6.core.side, s32[1]{0:T(128)} %bitcast.7.at_x, s32[1]{0:T(128)} %bitcast.8.at_z, ...), custom_call_target="tpu_custom_call", output_to_operand_aliasing={{0}: (5, {}), {1}: (6, {}), {2}: (7, {})} | custom-call | bytes 3145728 | tf_op jit(solution)/shard_map/place/pallas_call | solution.py:619
  (28 shorter events, 0.5 us)
Async XLA Ops:
  0.6 19.8 %collective-permute-start = (bf16[128,1024]{1,0:T(8,128)(2,1)}, bf16[128,1024]{1,0:T(8,128)(2,1)S(1)}, u32[]{:S(2)}, u32[]{:S(2)}) collective-permute-start(bf16[128,1024]{1,0:T(8,128)(2,1)} %tok.3), channel_id=1, source_target_pairs={{0,1},{1,2},{2,3},{3,4},{4,5},{5,6},{6,7},{7,8},{8,9},{9,10},{10,1... | collective-permute-start | bytes 786440 | tf_op jit(solution)/shard_map/ppermute | solution.py:686
  11.8 30.3 %all-to-all-start = ((bf16[32,48,128]{2,1,0:T(8,128)(2,1)}), bf16[32,48,128]{2,1,0:T(8,128)(2,1)S(1)}, u32[]{:S(2)}, u32[]{:S(2)}) async-start(bf16[32,48,128]{2,1,0:T(8,128)(2,1)} %bitcast.20), calls=%async_computation | async-start | bytes 786432 | tf_op jit(solution)/shard_map/all_to_all | solution.py:688
  20.4 0.7 copy-start.8
  25.6 33.8 %copy-start.1 = (bf16[128,1024]{1,0:T(8,128)(2,1)S(1)}, bf16[128,1024]{1,0:T(8,128)(2,1)}, u32[]{:S(2)}) copy-start(bf16[128,1024]{1,0:T(8,128)(2,1)} %tok.3) | copy-start | bytes 786436
  31.8 37.1 %collective-permute-start.1 = (bf16[2,128,1024]{2,1,0:T(8,128)(2,1)}, bf16[2,128,1024]{2,1,0:T(8,128)(2,1)S(1)}, u32[]{:S(2)}, u32[]{:S(2)}) collective-permute-start(bf16[2,128,1024]{2,1,0:T(8,128)(2,1)} %get-tuple-element.38), channel_id=1, source_target_pairs={{1,0},{2,1},{3,2},{4,3},{5,4},{6,5},{7,6},{8,7},{9,8},{10,9},{11,1... | collective-permute-start | bytes 1572872 | tf_op jit(solution)/shard_map/ppermute | solution.py:693
  42.2 0.7 copy-start.2
  43.0 10.9 %collective-permute-start.4 = (f32[40,128]{1,0:T(8,128)S(1)}, f32[40,128]{1,0:T(8,128)S(1)}, u32[]{:S(2)}, u32[]{:S(2)}) collective-permute-start(f32[40,128]{1,0:T(8,128)S(1)} %group_total.1), channel_id=1, source_target_pairs={{0,96},{32,0},{64,32},{96,64},{1,97},{33,1},{65,33},{97,65},{2,98}... | collective-permute-start | bytes 61448 | tf_op jit(solution)/shard_map/ppermute | solution.py:698
  43.0 10.8 %collective-permute-start.3 = (f32[40,128]{1,0:T(8,128)S(1)}, f32[40,128]{1,0:T(8,128)S(1)}, u32[]{:S(2)}, u32[]{:S(2)}) collective-permute-start(f32[40,128]{1,0:T(8,128)S(1)} %group_total.1), channel_id=1, source_target_pairs={{0,64},{32,96},{64,0},{96,32},{1,65},{33,97},{65,1},{97,33},{2,66}... | collective-permute-start | bytes 61448 | tf_op jit(solution)/shard_map/ppermute | solution.py:698
  44.4 9.5 %collective-permute-start.2 = (f32[40,128]{1,0:T(8,128)S(1)}, f32[40,128]{1,0:T(8,128)S(1)}, u32[]{:S(2)}, u32[]{:S(2)}) collective-permute-start(f32[40,128]{1,0:T(8,128)S(1)} %group_total.1), channel_id=1, source_target_pairs={{0,32},{32,64},{64,96},{96,0},{1,33},{33,65},{65,97},{97,1},{2,34}... | collective-permute-start | bytes 61448 | tf_op jit(solution)/shard_map/ppermute | solution.py:698
  54.8 14.1 %all-to-all-start.1 = ((bf16[32,32,128]{2,1,0:T(8,128)(2,1)}), bf16[32,32,128]{2,1,0:T(8,128)(2,1)S(1)}, u32[]{:S(2)}, u32[]{:S(2)}) async-start(bf16[32,32,128]{2,1,0:T(8,128)(2,1)} %bitcast.4), calls=%async_computation.1 | async-start | bytes 524288 | tf_op jit(solution)/shard_map/all_to_all | solution.py:704
  59.3 0.7 copy-start.3
  60.1 12.9 %collective-permute-start.7 = (bf16[1024,128]{1,0:T(8,128)(2,1)S(1)}, bf16[1024,128]{1,0:T(8,128)(2,1)S(1)}, u32[]{:S(2)}, u32[]{:S(2)}) collective-permute-start(bf16[1024,128]{1,0:T(8,128)(2,1)S(1)} %flip.1.refs_0_), channel_id=1, source_target_pairs={{0,24},{8,0},{16,8},{24,16},{1,25},{9,1},{17,9},{25,17},{2,26},{10... | collective-permute-start | bytes 786440 | tf_op jit(solution)/shard_map/ppermute | solution.py:703
  62.7 10.3 %collective-permute-start.6 = (bf16[1024,128]{1,0:T(8,128)(2,1)S(1)}, bf16[1024,128]{1,0:T(8,128)(2,1)S(1)}, u32[]{:S(2)}, u32[]{:S(2)}) collective-permute-start(bf16[1024,128]{1,0:T(8,128)(2,1)S(1)} %flip.1.refs_0_), channel_id=1, source_target_pairs={{0,16},{8,24},{16,0},{24,8},{1,17},{9,25},{17,1},{25,9},{2,18},{10... | collective-permute-start | bytes 786440 | tf_op jit(solution)/shard_map/ppermute | solution.py:703
  63.2 14.9 %collective-permute-start.5 = (bf16[1024,128]{1,0:T(8,128)(2,1)S(1)}, bf16[1024,128]{1,0:T(8,128)(2,1)S(1)}, u32[]{:S(2)}, u32[]{:S(2)}) collective-permute-start(bf16[1024,128]{1,0:T(8,128)(2,1)S(1)} %flip.1.refs_0_), channel_id=1, source_target_pairs={{0,8},{8,16},{16,24},{24,0},{1,9},{9,17},{17,25},{25,1},{2,10},{10... | collective-permute-start | bytes 786440 | tf_op jit(solution)/shard_map/ppermute | solution.py:703
  68.9 0.7 copy-start.6
  68.9 0.9 copy-start.7
  78.2 9.6 %copy-start = (bf16[4,1024,128]{2,1,0:T(8,128)(2,1)}, bf16[4,1024,128]{2,1,0:T(8,128)(2,1)S(1)}, u32[]{:S(2)}) copy-start(bf16[4,1024,128]{2,1,0:T(8,128)(2,1)S(1)} %stack.2.mine) | copy-start | bytes 3145732
  78.2 16.2 %collective-permute-start.8 = (bf16[4,1024,128]{2,1,0:T(8,128)(2,1)S(1)}, bf16[4,1024,128]{2,1,0:T(8,128)(2,1)S(1)}, u32[]{:S(2)}, u32[]{:S(2)}) collective-permute-start(bf16[4,1024,128]{2,1,0:T(8,128)(2,1)S(1)} %stack.2.mine), channel_id=1, source_target_pairs={{0,32},{32,0},{1,33},{33,1},{2,34},{34,2},{3,35},{35,3},{4,36},{36... | collective-permute-start | bytes 3145736 | tf_op jit(solution)/shard_map/ppermute | solution.py:710
  78.7 15.7 %all-to-all-start.2 = ((bf16[8,128,384]{2,1,0:T(8,128)(2,1)}), bf16[8,128,384]{2,1,0:T(8,128)(2,1)S(1)}, u32[]{:S(2)}, u32[]{:S(2)}) async-start(bf16[8,128,384]{2,1,0:T(8,128)(2,1)} %get-tuple-element.42.delta.refs_4_), calls=%async_computation.2 | async-start | bytes 1572864 | tf_op jit(solution)/shard_map/all_to_all | solution.py:708
  94.4 0.9 copy-start.4
  94.4 1.2 copy-start.5
  132.8 6.2 %collective-permute-start.11 = (bf16[8,128,384]{2,1,0:T(8,128)(2,1)S(1)}, bf16[8,128,384]{2,1,0:T(8,128)(2,1)S(1)}, u32[]{:S(2)}, u32[]{:S(2)}) collective-permute-start(bf16[8,128,384]{2,1,0:T(8,128)(2,1)S(1)} %bitcast.14), channel_id=1, source_target_pairs={{0,32},{32,0},{1,33},{33,1},{2,34},{34,2},{3,35},{35,3},{4,36},{36... | collective-permute-start | bytes 2359304 | tf_op jit(solution)/shard_map/ppermute | solution.py:660
  136.9 11.1 %collective-permute-start.10 = (bf16[8,128,384]{2,1,0:T(8,128)(2,1)S(1)}, bf16[8,128,384]{2,1,0:T(8,128)(2,1)S(1)}, u32[]{:S(2)}, u32[]{:S(2)}) collective-permute-start(bf16[8,128,384]{2,1,0:T(8,128)(2,1)S(1)} %bitcast.15), channel_id=1, source_target_pairs={{0,24},{32,38},{1,25},{33,39},{2,26},{34,32},{3,27},{35,33},{4,28}... | collective-permute-start | bytes 2359304 | tf_op jit(solution)/shard_map/ppermute | solution.py:573
  139.0 12.1 %collective-permute-start.9 = (bf16[8,128,384]{2,1,0:T(8,128)(2,1)S(1)}, bf16[8,128,384]{2,1,0:T(8,128)(2,1)S(1)}, u32[]{:S(2)}, u32[]{:S(2)}) collective-permute-start(bf16[8,128,384]{2,1,0:T(8,128)(2,1)S(1)} %bitcast.16), channel_id=1, source_target_pairs={{0,8},{32,34},{1,9},{33,35},{2,10},{34,36},{3,11},{35,37},{4,12},{... | collective-permute-start | bytes 2359304 | tf_op jit(solution)/shard_map/ppermute | solution.py:573
  151.2 3.5 %collective-permute-start.14 = (bf16[16,128,384]{2,1,0:T(8,128)(2,1)S(1)}, bf16[16,128,384]{2,1,0:T(8,128)(2,1)S(1)}, u32[]{:S(2)}, u32[]{:S(2)}) collective-permute-start(bf16[16,128,384]{2,1,0:T(8,128)(2,1)S(1)} %get-tuple-element.46.own), channel_id=1, source_target_pairs={{0,32},{32,0},{1,33},{33,1},{2,34},{34,2},{3,35},{35,3},{4,36},{36... | collective-permute-start | bytes 4718600 | tf_op jit(solution)/shard_map/ppermute | solution.py:660
  151.7 8.1 %collective-permute-start.12 = (bf16[4,128,384]{2,1,0:T(8,128)(2,1)S(1)}, bf16[4,128,384]{2,1,0:T(8,128)(2,1)S(1)}, u32[]{:S(2)}, u32[]{:S(2)}) collective-permute-start(bf16[4,128,384]{2,1,0:T(8,128)(2,1)S(1)} %get-tuple-element.44), channel_id=1, source_target_pairs={{0,8},{32,34},{1,9},{33,35},{2,10},{34,36},{3,11},{35,37},{4,12},{... | collective-permute-start | bytes 1179656 | tf_op jit(solution)/shard_map/ppermute | solution.py:573
  152.3 7.5 %collective-permute-start.13 = (bf16[4,128,384]{2,1,0:T(8,128)(2,1)S(1)}, bf16[4,128,384]{2,1,0:T(8,128)(2,1)S(1)}, u32[]{:S(2)}, u32[]{:S(2)}) collective-permute-start(bf16[4,128,384]{2,1,0:T(8,128)(2,1)S(1)} %get-tuple-element.45), channel_id=1, source_target_pairs={{0,24},{32,38},{1,25},{33,39},{2,26},{34,32},{3,27},{35,33},{4,28}... | collective-permute-start | bytes 1179656 | tf_op jit(solution)/shard_map/ppermute | solution.py:573
  159.9 3.0 %collective-permute-start.15 = (bf16[8,128,384]{2,1,0:T(8,128)(2,1)S(1)}, bf16[8,128,384]{2,1,0:T(8,128)(2,1)S(1)}, u32[]{:S(2)}, u32[]{:S(2)}) collective-permute-start(bf16[8,128,384]{2,1,0:T(8,128)(2,1)S(1)} %bitcast.12), channel_id=1, source_target_pairs={{0,32},{32,0},{1,33},{33,1},{2,34},{34,2},{3,35},{35,3},{4,36},{36... | collective-permute-start | bytes 2359304 | tf_op jit(solution)/shard_map/ppermute | solution.py:660

commit v8 on v6

--- a/solution.py
+++ b/solution.py
@@ -54,7 +54,7 @@
     )
 
 
-def project_kernel(lin_scale, tok, wq, wk, wv, decay, cot, q_out, kv_out, run_out, runt_out, msg, held, sems):
+def project_kernel(lin_scale, tok, wq, wk, wv, decay, cot, q_out, kv_out, run_out, runt_out, msg, tok_out, held, sems):
     width = tok.shape[1]
     wide = held.shape[3]
     copies = []
@@ -66,6 +66,7 @@
             copy.start()
             copies.append(copy)
     x = tok[...]
+    tok_out[...] = x
     ld = decay[...]
     lower = (iota((SEG, SEG), 0) >= iota((SEG, SEG), 1)).astype(F32)
     runt = dot(lower, ld, 1, 1, HIGH)
@@ -124,13 +125,14 @@
     return pl.pallas_call(
         functools.partial(project_kernel, lin_scale),
         in_specs=[vmem, hbm, hbm, hbm, vmem, vmem],
-        out_specs=[vmem] * 5,
+        out_specs=[vmem] * 6,
         out_shape=[
             jax.ShapeDtypeStruct((rows, width), BF),
             jax.ShapeDtypeStruct((2, rows, width), BF),
             jax.ShapeDtypeStruct((chunks, heads // chunks, rows), F32),
             jax.ShapeDtypeStruct((chunks, rows, heads // chunks), F32),
             jax.ShapeDtypeStruct((2, width, PAIR), BF),
+            jax.ShapeDtypeStruct((rows, width), BF),
         ],
         scratch_shapes=[
             VMEM((3, width // wide, width, wide), BF),
@@ -347,8 +349,7 @@
     )(place, blocks, q, kv, pkv, cot, run, runt)
 
 
-def join_kernel(lin_scale, near_out, dq_in, own, nxt, q, kv, cot, runt, states, *rest):
-    layer, delta = rest[-2:]
+def join_kernel(lin_scale, near_out, dq_in, own, nxt, q, kv, cot, runt, states, layer, delta):
     head_of = iota((SEG, PAIR), 1) // DH
     diag = iota((PAIR, PAIR), 0) // DH == iota((PAIR, PAIR), 1) // DH
     zero = jnp.zeros((), BF)
@@ -387,7 +388,7 @@
         delta[pair, :, 2 * PAIR :] = dv.astype(BF)
 
 
-def join(near_out, dq, own, nxt, q, kv, cot, runt, states, after, lin_scale):
+def join(near_out, dq, own, nxt, q, kv, cot, runt, states, lin_scale):
     rows, width = q.shape
     pairs = width // PAIR
     wide = 2 * CHUNK
@@ -406,8 +407,7 @@
             col,
             pl.BlockSpec((2, rows, runt.shape[2]), lambda i: (i, 0, 0)),
             pl.BlockSpec((2, wide // PAIR, DH, PAIR), lambda i: (0, i, 0, 0)),
-        ]
-        + [pl.BlockSpec(memory_space=pl.ANY)] * len(after),
+        ],
         out_specs=[col, pl.BlockSpec((wide // PAIR, rows, 3 * PAIR), lambda i: (i, 0, 0))],
         out_shape=[
             jax.ShapeDtypeStruct((rows, width), BF),
@@ -416,11 +416,12 @@
         compiler_params=params(58),
         cost_estimate=cost(8 * rows * PAIR * PAIR * pairs, 24 * rows * width),
         name="join",
-    )(near_out, dq, own, nxt, q, kv, cot, runt, states, *after)
-
-
-def back_kernel(delta, wq, wk, wv, out, total):
+    )(near_out, dq, own, nxt, q, kv, cot, runt, states)
+
+
+def back_kernel(delta, wq, wk, wv, out, mark, total):
     step = pl.program_id(0)
+    mark[...] = jnp.zeros_like(mark)
 
     @pl.when(step == 0)
     def _():
@@ -450,8 +451,14 @@
         back_kernel,
         grid=(pairs // 2,),
         in_specs=[pl.BlockSpec((2, rows, 3 * PAIR), lambda i: (i, 0, 0)), weight, weight, weight],
-        out_specs=pl.BlockSpec((rows, width), lambda i: (0, 0)),
-        out_shape=jax.ShapeDtypeStruct((rows, width), BF),
+        out_specs=[
+            pl.BlockSpec((rows, width), lambda i: (0, 0)),
+            pl.BlockSpec((8, PAIR), lambda i: (0, 0)),
+        ],
+        out_shape=[
+            jax.ShapeDtypeStruct((rows, width), BF),
+            jax.ShapeDtypeStruct((8, PAIR), F32),
+        ],
         scratch_shapes=[VMEM((rows, width), F32)],
         compiler_params=params(58),
         cost_estimate=cost(6 * rows * width * width, 6 * width * width + 8 * rows * width),
@@ -489,7 +496,7 @@
         ],
         out_specs=pl.BlockSpec((width // 2, cols), lambda i: (i, 0)),
         out_shape=jax.ShapeDtypeStruct((width, cols), BF),
-        compiler_params=params(58),
+        compiler_params=params(20),
         cost_estimate=cost(
             2 * near_count * rows * cols * width, 2 * near_count * rows * (width + cols)
         ),
@@ -524,11 +531,11 @@
     return lax.ppermute(array, AX, route)
 
 
-def place_kernel(pieces, side, at_x, at_z, own, other, *refs):
+def place_kernel(pieces, count, side, at_x, at_z, *refs):
     grads, mark, sems = refs[-5:-2], refs[-2], refs[-1]
     mark[...] = jnp.zeros_like(mark)
 
-    def put(zero, one):
+    def put(rank):
         copies = []
 
         def start(src, dst):
@@ -536,49 +543,51 @@
             copy.start()
             copies.append(copy)
 
-        rows = zero.shape[1]
-        for place, by in enumerate(pieces):
-            x = lax.rem(at_x[0] + by + 4, 4)
-            z = lax.rem(at_z[0] + by + 4, 4)
-            for part, grad in enumerate(grads):
-                lanes = pl.ds(part * PAIR, PAIR)
-                for i in range(8):
-                    start(
-                        zero.at[place * 8 + i, :, lanes],
-                        grad.at[pl.ds(i * rows, rows), pl.ds(pl.multiple_of(x * PAIR, PAIR), PAIR)],
-                    )
-                    to = pl.multiple_of(((i % 2) * 4 + z) * rows, rows)
-                    start(
-                        one.at[place * 8 + i, :, lanes],
-                        grad.at[pl.ds(to, rows), pl.ds((4 + i // 2) * PAIR, PAIR)],
-                    )
+        for n in range(count):
+            source = refs[n]
+            rows = source.shape[1]
+            by_row = rank[n]
+            for place, by in enumerate(pieces):
+                x = lax.rem(at_x[0] + by + 4, 4)
+                z = lax.rem(at_z[0] + by + 4, 4)
+                for part, grad in enumerate(grads):
+                    lanes = pl.ds(part * PAIR, PAIR)
+                    for i in range(8):
+                        if by_row:
+                            to = pl.multiple_of(((i % 2) * 4 + z) * rows, rows)
+                            at = (pl.ds(to, rows), pl.ds((4 + i // 2) * PAIR, PAIR))
+                        else:
+                            to = pl.multiple_of(x * PAIR, PAIR)
+                            at = (pl.ds(i * rows, rows), pl.ds(to, PAIR))
+                        start(source.at[place * 8 + i, :, lanes], grad.at[at])
         for copy in copies:
             copy.wait()
 
     @pl.when(side[0] == 0)
     def _():
-        put(own, other)
+        put((False, True))
 
     @pl.when(side[0] == 1)
     def _():
-        put(other, own)
-
-
-def place_tiles(where, pieces, own, other, grads, width):
+        put((True, False))
+
+
+def place_tiles(where, pieces, sources, grads, width):
     hbm = pl.BlockSpec(memory_space=pl.ANY)
     smem = pl.BlockSpec(memory_space=pltpu.SMEM)
-    return pl.pallas_call(
-        functools.partial(place_kernel, pieces),
-        in_specs=[smem] * 3 + [hbm] * (2 + len(grads)),
+    first = 3 + len(sources)
+    return pl.pallas_call(
+        functools.partial(place_kernel, pieces, len(sources)),
+        in_specs=[smem] * 3 + [hbm] * (len(sources) + len(grads)),
         out_specs=[hbm] * 3 + [pl.BlockSpec(memory_space=VMEM)],
         out_shape=[jax.ShapeDtypeStruct((width, width), BF)] * 3
         + [jax.ShapeDtypeStruct((8, PAIR), F32)],
-        scratch_shapes=[pltpu.SemaphoreType.DMA((6 * own.shape[0],))],
-        input_output_aliases={5 + i: i for i in range(len(grads))},
+        scratch_shapes=[pltpu.SemaphoreType.DMA((24 * len(pieces) * len(sources),))],
+        input_output_aliases={first + i: i for i in range(len(grads))},
         compiler_params=params(16),
-        cost_estimate=cost(0, 8 * own.size),
+        cost_estimate=cost(0, 4 * sum(a.size for a in sources)),
         name="place",
-    )(*where, own, other, *grads)
+    )(*where, *sources, *grads)
 
 
 def halves_kernel(behind, ahead, after, first, second, both):
@@ -616,13 +625,16 @@
     ).reshape(8, 2 * rows, cols)
     behind = ring(here, 1)
     ahead = ring(here, -1)
-    *grads, mark = place_tiles(where, (0,), here, swapped(here), (), width)
+    *grads, mark = place_tiles(where, (0,), (here, swapped(here)), (), width)
     half_a, half_b, both = halves(behind, ahead, mark)
     far_a = ring(half_a, 1)
     far_b = ring(half_b, -1)
-    *grads, mark = place_tiles(where, (-1, 1), both, swapped(both), grads, width)
+    *grads, mark = place_tiles(where, (-1, 1), (both, swapped(both)), grads, width)
     far = stack([far_a, far_b], mark).reshape(here.shape)
-    *grads, _ = place_tiles(where, (2,), far, swapped(far), grads, width)
+    far_c = swapped(far)
+    *grads, _ = place_tiles(where, (2,), (far,), grads, width)
+    core, *rest = where
+    *grads, _ = place_tiles((1 - core, *rest), (2,), (far_c,), grads, width)
     return grads
 
 
@@ -634,8 +646,8 @@
 
     at_x = lax.axis_index("x").astype(jnp.int32).reshape(1)
     swap = [(0, 1), (1, 0)]
-    prev_tokens = lax.ppermute(tokens, AX, [(i, i + 1) for i in range(DEVS - 1)])
-    q, kv, run, runt, msg = project(tokens, wq, wk, wv, log_decay, cot, lin_scale)
+    q, kv, run, runt, msg, own_tokens = project(tokens, wq, wk, wv, log_decay, cot, lin_scale)
+    prev_tokens = lax.ppermute(own_tokens, AX, [(i, i + 1) for i in range(DEVS - 1)])
     got = lax.all_to_all(msg.reshape(DEVS, 16, PAIR), AX, 0, 0)
     pkv = prior(prev_tokens, wk, wv, runt)
     near_out, dq, own, prev, mark = near(
@@ -647,13 +659,13 @@
     around = [lax.ppermute(tokt, "x", [(i, (i + d) % 4) for i in range(4)]) for d in (1, 2, 3)]
     states = lax.all_to_all(states.reshape(DEVS, 8, PAIR), AX, 0, 0)
     states = states.reshape(2, width // PAIR, DH, PAIR)
-    layer, delta = join(near_out, dq, own, nxt, q, kv, cot, runt, states, [], lin_scale)
+    layer, delta = join(near_out, dq, own, nxt, q, kv, cot, runt, states, lin_scale)
 
     delta8 = lax.all_to_all(delta, NEAR8, 0, 0)
     mine = stack([tokt, *around], delta)
     theirs = lax.ppermute(mine, "c", swap)
-    tokens_grad = back(delta, wq, wk, wv)
-    partial = outer(core, at_x, mine, theirs, delta8, tokens_grad)
+    tokens_grad, mark = back(delta, wq, wk, wv)
+    partial = outer(core, at_x, mine, theirs, delta8, mark)
     parts = lax.all_to_all(partial.reshape(16, width // 16, 3 * PAIR), FAR16, 0, 0)
     grad_norm = 1.0 / math.sqrt(rows * DEVS)
     piece = (jnp.sum(parts.astype(F32), axis=0) * grad_norm).astype(BF)

time: 156 us -> 155 us (level)
  waiting for transfers between devices: 32.4 us -> 34.8 us
  starting transfers between devices: 50.2 us -> 48.6 us
    ppermute x1, waiting for transfers between devices: 0.01 us -> 2.69 us  [shards(): lax.ppermute(own_tokens, AX, [(i, i + 1) for i in range(DEVS - 1)])]
    all_to_all x1, starting transfers between devices: 7.64 us -> 4.95 us  [shards(): delta8 = lax.all_to_all(delta, NEAR8, 0, 0)]
    ppermute x1, starting transfers between devices: 10.1 us -> 7.43 us  [shards(): nxt = lax.ppermute(prev, AX, [(i + 1, i) for i in range(DEVS - 1)])]
    pallas_call x1, Pallas kernels: 3.67 us -> 1.61 us  [outer(): pl.pallas_call(outer_kernel, grid=(2,), in_specs=[smem, smem, tok, tok, p...]
    ppermute x3, waiting for transfers between devices: 3.92 us -> 5.83 us  [shards(): lax.ppermute(tokt, 'x', [(i, (i + d) % 4) for i in range(4)])]
    ppermute x3, starting transfers between devices: 5.37 us -> 7.16 us  [swapped(): return lax.ppermute(array, 'c', swap)]
    pallas_call x3 -> x4, Pallas kernels: 6.13 us -> 7.31 us  [place_tiles(): pl.pallas_call(functools.partial(place_kernel, pieces, len(sources)), in_...]
    unnamed x18 -> x14, local copies, waits for them, and re-layouts: 4.18 us -> 3.64 us
  transfers between devices with their start and end apart: 16 -> 16, of which waited for: 9 -> 10; matrix products, arithmetic and copies ran while one was open for 0% -> 0% of each run, Pallas kernels for 20% -> 17%
where the time goes in v8:
time: 155 us; the launch traced here: 154 us
  starting transfers between devices  48.6 us (31%)
  Pallas kernels  35.6 us (23%)
  waiting for transfers between devices  34.8 us (22%)
  blocking collectives  30.2 us (19%)
  local copies, waits for them, and re-layouts  3.74 us (2%)
    all_to_all x1, blocking collectives, shards(): lax.all_to_all(partial.reshape(16, width // 16, 3 * PAIR), FAR16, 0, 0)  16.6 us
    all_to_all x1, blocking collectives, gather_tiles(): lax.all_to_all(jnp.broadcast_to(piece[None], (16, rows, cols)), AX, 0, 0,...  13.6 us
    ppermute x4, waiting for transfers between devices, ring(): return lax.ppermute(array, AX, route)  12.8 us
    all_to_all x1, starting transfers between devices, shards(): got = lax.all_to_all(msg.reshape(DEVS, 16, PAIR), AX, 0, 0)  9.71 us
    ppermute x1, starting transfers between devices, shards(): nxt = lax.ppermute(prev, AX, [(i + 1, i) for i in range(DEVS - 1)])  7.43 us
    pallas_call x4, Pallas kernels, place_tiles(): pl.pallas_call(functools.partial(place_kernel, pieces, len(sources)), in_...  7.31 us
    ppermute x3, starting transfers between devices, swapped(): return lax.ppermute(array, 'c', swap)  7.16 us
    all_to_all x1, waiting for transfers between devices, shards(): delta8 = lax.all_to_all(delta, NEAR8, 0, 0)  6.66 us
  transfers between devices with their start and end apart: 16, of which 10 were waited for; matrix products, arithmetic and copies ran while one was open for 0% of the time, Pallas kernels for 17%

profile of v8, /device:TPU:1, one launch (start us, length us, event | category | flops | bytes accessed | tf_op | source)
XLA Modules:
  0.0 153.9 jit_solution(539568272155756137)
XLA Ops:
  0.6 5.6 %project.1 = (bf16[128,1024]{1,0:T(8,128)(2,1)}, bf16[2,128,1024]{2,1,0:T(8,128)(2,1)}, f32[4,4,128]{2,1,0:T(4,128)}, f32[4,128,4]{2,1,0:T(8,128)}, bf16[2,1024,...) custom-call(bf16[128,1024]{1,0:T(8,128)(2,1)} %tok.3, bf16[1024,1024]{1,0:T(8,128)(2,1)} %wq.3, bf16[1024,1024]{1,0:T(8,128)(2,1)} %wk.5, ...), custom_call_target="tpu_custom_call" | custom-call | flops 805306368 | bytes 7864320 | tf_op jit(solution)/shard_map/project/pallas_call | solution.py:125
  6.2 5.7 %collective-permute-start = (bf16[128,1024]{1,0:T(8,128)(2,1)}, bf16[128,1024]{1,0:T(8,128)(2,1)S(1)}, u32[]{:S(2)}, u32[]{:S(2)}) collective-permute-start(bf16[128,1024]{1,0:T(8,128)(2,1)} %get-tuple-element.39), channel_id=1, source_target_pairs={{0,1},{1,2},{2,3},{3,4},{4,5},{5,6},{6,7},{7,8},{8,9},{9,10},{10,1... | collective-permute-start | bytes 786440 | tf_op jit(solution)/shard_map/ppermute | solution.py:650
  11.9 9.7 %all-to-all-start = ((bf16[128,16,128]{2,1,0:T(8,128)(2,1)}), bf16[128,16,128]{2,1,0:T(8,128)(2,1)S(1)}, u32[]{:S(2)}, u32[]{:S(2)}) async-start(bf16[128,16,128]{2,1,0:T(8,128)(2,1)} %bitcast.18), calls=%async_computation | async-start | bytes 1048576 | tf_op jit(solution)/shard_map/all_to_all | solution.py:651
  21.6 2.7 %collective-permute-done.tok = bf16[128,1024]{1,0:T(8,128)(2,1)S(1)} collective-permute-done((bf16[128,1024]{1,0:T(8,128)(2,1)}, bf16[128,1024]{1,0:T(8,128)(2,1)S(1)}, u32[]{:S(2)}, u32[]{:S(2)}) %collective-permute-start) | collective-permute-done | bytes 262176 | tf_op jit(solution)/shard_map/ppermute | solution.py:650
  24.3 0.7 copy-done.6
  25.0 4.4 %prior.1.pkv = bf16[2,128,1024]{2,1,0:T(8,128)(2,1)} custom-call(bf16[128,1024]{1,0:T(8,128)(2,1)} %copy-done.6, bf16[1024,1024]{1,0:T(8,128)(2,1)} %wk.5, bf16[1024,1024]{1,0:T(8,128)(2,1)} %wv.5, f32[4,128,4]{2,1,0:T(8,128)} %get-tuple-element.40.after.runt), custom_call_target="tpu_custom_call" | custom-call | flops 536870912 | bytes 4980736 | tf_op jit(solution)/shard_map/prior/pallas_call | solution.py:163
  29.5 6.2 %near.1 = (f32[128,1024]{1,0:T(8,128)}, f32[128,1024]{1,0:T(8,128)}, f32[2,128,1024]{2,1,0:T(8,128)}, bf16[2,128,1024]{2,1,0:T(8,128)(2,1)}, f32[8,128]{1,0:T(8,128)}) custom-call(s32[1]{0:T(128)} %bitcast.place, s32[1,4]{1,0:T(1,128)} %blocks.1, bf16[128,1024]{1,0:T(8,128)(2,1)} %get-tuple-element.37.q_ref.q, bf16[2,128,1024]{2,1,0:T(8,128)(2,1)} %get-tuple-element.38.kv, ...), custom_call_target="tpu_custom_call" | custom-call | flops 4000000000 | bytes 16000000 | tf_op jit(solution)/shard_map/near/pallas_call | solution.py:325
  35.7 7.4 %collective-permute-start.1 = (bf16[2,128,1024]{2,1,0:T(8,128)(2,1)}, bf16[2,128,1024]{2,1,0:T(8,128)(2,1)S(1)}, u32[]{:S(2)}, u32[]{:S(2)}) collective-permute-start(bf16[2,128,1024]{2,1,0:T(8,128)(2,1)} %get-tuple-element.45), channel_id=1, source_target_pairs={{1,0},{2,1},{3,2},{4,3},{5,4},{6,5},{7,6},{8,7},{9,8},{10,9},{11,1... | collective-permute-start | bytes 1572872 | tf_op jit(solution)/shard_map/ppermute | solution.py:656
  43.1 0.7 copy-done.1
  43.8 1.2 scan.1
  45.0 3.5 %all-to-all-start.1 = ((bf16[128,8,128]{2,1,0:T(8,128)(2,1)}), bf16[128,8,128]{2,1,0:T(8,128)(2,1)S(1)}, u32[]{:S(2)}, u32[]{:S(2)}) async-start(bf16[128,8,128]{2,1,0:T(8,128)(2,1)} %bitcast.2), calls=%async_computation.1 | async-start | bytes 524288 | tf_op jit(solution)/shard_map/all_to_all | solution.py:660
  48.6 0.7 copy-done.2
  49.3 0.1 flip.1.refs_0_
  49.4 0.6 collective-permute-start.2
  50.0 2.4 %collective-permute-start.3 = (bf16[1024,128]{1,0:T(8,128)(2,1)S(1)}, bf16[1024,128]{1,0:T(8,128)(2,1)S(1)}, u32[]{:S(2)}, u32[]{:S(2)}) collective-permute-start(bf16[1024,128]{1,0:T(8,128)(2,1)S(1)} %flip.1.refs_0_), channel_id=1, source_target_pairs={{0,16},{8,24},{16,0},{24,8},{1,17},{9,25},{17,1},{25,9},{2,18},{10... | collective-permute-start | bytes 786440 | tf_op jit(solution)/shard_map/ppermute | solution.py:659
  52.4 1.2 collective-permute-start.4
  53.6 5.6 %all-to-all-done.1 = bf16[128,8,128]{2,1,0:T(8,128)(2,1)S(1)} async-done(((bf16[128,8,128]{2,1,0:T(8,128)(2,1)}), bf16[128,8,128]{2,1,0:T(8,128)(2,1)S(1)}, u32[]{:S(2)}, u32[]{:S(2)}) %all-to-all-start.1) | async-done | bytes 262176 | tf_op jit(solution)/shard_map/all_to_all | solution.py:660
  59.1 0.7 copy-done.4
  59.9 0.2 copy-done.5
  60.0 3.3 %join.1 = (bf16[128,1024]{1,0:T(8,128)(2,1)}, bf16[8,128,384]{2,1,0:T(8,128)(2,1)}) custom-call(f32[128,1024]{1,0:T(8,128)} %get-tuple-element.42.near_out, f32[128,1024]{1,0:T(8,128)} %get-tuple-element.43.dq_in, f32[2,128,1024]{2,1,0:T(8,128)} %get-tuple-element.44.own, bf16[2,128,1024]{2,1,0:T(8,128)(2,1)} %copy-done.5, ...), custom_call_target="tpu_custom_call" | custom-call | flops 134217728 | bytes 3145728 | tf_op jit(solution)/shard_map/join/pallas_call | solution.py:397
  63.3 1.5 collective-permute-done.3.refs_2_
  64.8 4.3 %collective-permute-done.4.refs_3_ = bf16[1024,128]{1,0:T(8,128)(2,1)S(1)} collective-permute-done((bf16[1024,128]{1,0:T(8,128)(2,1)S(1)}, bf16[1024,128]{1,0:T(8,128)(2,1)S(1)}, u32[]{:S(2)}, u32[]{:S(2)}) %collective-permute-start.4) | collective-permute-done | bytes 262176 | tf_op jit(solution)/shard_map/ppermute | solution.py:659
  69.2 1.3 collective-permute-start.5
  70.5 5.0 %all-to-all-start.2 = ((bf16[8,128,384]{2,1,0:T(8,128)(2,1)}), bf16[8,128,384]{2,1,0:T(8,128)(2,1)S(1)}, u32[]{:S(2)}, u32[]{:S(2)}) async-start(bf16[8,128,384]{2,1,0:T(8,128)(2,1)} %get-tuple-element.49.delta.refs_4_), calls=%async_computation.2 | async-start | bytes 1572864 | tf_op jit(solution)/shard_map/all_to_all | solution.py:664
  75.4 5.5 %back.1 = (bf16[128,1024]{1,0:T(8,128)(2,1)}, f32[8,128]{1,0:T(8,128)}) custom-call(bf16[8,128,384]{2,1,0:T(8,128)(2,1)} %get-tuple-element.49.delta.refs_4_, bf16[1024,1024]{1,0:T(8,128)(2,1)} %wq.3, bf16[1024,1024]{1,0:T(8,128)(2,1)} %wk.5, bf16[1024,1024]{1,0:T(8,128)(2,1)} %wv.5), custom_call_target="tpu_custom_call" | custom-call | flops 805306368 | bytes 7340032 | tf_op jit(solution)/shard_map/back/pallas_call | solution.py:450
  80.9 6.7 %all-to-all-done.2.delta = bf16[8,128,384]{2,1,0:T(8,128)(2,1)S(1)} async-done(((bf16[8,128,384]{2,1,0:T(8,128)(2,1)}), bf16[8,128,384]{2,1,0:T(8,128)(2,1)S(1)}, u32[]{:S(2)}, u32[]{:S(2)}) %all-to-all-start.2) | async-done | bytes 786464 | tf_op jit(solution)/shard_map/all_to_all | solution.py:664
  87.6 0.7 copy-done.3
  88.3 1.6 %outer.1 = bf16[1024,384]{1,0:T(8,128)(2,1)S(1)} custom-call(s32[1]{0:T(128)} %bitcast.4.core.side, s32[1]{0:T(128)} %bitcast.5.at_x, bf16[4,1024,128]{2,1,0:T(8,128)(2,1)S(1)} %stack.2.mine, bf16[4,1024,128]{2,1,0:T(8,128)(2,1)S(1)} %collective-permute-done.5.theirs, bf16[8,128,384]{2,1,0:T(8,128)(2,1)S(1)} %all-to-all-done.2.delta, f32[8,128]{1,0:T(8,128)S(1)} %copy-done.3), custom_call_target="tpu_custom_call" | custom-call | flops 805306368 | bytes 2883584 | tf_op jit(solution)/shard_map/outer/pallas_call | solution.py:486
  89.9 16.6 %all_to_all.25 = bf16[16,64,384]{2,1,0:T(8,128)(2,1)S(1)} all-to-all(bf16[16,64,384]{2,1,0:T(8,128)(2,1)S(1)} %bitcast.10), channel_id=1, replica_groups=mesh['yl'=2,'c'=2,'x'=4,'z'=4,'yh'=2] {'yl','z','yh'}, dimensions={0} | all-to-all | bytes 1572864 | tf_op jit(solution)/shard_map/all_to_all | solution.py:669
  106.5 0.1 convert_reduce_fusion
  106.7 0.1 broadcast_in_dim.2
  106.8 13.6 %all_to_all.26 = bf16[16,64,384]{2,1,0:T(8,128)(2,1)S(1)} all-to-all(bf16[16,64,384]{2,1,0:T(8,128)(2,1)S(1)} %broadcast_in_dim.2), channel_id=1, replica_groups={{0,1,2,3,4,5,6,7,64,65,66,67,68,69,70,71},{8,9,10,11,12,13,14,15,72,73,..., dimensions={0} | all-to-all | bytes 1572864 | tf_op jit(solution)/shard_map/all_to_all | solution.py:623
  120.3 4.1 %collective-permute-start.8 = (bf16[8,128,384]{2,1,0:T(8,128)(2,1)S(1)}, bf16[8,128,384]{2,1,0:T(8,128)(2,1)S(1)}, u32[]{:S(2)}, u32[]{:S(2)}) collective-permute-start(bf16[8,128,384]{2,1,0:T(8,128)(2,1)S(1)} %bitcast.11), channel_id=1, source_target_pairs={{0,32},{32,0},{1,33},{33,1},{2,34},{34,2},{3,35},{35,3},{4,36},{36... | collective-permute-start | bytes 2359304 | tf_op jit(solution)/shard_map/ppermute | solution.py:620
  124.4 0.4 collective-permute-start.6
  124.8 2.2 %collective-permute-start.7 = (bf16[8,128,384]{2,1,0:T(8,128)(2,1)S(1)}, bf16[8,128,384]{2,1,0:T(8,128)(2,1)S(1)}, u32[]{:S(2)}, u32[]{:S(2)}) collective-permute-start(bf16[8,128,384]{2,1,0:T(8,128)(2,1)S(1)} %bitcast.13), channel_id=1, source_target_pairs={{0,24},{32,38},{1,25},{33,39},{2,26},{34,32},{3,27},{35,33},{4,28}... | collective-permute-start | bytes 2359304 | tf_op jit(solution)/shard_map/ppermute | solution.py:531
  127.1 1.5 place.4
  128.6 8.1 %collective-permute-done.6.behind = bf16[8,128,384]{2,1,0:T(8,128)(2,1)S(1)} collective-permute-done((bf16[8,128,384]{2,1,0:T(8,128)(2,1)S(1)}, bf16[8,128,384]{2,1,0:T(8,128)(2,1)S(1)}, u32[]{:S(2)}, u32[]{:S(2)}) %collective-permute-start.6) | collective-permute-done | bytes 786464 | tf_op jit(solution)/shard_map/ppermute | solution.py:531
  136.7 0.2 halves.1
  137.0 0.9 collective-permute-start.11
  137.9 2.1 %collective-permute-start.10 = (bf16[4,128,384]{2,1,0:T(8,128)(2,1)S(1)}, bf16[4,128,384]{2,1,0:T(8,128)(2,1)S(1)}, u32[]{:S(2)}, u32[]{:S(2)}) collective-permute-start(bf16[4,128,384]{2,1,0:T(8,128)(2,1)S(1)} %get-tuple-element.54), channel_id=1, source_target_pairs={{0,24},{32,38},{1,25},{33,39},{2,26},{34,32},{3,27},{35,33},{4,28}... | collective-permute-start | bytes 1179656 | tf_op jit(solution)/shard_map/ppermute | solution.py:531
  140.0 0.9 collective-permute-done.11.refs_1_
  140.9 2.5 %place.5 = (bf16[1024,1024]{1,0:T(8,128)(2,1)}, bf16[1024,1024]{1,0:T(8,128)(2,1)}, bf16[1024,1024]{1,0:T(8,128)(2,1)}, f32[8,128]{1,0:T(8,128)S(1)}) custom-call(s32[1]{0:T(128)} %bitcast.4.core.side, s32[1]{0:T(128)} %bitcast.5.at_x, s32[1]{0:T(128)} %bitcast.6.at_z, ...), custom_call_target="tpu_custom_call", output_to_operand_aliasing={{0}: (5, {}), {1}: (6, {}), {2}: (7, {})} | custom-call | bytes 6291456 | tf_op jit(solution)/shard_map/place/pallas_call | solution.py:579
  143.4 1.4 collective-permute-done.10.refs_1_
  144.8 3.3 %collective-permute-done.9.refs_0_ = bf16[4,128,384]{2,1,0:T(8,128)(2,1)S(1)} collective-permute-done((bf16[4,128,384]{2,1,0:T(8,128)(2,1)S(1)}, bf16[4,128,384]{2,1,0:T(8,128)(2,1)S(1)}, u32[]{:S(2)}, u32[]{:S(2)}) %collective-permute-start.9) | collective-permute-done | bytes 393248 | tf_op jit(solution)/shard_map/ppermute | solution.py:531
  148.2 2.1 %collective-permute-start.12 = (bf16[8,128,384]{2,1,0:T(8,128)(2,1)S(1)}, bf16[8,128,384]{2,1,0:T(8,128)(2,1)S(1)}, u32[]{:S(2)}, u32[]{:S(2)}) collective-permute-start(bf16[8,128,384]{2,1,0:T(8,128)(2,1)S(1)} %bitcast.15), channel_id=1, source_target_pairs={{0,32},{32,0},{1,33},{33,1},{2,34},{34,2},{3,35},{35,3},{4,36},{36... | collective-permute-start | bytes 2359304 | tf_op jit(solution)/shard_map/ppermute | solution.py:620
  150.3 1.7 %place.6 = (bf16[1024,1024]{1,0:T(8,128)(2,1)}, bf16[1024,1024]{1,0:T(8,128)(2,1)}, bf16[1024,1024]{1,0:T(8,128)(2,1)}, f32[8,128]{1,0:T(8,128)}) custom-call(s32[1]{0:T(128)} %bitcast.4.core.side, s32[1]{0:T(128)} %bitcast.5.at_x, s32[1]{0:T(128)} %bitcast.6.at_z, ...), custom_call_target="tpu_custom_call", output_to_operand_aliasing={{0}: (4, {}), {1}: (5, {}), {2}: (6, {})} | custom-call | bytes 1572864 | tf_op jit(solution)/shard_map/place/pallas_call | solution.py:579
  152.0 0.3 collective-permute-done.12.refs_0_
  152.3 1.7 %place.7 = (bf16[1024,1024]{1,0:T(8,128)(2,1)}, bf16[1024,1024]{1,0:T(8,128)(2,1)}, bf16[1024,1024]{1,0:T(8,128)(2,1)}, f32[8,128]{1,0:T(8,128)}) custom-call(s32[1]{0:T(128)S(6)} %sub.3.side, s32[1]{0:T(128)} %bitcast.5.at_x, s32[1]{0:T(128)} %bitcast.6.at_z, ...), custom_call_target="tpu_custom_call", output_to_operand_aliasing={{0}: (4, {}), {1}: (5, {}), {2}: (6, {})} | custom-call | bytes 1572864 | tf_op jit(solution)/shard_map/place/pallas_call | solution.py:579
  (18 shorter events, 0.2 us)
Async XLA Ops:
  6.2 18.1 %collective-permute-start = (bf16[128,1024]{1,0:T(8,128)(2,1)}, bf16[128,1024]{1,0:T(8,128)(2,1)S(1)}, u32[]{:S(2)}, u32[]{:S(2)}) collective-permute-start(bf16[128,1024]{1,0:T(8,128)(2,1)} %get-tuple-element.39), channel_id=1, source_target_pairs={{0,1},{1,2},{2,3},{3,4},{4,5},{5,6},{6,7},{7,8},{8,9},{9,10},{10,1... | collective-permute-start | bytes 786440 | tf_op jit(solution)/shard_map/ppermute | solution.py:650
  11.9 31.3 %all-to-all-start = ((bf16[128,16,128]{2,1,0:T(8,128)(2,1)}), bf16[128,16,128]{2,1,0:T(8,128)(2,1)S(1)}, u32[]{:S(2)}, u32[]{:S(2)}) async-start(bf16[128,16,128]{2,1,0:T(8,128)(2,1)} %bitcast.18), calls=%async_computation | async-start | bytes 1048576 | tf_op jit(solution)/shard_map/all_to_all | solution.py:651
  24.3 0.7 copy-start.6
  29.4 19.2 %copy-start = (bf16[128,1024]{1,0:T(8,128)(2,1)S(1)}, bf16[128,1024]{1,0:T(8,128)(2,1)}, u32[]{:S(2)}) copy-start(bf16[128,1024]{1,0:T(8,128)(2,1)} %tok.3) | copy-start | bytes 786436
  35.7 23.5 %collective-permute-start.1 = (bf16[2,128,1024]{2,1,0:T(8,128)(2,1)}, bf16[2,128,1024]{2,1,0:T(8,128)(2,1)S(1)}, u32[]{:S(2)}, u32[]{:S(2)}) collective-permute-start(bf16[2,128,1024]{2,1,0:T(8,128)(2,1)} %get-tuple-element.45), channel_id=1, source_target_pairs={{1,0},{2,1},{3,2},{4,3},{5,4},{6,5},{7,6},{8,7},{9,8},{10,9},{11,1... | collective-permute-start | bytes 1572872 | tf_op jit(solution)/shard_map/ppermute | solution.py:656
  43.1 0.7 copy-start.1
  45.0 14.1 %all-to-all-start.1 = ((bf16[128,8,128]{2,1,0:T(8,128)(2,1)}), bf16[128,8,128]{2,1,0:T(8,128)(2,1)S(1)}, u32[]{:S(2)}, u32[]{:S(2)}) async-start(bf16[128,8,128]{2,1,0:T(8,128)(2,1)} %bitcast.2), calls=%async_computation.1 | async-start | bytes 524288 | tf_op jit(solution)/shard_map/all_to_all | solution.py:660
  48.6 0.7 copy-start.2
  49.4 13.9 %collective-permute-start.2 = (bf16[1024,128]{1,0:T(8,128)(2,1)S(1)}, bf16[1024,128]{1,0:T(8,128)(2,1)S(1)}, u32[]{:S(2)}, u32[]{:S(2)}) collective-permute-start(bf16[1024,128]{1,0:T(8,128)(2,1)S(1)} %flip.1.refs_0_), channel_id=1, source_target_pairs={{0,8},{8,16},{16,24},{24,0},{1,9},{9,17},{17,25},{25,1},{2,10},{10... | collective-permute-start | bytes 786440 | tf_op jit(solution)/shard_map/ppermute | solution.py:659
  50.0 14.8 %collective-permute-start.3 = (bf16[1024,128]{1,0:T(8,128)(2,1)S(1)}, bf16[1024,128]{1,0:T(8,128)(2,1)S(1)}, u32[]{:S(2)}, u32[]{:S(2)}) collective-permute-start(bf16[1024,128]{1,0:T(8,128)(2,1)S(1)} %flip.1.refs_0_), channel_id=1, source_target_pairs={{0,16},{8,24},{16,0},{24,8},{1,17},{9,25},{17,1},{25,9},{2,18},{10... | collective-permute-start | bytes 786440 | tf_op jit(solution)/shard_map/ppermute | solution.py:659
  52.4 16.8 %collective-permute-start.4 = (bf16[1024,128]{1,0:T(8,128)(2,1)S(1)}, bf16[1024,128]{1,0:T(8,128)(2,1)S(1)}, u32[]{:S(2)}, u32[]{:S(2)}) collective-permute-start(bf16[1024,128]{1,0:T(8,128)(2,1)S(1)} %flip.1.refs_0_), channel_id=1, source_target_pairs={{0,24},{8,0},{16,8},{24,16},{1,25},{9,1},{17,9},{25,17},{2,26},{10... | collective-permute-start | bytes 786440 | tf_op jit(solution)/shard_map/ppermute | solution.py:659
  59.1 0.7 copy-start.4
  59.1 0.9 copy-start.5
  69.2 18.4 %collective-permute-start.5 = (bf16[4,1024,128]{2,1,0:T(8,128)(2,1)S(1)}, bf16[4,1024,128]{2,1,0:T(8,128)(2,1)S(1)}, u32[]{:S(2)}, u32[]{:S(2)}) collective-permute-start(bf16[4,1024,128]{2,1,0:T(8,128)(2,1)S(1)} %stack.2.mine), channel_id=1, source_target_pairs={{0,32},{32,0},{1,33},{33,1},{2,34},{34,2},{3,35},{35,3},{4,36},{36... | collective-permute-start | bytes 3145736 | tf_op jit(solution)/shard_map/ppermute | solution.py:666
  70.5 17.1 %all-to-all-start.2 = ((bf16[8,128,384]{2,1,0:T(8,128)(2,1)}), bf16[8,128,384]{2,1,0:T(8,128)(2,1)S(1)}, u32[]{:S(2)}, u32[]{:S(2)}) async-start(bf16[8,128,384]{2,1,0:T(8,128)(2,1)} %get-tuple-element.49.delta.refs_4_), calls=%async_computation.2 | async-start | bytes 1572864 | tf_op jit(solution)/shard_map/all_to_all | solution.py:664
  87.6 0.7 copy-start.3
  120.3 6.8 %collective-permute-start.8 = (bf16[8,128,384]{2,1,0:T(8,128)(2,1)S(1)}, bf16[8,128,384]{2,1,0:T(8,128)(2,1)S(1)}, u32[]{:S(2)}, u32[]{:S(2)}) collective-permute-start(bf16[8,128,384]{2,1,0:T(8,128)(2,1)S(1)} %bitcast.11), channel_id=1, source_target_pairs={{0,32},{32,0},{1,33},{33,1},{2,34},{34,2},{3,35},{35,3},{4,36},{36... | collective-permute-start | bytes 2359304 | tf_op jit(solution)/shard_map/ppermute | solution.py:620
  124.4 12.3 %collective-permute-start.6 = (bf16[8,128,384]{2,1,0:T(8,128)(2,1)S(1)}, bf16[8,128,384]{2,1,0:T(8,128)(2,1)S(1)}, u32[]{:S(2)}, u32[]{:S(2)}) collective-permute-start(bf16[8,128,384]{2,1,0:T(8,128)(2,1)S(1)} %bitcast.12), channel_id=1, source_target_pairs={{0,8},{32,34},{1,9},{33,35},{2,10},{34,36},{3,11},{35,37},{4,12},{... | collective-permute-start | bytes 2359304 | tf_op jit(solution)/shard_map/ppermute | solution.py:531
  124.8 11.9 %collective-permute-start.7 = (bf16[8,128,384]{2,1,0:T(8,128)(2,1)S(1)}, bf16[8,128,384]{2,1,0:T(8,128)(2,1)S(1)}, u32[]{:S(2)}, u32[]{:S(2)}) collective-permute-start(bf16[8,128,384]{2,1,0:T(8,128)(2,1)S(1)} %bitcast.13), channel_id=1, source_target_pairs={{0,24},{32,38},{1,25},{33,39},{2,26},{34,32},{3,27},{35,33},{4,28}... | collective-permute-start | bytes 2359304 | tf_op jit(solution)/shard_map/ppermute | solution.py:531
  137.0 4.0 %collective-permute-start.11 = (bf16[16,128,384]{2,1,0:T(8,128)(2,1)S(1)}, bf16[16,128,384]{2,1,0:T(8,128)(2,1)S(1)}, u32[]{:S(2)}, u32[]{:S(2)}) collective-permute-start(bf16[16,128,384]{2,1,0:T(8,128)(2,1)S(1)} %get-tuple-element.55.refs_0_), channel_id=1, source_target_pairs={{0,32},{32,0},{1,33},{33,1},{2,34},{34,2},{3,35},{35,3},{4,36},{36... | collective-permute-start | bytes 4718600 | tf_op jit(solution)/shard_map/ppermute | solution.py:620
  137.9 6.9 %collective-permute-start.10 = (bf16[4,128,384]{2,1,0:T(8,128)(2,1)S(1)}, bf16[4,128,384]{2,1,0:T(8,128)(2,1)S(1)}, u32[]{:S(2)}, u32[]{:S(2)}) collective-permute-start(bf16[4,128,384]{2,1,0:T(8,128)(2,1)S(1)} %get-tuple-element.54), channel_id=1, source_target_pairs={{0,24},{32,38},{1,25},{33,39},{2,26},{34,32},{3,27},{35,33},{4,28}... | collective-permute-start | bytes 1179656 | tf_op jit(solution)/shard_map/ppermute | solution.py:531
  140.0 8.1 %collective-permute-start.9 = (bf16[4,128,384]{2,1,0:T(8,128)(2,1)S(1)}, bf16[4,128,384]{2,1,0:T(8,128)(2,1)S(1)}, u32[]{:S(2)}, u32[]{:S(2)}) collective-permute-start(bf16[4,128,384]{2,1,0:T(8,128)(2,1)S(1)} %get-tuple-element.53), channel_id=1, source_target_pairs={{0,8},{32,34},{1,9},{33,35},{2,10},{34,36},{3,11},{35,37},{4,12},{... | collective-permute-start | bytes 1179656 | tf_op jit(solution)/shard_map/ppermute | solution.py:531
  148.2 4.1 %collective-permute-start.12 = (bf16[8,128,384]{2,1,0:T(8,128)(2,1)S(1)}, bf16[8,128,384]{2,1,0:T(8,128)(2,1)S(1)}, u32[]{:S(2)}, u32[]{:S(2)}) collective-permute-start(bf16[8,128,384]{2,1,0:T(8,128)(2,1)S(1)} %bitcast.15), channel_id=1, source_target_pairs={{0,32},{32,0},{1,33},{33,1},{2,34},{34,2},{3,35},{35,3},{4,36},{36... | collective-permute-start | bytes 2359304 | tf_op jit(solution)/shard_map/ppermute | solution.py:620

commit v9 on v8

--- a/solution.py
+++ b/solution.py
@@ -144,53 +144,27 @@
     )(tokens, wq, wk, wv, log_decay, cot)
 
 
-def prior_kernel(tok, wk, wv, after, out, held, sems):
-    del after
-    copies = [
-        pltpu.make_async_copy(w, held.at[part], sems.at[part]) for part, w in enumerate((wk, wv))
-    ]
-    for copy in copies:
-        copy.start()
-    for part in range(2):
-        copies[part].wait()
-        out[part] = dot(tok[...], held[part], 1, 0).astype(BF)
-
-
-def prior(tokens, wk, wv, after):
+def flip_kernel(tag, tok, out, tag_out):
+    tag_out[0] = tag[0]
+    out[...] = tok[...].T
+
+
+def flip(tag, tokens):
     rows, width = tokens.shape
-    vmem = pl.BlockSpec(memory_space=VMEM)
-    hbm = pl.BlockSpec(memory_space=pltpu.HBM)
-    return pl.pallas_call(
-        prior_kernel,
-        in_specs=[vmem, hbm, hbm, hbm],
-        out_specs=vmem,
-        out_shape=jax.ShapeDtypeStruct((2, rows, width), BF),
-        scratch_shapes=[
-            VMEM((2, width, width), BF),
-            pltpu.SemaphoreType.DMA((2,)),
-        ],
-        compiler_params=params(58),
-        cost_estimate=cost(4 * rows * width * width, 4 * width * width + 6 * rows * width),
-        name="prior",
-    )(tokens, wk, wv, after)
-
-
-def flip_kernel(tok, after, out):
-    del after
-    out[...] = tok[...].T
-
-
-def flip(tokens, after):
-    rows, width = tokens.shape
+    whole = pl.BlockSpec(memory_space=VMEM)
+    smem = pl.BlockSpec(memory_space=pltpu.SMEM)
     return pl.pallas_call(
         flip_kernel,
-        in_specs=[pl.BlockSpec(memory_space=VMEM), pl.BlockSpec(memory_space=pl.ANY)],
-        out_specs=pl.BlockSpec(memory_space=VMEM),
-        out_shape=jax.ShapeDtypeStruct((width, rows), BF),
+        in_specs=[smem, whole],
+        out_specs=[whole, smem],
+        out_shape=[
+            jax.ShapeDtypeStruct((width, rows), BF),
+            jax.ShapeDtypeStruct((1,), jnp.int32),
+        ],
         compiler_params=params(16),
         cost_estimate=cost(0, 4 * rows * width),
         name="flip",
-    )(tokens, after)
+    )(tag, tokens)
 
 
 def stack_kernel(*refs):
@@ -213,8 +187,7 @@
     )(*parts, after)
 
 
-def scan_kernel(place, got, after, out, xs, decays, states):
-    del after
+def scan_kernel(place, got, out, xs, decays, states):
     both = got[...].astype(F32)
     xs[...] = both[:, :8, :]
     total = both[:, 8:9, :] + both[:, 9:10, :] + both[:, 10:11, :]
@@ -230,26 +203,22 @@
     out[...] = states[...].reshape(DEVS * 8, PAIR).astype(BF)
 
 
-def scan(place, got, after):
+def scan(place, got):
     whole = pl.BlockSpec(memory_space=VMEM)
     return pl.pallas_call(
         scan_kernel,
-        in_specs=[
-            pl.BlockSpec(memory_space=pltpu.SMEM),
-            whole,
-            pl.BlockSpec(memory_space=pl.ANY),
-        ],
+        in_specs=[pl.BlockSpec(memory_space=pltpu.SMEM), whole],
         out_specs=whole,
         out_shape=jax.ShapeDtypeStruct((DEVS * 8, PAIR), BF),
         scratch_shapes=[VMEM((DEVS, 8, PAIR), F32)] * 3,
         compiler_params=params(24),
         cost_estimate=cost(2 * DEVS * 8 * PAIR, 4 * DEVS * 16 * PAIR),
         name="scan",
-    )(place, got, after)
-
-
-def near_kernel(lin_scale, place, blocks, q_ref, kv, pkv, cot, run, runt, out, dq_out, own, prev, mark):
-    mark[...] = jnp.zeros_like(mark)
+    )(place, got)
+
+
+def near_kernel(lin_scale, place, blocks, q_ref, kv, ptok, wk, wv, cot, run, runt, out, dq_out, own, prev, tag_out):
+    tag_out[0] = place[0]
     soft_scale = 1.0 / math.sqrt(DH)
     n_own = jnp.int32(0)
     n_prev = jnp.int32(0)
@@ -264,14 +233,16 @@
     head_of2 = iota((2 * SEG, PAIR), 1) // DH
     lower = iota((SEG, SEG), 0) >= iota((SEG, SEG), 1)
     zero = jnp.zeros((), BF)
+    pk = dot(ptok[...], wk[...], 1, 0).astype(BF)
+    pv = dot(ptok[...], wv[...], 1, 0).astype(BF)
     pairs = q_ref.shape[1] // PAIR
     work = []
     for pair in range(pairs):
         at = slice(pair * PAIR, (pair + 1) * PAIR)
         q = q_ref[:, at]
         g = cot[:, at]
-        kk = jnp.concatenate([kv[0, :, at], pkv[0, :, at]], axis=0)
-        vv = jnp.concatenate([kv[1, :, at], pkv[1, :, at]], axis=0)
+        kk = jnp.concatenate([kv[0, :, at], pk[:, at]], axis=0)
+        vv = jnp.concatenate([kv[1, :, at], pv[:, at]], axis=0)
         for i in range(2):
             mine = head_of == i
             work.append(
@@ -299,8 +270,8 @@
         at = slice(pair * PAIR, (pair + 1) * PAIR)
         q = q_ref[:, at]
         g = cot[:, at]
-        kk = jnp.concatenate([kv[0, :, at], pkv[0, :, at]], axis=0)
-        vv = jnp.concatenate([kv[1, :, at], pkv[1, :, at]], axis=0)
+        kk = jnp.concatenate([kv[0, :, at], pk[:, at]], axis=0)
+        vv = jnp.concatenate([kv[1, :, at], pv[:, at]], axis=0)
         qt = q.T
         gt = g.T
         res = []
@@ -316,12 +287,13 @@
             prev[part, :, at] = sums[SEG:].astype(BF)
 
 
-def near(place, blocks, q, kv, pkv, cot, run, runt, lin_scale):
+def near(place, blocks, q, kv, prev_tokens, wk, wv, cot, run, runt, lin_scale):
     rows, width = q.shape
     heads = run.shape[1]
     smem = pl.BlockSpec(memory_space=pltpu.SMEM)
     col = pl.BlockSpec((rows, CHUNK), lambda i: (0, i))
     two = pl.BlockSpec((2, rows, CHUNK), lambda i: (0, 0, i))
+    weight = pl.BlockSpec((width, CHUNK), lambda i: (0, i))
     return pl.pallas_call(
         functools.partial(near_kernel, lin_scale),
         grid=(width // CHUNK,),
@@ -330,23 +302,25 @@
             smem,
             col,
             two,
-            two,
+            pl.BlockSpec((rows, width), lambda i: (0, 0)),
+            weight,
+            weight,
             col,
             pl.BlockSpec((1, heads, rows), lambda i: (i, 0, 0)),
             pl.BlockSpec((1, rows, heads), lambda i: (i, 0, 0)),
         ],
-        out_specs=[col, col, two, two, pl.BlockSpec((8, PAIR), lambda i: (0, 0))],
+        out_specs=[col, col, two, two, smem],
         out_shape=[
             jax.ShapeDtypeStruct((rows, width), F32),
             jax.ShapeDtypeStruct((rows, width), F32),
             jax.ShapeDtypeStruct((2, rows, width), F32),
             jax.ShapeDtypeStruct((2, rows, width), BF),
-            jax.ShapeDtypeStruct((8, PAIR), F32),
+            jax.ShapeDtypeStruct((1,), jnp.int32),
         ],
         compiler_params=params(58),
         cost_estimate=cost(4000 * 1000 * 1000, 16 * 1000 * 1000, 1000 * 1000),
         name="near",
-    )(place, blocks, q, kv, pkv, cot, run, runt)
+    )(place, blocks, q, kv, prev_tokens, wk, wv, cot, run, runt)
 
 
 def join_kernel(lin_scale, near_out, dq_in, own, nxt, q, kv, cot, runt, states, layer, delta):
@@ -419,9 +393,9 @@
     )(near_out, dq, own, nxt, q, kv, cot, runt, states)
 
 
-def back_kernel(delta, wq, wk, wv, out, mark, total):
+def back_kernel(tag, delta, wq, wk, wv, out, tag_out, total):
     step = pl.program_id(0)
-    mark[...] = jnp.zeros_like(mark)
+    tag_out[0] = tag[0]
 
     @pl.when(step == 0)
     def _():
@@ -443,31 +417,31 @@
         out[...] = acc.astype(BF)
 
 
-def back(delta, wq, wk, wv):
+def back(tag, delta, wq, wk, wv):
     pairs, rows, _ = delta.shape
     width = wq.shape[0]
+    smem = pl.BlockSpec(memory_space=pltpu.SMEM)
     weight = pl.BlockSpec((width, 2 * PAIR), lambda i: (0, i))
     return pl.pallas_call(
         back_kernel,
         grid=(pairs // 2,),
-        in_specs=[pl.BlockSpec((2, rows, 3 * PAIR), lambda i: (i, 0, 0)), weight, weight, weight],
+        in_specs=[smem, pl.BlockSpec((2, rows, 3 * PAIR), lambda i: (i, 0, 0)), weight, weight, weight],
         out_specs=[
             pl.BlockSpec((rows, width), lambda i: (0, 0)),
-            pl.BlockSpec((8, PAIR), lambda i: (0, 0)),
+            smem,
         ],
         out_shape=[
             jax.ShapeDtypeStruct((rows, width), BF),
-            jax.ShapeDtypeStruct((8, PAIR), F32),
+            jax.ShapeDtypeStruct((1,), jnp.int32),
         ],
         scratch_shapes=[VMEM((rows, width), F32)],
         compiler_params=params(58),
         cost_estimate=cost(6 * rows * width * width, 6 * width * width + 8 * rows * width),
         name="back",
-    )(delta, wq, wk, wv)
-
-
-def outer_kernel(core, at_x, mine, theirs, delta, after, out):
-    del after
+    )(tag, delta, wq, wk, wv)
+
+
+def outer_kernel(core, at_x, mine, theirs, delta, out):
     near_x = mine.shape[0]
     left, right = [], []
     for tokt, c in ((mine, core[0]), (theirs, 1 - core[0])):
@@ -478,7 +452,7 @@
     out[...] = dot(left, jnp.concatenate(right, axis=0), 1, 0).astype(BF)
 
 
-def outer(core, at_x, mine, theirs, delta, after):
+def outer(core, at_x, mine, theirs, delta):
     near_count, rows, cols = delta.shape
     width = mine.shape[1]
     smem = pl.BlockSpec(memory_space=pltpu.SMEM)
@@ -492,7 +466,6 @@
             tok,
             tok,
             pl.BlockSpec((near_count, rows, cols), lambda i: (0, 0, 0)),
-            pl.BlockSpec(memory_space=pl.ANY),
         ],
         out_specs=pl.BlockSpec((width // 2, cols), lambda i: (i, 0)),
         out_shape=jax.ShapeDtypeStruct((width, cols), BF),
@@ -501,7 +474,7 @@
             2 * near_count * rows * cols * width, 2 * near_count * rows * (width + cols)
         ),
         name="outer",
-    )(core, at_x, mine, theirs, delta, after)
+    )(core, at_x, mine, theirs, delta)
 
 
 def device(yl, c, x, z, yh):
@@ -649,13 +622,12 @@
     q, kv, run, runt, msg, own_tokens = project(tokens, wq, wk, wv, log_decay, cot, lin_scale)
     prev_tokens = lax.ppermute(own_tokens, AX, [(i, i + 1) for i in range(DEVS - 1)])
     got = lax.all_to_all(msg.reshape(DEVS, 16, PAIR), AX, 0, 0)
-    pkv = prior(prev_tokens, wk, wv, runt)
-    near_out, dq, own, prev, mark = near(
-        place, neighbour_blocks, q, kv, pkv, cot, run, runt, lin_scale
+    near_out, dq, own, prev, place = near(
+        place, neighbour_blocks, q, kv, prev_tokens, wk, wv, cot, run, runt, lin_scale
     )
     nxt = lax.ppermute(prev, AX, [(i + 1, i) for i in range(DEVS - 1)])
-    states = scan(place, got, mark)
-    tokt = flip(tokens, mark)
+    states = scan(place, got)
+    tokt, _ = flip(place, own_tokens)
     around = [lax.ppermute(tokt, "x", [(i, (i + d) % 4) for i in range(4)]) for d in (1, 2, 3)]
     states = lax.all_to_all(states.reshape(DEVS, 8, PAIR), AX, 0, 0)
     states = states.reshape(2, width // PAIR, DH, PAIR)
@@ -664,8 +636,8 @@
     delta8 = lax.all_to_all(delta, NEAR8, 0, 0)
     mine = stack([tokt, *around], delta)
     theirs = lax.ppermute(mine, "c", swap)
-    tokens_grad, mark = back(delta, wq, wk, wv)
-    partial = outer(core, at_x, mine, theirs, delta8, mark)
+    tokens_grad, later_core = back(core, delta, wq, wk, wv)
+    partial = outer(later_core, at_x, mine, theirs, delta8)
     parts = lax.all_to_all(partial.reshape(16, width // 16, 3 * PAIR), FAR16, 0, 0)
     grad_norm = 1.0 / math.sqrt(rows * DEVS)
     piece = (jnp.sum(parts.astype(F32), axis=0) * grad_norm).astype(BF)

time: 155 us -> 152 us (0.981)
  local copies, waits for them, and re-layouts: 3.74 us -> 1.72 us
    pallas_call x3 -> x2, Pallas kernels: 10.1 us -> 6.79 us  [the longest x1 5.57 us: back(): pl.pallas_call(back_kernel, grid=(pairs // 2,), in_specs=[smem, pl.BlockS...]
    unnamed x14 -> x8, local copies, waits for them, and re-layouts: 3.64 us -> 1.63 us
    pallas_call x1, Pallas kernels: 6.22 us -> 7.96 us  [near(): pl.pallas_call(functools.partial(near_kernel, lin_scale), grid=(width //...]
where the time goes in v9:
time: 152 us; the launch traced here: 151 us
  starting transfers between devices  48.7 us (32%)
  Pallas kernels  35.4 us (23%)
  waiting for transfers between devices  34.2 us (23%)
  blocking collectives  30.1 us (20%)
  local copies, waits for them, and re-layouts  1.72 us (1%)
    all_to_all x1, blocking collectives, shards(): lax.all_to_all(partial.reshape(16, width // 16, 3 * PAIR), FAR16, 0, 0)  16.6 us
    all_to_all x1, blocking collectives, gather_tiles(): lax.all_to_all(jnp.broadcast_to(piece[None], (16, rows, cols)), AX, 0, 0,...  13.6 us
    ppermute x4, waiting for transfers between devices, ring(): return lax.ppermute(array, AX, route)  12.8 us
    all_to_all x1, starting transfers between devices, shards(): got = lax.all_to_all(msg.reshape(DEVS, 16, PAIR), AX, 0, 0)  9.71 us
    pallas_call x1, Pallas kernels, near(): pl.pallas_call(functools.partial(near_kernel, lin_scale), grid=(width //...  7.96 us
    ppermute x1, starting transfers between devices, shards(): nxt = lax.ppermute(prev, AX, [(i + 1, i) for i in range(DEVS - 1)])  7.42 us
    pallas_call x4, Pallas kernels, place_tiles(): pl.pallas_call(functools.partial(place_kernel, pieces, len(sources)), in_...  7.32 us
    ppermute x3, starting transfers between devices, swapped(): return lax.ppermute(array, 'c', swap)  7.16 us
  transfers between devices with their start and end apart: 16, of which 10 were waited for; matrix products, arithmetic and copies ran while one was open for 0% of the time, Pallas kernels for 17%

profile of v9, /device:TPU:1, one launch (start us, length us, event | category | flops | bytes accessed | tf_op | source)
XLA Modules:
  0.0 151.1 jit_solution(14099067730389600571)
XLA Ops:
  0.6 5.6 %project.1 = (bf16[128,1024]{1,0:T(8,128)(2,1)}, bf16[2,128,1024]{2,1,0:T(8,128)(2,1)}, f32[4,4,128]{2,1,0:T(4,128)}, f32[4,128,4]{2,1,0:T(8,128)}, bf16[2,1024,...) custom-call(bf16[128,1024]{1,0:T(8,128)(2,1)} %tok.1, bf16[1024,1024]{1,0:T(8,128)(2,1)} %wq.3, bf16[1024,1024]{1,0:T(8,128)(2,1)} %wk.5, ...), custom_call_target="tpu_custom_call" | custom-call | flops 805306368 | bytes 7864320 | tf_op jit(solution)/shard_map/project/pallas_call | solution.py:125
  6.2 5.7 %collective-permute-start = (bf16[128,1024]{1,0:T(8,128)(2,1)}, bf16[128,1024]{1,0:T(8,128)(2,1)S(1)}, u32[]{:S(2)}, u32[]{:S(2)}) collective-permute-start(bf16[128,1024]{1,0:T(8,128)(2,1)} %get-tuple-element.40.tok), channel_id=1, source_target_pairs={{0,1},{1,2},{2,3},{3,4},{4,5},{5,6},{6,7},{7,8},{8,9},{9,10},{10,1... | collective-permute-start | bytes 786440 | tf_op jit(solution)/shard_map/ppermute | solution.py:623
  11.9 9.7 %all-to-all-start = ((bf16[128,16,128]{2,1,0:T(8,128)(2,1)}), bf16[128,16,128]{2,1,0:T(8,128)(2,1)S(1)}, u32[]{:S(2)}, u32[]{:S(2)}) async-start(bf16[128,16,128]{2,1,0:T(8,128)(2,1)} %bitcast.18), calls=%async_computation | async-start | bytes 1048576 | tf_op jit(solution)/shard_map/all_to_all | solution.py:624
  21.6 2.7 %collective-permute-done.ptok = bf16[128,1024]{1,0:T(8,128)(2,1)S(1)} collective-permute-done((bf16[128,1024]{1,0:T(8,128)(2,1)}, bf16[128,1024]{1,0:T(8,128)(2,1)S(1)}, u32[]{:S(2)}, u32[]{:S(2)}) %collective-permute-start) | collective-permute-done | bytes 262176 | tf_op jit(solution)/shard_map/ppermute | solution.py:623
  24.3 0.7 copy-done.3
  25.0 8.0 %near.1 = (f32[128,1024]{1,0:T(8,128)}, f32[128,1024]{1,0:T(8,128)}, f32[2,128,1024]{2,1,0:T(8,128)}, bf16[2,128,1024]{2,1,0:T(8,128)(2,1)}, s32[1]{0:T(128)}) custom-call(s32[1]{0:T(128)} %bitcast.place, s32[1,4]{1,0:T(1,128)} %blocks.1, bf16[128,1024]{1,0:T(8,128)(2,1)} %get-tuple-element.38.q_ref.q, bf16[2,128,1024]{2,1,0:T(8,128)(2,1)} %get-tuple-element.39.kv, ...), custom_call_target="tpu_custom_call" | custom-call | flops 4000000000 | bytes 16000000 | tf_op jit(solution)/shard_map/near/pallas_call | solution.py:297
  33.0 7.4 %collective-permute-start.1 = (bf16[2,128,1024]{2,1,0:T(8,128)(2,1)}, bf16[2,128,1024]{2,1,0:T(8,128)(2,1)S(1)}, u32[]{:S(2)}, u32[]{:S(2)}) collective-permute-start(bf16[2,128,1024]{2,1,0:T(8,128)(2,1)} %get-tuple-element.46), channel_id=1, source_target_pairs={{1,0},{2,1},{3,2},{4,3},{5,4},{6,5},{7,6},{8,7},{9,8},{10,9},{11,1... | collective-permute-start | bytes 1572872 | tf_op jit(solution)/shard_map/ppermute | solution.py:628
  40.4 1.9 %scan.1 = bf16[1024,128]{1,0:T(8,128)(2,1)} custom-call(s32[1]{0:T(128)} %get-tuple-element.47.place.tag, bf16[128,16,128]{2,1,0:T(8,128)(2,1)S(1)} %all-to-all-done.got), custom_call_target="tpu_custom_call" | custom-call | flops 262144 | bytes 1048576 | tf_op jit(solution)/shard_map/scan/pallas_call | solution.py:208
  42.3 3.5 %all-to-all-start.1 = ((bf16[128,8,128]{2,1,0:T(8,128)(2,1)}), bf16[128,8,128]{2,1,0:T(8,128)(2,1)S(1)}, u32[]{:S(2)}, u32[]{:S(2)}) async-start(bf16[128,8,128]{2,1,0:T(8,128)(2,1)} %bitcast.2), calls=%async_computation.1 | async-start | bytes 524288 | tf_op jit(solution)/shard_map/all_to_all | solution.py:632
  45.9 1.2 flip.1
  47.1 0.6 collective-permute-start.2
  47.7 2.4 %collective-permute-start.3 = (bf16[1024,128]{1,0:T(8,128)(2,1)S(1)}, bf16[1024,128]{1,0:T(8,128)(2,1)S(1)}, u32[]{:S(2)}, u32[]{:S(2)}) collective-permute-start(bf16[1024,128]{1,0:T(8,128)(2,1)S(1)} %get-tuple-element.53.refs_0_), channel_id=1, source_target_pairs={{0,16},{8,24},{16,0},{24,8},{1,17},{9,25},{17,1},{25,9},{2,18},{10... | collective-permute-start | bytes 786440 | tf_op jit(solution)/shard_map/ppermute | solution.py:631
  50.1 1.2 collective-permute-start.4
  51.3 4.9 %all-to-all-done.1 = bf16[128,8,128]{2,1,0:T(8,128)(2,1)S(1)} async-done(((bf16[128,8,128]{2,1,0:T(8,128)(2,1)}), bf16[128,8,128]{2,1,0:T(8,128)(2,1)S(1)}, u32[]{:S(2)}, u32[]{:S(2)}) %all-to-all-start.1) | async-done | bytes 262176 | tf_op jit(solution)/shard_map/all_to_all | solution.py:632
  56.2 0.0 collective-permute-done.1.nxt
  56.2 0.7 copy-done.1
  56.9 0.2 copy-done.2
  57.1 3.3 %join.1 = (bf16[128,1024]{1,0:T(8,128)(2,1)}, bf16[8,128,384]{2,1,0:T(8,128)(2,1)}) custom-call(f32[128,1024]{1,0:T(8,128)} %get-tuple-element.43.near_out, f32[128,1024]{1,0:T(8,128)} %get-tuple-element.44.dq_in, f32[2,128,1024]{2,1,0:T(8,128)} %get-tuple-element.45.own, bf16[2,128,1024]{2,1,0:T(8,128)(2,1)} %copy-done.2, ...), custom_call_target="tpu_custom_call" | custom-call | flops 134217728 | bytes 3145728 | tf_op jit(solution)/shard_map/join/pallas_call | solution.py:371
  60.4 0.0 collective-permute-done.2.refs_1_
  60.4 1.4 collective-permute-done.3.refs_2_
  61.8 4.6 %collective-permute-done.4.refs_3_ = bf16[1024,128]{1,0:T(8,128)(2,1)S(1)} collective-permute-done((bf16[1024,128]{1,0:T(8,128)(2,1)S(1)}, bf16[1024,128]{1,0:T(8,128)(2,1)S(1)}, u32[]{:S(2)}, u32[]{:S(2)}) %collective-permute-start.4) | collective-permute-done | bytes 262176 | tf_op jit(solution)/shard_map/ppermute | solution.py:631
  66.4 0.1 stack.2.mine
  66.5 1.3 collective-permute-start.5
  67.7 5.0 %all-to-all-start.2 = ((bf16[8,128,384]{2,1,0:T(8,128)(2,1)}), bf16[8,128,384]{2,1,0:T(8,128)(2,1)S(1)}, u32[]{:S(2)}, u32[]{:S(2)}) async-start(bf16[8,128,384]{2,1,0:T(8,128)(2,1)} %get-tuple-element.50.delta.refs_4_), calls=%async_computation.2 | async-start | bytes 1572864 | tf_op jit(solution)/shard_map/all_to_all | solution.py:636
  72.7 5.6 %back.1 = (bf16[128,1024]{1,0:T(8,128)(2,1)}, s32[1]{0:T(128)}) custom-call(s32[1]{0:T(128)} %bitcast.4.tag.side, bf16[8,128,384]{2,1,0:T(8,128)(2,1)} %get-tuple-element.50.delta.refs_4_, bf16[1024,1024]{1,0:T(8,128)(2,1)} %wq.3, bf16[1024,1024]{1,0:T(8,128)(2,1)} %wk.5, bf16[1024,1024]{1,0:T(8,128)(2,1)} %wv.5), custom_call_target="tpu_custom_call" | custom-call | flops 805306368 | bytes 7340032 | tf_op jit(solution)/shard_map/back/pallas_call | solution.py:425
  78.3 6.6 %all-to-all-done.2.delta = bf16[8,128,384]{2,1,0:T(8,128)(2,1)S(1)} async-done(((bf16[8,128,384]{2,1,0:T(8,128)(2,1)}), bf16[8,128,384]{2,1,0:T(8,128)(2,1)S(1)}, u32[]{:S(2)}, u32[]{:S(2)}) %all-to-all-start.2) | async-done | bytes 786464 | tf_op jit(solution)/shard_map/all_to_all | solution.py:636
  84.9 2.3 %outer.1 = bf16[1024,384]{1,0:T(8,128)(2,1)S(1)} custom-call(s32[1]{0:T(128)} %get-tuple-element.52.core, s32[1]{0:T(128)} %bitcast.5.at_x, bf16[4,1024,128]{2,1,0:T(8,128)(2,1)S(1)} %stack.2.mine, bf16[4,1024,128]{2,1,0:T(8,128)(2,1)S(1)} %collective-permute-done.5.theirs, bf16[8,128,384]{2,1,0:T(8,128)(2,1)S(1)} %all-to-all-done.2.delta), custom_call_target="tpu_custom_call" | custom-call | flops 805306368 | bytes 2883584 | tf_op jit(solution)/shard_map/outer/pallas_call | solution.py:460
  87.2 16.6 %all_to_all.25 = bf16[16,64,384]{2,1,0:T(8,128)(2,1)S(1)} all-to-all(bf16[16,64,384]{2,1,0:T(8,128)(2,1)S(1)} %bitcast.14), channel_id=1, replica_groups=mesh['yl'=2,'c'=2,'x'=4,'z'=4,'yh'=2] {'yl','z','yh'}, dimensions={0} | all-to-all | bytes 1572864 | tf_op jit(solution)/shard_map/all_to_all | solution.py:641
  103.8 0.1 convert_reduce_fusion
  103.9 0.1 broadcast_in_dim.2
  104.0 13.6 %all_to_all.26 = bf16[16,64,384]{2,1,0:T(8,128)(2,1)S(1)} all-to-all(bf16[16,64,384]{2,1,0:T(8,128)(2,1)S(1)} %broadcast_in_dim.2), channel_id=1, replica_groups={{0,1,2,3,4,5,6,7,64,65,66,67,68,69,70,71},{8,9,10,11,12,13,14,15,72,73,..., dimensions={0} | all-to-all | bytes 1572864 | tf_op jit(solution)/shard_map/all_to_all | solution.py:596
  117.5 4.1 %collective-permute-start.8 = (bf16[8,128,384]{2,1,0:T(8,128)(2,1)S(1)}, bf16[8,128,384]{2,1,0:T(8,128)(2,1)S(1)}, u32[]{:S(2)}, u32[]{:S(2)}) collective-permute-start(bf16[8,128,384]{2,1,0:T(8,128)(2,1)S(1)} %bitcast.10), channel_id=1, source_target_pairs={{0,32},{32,0},{1,33},{33,1},{2,34},{34,2},{3,35},{35,3},{4,36},{36... | collective-permute-start | bytes 2359304 | tf_op jit(solution)/shard_map/ppermute | solution.py:593
  121.6 0.4 collective-permute-start.6
  122.1 2.2 %collective-permute-start.7 = (bf16[8,128,384]{2,1,0:T(8,128)(2,1)S(1)}, bf16[8,128,384]{2,1,0:T(8,128)(2,1)S(1)}, u32[]{:S(2)}, u32[]{:S(2)}) collective-permute-start(bf16[8,128,384]{2,1,0:T(8,128)(2,1)S(1)} %bitcast.12), channel_id=1, source_target_pairs={{0,24},{32,38},{1,25},{33,39},{2,26},{34,32},{3,27},{35,33},{4,28}... | collective-permute-start | bytes 2359304 | tf_op jit(solution)/shard_map/ppermute | solution.py:504
  124.3 1.5 %place.4 = (bf16[1024,1024]{1,0:T(8,128)(2,1)}, bf16[1024,1024]{1,0:T(8,128)(2,1)}, bf16[1024,1024]{1,0:T(8,128)(2,1)}, f32[8,128]{1,0:T(8,128)S(1)}) custom-call(s32[1]{0:T(128)} %bitcast.4.tag.side, s32[1]{0:T(128)} %bitcast.5.at_x, s32[1]{0:T(128)} %bitcast.6.at_z, bf16[8,128,384]{2,1,0:T(8,128)(2,1)S(1)} %bitcast.13, ...), custom_call_target="tpu_custom_call" | custom-call | bytes 3145728 | tf_op jit(solution)/shard_map/place/pallas_call | solution.py:552
  125.8 8.1 %collective-permute-done.6.behind = bf16[8,128,384]{2,1,0:T(8,128)(2,1)S(1)} collective-permute-done((bf16[8,128,384]{2,1,0:T(8,128)(2,1)S(1)}, bf16[8,128,384]{2,1,0:T(8,128)(2,1)S(1)}, u32[]{:S(2)}, u32[]{:S(2)}) %collective-permute-start.6) | collective-permute-done | bytes 786464 | tf_op jit(solution)/shard_map/ppermute | solution.py:504
  134.0 0.2 halves.1
  134.2 0.9 collective-permute-start.11
  135.1 2.1 %collective-permute-start.10 = (bf16[4,128,384]{2,1,0:T(8,128)(2,1)S(1)}, bf16[4,128,384]{2,1,0:T(8,128)(2,1)S(1)}, u32[]{:S(2)}, u32[]{:S(2)}) collective-permute-start(bf16[4,128,384]{2,1,0:T(8,128)(2,1)S(1)} %get-tuple-element.56), channel_id=1, source_target_pairs={{0,24},{32,38},{1,25},{33,39},{2,26},{34,32},{3,27},{35,33},{4,28}... | collective-permute-start | bytes 1179656 | tf_op jit(solution)/shard_map/ppermute | solution.py:504
  137.2 0.9 collective-permute-done.11.refs_1_
  138.1 2.5 %place.5 = (bf16[1024,1024]{1,0:T(8,128)(2,1)}, bf16[1024,1024]{1,0:T(8,128)(2,1)}, bf16[1024,1024]{1,0:T(8,128)(2,1)}, f32[8,128]{1,0:T(8,128)S(1)}) custom-call(s32[1]{0:T(128)} %bitcast.4.tag.side, s32[1]{0:T(128)} %bitcast.5.at_x, s32[1]{0:T(128)} %bitcast.6.at_z, ...), custom_call_target="tpu_custom_call", output_to_operand_aliasing={{0}: (5, {}), {1}: (6, {}), {2}: (7, {})} | custom-call | bytes 6291456 | tf_op jit(solution)/shard_map/place/pallas_call | solution.py:552
  140.6 1.4 collective-permute-done.10.refs_1_
  142.0 3.3 %collective-permute-done.9.refs_0_ = bf16[4,128,384]{2,1,0:T(8,128)(2,1)S(1)} collective-permute-done((bf16[4,128,384]{2,1,0:T(8,128)(2,1)S(1)}, bf16[4,128,384]{2,1,0:T(8,128)(2,1)S(1)}, u32[]{:S(2)}, u32[]{:S(2)}) %collective-permute-start.9) | collective-permute-done | bytes 393248 | tf_op jit(solution)/shard_map/ppermute | solution.py:504
  145.3 0.1 stack.3
  145.4 2.1 %collective-permute-start.12 = (bf16[8,128,384]{2,1,0:T(8,128)(2,1)S(1)}, bf16[8,128,384]{2,1,0:T(8,128)(2,1)S(1)}, u32[]{:S(2)}, u32[]{:S(2)}) collective-permute-start(bf16[8,128,384]{2,1,0:T(8,128)(2,1)S(1)} %bitcast.15), channel_id=1, source_target_pairs={{0,32},{32,0},{1,33},{33,1},{2,34},{34,2},{3,35},{35,3},{4,36},{36... | collective-permute-start | bytes 2359304 | tf_op jit(solution)/shard_map/ppermute | solution.py:593
  147.6 1.7 %place.6 = (bf16[1024,1024]{1,0:T(8,128)(2,1)}, bf16[1024,1024]{1,0:T(8,128)(2,1)}, bf16[1024,1024]{1,0:T(8,128)(2,1)}, f32[8,128]{1,0:T(8,128)}) custom-call(s32[1]{0:T(128)} %bitcast.4.tag.side, s32[1]{0:T(128)} %bitcast.5.at_x, s32[1]{0:T(128)} %bitcast.6.at_z, ...), custom_call_target="tpu_custom_call", output_to_operand_aliasing={{0}: (4, {}), {1}: (5, {}), {2}: (6, {})} | custom-call | bytes 1572864 | tf_op jit(solution)/shard_map/place/pallas_call | solution.py:552
  149.2 0.2 collective-permute-done.12.refs_0_
  149.5 1.7 %place.7 = (bf16[1024,1024]{1,0:T(8,128)(2,1)}, bf16[1024,1024]{1,0:T(8,128)(2,1)}, bf16[1024,1024]{1,0:T(8,128)(2,1)}, f32[8,128]{1,0:T(8,128)}) custom-call(s32[1]{0:T(128)S(6)} %sub.3.side, s32[1]{0:T(128)} %bitcast.5.at_x, s32[1]{0:T(128)} %bitcast.6.at_z, ...), custom_call_target="tpu_custom_call", output_to_operand_aliasing={{0}: (4, {}), {1}: (5, {}), {2}: (6, {})} | custom-call | bytes 1572864 | tf_op jit(solution)/shard_map/place/pallas_call | solution.py:552
  (11 shorter events, 0.0 us)
Async XLA Ops:
  6.2 18.1 %collective-permute-start = (bf16[128,1024]{1,0:T(8,128)(2,1)}, bf16[128,1024]{1,0:T(8,128)(2,1)S(1)}, u32[]{:S(2)}, u32[]{:S(2)}) collective-permute-start(bf16[128,1024]{1,0:T(8,128)(2,1)} %get-tuple-element.40.tok), channel_id=1, source_target_pairs={{0,1},{1,2},{2,3},{3,4},{4,5},{5,6},{6,7},{7,8},{8,9},{9,10},{10,1... | collective-permute-start | bytes 786440 | tf_op jit(solution)/shard_map/ppermute | solution.py:623
  11.9 28.5 %all-to-all-start = ((bf16[128,16,128]{2,1,0:T(8,128)(2,1)}), bf16[128,16,128]{2,1,0:T(8,128)(2,1)S(1)}, u32[]{:S(2)}, u32[]{:S(2)}) async-start(bf16[128,16,128]{2,1,0:T(8,128)(2,1)} %bitcast.18), calls=%async_computation | async-start | bytes 1048576 | tf_op jit(solution)/shard_map/all_to_all | solution.py:624
  24.3 0.7 copy-start.3
  25.0 20.9 %copy-start = (bf16[128,1024]{1,0:T(8,128)(2,1)S(1)}, bf16[128,1024]{1,0:T(8,128)(2,1)}, u32[]{:S(2)}) copy-start(bf16[128,1024]{1,0:T(8,128)(2,1)} %get-tuple-element.40.tok) | copy-start | bytes 786436
  33.0 23.2 %collective-permute-start.1 = (bf16[2,128,1024]{2,1,0:T(8,128)(2,1)}, bf16[2,128,1024]{2,1,0:T(8,128)(2,1)S(1)}, u32[]{:S(2)}, u32[]{:S(2)}) collective-permute-start(bf16[2,128,1024]{2,1,0:T(8,128)(2,1)} %get-tuple-element.46), channel_id=1, source_target_pairs={{1,0},{2,1},{3,2},{4,3},{5,4},{6,5},{7,6},{8,7},{9,8},{10,9},{11,1... | collective-permute-start | bytes 1572872 | tf_op jit(solution)/shard_map/ppermute | solution.py:628
  42.3 13.8 %all-to-all-start.1 = ((bf16[128,8,128]{2,1,0:T(8,128)(2,1)}), bf16[128,8,128]{2,1,0:T(8,128)(2,1)S(1)}, u32[]{:S(2)}, u32[]{:S(2)}) async-start(bf16[128,8,128]{2,1,0:T(8,128)(2,1)} %bitcast.2), calls=%async_computation.1 | async-start | bytes 524288 | tf_op jit(solution)/shard_map/all_to_all | solution.py:632
  47.1 13.2 %collective-permute-start.2 = (bf16[1024,128]{1,0:T(8,128)(2,1)S(1)}, bf16[1024,128]{1,0:T(8,128)(2,1)S(1)}, u32[]{:S(2)}, u32[]{:S(2)}) collective-permute-start(bf16[1024,128]{1,0:T(8,128)(2,1)S(1)} %get-tuple-element.53.refs_0_), channel_id=1, source_target_pairs={{0,8},{8,16},{16,24},{24,0},{1,9},{9,17},{17,25},{25,1},{2,10},{10... | collective-permute-start | bytes 786440 | tf_op jit(solution)/shard_map/ppermute | solution.py:631
  47.7 14.1 %collective-permute-start.3 = (bf16[1024,128]{1,0:T(8,128)(2,1)S(1)}, bf16[1024,128]{1,0:T(8,128)(2,1)S(1)}, u32[]{:S(2)}, u32[]{:S(2)}) collective-permute-start(bf16[1024,128]{1,0:T(8,128)(2,1)S(1)} %get-tuple-element.53.refs_0_), channel_id=1, source_target_pairs={{0,16},{8,24},{16,0},{24,8},{1,17},{9,25},{17,1},{25,9},{2,18},{10... | collective-permute-start | bytes 786440 | tf_op jit(solution)/shard_map/ppermute | solution.py:631
  50.1 16.3 %collective-permute-start.4 = (bf16[1024,128]{1,0:T(8,128)(2,1)S(1)}, bf16[1024,128]{1,0:T(8,128)(2,1)S(1)}, u32[]{:S(2)}, u32[]{:S(2)}) collective-permute-start(bf16[1024,128]{1,0:T(8,128)(2,1)S(1)} %get-tuple-element.53.refs_0_), channel_id=1, source_target_pairs={{0,24},{8,0},{16,8},{24,16},{1,25},{9,1},{17,9},{25,17},{2,26},{10... | collective-permute-start | bytes 786440 | tf_op jit(solution)/shard_map/ppermute | solution.py:631
  56.2 0.7 copy-start.1
  56.2 0.9 copy-start.2
  66.5 18.5 %collective-permute-start.5 = (bf16[4,1024,128]{2,1,0:T(8,128)(2,1)S(1)}, bf16[4,1024,128]{2,1,0:T(8,128)(2,1)S(1)}, u32[]{:S(2)}, u32[]{:S(2)}) collective-permute-start(bf16[4,1024,128]{2,1,0:T(8,128)(2,1)S(1)} %stack.2.mine), channel_id=1, source_target_pairs={{0,32},{32,0},{1,33},{33,1},{2,34},{34,2},{3,35},{35,3},{4,36},{36... | collective-permute-start | bytes 3145736 | tf_op jit(solution)/shard_map/ppermute | solution.py:638
  67.7 17.2 %all-to-all-start.2 = ((bf16[8,128,384]{2,1,0:T(8,128)(2,1)}), bf16[8,128,384]{2,1,0:T(8,128)(2,1)S(1)}, u32[]{:S(2)}, u32[]{:S(2)}) async-start(bf16[8,128,384]{2,1,0:T(8,128)(2,1)} %get-tuple-element.50.delta.refs_4_), calls=%async_computation.2 | async-start | bytes 1572864 | tf_op jit(solution)/shard_map/all_to_all | solution.py:636
  117.5 6.8 %collective-permute-start.8 = (bf16[8,128,384]{2,1,0:T(8,128)(2,1)S(1)}, bf16[8,128,384]{2,1,0:T(8,128)(2,1)S(1)}, u32[]{:S(2)}, u32[]{:S(2)}) collective-permute-start(bf16[8,128,384]{2,1,0:T(8,128)(2,1)S(1)} %bitcast.10), channel_id=1, source_target_pairs={{0,32},{32,0},{1,33},{33,1},{2,34},{34,2},{3,35},{35,3},{4,36},{36... | collective-permute-start | bytes 2359304 | tf_op jit(solution)/shard_map/ppermute | solution.py:593
  121.6 12.3 %collective-permute-start.6 = (bf16[8,128,384]{2,1,0:T(8,128)(2,1)S(1)}, bf16[8,128,384]{2,1,0:T(8,128)(2,1)S(1)}, u32[]{:S(2)}, u32[]{:S(2)}) collective-permute-start(bf16[8,128,384]{2,1,0:T(8,128)(2,1)S(1)} %bitcast.11), channel_id=1, source_target_pairs={{0,8},{32,34},{1,9},{33,35},{2,10},{34,36},{3,11},{35,37},{4,12},{... | collective-permute-start | bytes 2359304 | tf_op jit(solution)/shard_map/ppermute | solution.py:504
  122.1 11.9 %collective-permute-start.7 = (bf16[8,128,384]{2,1,0:T(8,128)(2,1)S(1)}, bf16[8,128,384]{2,1,0:T(8,128)(2,1)S(1)}, u32[]{:S(2)}, u32[]{:S(2)}) collective-permute-start(bf16[8,128,384]{2,1,0:T(8,128)(2,1)S(1)} %bitcast.12), channel_id=1, source_target_pairs={{0,24},{32,38},{1,25},{33,39},{2,26},{34,32},{3,27},{35,33},{4,28}... | collective-permute-start | bytes 2359304 | tf_op jit(solution)/shard_map/ppermute | solution.py:504
  134.2 4.0 %collective-permute-start.11 = (bf16[16,128,384]{2,1,0:T(8,128)(2,1)S(1)}, bf16[16,128,384]{2,1,0:T(8,128)(2,1)S(1)}, u32[]{:S(2)}, u32[]{:S(2)}) collective-permute-start(bf16[16,128,384]{2,1,0:T(8,128)(2,1)S(1)} %get-tuple-element.57.refs_0_), channel_id=1, source_target_pairs={{0,32},{32,0},{1,33},{33,1},{2,34},{34,2},{3,35},{35,3},{4,36},{36... | collective-permute-start | bytes 4718600 | tf_op jit(solution)/shard_map/ppermute | solution.py:593
  135.1 6.9 %collective-permute-start.10 = (bf16[4,128,384]{2,1,0:T(8,128)(2,1)S(1)}, bf16[4,128,384]{2,1,0:T(8,128)(2,1)S(1)}, u32[]{:S(2)}, u32[]{:S(2)}) collective-permute-start(bf16[4,128,384]{2,1,0:T(8,128)(2,1)S(1)} %get-tuple-element.56), channel_id=1, source_target_pairs={{0,24},{32,38},{1,25},{33,39},{2,26},{34,32},{3,27},{35,33},{4,28}... | collective-permute-start | bytes 1179656 | tf_op jit(solution)/shard_map/ppermute | solution.py:504
  137.2 8.1 %collective-permute-start.9 = (bf16[4,128,384]{2,1,0:T(8,128)(2,1)S(1)}, bf16[4,128,384]{2,1,0:T(8,128)(2,1)S(1)}, u32[]{:S(2)}, u32[]{:S(2)}) collective-permute-start(bf16[4,128,384]{2,1,0:T(8,128)(2,1)S(1)} %get-tuple-element.55), channel_id=1, source_target_pairs={{0,8},{32,34},{1,9},{33,35},{2,10},{34,36},{3,11},{35,37},{4,12},{... | collective-permute-start | bytes 1179656 | tf_op jit(solution)/shard_map/ppermute | solution.py:504
  145.4 4.1 %collective-permute-start.12 = (bf16[8,128,384]{2,1,0:T(8,128)(2,1)S(1)}, bf16[8,128,384]{2,1,0:T(8,128)(2,1)S(1)}, u32[]{:S(2)}, u32[]{:S(2)}) collective-permute-start(bf16[8,128,384]{2,1,0:T(8,128)(2,1)S(1)} %bitcast.15), channel_id=1, source_target_pairs={{0,32},{32,0},{1,33},{33,1},{2,34},{34,2},{3,35},{35,3},{4,36},{36... | collective-permute-start | bytes 2359304 | tf_op jit(solution)/shard_map/ppermute | solution.py:593

commit v10 on v9

--- a/solution.py
+++ b/solution.py
@@ -626,9 +626,9 @@
         place, neighbour_blocks, q, kv, prev_tokens, wk, wv, cot, run, runt, lin_scale
     )
     nxt = lax.ppermute(prev, AX, [(i + 1, i) for i in range(DEVS - 1)])
+    tokt, place = flip(place, own_tokens)
+    around = [lax.ppermute(tokt, "x", [(i, (i + d) % 4) for i in range(4)]) for d in (1, 2, 3)]
     states = scan(place, got)
-    tokt, _ = flip(place, own_tokens)
-    around = [lax.ppermute(tokt, "x", [(i, (i + d) % 4) for i in range(4)]) for d in (1, 2, 3)]
     states = lax.all_to_all(states.reshape(DEVS, 8, PAIR), AX, 0, 0)
     states = states.reshape(2, width // PAIR, DH, PAIR)
     layer, delta = join(near_out, dq, own, nxt, q, kv, cot, runt, states, lin_scale)

time: 152 us -> 152 us (level)
    ppermute x3, waiting for transfers between devices: 6.01 us -> 4.09 us  [shards(): lax.ppermute(tokt, 'x', [(i, (i + d) % 4) for i in range(4)])]
where the time goes in v10:
time: 152 us; the launch traced here: 151 us
  starting transfers between devices  49 us (32%)
  Pallas kernels  35.3 us (23%)
  waiting for transfers between devices  33.6 us (22%)
  blocking collectives  30.8 us (20%)
  local copies, waits for them, and re-layouts  1.72 us (1%)
    all_to_all x1, blocking collectives, shards(): lax.all_to_all(partial.reshape(16, width // 16, 3 * PAIR), FAR16, 0, 0)  17.3 us
    all_to_all x1, blocking collectives, gather_tiles(): lax.all_to_all(jnp.broadcast_to(piece[None], (16, rows, cols)), AX, 0, 0,...  13.6 us
    ppermute x4, waiting for transfers between devices, ring(): return lax.ppermute(array, AX, route)  12.8 us
    all_to_all x1, starting transfers between devices, shards(): got = lax.all_to_all(msg.reshape(DEVS, 16, PAIR), AX, 0, 0)  9.71 us
    pallas_call x1, Pallas kernels, near(): pl.pallas_call(functools.partial(near_kernel, lin_scale), grid=(width //...  7.96 us
    ppermute x1, starting transfers between devices, shards(): nxt = lax.ppermute(prev, AX, [(i + 1, i) for i in range(DEVS - 1)])  7.42 us
    pallas_call x4, Pallas kernels, place_tiles(): pl.pallas_call(functools.partial(place_kernel, pieces, len(sources)), in_...  7.32 us
    ppermute x3, starting transfers between devices, swapped(): return lax.ppermute(array, 'c', swap)  7.16 us
  transfers between devices with their start and end apart: 16, of which 10 were waited for; matrix products, arithmetic and copies ran while one was open for 0% of the time, Pallas kernels for 17%

profile of v10, /device:TPU:1, one launch (start us, length us, event | category | flops | bytes accessed | tf_op | source)
XLA Modules:
  0.0 151.4 jit_solution(10403095776166846304)
XLA Ops:
  0.6 5.6 %project.1 = (bf16[128,1024]{1,0:T(8,128)(2,1)}, bf16[2,128,1024]{2,1,0:T(8,128)(2,1)}, f32[4,4,128]{2,1,0:T(4,128)}, f32[4,128,4]{2,1,0:T(8,128)}, bf16[2,1024,...) custom-call(bf16[128,1024]{1,0:T(8,128)(2,1)} %tok.1, bf16[1024,1024]{1,0:T(8,128)(2,1)} %wq.3, bf16[1024,1024]{1,0:T(8,128)(2,1)} %wk.5, ...), custom_call_target="tpu_custom_call" | custom-call | flops 805306368 | bytes 7864320 | tf_op jit(solution)/shard_map/project/pallas_call | solution.py:125
  6.2 5.7 %collective-permute-start = (bf16[128,1024]{1,0:T(8,128)(2,1)}, bf16[128,1024]{1,0:T(8,128)(2,1)S(1)}, u32[]{:S(2)}, u32[]{:S(2)}) collective-permute-start(bf16[128,1024]{1,0:T(8,128)(2,1)} %get-tuple-element.41.tok), channel_id=1, source_target_pairs={{0,1},{1,2},{2,3},{3,4},{4,5},{5,6},{6,7},{7,8},{8,9},{9,10},{10,1... | collective-permute-start | bytes 786440 | tf_op jit(solution)/shard_map/ppermute | solution.py:623
  11.9 9.7 %all-to-all-start = ((bf16[128,16,128]{2,1,0:T(8,128)(2,1)}), bf16[128,16,128]{2,1,0:T(8,128)(2,1)S(1)}, u32[]{:S(2)}, u32[]{:S(2)}) async-start(bf16[128,16,128]{2,1,0:T(8,128)(2,1)} %bitcast.18), calls=%async_computation | async-start | bytes 1048576 | tf_op jit(solution)/shard_map/all_to_all | solution.py:624
  21.6 2.7 %collective-permute-done.ptok = bf16[128,1024]{1,0:T(8,128)(2,1)S(1)} collective-permute-done((bf16[128,1024]{1,0:T(8,128)(2,1)}, bf16[128,1024]{1,0:T(8,128)(2,1)S(1)}, u32[]{:S(2)}, u32[]{:S(2)}) %collective-permute-start) | collective-permute-done | bytes 262176 | tf_op jit(solution)/shard_map/ppermute | solution.py:623
  24.3 0.7 copy-done.3
  25.0 8.0 %near.1 = (f32[128,1024]{1,0:T(8,128)}, f32[128,1024]{1,0:T(8,128)}, f32[2,128,1024]{2,1,0:T(8,128)}, bf16[2,128,1024]{2,1,0:T(8,128)(2,1)}, s32[1]{0:T(128)}) custom-call(s32[1]{0:T(128)} %bitcast.place, s32[1,4]{1,0:T(1,128)} %blocks.1, bf16[128,1024]{1,0:T(8,128)(2,1)} %get-tuple-element.39.q_ref.q, bf16[2,128,1024]{2,1,0:T(8,128)(2,1)} %get-tuple-element.40.kv, ...), custom_call_target="tpu_custom_call" | custom-call | flops 4000000000 | bytes 16000000 | tf_op jit(solution)/shard_map/near/pallas_call | solution.py:297
  33.0 7.4 %collective-permute-start.1 = (bf16[2,128,1024]{2,1,0:T(8,128)(2,1)}, bf16[2,128,1024]{2,1,0:T(8,128)(2,1)S(1)}, u32[]{:S(2)}, u32[]{:S(2)}) collective-permute-start(bf16[2,128,1024]{2,1,0:T(8,128)(2,1)} %get-tuple-element.47), channel_id=1, source_target_pairs={{1,0},{2,1},{3,2},{4,3},{5,4},{6,5},{7,6},{8,7},{9,8},{10,9},{11,1... | collective-permute-start | bytes 1572872 | tf_op jit(solution)/shard_map/ppermute | solution.py:628
  40.4 1.2 flip.1
  41.6 1.8 %scan.1 = bf16[1024,128]{1,0:T(8,128)(2,1)} custom-call(s32[1]{0:T(128)} %get-tuple-element.49.place, bf16[128,16,128]{2,1,0:T(8,128)(2,1)S(1)} %all-to-all-done.got), custom_call_target="tpu_custom_call" | custom-call | flops 262144 | bytes 1048576 | tf_op jit(solution)/shard_map/scan/pallas_call | solution.py:208
  43.5 3.5 %all-to-all-start.1 = ((bf16[128,8,128]{2,1,0:T(8,128)(2,1)}), bf16[128,8,128]{2,1,0:T(8,128)(2,1)S(1)}, u32[]{:S(2)}, u32[]{:S(2)}) async-start(bf16[128,8,128]{2,1,0:T(8,128)(2,1)} %bitcast.2), calls=%async_computation.1 | async-start | bytes 524288 | tf_op jit(solution)/shard_map/all_to_all | solution.py:632
  47.0 0.6 collective-permute-start.2
  47.6 2.4 %collective-permute-start.3 = (bf16[1024,128]{1,0:T(8,128)(2,1)S(1)}, bf16[1024,128]{1,0:T(8,128)(2,1)S(1)}, u32[]{:S(2)}, u32[]{:S(2)}) collective-permute-start(bf16[1024,128]{1,0:T(8,128)(2,1)S(1)} %get-tuple-element.55.refs_0_), channel_id=1, source_target_pairs={{0,16},{8,24},{16,0},{24,8},{1,17},{9,25},{17,1},{25,9},{2,18},{10... | collective-permute-start | bytes 786440 | tf_op jit(solution)/shard_map/ppermute | solution.py:630
  50.0 1.2 collective-permute-start.4
  51.2 6.2 %all-to-all-done.1 = bf16[128,8,128]{2,1,0:T(8,128)(2,1)S(1)} async-done(((bf16[128,8,128]{2,1,0:T(8,128)(2,1)}), bf16[128,8,128]{2,1,0:T(8,128)(2,1)S(1)}, u32[]{:S(2)}, u32[]{:S(2)}) %all-to-all-start.1) | async-done | bytes 262176 | tf_op jit(solution)/shard_map/all_to_all | solution.py:632
  57.3 0.0 collective-permute-done.1.nxt
  57.4 0.7 copy-done.1
  58.1 0.2 copy-done.2
  58.3 3.3 %join.1 = (bf16[128,1024]{1,0:T(8,128)(2,1)}, bf16[8,128,384]{2,1,0:T(8,128)(2,1)}) custom-call(f32[128,1024]{1,0:T(8,128)} %get-tuple-element.44.near_out, f32[128,1024]{1,0:T(8,128)} %get-tuple-element.45.dq_in, f32[2,128,1024]{2,1,0:T(8,128)} %get-tuple-element.46.own, bf16[2,128,1024]{2,1,0:T(8,128)(2,1)} %copy-done.2, ...), custom_call_target="tpu_custom_call" | custom-call | flops 134217728 | bytes 3145728 | tf_op jit(solution)/shard_map/join/pallas_call | solution.py:371
  61.5 1.6 %collective-permute-done.3.refs_2_ = bf16[1024,128]{1,0:T(8,128)(2,1)S(1)} collective-permute-done((bf16[1024,128]{1,0:T(8,128)(2,1)S(1)}, bf16[1024,128]{1,0:T(8,128)(2,1)S(1)}, u32[]{:S(2)}, u32[]{:S(2)}) %collective-permute-start.3) | collective-permute-done | bytes 262176 | tf_op jit(solution)/shard_map/ppermute | solution.py:630
  63.2 2.4 %collective-permute-done.4.refs_3_ = bf16[1024,128]{1,0:T(8,128)(2,1)S(1)} collective-permute-done((bf16[1024,128]{1,0:T(8,128)(2,1)S(1)}, bf16[1024,128]{1,0:T(8,128)(2,1)S(1)}, u32[]{:S(2)}, u32[]{:S(2)}) %collective-permute-start.4) | collective-permute-done | bytes 262176 | tf_op jit(solution)/shard_map/ppermute | solution.py:630
  65.6 0.1 stack.2.mine
  65.7 1.3 collective-permute-start.5
  67.0 5.3 %all-to-all-start.2 = ((bf16[8,128,384]{2,1,0:T(8,128)(2,1)}), bf16[8,128,384]{2,1,0:T(8,128)(2,1)S(1)}, u32[]{:S(2)}, u32[]{:S(2)}) async-start(bf16[8,128,384]{2,1,0:T(8,128)(2,1)} %get-tuple-element.52.delta.refs_4_), calls=%async_computation.2 | async-start | bytes 1572864 | tf_op jit(solution)/shard_map/all_to_all | solution.py:636
  72.3 5.6 %back.1 = (bf16[128,1024]{1,0:T(8,128)(2,1)}, s32[1]{0:T(128)}) custom-call(s32[1]{0:T(128)} %bitcast.4.tag.side, bf16[8,128,384]{2,1,0:T(8,128)(2,1)} %get-tuple-element.52.delta.refs_4_, bf16[1024,1024]{1,0:T(8,128)(2,1)} %wq.3, bf16[1024,1024]{1,0:T(8,128)(2,1)} %wk.5, bf16[1024,1024]{1,0:T(8,128)(2,1)} %wv.5), custom_call_target="tpu_custom_call" | custom-call | flops 805306368 | bytes 7340032 | tf_op jit(solution)/shard_map/back/pallas_call | solution.py:425
  77.9 6.6 %all-to-all-done.2.delta = bf16[8,128,384]{2,1,0:T(8,128)(2,1)S(1)} async-done(((bf16[8,128,384]{2,1,0:T(8,128)(2,1)}), bf16[8,128,384]{2,1,0:T(8,128)(2,1)S(1)}, u32[]{:S(2)}, u32[]{:S(2)}) %all-to-all-start.2) | async-done | bytes 786464 | tf_op jit(solution)/shard_map/all_to_all | solution.py:636
  84.5 0.0 collective-permute-done.5.theirs
  84.5 2.3 %outer.1 = bf16[1024,384]{1,0:T(8,128)(2,1)S(1)} custom-call(s32[1]{0:T(128)} %get-tuple-element.54.core, s32[1]{0:T(128)} %bitcast.5.at_x, bf16[4,1024,128]{2,1,0:T(8,128)(2,1)S(1)} %stack.2.mine, bf16[4,1024,128]{2,1,0:T(8,128)(2,1)S(1)} %collective-permute-done.5.theirs, bf16[8,128,384]{2,1,0:T(8,128)(2,1)S(1)} %all-to-all-done.2.delta), custom_call_target="tpu_custom_call" | custom-call | flops 805306368 | bytes 2883584 | tf_op jit(solution)/shard_map/outer/pallas_call | solution.py:460
  86.7 17.3 %all_to_all.25 = bf16[16,64,384]{2,1,0:T(8,128)(2,1)S(1)} all-to-all(bf16[16,64,384]{2,1,0:T(8,128)(2,1)S(1)} %bitcast.14), channel_id=1, replica_groups=mesh['yl'=2,'c'=2,'x'=4,'z'=4,'yh'=2] {'yl','z','yh'}, dimensions={0} | all-to-all | bytes 1572864 | tf_op jit(solution)/shard_map/all_to_all | solution.py:641
  104.0 0.1 convert_reduce_fusion
  104.2 0.1 broadcast_in_dim.2
  104.3 13.6 %all_to_all.26 = bf16[16,64,384]{2,1,0:T(8,128)(2,1)S(1)} all-to-all(bf16[16,64,384]{2,1,0:T(8,128)(2,1)S(1)} %broadcast_in_dim.2), channel_id=1, replica_groups={{0,1,2,3,4,5,6,7,64,65,66,67,68,69,70,71},{8,9,10,11,12,13,14,15,72,73,..., dimensions={0} | all-to-all | bytes 1572864 | tf_op jit(solution)/shard_map/all_to_all | solution.py:596
  117.8 4.1 %collective-permute-start.8 = (bf16[8,128,384]{2,1,0:T(8,128)(2,1)S(1)}, bf16[8,128,384]{2,1,0:T(8,128)(2,1)S(1)}, u32[]{:S(2)}, u32[]{:S(2)}) collective-permute-start(bf16[8,128,384]{2,1,0:T(8,128)(2,1)S(1)} %bitcast.10), channel_id=1, source_target_pairs={{0,32},{32,0},{1,33},{33,1},{2,34},{34,2},{3,35},{35,3},{4,36},{36... | collective-permute-start | bytes 2359304 | tf_op jit(solution)/shard_map/ppermute | solution.py:593
  121.9 0.4 collective-permute-start.6
  122.3 2.2 %collective-permute-start.7 = (bf16[8,128,384]{2,1,0:T(8,128)(2,1)S(1)}, bf16[8,128,384]{2,1,0:T(8,128)(2,1)S(1)}, u32[]{:S(2)}, u32[]{:S(2)}) collective-permute-start(bf16[8,128,384]{2,1,0:T(8,128)(2,1)S(1)} %bitcast.12), channel_id=1, source_target_pairs={{0,24},{32,38},{1,25},{33,39},{2,26},{34,32},{3,27},{35,33},{4,28}... | collective-permute-start | bytes 2359304 | tf_op jit(solution)/shard_map/ppermute | solution.py:504
  124.6 1.5 %place.4 = (bf16[1024,1024]{1,0:T(8,128)(2,1)}, bf16[1024,1024]{1,0:T(8,128)(2,1)}, bf16[1024,1024]{1,0:T(8,128)(2,1)}, f32[8,128]{1,0:T(8,128)S(1)}) custom-call(s32[1]{0:T(128)} %bitcast.4.tag.side, s32[1]{0:T(128)} %bitcast.5.at_x, s32[1]{0:T(128)} %bitcast.6.at_z, bf16[8,128,384]{2,1,0:T(8,128)(2,1)S(1)} %bitcast.13, ...), custom_call_target="tpu_custom_call" | custom-call | bytes 3145728 | tf_op jit(solution)/shard_map/place/pallas_call | solution.py:552
  126.1 8.1 %collective-permute-done.6.behind = bf16[8,128,384]{2,1,0:T(8,128)(2,1)S(1)} collective-permute-done((bf16[8,128,384]{2,1,0:T(8,128)(2,1)S(1)}, bf16[8,128,384]{2,1,0:T(8,128)(2,1)S(1)}, u32[]{:S(2)}, u32[]{:S(2)}) %collective-permute-start.6) | collective-permute-done | bytes 786464 | tf_op jit(solution)/shard_map/ppermute | solution.py:504
  134.2 0.2 halves.1
  134.4 0.9 collective-permute-start.11
  135.4 2.1 %collective-permute-start.10 = (bf16[4,128,384]{2,1,0:T(8,128)(2,1)S(1)}, bf16[4,128,384]{2,1,0:T(8,128)(2,1)S(1)}, u32[]{:S(2)}, u32[]{:S(2)}) collective-permute-start(bf16[4,128,384]{2,1,0:T(8,128)(2,1)S(1)} %get-tuple-element.58), channel_id=1, source_target_pairs={{0,24},{32,38},{1,25},{33,39},{2,26},{34,32},{3,27},{35,33},{4,28}... | collective-permute-start | bytes 1179656 | tf_op jit(solution)/shard_map/ppermute | solution.py:504
  137.5 0.9 collective-permute-done.11.refs_1_
  138.4 2.5 %place.5 = (bf16[1024,1024]{1,0:T(8,128)(2,1)}, bf16[1024,1024]{1,0:T(8,128)(2,1)}, bf16[1024,1024]{1,0:T(8,128)(2,1)}, f32[8,128]{1,0:T(8,128)S(1)}) custom-call(s32[1]{0:T(128)} %bitcast.4.tag.side, s32[1]{0:T(128)} %bitcast.5.at_x, s32[1]{0:T(128)} %bitcast.6.at_z, ...), custom_call_target="tpu_custom_call", output_to_operand_aliasing={{0}: (5, {}), {1}: (6, {}), {2}: (7, {})} | custom-call | bytes 6291456 | tf_op jit(solution)/shard_map/place/pallas_call | solution.py:552
  140.9 1.4 collective-permute-done.10.refs_1_
  142.3 3.3 %collective-permute-done.9.refs_0_ = bf16[4,128,384]{2,1,0:T(8,128)(2,1)S(1)} collective-permute-done((bf16[4,128,384]{2,1,0:T(8,128)(2,1)S(1)}, bf16[4,128,384]{2,1,0:T(8,128)(2,1)S(1)}, u32[]{:S(2)}, u32[]{:S(2)}) %collective-permute-start.9) | collective-permute-done | bytes 393248 | tf_op jit(solution)/shard_map/ppermute | solution.py:504
  145.6 0.1 stack.3
  145.7 2.1 %collective-permute-start.12 = (bf16[8,128,384]{2,1,0:T(8,128)(2,1)S(1)}, bf16[8,128,384]{2,1,0:T(8,128)(2,1)S(1)}, u32[]{:S(2)}, u32[]{:S(2)}) collective-permute-start(bf16[8,128,384]{2,1,0:T(8,128)(2,1)S(1)} %bitcast.15), channel_id=1, source_target_pairs={{0,32},{32,0},{1,33},{33,1},{2,34},{34,2},{3,35},{35,3},{4,36},{36... | collective-permute-start | bytes 2359304 | tf_op jit(solution)/shard_map/ppermute | solution.py:593
  147.8 1.7 %place.6 = (bf16[1024,1024]{1,0:T(8,128)(2,1)}, bf16[1024,1024]{1,0:T(8,128)(2,1)}, bf16[1024,1024]{1,0:T(8,128)(2,1)}, f32[8,128]{1,0:T(8,128)}) custom-call(s32[1]{0:T(128)} %bitcast.4.tag.side, s32[1]{0:T(128)} %bitcast.5.at_x, s32[1]{0:T(128)} %bitcast.6.at_z, ...), custom_call_target="tpu_custom_call", output_to_operand_aliasing={{0}: (4, {}), {1}: (5, {}), {2}: (6, {})} | custom-call | bytes 1572864 | tf_op jit(solution)/shard_map/place/pallas_call | solution.py:552
  149.5 0.2 collective-permute-done.12.refs_0_
  149.8 1.7 %place.7 = (bf16[1024,1024]{1,0:T(8,128)(2,1)}, bf16[1024,1024]{1,0:T(8,128)(2,1)}, bf16[1024,1024]{1,0:T(8,128)(2,1)}, f32[8,128]{1,0:T(8,128)}) custom-call(s32[1]{0:T(128)S(6)} %sub.3.side, s32[1]{0:T(128)} %bitcast.5.at_x, s32[1]{0:T(128)} %bitcast.6.at_z, ...), custom_call_target="tpu_custom_call", output_to_operand_aliasing={{0}: (4, {}), {1}: (5, {}), {2}: (6, {})} | custom-call | bytes 1572864 | tf_op jit(solution)/shard_map/place/pallas_call | solution.py:552
  (11 shorter events, 0.0 us)
Async XLA Ops:
  6.2 18.1 %collective-permute-start = (bf16[128,1024]{1,0:T(8,128)(2,1)}, bf16[128,1024]{1,0:T(8,128)(2,1)S(1)}, u32[]{:S(2)}, u32[]{:S(2)}) collective-permute-start(bf16[128,1024]{1,0:T(8,128)(2,1)} %get-tuple-element.41.tok), channel_id=1, source_target_pairs={{0,1},{1,2},{2,3},{3,4},{4,5},{5,6},{6,7},{7,8},{8,9},{9,10},{10,1... | collective-permute-start | bytes 786440 | tf_op jit(solution)/shard_map/ppermute | solution.py:623
  11.9 29.8 %all-to-all-start = ((bf16[128,16,128]{2,1,0:T(8,128)(2,1)}), bf16[128,16,128]{2,1,0:T(8,128)(2,1)S(1)}, u32[]{:S(2)}, u32[]{:S(2)}) async-start(bf16[128,16,128]{2,1,0:T(8,128)(2,1)} %bitcast.18), calls=%async_computation | async-start | bytes 1048576 | tf_op jit(solution)/shard_map/all_to_all | solution.py:624
  24.3 0.7 copy-start.3
  25.0 15.4 %copy-start = (bf16[128,1024]{1,0:T(8,128)(2,1)S(1)}, bf16[128,1024]{1,0:T(8,128)(2,1)}, u32[]{:S(2)}) copy-start(bf16[128,1024]{1,0:T(8,128)(2,1)} %get-tuple-element.41.tok) | copy-start | bytes 786436
  33.0 24.4 %collective-permute-start.1 = (bf16[2,128,1024]{2,1,0:T(8,128)(2,1)}, bf16[2,128,1024]{2,1,0:T(8,128)(2,1)S(1)}, u32[]{:S(2)}, u32[]{:S(2)}) collective-permute-start(bf16[2,128,1024]{2,1,0:T(8,128)(2,1)} %get-tuple-element.47), channel_id=1, source_target_pairs={{1,0},{2,1},{3,2},{4,3},{5,4},{6,5},{7,6},{8,7},{9,8},{10,9},{11,1... | collective-permute-start | bytes 1572872 | tf_op jit(solution)/shard_map/ppermute | solution.py:628
  43.5 13.9 %all-to-all-start.1 = ((bf16[128,8,128]{2,1,0:T(8,128)(2,1)}), bf16[128,8,128]{2,1,0:T(8,128)(2,1)S(1)}, u32[]{:S(2)}, u32[]{:S(2)}) async-start(bf16[128,8,128]{2,1,0:T(8,128)(2,1)} %bitcast.2), calls=%async_computation.1 | async-start | bytes 524288 | tf_op jit(solution)/shard_map/all_to_all | solution.py:632
  47.0 14.5 %collective-permute-start.2 = (bf16[1024,128]{1,0:T(8,128)(2,1)S(1)}, bf16[1024,128]{1,0:T(8,128)(2,1)S(1)}, u32[]{:S(2)}, u32[]{:S(2)}) collective-permute-start(bf16[1024,128]{1,0:T(8,128)(2,1)S(1)} %get-tuple-element.55.refs_0_), channel_id=1, source_target_pairs={{0,8},{8,16},{16,24},{24,0},{1,9},{9,17},{17,25},{25,1},{2,10},{10... | collective-permute-start | bytes 786440 | tf_op jit(solution)/shard_map/ppermute | solution.py:630
  47.6 15.6 %collective-permute-start.3 = (bf16[1024,128]{1,0:T(8,128)(2,1)S(1)}, bf16[1024,128]{1,0:T(8,128)(2,1)S(1)}, u32[]{:S(2)}, u32[]{:S(2)}) collective-permute-start(bf16[1024,128]{1,0:T(8,128)(2,1)S(1)} %get-tuple-element.55.refs_0_), channel_id=1, source_target_pairs={{0,16},{8,24},{16,0},{24,8},{1,17},{9,25},{17,1},{25,9},{2,18},{10... | collective-permute-start | bytes 786440 | tf_op jit(solution)/shard_map/ppermute | solution.py:630
  50.0 15.6 %collective-permute-start.4 = (bf16[1024,128]{1,0:T(8,128)(2,1)S(1)}, bf16[1024,128]{1,0:T(8,128)(2,1)S(1)}, u32[]{:S(2)}, u32[]{:S(2)}) collective-permute-start(bf16[1024,128]{1,0:T(8,128)(2,1)S(1)} %get-tuple-element.55.refs_0_), channel_id=1, source_target_pairs={{0,24},{8,0},{16,8},{24,16},{1,25},{9,1},{17,9},{25,17},{2,26},{10... | collective-permute-start | bytes 786440 | tf_op jit(solution)/shard_map/ppermute | solution.py:630
  57.3 0.7 copy-start.1
  57.3 0.9 copy-start.2
  65.7 18.8 %collective-permute-start.5 = (bf16[4,1024,128]{2,1,0:T(8,128)(2,1)S(1)}, bf16[4,1024,128]{2,1,0:T(8,128)(2,1)S(1)}, u32[]{:S(2)}, u32[]{:S(2)}) collective-permute-start(bf16[4,1024,128]{2,1,0:T(8,128)(2,1)S(1)} %stack.2.mine), channel_id=1, source_target_pairs={{0,32},{32,0},{1,33},{33,1},{2,34},{34,2},{3,35},{35,3},{4,36},{36... | collective-permute-start | bytes 3145736 | tf_op jit(solution)/shard_map/ppermute | solution.py:638
  67.0 17.5 %all-to-all-start.2 = ((bf16[8,128,384]{2,1,0:T(8,128)(2,1)}), bf16[8,128,384]{2,1,0:T(8,128)(2,1)S(1)}, u32[]{:S(2)}, u32[]{:S(2)}) async-start(bf16[8,128,384]{2,1,0:T(8,128)(2,1)} %get-tuple-element.52.delta.refs_4_), calls=%async_computation.2 | async-start | bytes 1572864 | tf_op jit(solution)/shard_map/all_to_all | solution.py:636
  117.8 6.8 %collective-permute-start.8 = (bf16[8,128,384]{2,1,0:T(8,128)(2,1)S(1)}, bf16[8,128,384]{2,1,0:T(8,128)(2,1)S(1)}, u32[]{:S(2)}, u32[]{:S(2)}) collective-permute-start(bf16[8,128,384]{2,1,0:T(8,128)(2,1)S(1)} %bitcast.10), channel_id=1, source_target_pairs={{0,32},{32,0},{1,33},{33,1},{2,34},{34,2},{3,35},{35,3},{4,36},{36... | collective-permute-start | bytes 2359304 | tf_op jit(solution)/shard_map/ppermute | solution.py:593
  121.9 12.3 %collective-permute-start.6 = (bf16[8,128,384]{2,1,0:T(8,128)(2,1)S(1)}, bf16[8,128,384]{2,1,0:T(8,128)(2,1)S(1)}, u32[]{:S(2)}, u32[]{:S(2)}) collective-permute-start(bf16[8,128,384]{2,1,0:T(8,128)(2,1)S(1)} %bitcast.11), channel_id=1, source_target_pairs={{0,8},{32,34},{1,9},{33,35},{2,10},{34,36},{3,11},{35,37},{4,12},{... | collective-permute-start | bytes 2359304 | tf_op jit(solution)/shard_map/ppermute | solution.py:504
  122.3 11.9 %collective-permute-start.7 = (bf16[8,128,384]{2,1,0:T(8,128)(2,1)S(1)}, bf16[8,128,384]{2,1,0:T(8,128)(2,1)S(1)}, u32[]{:S(2)}, u32[]{:S(2)}) collective-permute-start(bf16[8,128,384]{2,1,0:T(8,128)(2,1)S(1)} %bitcast.12), channel_id=1, source_target_pairs={{0,24},{32,38},{1,25},{33,39},{2,26},{34,32},{3,27},{35,33},{4,28}... | collective-permute-start | bytes 2359304 | tf_op jit(solution)/shard_map/ppermute | solution.py:504
  134.4 4.0 %collective-permute-start.11 = (bf16[16,128,384]{2,1,0:T(8,128)(2,1)S(1)}, bf16[16,128,384]{2,1,0:T(8,128)(2,1)S(1)}, u32[]{:S(2)}, u32[]{:S(2)}) collective-permute-start(bf16[16,128,384]{2,1,0:T(8,128)(2,1)S(1)} %get-tuple-element.59.refs_0_), channel_id=1, source_target_pairs={{0,32},{32,0},{1,33},{33,1},{2,34},{34,2},{3,35},{35,3},{4,36},{36... | collective-permute-start | bytes 4718600 | tf_op jit(solution)/shard_map/ppermute | solution.py:593
  135.4 6.9 %collective-permute-start.10 = (bf16[4,128,384]{2,1,0:T(8,128)(2,1)S(1)}, bf16[4,128,384]{2,1,0:T(8,128)(2,1)S(1)}, u32[]{:S(2)}, u32[]{:S(2)}) collective-permute-start(bf16[4,128,384]{2,1,0:T(8,128)(2,1)S(1)} %get-tuple-element.58), channel_id=1, source_target_pairs={{0,24},{32,38},{1,25},{33,39},{2,26},{34,32},{3,27},{35,33},{4,28}... | collective-permute-start | bytes 1179656 | tf_op jit(solution)/shard_map/ppermute | solution.py:504
  137.5 8.1 %collective-permute-start.9 = (bf16[4,128,384]{2,1,0:T(8,128)(2,1)S(1)}, bf16[4,128,384]{2,1,0:T(8,128)(2,1)S(1)}, u32[]{:S(2)}, u32[]{:S(2)}) collective-permute-start(bf16[4,128,384]{2,1,0:T(8,128)(2,1)S(1)} %get-tuple-element.57), channel_id=1, source_target_pairs={{0,8},{32,34},{1,9},{33,35},{2,10},{34,36},{3,11},{35,37},{4,12},{... | collective-permute-start | bytes 1179656 | tf_op jit(solution)/shard_map/ppermute | solution.py:504
  145.7 4.1 %collective-permute-start.12 = (bf16[8,128,384]{2,1,0:T(8,128)(2,1)S(1)}, bf16[8,128,384]{2,1,0:T(8,128)(2,1)S(1)}, u32[]{:S(2)}, u32[]{:S(2)}) collective-permute-start(bf16[8,128,384]{2,1,0:T(8,128)(2,1)S(1)} %bitcast.15), channel_id=1, source_target_pairs={{0,32},{32,0},{1,33},{33,1},{2,34},{34,2},{3,35},{35,3},{4,36},{36... | collective-permute-start | bytes 2359304 | tf_op jit(solution)/shard_map/ppermute | solution.py:593

commit v11 on v10

--- a/solution.py
+++ b/solution.py
@@ -19,6 +19,7 @@
 PAIR = 128
 DH = 64
 DEVS = 128
+BACK = (0, 2, 1, 3)
 VMEM = pltpu.VMEM
 HIGH = lax.Precision.HIGHEST
 
@@ -447,7 +448,7 @@
     for tokt, c in ((mine, core[0]), (theirs, 1 - core[0])):
         for i in range(near_x):
             left.append(tokt[i])
-            right.append(delta[c * near_x + lax.rem(at_x[0] + near_x - i, near_x)])
+            right.append(delta[c * near_x + lax.rem(at_x[0] + near_x - BACK[i], near_x)])
     left = jnp.concatenate(left, axis=1)
     out[...] = dot(left, jnp.concatenate(right, axis=0), 1, 0).astype(BF)
 
@@ -627,7 +628,7 @@
     )
     nxt = lax.ppermute(prev, AX, [(i + 1, i) for i in range(DEVS - 1)])
     tokt, place = flip(place, own_tokens)
-    around = [lax.ppermute(tokt, "x", [(i, (i + d) % 4) for i in range(4)]) for d in (1, 2, 3)]
+    around = [lax.ppermute(tokt, "x", [(i, (i + d) % 4) for i in range(4)]) for d in BACK[1:]]
     states = scan(place, got)
     states = lax.all_to_all(states.reshape(DEVS, 8, PAIR), AX, 0, 0)
     states = states.reshape(2, width // PAIR, DH, PAIR)

time: 152 us -> 152 us (level)
  no operation moved by 1% of the time
where the time goes in v11:
time: 152 us; the launch traced here: 151 us
  starting transfers between devices  49.6 us (33%)
  Pallas kernels  35.3 us (23%)
  waiting for transfers between devices  33 us (22%)
  blocking collectives  30.8 us (20%)
  local copies, waits for them, and re-layouts  1.72 us (1%)
    all_to_all x1, blocking collectives, shards(): lax.all_to_all(partial.reshape(16, width // 16, 3 * PAIR), FAR16, 0, 0)  17.3 us
    all_to_all x1, blocking collectives, gather_tiles(): lax.all_to_all(jnp.broadcast_to(piece[None], (16, rows, cols)), AX, 0, 0,...  13.6 us
    ppermute x4, waiting for transfers between devices, ring(): return lax.ppermute(array, AX, route)  12.8 us
    all_to_all x1, starting transfers between devices, shards(): got = lax.all_to_all(msg.reshape(DEVS, 16, PAIR), AX, 0, 0)  9.71 us
    pallas_call x1, Pallas kernels, near(): pl.pallas_call(functools.partial(near_kernel, lin_scale), grid=(width //...  7.96 us
    ppermute x1, starting transfers between devices, shards(): nxt = lax.ppermute(prev, AX, [(i + 1, i) for i in range(DEVS - 1)])  7.42 us
    pallas_call x4, Pallas kernels, place_tiles(): pl.pallas_call(functools.partial(place_kernel, pieces, len(sources)), in_...  7.32 us
    ppermute x3, starting transfers between devices, swapped(): return lax.ppermute(array, 'c', swap)  7.16 us
  transfers between devices with their start and end apart: 16, of which 10 were waited for; matrix products, arithmetic and copies ran while one was open for 0% of the time, Pallas kernels for 17%

profile of v11, /device:TPU:1, one launch (start us, length us, event | category | flops | bytes accessed | tf_op | source)
XLA Modules:
  0.0 151.4 jit_solution(12398966890591046882)
XLA Ops:
  0.6 5.6 %project.1 = (bf16[128,1024]{1,0:T(8,128)(2,1)}, bf16[2,128,1024]{2,1,0:T(8,128)(2,1)}, f32[4,4,128]{2,1,0:T(4,128)}, f32[4,128,4]{2,1,0:T(8,128)}, bf16[2,1024,...) custom-call(bf16[128,1024]{1,0:T(8,128)(2,1)} %tok.1, bf16[1024,1024]{1,0:T(8,128)(2,1)} %wq.3, bf16[1024,1024]{1,0:T(8,128)(2,1)} %wk.5, ...), custom_call_target="tpu_custom_call" | custom-call | flops 805306368 | bytes 7864320 | tf_op jit(solution)/shard_map/project/pallas_call | solution.py:126
  6.2 5.7 %collective-permute-start = (bf16[128,1024]{1,0:T(8,128)(2,1)}, bf16[128,1024]{1,0:T(8,128)(2,1)S(1)}, u32[]{:S(2)}, u32[]{:S(2)}) collective-permute-start(bf16[128,1024]{1,0:T(8,128)(2,1)} %get-tuple-element.41.tok), channel_id=1, source_target_pairs={{0,1},{1,2},{2,3},{3,4},{4,5},{5,6},{6,7},{7,8},{8,9},{9,10},{10,1... | collective-permute-start | bytes 786440 | tf_op jit(solution)/shard_map/ppermute | solution.py:624
  11.9 9.7 %all-to-all-start = ((bf16[128,16,128]{2,1,0:T(8,128)(2,1)}), bf16[128,16,128]{2,1,0:T(8,128)(2,1)S(1)}, u32[]{:S(2)}, u32[]{:S(2)}) async-start(bf16[128,16,128]{2,1,0:T(8,128)(2,1)} %bitcast.18), calls=%async_computation | async-start | bytes 1048576 | tf_op jit(solution)/shard_map/all_to_all | solution.py:625
  21.6 2.7 %collective-permute-done.ptok = bf16[128,1024]{1,0:T(8,128)(2,1)S(1)} collective-permute-done((bf16[128,1024]{1,0:T(8,128)(2,1)}, bf16[128,1024]{1,0:T(8,128)(2,1)S(1)}, u32[]{:S(2)}, u32[]{:S(2)}) %collective-permute-start) | collective-permute-done | bytes 262176 | tf_op jit(solution)/shard_map/ppermute | solution.py:624
  24.3 0.7 copy-done.3
  25.0 8.0 %near.1 = (f32[128,1024]{1,0:T(8,128)}, f32[128,1024]{1,0:T(8,128)}, f32[2,128,1024]{2,1,0:T(8,128)}, bf16[2,128,1024]{2,1,0:T(8,128)(2,1)}, s32[1]{0:T(128)}) custom-call(s32[1]{0:T(128)} %bitcast.place, s32[1,4]{1,0:T(1,128)} %blocks.1, bf16[128,1024]{1,0:T(8,128)(2,1)} %get-tuple-element.39.q_ref.q, bf16[2,128,1024]{2,1,0:T(8,128)(2,1)} %get-tuple-element.40.kv, ...), custom_call_target="tpu_custom_call" | custom-call | flops 4000000000 | bytes 16000000 | tf_op jit(solution)/shard_map/near/pallas_call | solution.py:298
  33.0 7.4 %collective-permute-start.1 = (bf16[2,128,1024]{2,1,0:T(8,128)(2,1)}, bf16[2,128,1024]{2,1,0:T(8,128)(2,1)S(1)}, u32[]{:S(2)}, u32[]{:S(2)}) collective-permute-start(bf16[2,128,1024]{2,1,0:T(8,128)(2,1)} %get-tuple-element.47), channel_id=1, source_target_pairs={{1,0},{2,1},{3,2},{4,3},{5,4},{6,5},{7,6},{8,7},{9,8},{10,9},{11,1... | collective-permute-start | bytes 1572872 | tf_op jit(solution)/shard_map/ppermute | solution.py:629
  40.4 1.2 flip.1
  41.6 1.8 %scan.1 = bf16[1024,128]{1,0:T(8,128)(2,1)} custom-call(s32[1]{0:T(128)} %get-tuple-element.49.place, bf16[128,16,128]{2,1,0:T(8,128)(2,1)S(1)} %all-to-all-done.got), custom_call_target="tpu_custom_call" | custom-call | flops 262144 | bytes 1048576 | tf_op jit(solution)/shard_map/scan/pallas_call | solution.py:209
  43.5 3.5 %all-to-all-start.1 = ((bf16[128,8,128]{2,1,0:T(8,128)(2,1)}), bf16[128,8,128]{2,1,0:T(8,128)(2,1)S(1)}, u32[]{:S(2)}, u32[]{:S(2)}) async-start(bf16[128,8,128]{2,1,0:T(8,128)(2,1)} %bitcast.2), calls=%async_computation.1 | async-start | bytes 524288 | tf_op jit(solution)/shard_map/all_to_all | solution.py:633
  47.0 2.1 %collective-permute-start.2 = (bf16[1024,128]{1,0:T(8,128)(2,1)S(1)}, bf16[1024,128]{1,0:T(8,128)(2,1)S(1)}, u32[]{:S(2)}, u32[]{:S(2)}) collective-permute-start(bf16[1024,128]{1,0:T(8,128)(2,1)S(1)} %get-tuple-element.55.refs_0_), channel_id=1, source_target_pairs={{0,16},{8,24},{16,0},{24,8},{1,17},{9,25},{17,1},{25,9},{2,18},{10... | collective-permute-start | bytes 786440 | tf_op jit(solution)/shard_map/ppermute | solution.py:631
  49.1 0.3 collective-permute-start.3
  49.4 2.4 %collective-permute-start.4 = (bf16[1024,128]{1,0:T(8,128)(2,1)S(1)}, bf16[1024,128]{1,0:T(8,128)(2,1)S(1)}, u32[]{:S(2)}, u32[]{:S(2)}) collective-permute-start(bf16[1024,128]{1,0:T(8,128)(2,1)S(1)} %get-tuple-element.55.refs_0_), channel_id=1, source_target_pairs={{0,24},{8,0},{16,8},{24,16},{1,25},{9,1},{17,9},{25,17},{2,26},{10... | collective-permute-start | bytes 786440 | tf_op jit(solution)/shard_map/ppermute | solution.py:631
  51.8 5.1 %all-to-all-done.1 = bf16[128,8,128]{2,1,0:T(8,128)(2,1)S(1)} async-done(((bf16[128,8,128]{2,1,0:T(8,128)(2,1)}), bf16[128,8,128]{2,1,0:T(8,128)(2,1)S(1)}, u32[]{:S(2)}, u32[]{:S(2)}) %all-to-all-start.1) | async-done | bytes 262176 | tf_op jit(solution)/shard_map/all_to_all | solution.py:633
  56.9 0.0 collective-permute-done.1.nxt
  56.9 0.7 copy-done.1
  57.6 0.2 copy-done.2
  57.8 3.3 %join.1 = (bf16[128,1024]{1,0:T(8,128)(2,1)}, bf16[8,128,384]{2,1,0:T(8,128)(2,1)}) custom-call(f32[128,1024]{1,0:T(8,128)} %get-tuple-element.44.near_out, f32[128,1024]{1,0:T(8,128)} %get-tuple-element.45.dq_in, f32[2,128,1024]{2,1,0:T(8,128)} %get-tuple-element.46.own, bf16[2,128,1024]{2,1,0:T(8,128)(2,1)} %copy-done.2, ...), custom_call_target="tpu_custom_call" | custom-call | flops 134217728 | bytes 3145728 | tf_op jit(solution)/shard_map/join/pallas_call | solution.py:372
  61.1 2.5 %collective-permute-done.3.refs_2_ = bf16[1024,128]{1,0:T(8,128)(2,1)S(1)} collective-permute-done((bf16[1024,128]{1,0:T(8,128)(2,1)S(1)}, bf16[1024,128]{1,0:T(8,128)(2,1)S(1)}, u32[]{:S(2)}, u32[]{:S(2)}) %collective-permute-start.3) | collective-permute-done | bytes 262176 | tf_op jit(solution)/shard_map/ppermute | solution.py:631
  63.6 2.0 %collective-permute-done.4.refs_3_ = bf16[1024,128]{1,0:T(8,128)(2,1)S(1)} collective-permute-done((bf16[1024,128]{1,0:T(8,128)(2,1)S(1)}, bf16[1024,128]{1,0:T(8,128)(2,1)S(1)}, u32[]{:S(2)}, u32[]{:S(2)}) %collective-permute-start.4) | collective-permute-done | bytes 262176 | tf_op jit(solution)/shard_map/ppermute | solution.py:631
  65.6 0.1 stack.2.mine
  65.7 1.3 collective-permute-start.5
  67.0 5.3 %all-to-all-start.2 = ((bf16[8,128,384]{2,1,0:T(8,128)(2,1)}), bf16[8,128,384]{2,1,0:T(8,128)(2,1)S(1)}, u32[]{:S(2)}, u32[]{:S(2)}) async-start(bf16[8,128,384]{2,1,0:T(8,128)(2,1)} %get-tuple-element.52.delta.refs_4_), calls=%async_computation.2 | async-start | bytes 1572864 | tf_op jit(solution)/shard_map/all_to_all | solution.py:637
  72.3 5.6 %back.1 = (bf16[128,1024]{1,0:T(8,128)(2,1)}, s32[1]{0:T(128)}) custom-call(s32[1]{0:T(128)} %bitcast.4.tag.side, bf16[8,128,384]{2,1,0:T(8,128)(2,1)} %get-tuple-element.52.delta.refs_4_, bf16[1024,1024]{1,0:T(8,128)(2,1)} %wq.3, bf16[1024,1024]{1,0:T(8,128)(2,1)} %wk.5, bf16[1024,1024]{1,0:T(8,128)(2,1)} %wv.5), custom_call_target="tpu_custom_call" | custom-call | flops 805306368 | bytes 7340032 | tf_op jit(solution)/shard_map/back/pallas_call | solution.py:426
  77.9 6.6 %all-to-all-done.2.delta = bf16[8,128,384]{2,1,0:T(8,128)(2,1)S(1)} async-done(((bf16[8,128,384]{2,1,0:T(8,128)(2,1)}), bf16[8,128,384]{2,1,0:T(8,128)(2,1)S(1)}, u32[]{:S(2)}, u32[]{:S(2)}) %all-to-all-start.2) | async-done | bytes 786464 | tf_op jit(solution)/shard_map/all_to_all | solution.py:637
  84.5 0.0 collective-permute-done.5.theirs
  84.5 2.3 %outer.1 = bf16[1024,384]{1,0:T(8,128)(2,1)S(1)} custom-call(s32[1]{0:T(128)} %get-tuple-element.54.core, s32[1]{0:T(128)} %bitcast.5.at_x, bf16[4,1024,128]{2,1,0:T(8,128)(2,1)S(1)} %stack.2.mine, bf16[4,1024,128]{2,1,0:T(8,128)(2,1)S(1)} %collective-permute-done.5.theirs, bf16[8,128,384]{2,1,0:T(8,128)(2,1)S(1)} %all-to-all-done.2.delta), custom_call_target="tpu_custom_call" | custom-call | flops 805306368 | bytes 2883584 | tf_op jit(solution)/shard_map/outer/pallas_call | solution.py:461
  86.7 17.3 %all_to_all.25 = bf16[16,64,384]{2,1,0:T(8,128)(2,1)S(1)} all-to-all(bf16[16,64,384]{2,1,0:T(8,128)(2,1)S(1)} %bitcast.14), channel_id=1, replica_groups=mesh['yl'=2,'c'=2,'x'=4,'z'=4,'yh'=2] {'yl','z','yh'}, dimensions={0} | all-to-all | bytes 1572864 | tf_op jit(solution)/shard_map/all_to_all | solution.py:642
  104.0 0.1 convert_reduce_fusion
  104.2 0.1 broadcast_in_dim.2
  104.3 13.6 %all_to_all.26 = bf16[16,64,384]{2,1,0:T(8,128)(2,1)S(1)} all-to-all(bf16[16,64,384]{2,1,0:T(8,128)(2,1)S(1)} %broadcast_in_dim.2), channel_id=1, replica_groups={{0,1,2,3,4,5,6,7,64,65,66,67,68,69,70,71},{8,9,10,11,12,13,14,15,72,73,..., dimensions={0} | all-to-all | bytes 1572864 | tf_op jit(solution)/shard_map/all_to_all | solution.py:597
  117.8 4.1 %collective-permute-start.8 = (bf16[8,128,384]{2,1,0:T(8,128)(2,1)S(1)}, bf16[8,128,384]{2,1,0:T(8,128)(2,1)S(1)}, u32[]{:S(2)}, u32[]{:S(2)}) collective-permute-start(bf16[8,128,384]{2,1,0:T(8,128)(2,1)S(1)} %bitcast.10), channel_id=1, source_target_pairs={{0,32},{32,0},{1,33},{33,1},{2,34},{34,2},{3,35},{35,3},{4,36},{36... | collective-permute-start | bytes 2359304 | tf_op jit(solution)/shard_map/ppermute | solution.py:594
  121.9 0.4 collective-permute-start.6
  122.3 2.2 %collective-permute-start.7 = (bf16[8,128,384]{2,1,0:T(8,128)(2,1)S(1)}, bf16[8,128,384]{2,1,0:T(8,128)(2,1)S(1)}, u32[]{:S(2)}, u32[]{:S(2)}) collective-permute-start(bf16[8,128,384]{2,1,0:T(8,128)(2,1)S(1)} %bitcast.12), channel_id=1, source_target_pairs={{0,24},{32,38},{1,25},{33,39},{2,26},{34,32},{3,27},{35,33},{4,28}... | collective-permute-start | bytes 2359304 | tf_op jit(solution)/shard_map/ppermute | solution.py:505
  124.6 1.5 %place.4 = (bf16[1024,1024]{1,0:T(8,128)(2,1)}, bf16[1024,1024]{1,0:T(8,128)(2,1)}, bf16[1024,1024]{1,0:T(8,128)(2,1)}, f32[8,128]{1,0:T(8,128)S(1)}) custom-call(s32[1]{0:T(128)} %bitcast.4.tag.side, s32[1]{0:T(128)} %bitcast.5.at_x, s32[1]{0:T(128)} %bitcast.6.at_z, bf16[8,128,384]{2,1,0:T(8,128)(2,1)S(1)} %bitcast.13, ...), custom_call_target="tpu_custom_call" | custom-call | bytes 3145728 | tf_op jit(solution)/shard_map/place/pallas_call | solution.py:553
  126.1 8.1 %collective-permute-done.6.behind = bf16[8,128,384]{2,1,0:T(8,128)(2,1)S(1)} collective-permute-done((bf16[8,128,384]{2,1,0:T(8,128)(2,1)S(1)}, bf16[8,128,384]{2,1,0:T(8,128)(2,1)S(1)}, u32[]{:S(2)}, u32[]{:S(2)}) %collective-permute-start.6) | collective-permute-done | bytes 786464 | tf_op jit(solution)/shard_map/ppermute | solution.py:505
  134.2 0.2 halves.1
  134.4 0.9 collective-permute-start.11
  135.4 2.1 %collective-permute-start.10 = (bf16[4,128,384]{2,1,0:T(8,128)(2,1)S(1)}, bf16[4,128,384]{2,1,0:T(8,128)(2,1)S(1)}, u32[]{:S(2)}, u32[]{:S(2)}) collective-permute-start(bf16[4,128,384]{2,1,0:T(8,128)(2,1)S(1)} %get-tuple-element.58), channel_id=1, source_target_pairs={{0,24},{32,38},{1,25},{33,39},{2,26},{34,32},{3,27},{35,33},{4,28}... | collective-permute-start | bytes 1179656 | tf_op jit(solution)/shard_map/ppermute | solution.py:505
  137.5 0.9 collective-permute-done.11.refs_1_
  138.4 2.5 %place.5 = (bf16[1024,1024]{1,0:T(8,128)(2,1)}, bf16[1024,1024]{1,0:T(8,128)(2,1)}, bf16[1024,1024]{1,0:T(8,128)(2,1)}, f32[8,128]{1,0:T(8,128)S(1)}) custom-call(s32[1]{0:T(128)} %bitcast.4.tag.side, s32[1]{0:T(128)} %bitcast.5.at_x, s32[1]{0:T(128)} %bitcast.6.at_z, ...), custom_call_target="tpu_custom_call", output_to_operand_aliasing={{0}: (5, {}), {1}: (6, {}), {2}: (7, {})} | custom-call | bytes 6291456 | tf_op jit(solution)/shard_map/place/pallas_call | solution.py:553
  140.9 1.4 collective-permute-done.10.refs_1_
  142.3 3.3 %collective-permute-done.9.refs_0_ = bf16[4,128,384]{2,1,0:T(8,128)(2,1)S(1)} collective-permute-done((bf16[4,128,384]{2,1,0:T(8,128)(2,1)S(1)}, bf16[4,128,384]{2,1,0:T(8,128)(2,1)S(1)}, u32[]{:S(2)}, u32[]{:S(2)}) %collective-permute-start.9) | collective-permute-done | bytes 393248 | tf_op jit(solution)/shard_map/ppermute | solution.py:505
  145.6 0.1 stack.3
  145.7 2.1 %collective-permute-start.12 = (bf16[8,128,384]{2,1,0:T(8,128)(2,1)S(1)}, bf16[8,128,384]{2,1,0:T(8,128)(2,1)S(1)}, u32[]{:S(2)}, u32[]{:S(2)}) collective-permute-start(bf16[8,128,384]{2,1,0:T(8,128)(2,1)S(1)} %bitcast.15), channel_id=1, source_target_pairs={{0,32},{32,0},{1,33},{33,1},{2,34},{34,2},{3,35},{35,3},{4,36},{36... | collective-permute-start | bytes 2359304 | tf_op jit(solution)/shard_map/ppermute | solution.py:594
  147.8 1.7 %place.6 = (bf16[1024,1024]{1,0:T(8,128)(2,1)}, bf16[1024,1024]{1,0:T(8,128)(2,1)}, bf16[1024,1024]{1,0:T(8,128)(2,1)}, f32[8,128]{1,0:T(8,128)}) custom-call(s32[1]{0:T(128)} %bitcast.4.tag.side, s32[1]{0:T(128)} %bitcast.5.at_x, s32[1]{0:T(128)} %bitcast.6.at_z, ...), custom_call_target="tpu_custom_call", output_to_operand_aliasing={{0}: (4, {}), {1}: (5, {}), {2}: (6, {})} | custom-call | bytes 1572864 | tf_op jit(solution)/shard_map/place/pallas_call | solution.py:553
  149.5 0.2 collective-permute-done.12.refs_0_
  149.8 1.7 %place.7 = (bf16[1024,1024]{1,0:T(8,128)(2,1)}, bf16[1024,1024]{1,0:T(8,128)(2,1)}, bf16[1024,1024]{1,0:T(8,128)(2,1)}, f32[8,128]{1,0:T(8,128)}) custom-call(s32[1]{0:T(128)S(6)} %sub.3.side, s32[1]{0:T(128)} %bitcast.5.at_x, s32[1]{0:T(128)} %bitcast.6.at_z, ...), custom_call_target="tpu_custom_call", output_to_operand_aliasing={{0}: (4, {}), {1}: (5, {}), {2}: (6, {})} | custom-call | bytes 1572864 | tf_op jit(solution)/shard_map/place/pallas_call | solution.py:553
  (11 shorter events, 0.0 us)
Async XLA Ops:
  6.2 18.1 %collective-permute-start = (bf16[128,1024]{1,0:T(8,128)(2,1)}, bf16[128,1024]{1,0:T(8,128)(2,1)S(1)}, u32[]{:S(2)}, u32[]{:S(2)}) collective-permute-start(bf16[128,1024]{1,0:T(8,128)(2,1)} %get-tuple-element.41.tok), channel_id=1, source_target_pairs={{0,1},{1,2},{2,3},{3,4},{4,5},{5,6},{6,7},{7,8},{8,9},{9,10},{10,1... | collective-permute-start | bytes 786440 | tf_op jit(solution)/shard_map/ppermute | solution.py:624
  11.9 29.8 %all-to-all-start = ((bf16[128,16,128]{2,1,0:T(8,128)(2,1)}), bf16[128,16,128]{2,1,0:T(8,128)(2,1)S(1)}, u32[]{:S(2)}, u32[]{:S(2)}) async-start(bf16[128,16,128]{2,1,0:T(8,128)(2,1)} %bitcast.18), calls=%async_computation | async-start | bytes 1048576 | tf_op jit(solution)/shard_map/all_to_all | solution.py:625
  24.3 0.7 copy-start.3
  25.0 15.4 %copy-start = (bf16[128,1024]{1,0:T(8,128)(2,1)S(1)}, bf16[128,1024]{1,0:T(8,128)(2,1)}, u32[]{:S(2)}) copy-start(bf16[128,1024]{1,0:T(8,128)(2,1)} %get-tuple-element.41.tok) | copy-start | bytes 786436
  33.0 23.9 %collective-permute-start.1 = (bf16[2,128,1024]{2,1,0:T(8,128)(2,1)}, bf16[2,128,1024]{2,1,0:T(8,128)(2,1)S(1)}, u32[]{:S(2)}, u32[]{:S(2)}) collective-permute-start(bf16[2,128,1024]{2,1,0:T(8,128)(2,1)} %get-tuple-element.47), channel_id=1, source_target_pairs={{1,0},{2,1},{3,2},{4,3},{5,4},{6,5},{7,6},{8,7},{9,8},{10,9},{11,1... | collective-permute-start | bytes 1572872 | tf_op jit(solution)/shard_map/ppermute | solution.py:629
  43.5 13.4 %all-to-all-start.1 = ((bf16[128,8,128]{2,1,0:T(8,128)(2,1)}), bf16[128,8,128]{2,1,0:T(8,128)(2,1)S(1)}, u32[]{:S(2)}, u32[]{:S(2)}) async-start(bf16[128,8,128]{2,1,0:T(8,128)(2,1)} %bitcast.2), calls=%async_computation.1 | async-start | bytes 524288 | tf_op jit(solution)/shard_map/all_to_all | solution.py:633
  47.0 14.1 %collective-permute-start.2 = (bf16[1024,128]{1,0:T(8,128)(2,1)S(1)}, bf16[1024,128]{1,0:T(8,128)(2,1)S(1)}, u32[]{:S(2)}, u32[]{:S(2)}) collective-permute-start(bf16[1024,128]{1,0:T(8,128)(2,1)S(1)} %get-tuple-element.55.refs_0_), channel_id=1, source_target_pairs={{0,16},{8,24},{16,0},{24,8},{1,17},{9,25},{17,1},{25,9},{2,18},{10... | collective-permute-start | bytes 786440 | tf_op jit(solution)/shard_map/ppermute | solution.py:631
  49.1 14.5 %collective-permute-start.3 = (bf16[1024,128]{1,0:T(8,128)(2,1)S(1)}, bf16[1024,128]{1,0:T(8,128)(2,1)S(1)}, u32[]{:S(2)}, u32[]{:S(2)}) collective-permute-start(bf16[1024,128]{1,0:T(8,128)(2,1)S(1)} %get-tuple-element.55.refs_0_), channel_id=1, source_target_pairs={{0,8},{8,16},{16,24},{24,0},{1,9},{9,17},{17,25},{25,1},{2,10},{10... | collective-permute-start | bytes 786440 | tf_op jit(solution)/shard_map/ppermute | solution.py:631
  49.4 16.2 %collective-permute-start.4 = (bf16[1024,128]{1,0:T(8,128)(2,1)S(1)}, bf16[1024,128]{1,0:T(8,128)(2,1)S(1)}, u32[]{:S(2)}, u32[]{:S(2)}) collective-permute-start(bf16[1024,128]{1,0:T(8,128)(2,1)S(1)} %get-tuple-element.55.refs_0_), channel_id=1, source_target_pairs={{0,24},{8,0},{16,8},{24,16},{1,25},{9,1},{17,9},{25,17},{2,26},{10... | collective-permute-start | bytes 786440 | tf_op jit(solution)/shard_map/ppermute | solution.py:631
  56.9 0.7 copy-start.1
  56.9 0.9 copy-start.2
  65.7 18.7 %collective-permute-start.5 = (bf16[4,1024,128]{2,1,0:T(8,128)(2,1)S(1)}, bf16[4,1024,128]{2,1,0:T(8,128)(2,1)S(1)}, u32[]{:S(2)}, u32[]{:S(2)}) collective-permute-start(bf16[4,1024,128]{2,1,0:T(8,128)(2,1)S(1)} %stack.2.mine), channel_id=1, source_target_pairs={{0,32},{32,0},{1,33},{33,1},{2,34},{34,2},{3,35},{35,3},{4,36},{36... | collective-permute-start | bytes 3145736 | tf_op jit(solution)/shard_map/ppermute | solution.py:639
  67.0 17.5 %all-to-all-start.2 = ((bf16[8,128,384]{2,1,0:T(8,128)(2,1)}), bf16[8,128,384]{2,1,0:T(8,128)(2,1)S(1)}, u32[]{:S(2)}, u32[]{:S(2)}) async-start(bf16[8,128,384]{2,1,0:T(8,128)(2,1)} %get-tuple-element.52.delta.refs_4_), calls=%async_computation.2 | async-start | bytes 1572864 | tf_op jit(solution)/shard_map/all_to_all | solution.py:637
  117.8 6.8 %collective-permute-start.8 = (bf16[8,128,384]{2,1,0:T(8,128)(2,1)S(1)}, bf16[8,128,384]{2,1,0:T(8,128)(2,1)S(1)}, u32[]{:S(2)}, u32[]{:S(2)}) collective-permute-start(bf16[8,128,384]{2,1,0:T(8,128)(2,1)S(1)} %bitcast.10), channel_id=1, source_target_pairs={{0,32},{32,0},{1,33},{33,1},{2,34},{34,2},{3,35},{35,3},{4,36},{36... | collective-permute-start | bytes 2359304 | tf_op jit(solution)/shard_map/ppermute | solution.py:594
  121.9 12.3 %collective-permute-start.6 = (bf16[8,128,384]{2,1,0:T(8,128)(2,1)S(1)}, bf16[8,128,384]{2,1,0:T(8,128)(2,1)S(1)}, u32[]{:S(2)}, u32[]{:S(2)}) collective-permute-start(bf16[8,128,384]{2,1,0:T(8,128)(2,1)S(1)} %bitcast.11), channel_id=1, source_target_pairs={{0,8},{32,34},{1,9},{33,35},{2,10},{34,36},{3,11},{35,37},{4,12},{... | collective-permute-start | bytes 2359304 | tf_op jit(solution)/shard_map/ppermute | solution.py:505
  122.3 11.9 %collective-permute-start.7 = (bf16[8,128,384]{2,1,0:T(8,128)(2,1)S(1)}, bf16[8,128,384]{2,1,0:T(8,128)(2,1)S(1)}, u32[]{:S(2)}, u32[]{:S(2)}) collective-permute-start(bf16[8,128,384]{2,1,0:T(8,128)(2,1)S(1)} %bitcast.12), channel_id=1, source_target_pairs={{0,24},{32,38},{1,25},{33,39},{2,26},{34,32},{3,27},{35,33},{4,28}... | collective-permute-start | bytes 2359304 | tf_op jit(solution)/shard_map/ppermute | solution.py:505
  134.4 4.0 %collective-permute-start.11 = (bf16[16,128,384]{2,1,0:T(8,128)(2,1)S(1)}, bf16[16,128,384]{2,1,0:T(8,128)(2,1)S(1)}, u32[]{:S(2)}, u32[]{:S(2)}) collective-permute-start(bf16[16,128,384]{2,1,0:T(8,128)(2,1)S(1)} %get-tuple-element.59.refs_0_), channel_id=1, source_target_pairs={{0,32},{32,0},{1,33},{33,1},{2,34},{34,2},{3,35},{35,3},{4,36},{36... | collective-permute-start | bytes 4718600 | tf_op jit(solution)/shard_map/ppermute | solution.py:594
  135.4 6.9 %collective-permute-start.10 = (bf16[4,128,384]{2,1,0:T(8,128)(2,1)S(1)}, bf16[4,128,384]{2,1,0:T(8,128)(2,1)S(1)}, u32[]{:S(2)}, u32[]{:S(2)}) collective-permute-start(bf16[4,128,384]{2,1,0:T(8,128)(2,1)S(1)} %get-tuple-element.58), channel_id=1, source_target_pairs={{0,24},{32,38},{1,25},{33,39},{2,26},{34,32},{3,27},{35,33},{4,28}... | collective-permute-start | bytes 1179656 | tf_op jit(solution)/shard_map/ppermute | solution.py:505
  137.5 8.1 %collective-permute-start.9 = (bf16[4,128,384]{2,1,0:T(8,128)(2,1)S(1)}, bf16[4,128,384]{2,1,0:T(8,128)(2,1)S(1)}, u32[]{:S(2)}, u32[]{:S(2)}) collective-permute-start(bf16[4,128,384]{2,1,0:T(8,128)(2,1)S(1)} %get-tuple-element.57), channel_id=1, source_target_pairs={{0,8},{32,34},{1,9},{33,35},{2,10},{34,36},{3,11},{35,37},{4,12},{... | collective-permute-start | bytes 1179656 | tf_op jit(solution)/shard_map/ppermute | solution.py:505
  145.7 4.1 %collective-permute-start.12 = (bf16[8,128,384]{2,1,0:T(8,128)(2,1)S(1)}, bf16[8,128,384]{2,1,0:T(8,128)(2,1)S(1)}, u32[]{:S(2)}, u32[]{:S(2)}) collective-permute-start(bf16[8,128,384]{2,1,0:T(8,128)(2,1)S(1)} %bitcast.15), channel_id=1, source_target_pairs={{0,32},{32,0},{1,33},{33,1},{2,34},{34,2},{3,35},{35,3},{4,36},{36... | collective-permute-start | bytes 2359304 | tf_op jit(solution)/shard_map/ppermute | solution.py:594

commit v12 on v9

--- a/solution.py
+++ b/solution.py
@@ -518,21 +518,23 @@
 
         for n in range(count):
             source = refs[n]
-            rows = source.shape[1]
             by_row = rank[n]
             for place, by in enumerate(pieces):
                 x = lax.rem(at_x[0] + by + 4, 4)
                 z = lax.rem(at_z[0] + by + 4, 4)
                 for part, grad in enumerate(grads):
                     lanes = pl.ds(part * PAIR, PAIR)
-                    for i in range(8):
-                        if by_row:
-                            to = pl.multiple_of(((i % 2) * 4 + z) * rows, rows)
-                            at = (pl.ds(to, rows), pl.ds((4 + i // 2) * PAIR, PAIR))
-                        else:
-                            to = pl.multiple_of(x * PAIR, PAIR)
-                            at = (pl.ds(i * rows, rows), pl.ds(to, PAIR))
-                        start(source.at[place * 8 + i, :, lanes], grad.at[at])
+                    if by_row:
+                        for i in range(8):
+                            start(
+                                source.at[place * 8 + i, :, lanes],
+                                grad.at[(i % 2) * 4 + z, :, pl.ds((4 + i // 2) * PAIR, PAIR)],
+                            )
+                    else:
+                        start(
+                            source.at[pl.ds(place * 8, 8), :, lanes],
+                            grad.at[:, :, pl.ds(pl.multiple_of(x * PAIR, PAIR), PAIR)],
+                        )
         for copy in copies:
             copy.wait()
 
@@ -553,7 +555,7 @@
         functools.partial(place_kernel, pieces, len(sources)),
         in_specs=[smem] * 3 + [hbm] * (len(sources) + len(grads)),
         out_specs=[hbm] * 3 + [pl.BlockSpec(memory_space=VMEM)],
-        out_shape=[jax.ShapeDtypeStruct((width, width), BF)] * 3
+        out_shape=[jax.ShapeDtypeStruct((8, width // 8, width), BF)] * 3
         + [jax.ShapeDtypeStruct((8, PAIR), F32)],
         scratch_shapes=[pltpu.SemaphoreType.DMA((24 * len(pieces) * len(sources),))],
         input_output_aliases={first + i: i for i in range(len(grads))},
@@ -608,7 +610,7 @@
     *grads, _ = place_tiles(where, (2,), (far,), grads, width)
     core, *rest = where
     *grads, _ = place_tiles((1 - core, *rest), (2,), (far_c,), grads, width)
-    return grads
+    return [grad.reshape(width, width) for grad in grads]
 
 
 def shards(tokens, wq, wk, wv, log_decay, neighbour_blocks, cot):

time: 152 us -> 152 us (level)
  no operation moved by 1% of the time
where the time goes in v12:
time: 152 us; the launch traced here: 151 us
  starting transfers between devices  48.7 us (32%)
  Pallas kernels  35.5 us (23%)
  waiting for transfers between devices  34.2 us (23%)
  blocking collectives  30.1 us (20%)
  local copies, waits for them, and re-layouts  1.72 us (1%)
    all_to_all x1, blocking collectives, shards(): lax.all_to_all(partial.reshape(16, width // 16, 3 * PAIR), FAR16, 0, 0)  16.6 us
    all_to_all x1, blocking collectives, gather_tiles(): lax.all_to_all(jnp.broadcast_to(piece[None], (16, rows, cols)), AX, 0, 0,...  13.6 us
    ppermute x4, waiting for transfers between devices, ring(): return lax.ppermute(array, AX, route)  12.8 us
    all_to_all x1, starting transfers between devices, shards(): got = lax.all_to_all(msg.reshape(DEVS, 16, PAIR), AX, 0, 0)  9.71 us
    pallas_call x1, Pallas kernels, near(): pl.pallas_call(functools.partial(near_kernel, lin_scale), grid=(width //...  7.96 us
    ppermute x1, starting transfers between devices, shards(): nxt = lax.ppermute(prev, AX, [(i + 1, i) for i in range(DEVS - 1)])  7.42 us
    pallas_call x4, Pallas kernels, place_tiles(): pl.pallas_call(functools.partial(place_kernel, pieces, len(sources)), in_...  7.38 us
    ppermute x3, starting transfers between devices, swapped(): return lax.ppermute(array, 'c', swap)  7.16 us
  transfers between devices with their start and end apart: 16, of which 10 were waited for; matrix products, arithmetic and copies ran while one was open for 0% of the time, Pallas kernels for 17%

profile of v12, /device:TPU:1, one launch (start us, length us, event | category | flops | bytes accessed | tf_op | source)
XLA Modules:
  0.0 151.2 jit_solution(6255058255826851187)
XLA Ops:
  0.6 5.6 %project.1 = (bf16[128,1024]{1,0:T(8,128)(2,1)}, bf16[2,128,1024]{2,1,0:T(8,128)(2,1)}, f32[4,4,128]{2,1,0:T(4,128)}, f32[4,128,4]{2,1,0:T(8,128)}, bf16[2,1024,...) custom-call(bf16[128,1024]{1,0:T(8,128)(2,1)} %tok.1, bf16[1024,1024]{1,0:T(8,128)(2,1)} %wq.3, bf16[1024,1024]{1,0:T(8,128)(2,1)} %wk.5, ...), custom_call_target="tpu_custom_call" | custom-call | flops 805306368 | bytes 7864320 | tf_op jit(solution)/shard_map/project/pallas_call | solution.py:125
  6.2 5.7 %collective-permute-start = (bf16[128,1024]{1,0:T(8,128)(2,1)}, bf16[128,1024]{1,0:T(8,128)(2,1)S(1)}, u32[]{:S(2)}, u32[]{:S(2)}) collective-permute-start(bf16[128,1024]{1,0:T(8,128)(2,1)} %get-tuple-element.40.tok), channel_id=1, source_target_pairs={{0,1},{1,2},{2,3},{3,4},{4,5},{5,6},{6,7},{7,8},{8,9},{9,10},{10,1... | collective-permute-start | bytes 786440 | tf_op jit(solution)/shard_map/ppermute | solution.py:625
  11.9 9.7 %all-to-all-start = ((bf16[128,16,128]{2,1,0:T(8,128)(2,1)}), bf16[128,16,128]{2,1,0:T(8,128)(2,1)S(1)}, u32[]{:S(2)}, u32[]{:S(2)}) async-start(bf16[128,16,128]{2,1,0:T(8,128)(2,1)} %bitcast.24), calls=%async_computation | async-start | bytes 1048576 | tf_op jit(solution)/shard_map/all_to_all | solution.py:626
  21.6 2.7 %collective-permute-done.ptok = bf16[128,1024]{1,0:T(8,128)(2,1)S(1)} collective-permute-done((bf16[128,1024]{1,0:T(8,128)(2,1)}, bf16[128,1024]{1,0:T(8,128)(2,1)S(1)}, u32[]{:S(2)}, u32[]{:S(2)}) %collective-permute-start) | collective-permute-done | bytes 262176 | tf_op jit(solution)/shard_map/ppermute | solution.py:625
  24.3 0.7 copy-done.3
  25.0 8.0 %near.1 = (f32[128,1024]{1,0:T(8,128)}, f32[128,1024]{1,0:T(8,128)}, f32[2,128,1024]{2,1,0:T(8,128)}, bf16[2,128,1024]{2,1,0:T(8,128)(2,1)}, s32[1]{0:T(128)}) custom-call(s32[1]{0:T(128)} %bitcast.place, s32[1,4]{1,0:T(1,128)} %blocks.1, bf16[128,1024]{1,0:T(8,128)(2,1)} %get-tuple-element.38.q_ref.q, bf16[2,128,1024]{2,1,0:T(8,128)(2,1)} %get-tuple-element.39.kv, ...), custom_call_target="tpu_custom_call" | custom-call | flops 4000000000 | bytes 16000000 | tf_op jit(solution)/shard_map/near/pallas_call | solution.py:297
  33.0 7.4 %collective-permute-start.1 = (bf16[2,128,1024]{2,1,0:T(8,128)(2,1)}, bf16[2,128,1024]{2,1,0:T(8,128)(2,1)S(1)}, u32[]{:S(2)}, u32[]{:S(2)}) collective-permute-start(bf16[2,128,1024]{2,1,0:T(8,128)(2,1)} %get-tuple-element.46), channel_id=1, source_target_pairs={{1,0},{2,1},{3,2},{4,3},{5,4},{6,5},{7,6},{8,7},{9,8},{10,9},{11,1... | collective-permute-start | bytes 1572872 | tf_op jit(solution)/shard_map/ppermute | solution.py:630
  40.4 0.0 all-to-all-done.got
  40.4 1.9 %scan.1 = bf16[1024,128]{1,0:T(8,128)(2,1)} custom-call(s32[1]{0:T(128)} %get-tuple-element.47.place.tag, bf16[128,16,128]{2,1,0:T(8,128)(2,1)S(1)} %all-to-all-done.got), custom_call_target="tpu_custom_call" | custom-call | flops 262144 | bytes 1048576 | tf_op jit(solution)/shard_map/scan/pallas_call | solution.py:208
  42.3 3.5 %all-to-all-start.1 = ((bf16[128,8,128]{2,1,0:T(8,128)(2,1)}), bf16[128,8,128]{2,1,0:T(8,128)(2,1)S(1)}, u32[]{:S(2)}, u32[]{:S(2)}) async-start(bf16[128,8,128]{2,1,0:T(8,128)(2,1)} %bitcast.2), calls=%async_computation.1 | async-start | bytes 524288 | tf_op jit(solution)/shard_map/all_to_all | solution.py:634
  45.9 1.2 flip.1
  47.1 0.6 collective-permute-start.2
  47.7 2.4 %collective-permute-start.3 = (bf16[1024,128]{1,0:T(8,128)(2,1)S(1)}, bf16[1024,128]{1,0:T(8,128)(2,1)S(1)}, u32[]{:S(2)}, u32[]{:S(2)}) collective-permute-start(bf16[1024,128]{1,0:T(8,128)(2,1)S(1)} %get-tuple-element.53.refs_0_), channel_id=1, source_target_pairs={{0,16},{8,24},{16,0},{24,8},{1,17},{9,25},{17,1},{25,9},{2,18},{10... | collective-permute-start | bytes 786440 | tf_op jit(solution)/shard_map/ppermute | solution.py:633
  50.1 1.2 collective-permute-start.4
  51.3 4.9 %all-to-all-done.1 = bf16[128,8,128]{2,1,0:T(8,128)(2,1)S(1)} async-done(((bf16[128,8,128]{2,1,0:T(8,128)(2,1)}), bf16[128,8,128]{2,1,0:T(8,128)(2,1)S(1)}, u32[]{:S(2)}, u32[]{:S(2)}) %all-to-all-start.1) | async-done | bytes 262176 | tf_op jit(solution)/shard_map/all_to_all | solution.py:634
  56.2 0.7 copy-done.1
  56.9 0.2 copy-done.2
  57.1 3.3 %join.1 = (bf16[128,1024]{1,0:T(8,128)(2,1)}, bf16[8,128,384]{2,1,0:T(8,128)(2,1)}) custom-call(f32[128,1024]{1,0:T(8,128)} %get-tuple-element.43.near_out, f32[128,1024]{1,0:T(8,128)} %get-tuple-element.44.dq_in, f32[2,128,1024]{2,1,0:T(8,128)} %get-tuple-element.45.own, bf16[2,128,1024]{2,1,0:T(8,128)(2,1)} %copy-done.2, ...), custom_call_target="tpu_custom_call" | custom-call | flops 134217728 | bytes 3145728 | tf_op jit(solution)/shard_map/join/pallas_call | solution.py:371
  60.4 0.0 collective-permute-done.2.refs_1_
  60.4 1.4 collective-permute-done.3.refs_2_
  61.8 4.6 %collective-permute-done.4.refs_3_ = bf16[1024,128]{1,0:T(8,128)(2,1)S(1)} collective-permute-done((bf16[1024,128]{1,0:T(8,128)(2,1)S(1)}, bf16[1024,128]{1,0:T(8,128)(2,1)S(1)}, u32[]{:S(2)}, u32[]{:S(2)}) %collective-permute-start.4) | collective-permute-done | bytes 262176 | tf_op jit(solution)/shard_map/ppermute | solution.py:633
  66.4 0.1 stack.2.mine
  66.5 1.3 collective-permute-start.5
  67.7 5.0 %all-to-all-start.2 = ((bf16[8,128,384]{2,1,0:T(8,128)(2,1)}), bf16[8,128,384]{2,1,0:T(8,128)(2,1)S(1)}, u32[]{:S(2)}, u32[]{:S(2)}) async-start(bf16[8,128,384]{2,1,0:T(8,128)(2,1)} %get-tuple-element.50.delta.refs_4_), calls=%async_computation.2 | async-start | bytes 1572864 | tf_op jit(solution)/shard_map/all_to_all | solution.py:638
  72.7 5.6 %back.1 = (bf16[128,1024]{1,0:T(8,128)(2,1)}, s32[1]{0:T(128)}) custom-call(s32[1]{0:T(128)} %bitcast.4.tag.side, bf16[8,128,384]{2,1,0:T(8,128)(2,1)} %get-tuple-element.50.delta.refs_4_, bf16[1024,1024]{1,0:T(8,128)(2,1)} %wq.3, bf16[1024,1024]{1,0:T(8,128)(2,1)} %wk.5, bf16[1024,1024]{1,0:T(8,128)(2,1)} %wv.5), custom_call_target="tpu_custom_call" | custom-call | flops 805306368 | bytes 7340032 | tf_op jit(solution)/shard_map/back/pallas_call | solution.py:425
  78.3 6.6 %all-to-all-done.2.delta = bf16[8,128,384]{2,1,0:T(8,128)(2,1)S(1)} async-done(((bf16[8,128,384]{2,1,0:T(8,128)(2,1)}), bf16[8,128,384]{2,1,0:T(8,128)(2,1)S(1)}, u32[]{:S(2)}, u32[]{:S(2)}) %all-to-all-start.2) | async-done | bytes 786464 | tf_op jit(solution)/shard_map/all_to_all | solution.py:638
  84.9 2.3 %outer.1 = bf16[1024,384]{1,0:T(8,128)(2,1)S(1)} custom-call(s32[1]{0:T(128)} %get-tuple-element.52.core, s32[1]{0:T(128)} %bitcast.5.at_x, bf16[4,1024,128]{2,1,0:T(8,128)(2,1)S(1)} %stack.2.mine, bf16[4,1024,128]{2,1,0:T(8,128)(2,1)S(1)} %collective-permute-done.5.theirs, bf16[8,128,384]{2,1,0:T(8,128)(2,1)S(1)} %all-to-all-done.2.delta), custom_call_target="tpu_custom_call" | custom-call | flops 805306368 | bytes 2883584 | tf_op jit(solution)/shard_map/outer/pallas_call | solution.py:460
  87.2 16.6 %all_to_all.25 = bf16[16,64,384]{2,1,0:T(8,128)(2,1)S(1)} all-to-all(bf16[16,64,384]{2,1,0:T(8,128)(2,1)S(1)} %bitcast.17), channel_id=1, replica_groups=mesh['yl'=2,'c'=2,'x'=4,'z'=4,'yh'=2] {'yl','z','yh'}, dimensions={0} | all-to-all | bytes 1572864 | tf_op jit(solution)/shard_map/all_to_all | solution.py:643
  103.8 0.1 convert_reduce_fusion
  103.9 0.1 broadcast_in_dim.2
  104.0 13.6 %all_to_all.26 = bf16[16,64,384]{2,1,0:T(8,128)(2,1)S(1)} all-to-all(bf16[16,64,384]{2,1,0:T(8,128)(2,1)S(1)} %broadcast_in_dim.2), channel_id=1, replica_groups={{0,1,2,3,4,5,6,7,64,65,66,67,68,69,70,71},{8,9,10,11,12,13,14,15,72,73,..., dimensions={0} | all-to-all | bytes 1572864 | tf_op jit(solution)/shard_map/all_to_all | solution.py:598
  117.5 4.1 %collective-permute-start.8 = (bf16[8,128,384]{2,1,0:T(8,128)(2,1)S(1)}, bf16[8,128,384]{2,1,0:T(8,128)(2,1)S(1)}, u32[]{:S(2)}, u32[]{:S(2)}) collective-permute-start(bf16[8,128,384]{2,1,0:T(8,128)(2,1)S(1)} %bitcast.13), channel_id=1, source_target_pairs={{0,32},{32,0},{1,33},{33,1},{2,34},{34,2},{3,35},{35,3},{4,36},{36... | collective-permute-start | bytes 2359304 | tf_op jit(solution)/shard_map/ppermute | solution.py:595
  121.6 0.4 collective-permute-start.6
  122.1 2.2 %collective-permute-start.7 = (bf16[8,128,384]{2,1,0:T(8,128)(2,1)S(1)}, bf16[8,128,384]{2,1,0:T(8,128)(2,1)S(1)}, u32[]{:S(2)}, u32[]{:S(2)}) collective-permute-start(bf16[8,128,384]{2,1,0:T(8,128)(2,1)S(1)} %bitcast.15), channel_id=1, source_target_pairs={{0,24},{32,38},{1,25},{33,39},{2,26},{34,32},{3,27},{35,33},{4,28}... | collective-permute-start | bytes 2359304 | tf_op jit(solution)/shard_map/ppermute | solution.py:504
  124.3 1.6 %place.4 = (bf16[8,128,1024]{2,1,0:T(8,128)(2,1)}, bf16[8,128,1024]{2,1,0:T(8,128)(2,1)}, bf16[8,128,1024]{2,1,0:T(8,128)(2,1)}, f32[8,128]{1,0:T(8,128)S(1)}) custom-call(s32[1]{0:T(128)} %bitcast.4.tag.side, s32[1]{0:T(128)} %bitcast.5.at_x, s32[1]{0:T(128)} %bitcast.6.at_z, bf16[8,128,384]{2,1,0:T(8,128)(2,1)S(1)} %bitcast.16, ...), custom_call_target="tpu_custom_call" | custom-call | bytes 3145728 | tf_op jit(solution)/shard_map/place/pallas_call | solution.py:554
  125.9 8.1 %collective-permute-done.6.behind = bf16[8,128,384]{2,1,0:T(8,128)(2,1)S(1)} collective-permute-done((bf16[8,128,384]{2,1,0:T(8,128)(2,1)S(1)}, bf16[8,128,384]{2,1,0:T(8,128)(2,1)S(1)}, u32[]{:S(2)}, u32[]{:S(2)}) %collective-permute-start.6) | collective-permute-done | bytes 786464 | tf_op jit(solution)/shard_map/ppermute | solution.py:504
  134.0 0.2 halves.1
  134.2 0.9 collective-permute-start.11
  135.1 2.1 %collective-permute-start.10 = (bf16[4,128,384]{2,1,0:T(8,128)(2,1)S(1)}, bf16[4,128,384]{2,1,0:T(8,128)(2,1)S(1)}, u32[]{:S(2)}, u32[]{:S(2)}) collective-permute-start(bf16[4,128,384]{2,1,0:T(8,128)(2,1)S(1)} %get-tuple-element.56), channel_id=1, source_target_pairs={{0,24},{32,38},{1,25},{33,39},{2,26},{34,32},{3,27},{35,33},{4,28}... | collective-permute-start | bytes 1179656 | tf_op jit(solution)/shard_map/ppermute | solution.py:504
  137.2 0.9 collective-permute-done.11.refs_1_
  138.1 2.5 %place.5 = (bf16[8,128,1024]{2,1,0:T(8,128)(2,1)}, bf16[8,128,1024]{2,1,0:T(8,128)(2,1)}, bf16[8,128,1024]{2,1,0:T(8,128)(2,1)}, f32[8,128]{1,0:T(8,128)S(1)}) custom-call(s32[1]{0:T(128)} %bitcast.4.tag.side, s32[1]{0:T(128)} %bitcast.5.at_x, s32[1]{0:T(128)} %bitcast.6.at_z, ...), custom_call_target="tpu_custom_call", output_to_operand_aliasing={{0}: (5, {}), {1}: (6, {}), {2}: (7, {})} | custom-call | bytes 6291456 | tf_op jit(solution)/shard_map/place/pallas_call | solution.py:554
  140.6 1.4 collective-permute-done.10.refs_1_
  142.0 3.3 %collective-permute-done.9.refs_0_ = bf16[4,128,384]{2,1,0:T(8,128)(2,1)S(1)} collective-permute-done((bf16[4,128,384]{2,1,0:T(8,128)(2,1)S(1)}, bf16[4,128,384]{2,1,0:T(8,128)(2,1)S(1)}, u32[]{:S(2)}, u32[]{:S(2)}) %collective-permute-start.9) | collective-permute-done | bytes 393248 | tf_op jit(solution)/shard_map/ppermute | solution.py:504
  145.3 0.1 stack.3
  145.4 2.1 %collective-permute-start.12 = (bf16[8,128,384]{2,1,0:T(8,128)(2,1)S(1)}, bf16[8,128,384]{2,1,0:T(8,128)(2,1)S(1)}, u32[]{:S(2)}, u32[]{:S(2)}) collective-permute-start(bf16[8,128,384]{2,1,0:T(8,128)(2,1)S(1)} %bitcast.18), channel_id=1, source_target_pairs={{0,32},{32,0},{1,33},{33,1},{2,34},{34,2},{3,35},{35,3},{4,36},{36... | collective-permute-start | bytes 2359304 | tf_op jit(solution)/shard_map/ppermute | solution.py:595
  147.6 1.7 %place.6 = (bf16[8,128,1024]{2,1,0:T(8,128)(2,1)}, bf16[8,128,1024]{2,1,0:T(8,128)(2,1)}, bf16[8,128,1024]{2,1,0:T(8,128)(2,1)}, f32[8,128]{1,0:T(8,128)}) custom-call(s32[1]{0:T(128)} %bitcast.4.tag.side, s32[1]{0:T(128)} %bitcast.5.at_x, s32[1]{0:T(128)} %bitcast.6.at_z, ...), custom_call_target="tpu_custom_call", output_to_operand_aliasing={{0}: (4, {}), {1}: (5, {}), {2}: (6, {})} | custom-call | bytes 1572864 | tf_op jit(solution)/shard_map/place/pallas_call | solution.py:554
  149.2 0.2 collective-permute-done.12.refs_0_
  149.5 1.7 %place.7 = (bf16[8,128,1024]{2,1,0:T(8,128)(2,1)}, bf16[8,128,1024]{2,1,0:T(8,128)(2,1)}, bf16[8,128,1024]{2,1,0:T(8,128)(2,1)}, f32[8,128]{1,0:T(8,128)}) custom-call(s32[1]{0:T(128)S(6)} %sub.3.side, s32[1]{0:T(128)} %bitcast.5.at_x, s32[1]{0:T(128)} %bitcast.6.at_z, ...), custom_call_target="tpu_custom_call", output_to_operand_aliasing={{0}: (4, {}), {1}: (5, {}), {2}: (6, {})} | custom-call | bytes 1572864 | tf_op jit(solution)/shard_map/place/pallas_call | solution.py:554
  (11 shorter events, 0.0 us)
Async XLA Ops:
  6.2 18.1 %collective-permute-start = (bf16[128,1024]{1,0:T(8,128)(2,1)}, bf16[128,1024]{1,0:T(8,128)(2,1)S(1)}, u32[]{:S(2)}, u32[]{:S(2)}) collective-permute-start(bf16[128,1024]{1,0:T(8,128)(2,1)} %get-tuple-element.40.tok), channel_id=1, source_target_pairs={{0,1},{1,2},{2,3},{3,4},{4,5},{5,6},{6,7},{7,8},{8,9},{9,10},{10,1... | collective-permute-start | bytes 786440 | tf_op jit(solution)/shard_map/ppermute | solution.py:625
  11.9 28.5 %all-to-all-start = ((bf16[128,16,128]{2,1,0:T(8,128)(2,1)}), bf16[128,16,128]{2,1,0:T(8,128)(2,1)S(1)}, u32[]{:S(2)}, u32[]{:S(2)}) async-start(bf16[128,16,128]{2,1,0:T(8,128)(2,1)} %bitcast.24), calls=%async_computation | async-start | bytes 1048576 | tf_op jit(solution)/shard_map/all_to_all | solution.py:626
  24.3 0.7 copy-start.3
  25.0 20.9 %copy-start = (bf16[128,1024]{1,0:T(8,128)(2,1)S(1)}, bf16[128,1024]{1,0:T(8,128)(2,1)}, u32[]{:S(2)}) copy-start(bf16[128,1024]{1,0:T(8,128)(2,1)} %get-tuple-element.40.tok) | copy-start | bytes 786436
  33.0 23.2 %collective-permute-start.1 = (bf16[2,128,1024]{2,1,0:T(8,128)(2,1)}, bf16[2,128,1024]{2,1,0:T(8,128)(2,1)S(1)}, u32[]{:S(2)}, u32[]{:S(2)}) collective-permute-start(bf16[2,128,1024]{2,1,0:T(8,128)(2,1)} %get-tuple-element.46), channel_id=1, source_target_pairs={{1,0},{2,1},{3,2},{4,3},{5,4},{6,5},{7,6},{8,7},{9,8},{10,9},{11,1... | collective-permute-start | bytes 1572872 | tf_op jit(solution)/shard_map/ppermute | solution.py:630
  42.3 13.8 %all-to-all-start.1 = ((bf16[128,8,128]{2,1,0:T(8,128)(2,1)}), bf16[128,8,128]{2,1,0:T(8,128)(2,1)S(1)}, u32[]{:S(2)}, u32[]{:S(2)}) async-start(bf16[128,8,128]{2,1,0:T(8,128)(2,1)} %bitcast.2), calls=%async_computation.1 | async-start | bytes 524288 | tf_op jit(solution)/shard_map/all_to_all | solution.py:634
  47.1 13.2 %collective-permute-start.2 = (bf16[1024,128]{1,0:T(8,128)(2,1)S(1)}, bf16[1024,128]{1,0:T(8,128)(2,1)S(1)}, u32[]{:S(2)}, u32[]{:S(2)}) collective-permute-start(bf16[1024,128]{1,0:T(8,128)(2,1)S(1)} %get-tuple-element.53.refs_0_), channel_id=1, source_target_pairs={{0,8},{8,16},{16,24},{24,0},{1,9},{9,17},{17,25},{25,1},{2,10},{10... | collective-permute-start | bytes 786440 | tf_op jit(solution)/shard_map/ppermute | solution.py:633
  47.7 14.1 %collective-permute-start.3 = (bf16[1024,128]{1,0:T(8,128)(2,1)S(1)}, bf16[1024,128]{1,0:T(8,128)(2,1)S(1)}, u32[]{:S(2)}, u32[]{:S(2)}) collective-permute-start(bf16[1024,128]{1,0:T(8,128)(2,1)S(1)} %get-tuple-element.53.refs_0_), channel_id=1, source_target_pairs={{0,16},{8,24},{16,0},{24,8},{1,17},{9,25},{17,1},{25,9},{2,18},{10... | collective-permute-start | bytes 786440 | tf_op jit(solution)/shard_map/ppermute | solution.py:633
  50.1 16.3 %collective-permute-start.4 = (bf16[1024,128]{1,0:T(8,128)(2,1)S(1)}, bf16[1024,128]{1,0:T(8,128)(2,1)S(1)}, u32[]{:S(2)}, u32[]{:S(2)}) collective-permute-start(bf16[1024,128]{1,0:T(8,128)(2,1)S(1)} %get-tuple-element.53.refs_0_), channel_id=1, source_target_pairs={{0,24},{8,0},{16,8},{24,16},{1,25},{9,1},{17,9},{25,17},{2,26},{10... | collective-permute-start | bytes 786440 | tf_op jit(solution)/shard_map/ppermute | solution.py:633
  56.2 0.7 copy-start.1
  56.2 0.9 copy-start.2
  66.5 18.5 %collective-permute-start.5 = (bf16[4,1024,128]{2,1,0:T(8,128)(2,1)S(1)}, bf16[4,1024,128]{2,1,0:T(8,128)(2,1)S(1)}, u32[]{:S(2)}, u32[]{:S(2)}) collective-permute-start(bf16[4,1024,128]{2,1,0:T(8,128)(2,1)S(1)} %stack.2.mine), channel_id=1, source_target_pairs={{0,32},{32,0},{1,33},{33,1},{2,34},{34,2},{3,35},{35,3},{4,36},{36... | collective-permute-start | bytes 3145736 | tf_op jit(solution)/shard_map/ppermute | solution.py:640
  67.7 17.2 %all-to-all-start.2 = ((bf16[8,128,384]{2,1,0:T(8,128)(2,1)}), bf16[8,128,384]{2,1,0:T(8,128)(2,1)S(1)}, u32[]{:S(2)}, u32[]{:S(2)}) async-start(bf16[8,128,384]{2,1,0:T(8,128)(2,1)} %get-tuple-element.50.delta.refs_4_), calls=%async_computation.2 | async-start | bytes 1572864 | tf_op jit(solution)/shard_map/all_to_all | solution.py:638
  117.5 6.8 %collective-permute-start.8 = (bf16[8,128,384]{2,1,0:T(8,128)(2,1)S(1)}, bf16[8,128,384]{2,1,0:T(8,128)(2,1)S(1)}, u32[]{:S(2)}, u32[]{:S(2)}) collective-permute-start(bf16[8,128,384]{2,1,0:T(8,128)(2,1)S(1)} %bitcast.13), channel_id=1, source_target_pairs={{0,32},{32,0},{1,33},{33,1},{2,34},{34,2},{3,35},{35,3},{4,36},{36... | collective-permute-start | bytes 2359304 | tf_op jit(solution)/shard_map/ppermute | solution.py:595
  121.6 12.3 %collective-permute-start.6 = (bf16[8,128,384]{2,1,0:T(8,128)(2,1)S(1)}, bf16[8,128,384]{2,1,0:T(8,128)(2,1)S(1)}, u32[]{:S(2)}, u32[]{:S(2)}) collective-permute-start(bf16[8,128,384]{2,1,0:T(8,128)(2,1)S(1)} %bitcast.14), channel_id=1, source_target_pairs={{0,8},{32,34},{1,9},{33,35},{2,10},{34,36},{3,11},{35,37},{4,12},{... | collective-permute-start | bytes 2359304 | tf_op jit(solution)/shard_map/ppermute | solution.py:504
  122.1 11.9 %collective-permute-start.7 = (bf16[8,128,384]{2,1,0:T(8,128)(2,1)S(1)}, bf16[8,128,384]{2,1,0:T(8,128)(2,1)S(1)}, u32[]{:S(2)}, u32[]{:S(2)}) collective-permute-start(bf16[8,128,384]{2,1,0:T(8,128)(2,1)S(1)} %bitcast.15), channel_id=1, source_target_pairs={{0,24},{32,38},{1,25},{33,39},{2,26},{34,32},{3,27},{35,33},{4,28}... | collective-permute-start | bytes 2359304 | tf_op jit(solution)/shard_map/ppermute | solution.py:504
  134.2 4.0 %collective-permute-start.11 = (bf16[16,128,384]{2,1,0:T(8,128)(2,1)S(1)}, bf16[16,128,384]{2,1,0:T(8,128)(2,1)S(1)}, u32[]{:S(2)}, u32[]{:S(2)}) collective-permute-start(bf16[16,128,384]{2,1,0:T(8,128)(2,1)S(1)} %get-tuple-element.57.refs_0_), channel_id=1, source_target_pairs={{0,32},{32,0},{1,33},{33,1},{2,34},{34,2},{3,35},{35,3},{4,36},{36... | collective-permute-start | bytes 4718600 | tf_op jit(solution)/shard_map/ppermute | solution.py:595
  135.1 6.9 %collective-permute-start.10 = (bf16[4,128,384]{2,1,0:T(8,128)(2,1)S(1)}, bf16[4,128,384]{2,1,0:T(8,128)(2,1)S(1)}, u32[]{:S(2)}, u32[]{:S(2)}) collective-permute-start(bf16[4,128,384]{2,1,0:T(8,128)(2,1)S(1)} %get-tuple-element.56), channel_id=1, source_target_pairs={{0,24},{32,38},{1,25},{33,39},{2,26},{34,32},{3,27},{35,33},{4,28}... | collective-permute-start | bytes 1179656 | tf_op jit(solution)/shard_map/ppermute | solution.py:504
  137.2 8.1 %collective-permute-start.9 = (bf16[4,128,384]{2,1,0:T(8,128)(2,1)S(1)}, bf16[4,128,384]{2,1,0:T(8,128)(2,1)S(1)}, u32[]{:S(2)}, u32[]{:S(2)}) collective-permute-start(bf16[4,128,384]{2,1,0:T(8,128)(2,1)S(1)} %get-tuple-element.55), channel_id=1, source_target_pairs={{0,8},{32,34},{1,9},{33,35},{2,10},{34,36},{3,11},{35,37},{4,12},{... | collective-permute-start | bytes 1179656 | tf_op jit(solution)/shard_map/ppermute | solution.py:504
  145.4 4.1 %collective-permute-start.12 = (bf16[8,128,384]{2,1,0:T(8,128)(2,1)S(1)}, bf16[8,128,384]{2,1,0:T(8,128)(2,1)S(1)}, u32[]{:S(2)}, u32[]{:S(2)}) collective-permute-start(bf16[8,128,384]{2,1,0:T(8,128)(2,1)S(1)} %bitcast.18), channel_id=1, source_target_pairs={{0,32},{32,0},{1,33},{33,1},{2,34},{34,2},{3,35},{35,3},{4,36},{36... | collective-permute-start | bytes 2359304 | tf_op jit(solution)/shard_map/ppermute | solution.py:595

commit v13 on v12

--- a/solution.py
+++ b/solution.py
@@ -456,10 +456,10 @@
     near_count, rows, cols = delta.shape
     width = mine.shape[1]
     smem = pl.BlockSpec(memory_space=pltpu.SMEM)
-    tok = pl.BlockSpec((near_count // 2, width // 2, rows), lambda i: (0, i, 0))
+    tok = pl.BlockSpec((near_count // 2, width, rows), lambda i: (0, i, 0))
     return pl.pallas_call(
         outer_kernel,
-        grid=(2,),
+        grid=(1,),
         in_specs=[
             smem,
             smem,
@@ -467,7 +467,7 @@
             tok,
             pl.BlockSpec((near_count, rows, cols), lambda i: (0, 0, 0)),
         ],
-        out_specs=pl.BlockSpec((width // 2, cols), lambda i: (i, 0)),
+        out_specs=pl.BlockSpec((width, cols), lambda i: (i, 0)),
         out_shape=jax.ShapeDtypeStruct((width, cols), BF),
         compiler_params=params(20),
         cost_estimate=cost(

time: 152 us -> 151 us (level)
  no operation moved by 1% of the time
where the time goes in v13:
time: 151 us
  starting transfers between devices  48.7 us (32%)
  Pallas kernels  35.1 us (23%)
  waiting for transfers between devices  34.2 us (23%)
  blocking collectives  30.1 us (20%)
  local copies, waits for them, and re-layouts  1.72 us (1%)
    all_to_all x1, blocking collectives, shards(): lax.all_to_all(partial.reshape(16, width // 16, 3 * PAIR), FAR16, 0, 0)  16.6 us
    all_to_all x1, blocking collectives, gather_tiles(): lax.all_to_all(jnp.broadcast_to(piece[None], (16, rows, cols)), AX, 0, 0,...  13.6 us
    ppermute x4, waiting for transfers between devices, ring(): return lax.ppermute(array, AX, route)  12.8 us
    all_to_all x1, starting transfers between devices, shards(): got = lax.all_to_all(msg.reshape(DEVS, 16, PAIR), AX, 0, 0)  9.71 us
    pallas_call x1, Pallas kernels, near(): pl.pallas_call(functools.partial(near_kernel, lin_scale), grid=(width //...  7.96 us
    ppermute x1, starting transfers between devices, shards(): nxt = lax.ppermute(prev, AX, [(i + 1, i) for i in range(DEVS - 1)])  7.42 us
    pallas_call x4, Pallas kernels, place_tiles(): pl.pallas_call(functools.partial(place_kernel, pieces, len(sources)), in_...  7.38 us
    ppermute x3, starting transfers between devices, swapped(): return lax.ppermute(array, 'c', swap)  7.16 us
  transfers between devices with their start and end apart: 16, of which 10 were waited for; matrix products, arithmetic and copies ran while one was open for 0% of the time, Pallas kernels for 17%

profile of v13, /device:TPU:1, one launch (start us, length us, event | category | flops | bytes accessed | tf_op | source)
XLA Modules:
  0.0 150.8 jit_solution(10987712868621176346)
XLA Ops:
  0.6 5.6 %project.1 = (bf16[128,1024]{1,0:T(8,128)(2,1)}, bf16[2,128,1024]{2,1,0:T(8,128)(2,1)}, f32[4,4,128]{2,1,0:T(4,128)}, f32[4,128,4]{2,1,0:T(8,128)}, bf16[2,1024,...) custom-call(bf16[128,1024]{1,0:T(8,128)(2,1)} %tok.1, bf16[1024,1024]{1,0:T(8,128)(2,1)} %wq.3, bf16[1024,1024]{1,0:T(8,128)(2,1)} %wk.5, ...), custom_call_target="tpu_custom_call" | custom-call | flops 805306368 | bytes 7864320 | tf_op jit(solution)/shard_map/project/pallas_call | solution.py:125
  6.2 5.7 %collective-permute-start = (bf16[128,1024]{1,0:T(8,128)(2,1)}, bf16[128,1024]{1,0:T(8,128)(2,1)S(1)}, u32[]{:S(2)}, u32[]{:S(2)}) collective-permute-start(bf16[128,1024]{1,0:T(8,128)(2,1)} %get-tuple-element.40.tok), channel_id=1, source_target_pairs={{0,1},{1,2},{2,3},{3,4},{4,5},{5,6},{6,7},{7,8},{8,9},{9,10},{10,1... | collective-permute-start | bytes 786440 | tf_op jit(solution)/shard_map/ppermute | solution.py:625
  11.9 9.7 %all-to-all-start = ((bf16[128,16,128]{2,1,0:T(8,128)(2,1)}), bf16[128,16,128]{2,1,0:T(8,128)(2,1)S(1)}, u32[]{:S(2)}, u32[]{:S(2)}) async-start(bf16[128,16,128]{2,1,0:T(8,128)(2,1)} %bitcast.24), calls=%async_computation | async-start | bytes 1048576 | tf_op jit(solution)/shard_map/all_to_all | solution.py:626
  21.6 2.7 %collective-permute-done.ptok = bf16[128,1024]{1,0:T(8,128)(2,1)S(1)} collective-permute-done((bf16[128,1024]{1,0:T(8,128)(2,1)}, bf16[128,1024]{1,0:T(8,128)(2,1)S(1)}, u32[]{:S(2)}, u32[]{:S(2)}) %collective-permute-start) | collective-permute-done | bytes 262176 | tf_op jit(solution)/shard_map/ppermute | solution.py:625
  24.3 0.7 copy-done.3
  25.0 8.0 %near.1 = (f32[128,1024]{1,0:T(8,128)}, f32[128,1024]{1,0:T(8,128)}, f32[2,128,1024]{2,1,0:T(8,128)}, bf16[2,128,1024]{2,1,0:T(8,128)(2,1)}, s32[1]{0:T(128)}) custom-call(s32[1]{0:T(128)} %bitcast.place, s32[1,4]{1,0:T(1,128)} %blocks.1, bf16[128,1024]{1,0:T(8,128)(2,1)} %get-tuple-element.38.q_ref.q, bf16[2,128,1024]{2,1,0:T(8,128)(2,1)} %get-tuple-element.39.kv, ...), custom_call_target="tpu_custom_call" | custom-call | flops 4000000000 | bytes 16000000 | tf_op jit(solution)/shard_map/near/pallas_call | solution.py:297
  33.0 7.4 %collective-permute-start.1 = (bf16[2,128,1024]{2,1,0:T(8,128)(2,1)}, bf16[2,128,1024]{2,1,0:T(8,128)(2,1)S(1)}, u32[]{:S(2)}, u32[]{:S(2)}) collective-permute-start(bf16[2,128,1024]{2,1,0:T(8,128)(2,1)} %get-tuple-element.46), channel_id=1, source_target_pairs={{1,0},{2,1},{3,2},{4,3},{5,4},{6,5},{7,6},{8,7},{9,8},{10,9},{11,1... | collective-permute-start | bytes 1572872 | tf_op jit(solution)/shard_map/ppermute | solution.py:630
  40.4 1.9 %scan.1 = bf16[1024,128]{1,0:T(8,128)(2,1)} custom-call(s32[1]{0:T(128)} %get-tuple-element.47.place.tag, bf16[128,16,128]{2,1,0:T(8,128)(2,1)S(1)} %all-to-all-done.got), custom_call_target="tpu_custom_call" | custom-call | flops 262144 | bytes 1048576 | tf_op jit(solution)/shard_map/scan/pallas_call | solution.py:208
  42.3 3.5 %all-to-all-start.1 = ((bf16[128,8,128]{2,1,0:T(8,128)(2,1)}), bf16[128,8,128]{2,1,0:T(8,128)(2,1)S(1)}, u32[]{:S(2)}, u32[]{:S(2)}) async-start(bf16[128,8,128]{2,1,0:T(8,128)(2,1)} %bitcast.2), calls=%async_computation.1 | async-start | bytes 524288 | tf_op jit(solution)/shard_map/all_to_all | solution.py:634
  45.9 1.2 flip.1
  47.1 0.6 collective-permute-start.2
  47.7 2.4 %collective-permute-start.3 = (bf16[1024,128]{1,0:T(8,128)(2,1)S(1)}, bf16[1024,128]{1,0:T(8,128)(2,1)S(1)}, u32[]{:S(2)}, u32[]{:S(2)}) collective-permute-start(bf16[1024,128]{1,0:T(8,128)(2,1)S(1)} %get-tuple-element.53.refs_0_), channel_id=1, source_target_pairs={{0,16},{8,24},{16,0},{24,8},{1,17},{9,25},{17,1},{25,9},{2,18},{10... | collective-permute-start | bytes 786440 | tf_op jit(solution)/shard_map/ppermute | solution.py:633
  50.1 1.2 collective-permute-start.4
  51.3 4.9 %all-to-all-done.1 = bf16[128,8,128]{2,1,0:T(8,128)(2,1)S(1)} async-done(((bf16[128,8,128]{2,1,0:T(8,128)(2,1)}), bf16[128,8,128]{2,1,0:T(8,128)(2,1)S(1)}, u32[]{:S(2)}, u32[]{:S(2)}) %all-to-all-start.1) | async-done | bytes 262176 | tf_op jit(solution)/shard_map/all_to_all | solution.py:634
  56.2 0.0 collective-permute-done.1.nxt
  56.2 0.7 copy-done.1
  56.9 0.2 copy-done.2
  57.1 3.3 %join.1 = (bf16[128,1024]{1,0:T(8,128)(2,1)}, bf16[8,128,384]{2,1,0:T(8,128)(2,1)}) custom-call(f32[128,1024]{1,0:T(8,128)} %get-tuple-element.43.near_out, f32[128,1024]{1,0:T(8,128)} %get-tuple-element.44.dq_in, f32[2,128,1024]{2,1,0:T(8,128)} %get-tuple-element.45.own, bf16[2,128,1024]{2,1,0:T(8,128)(2,1)} %copy-done.2, ...), custom_call_target="tpu_custom_call" | custom-call | flops 134217728 | bytes 3145728 | tf_op jit(solution)/shard_map/join/pallas_call | solution.py:371
  60.4 0.0 collective-permute-done.2.refs_1_
  60.4 1.4 collective-permute-done.3.refs_2_
  61.8 4.6 %collective-permute-done.4.refs_3_ = bf16[1024,128]{1,0:T(8,128)(2,1)S(1)} collective-permute-done((bf16[1024,128]{1,0:T(8,128)(2,1)S(1)}, bf16[1024,128]{1,0:T(8,128)(2,1)S(1)}, u32[]{:S(2)}, u32[]{:S(2)}) %collective-permute-start.4) | collective-permute-done | bytes 262176 | tf_op jit(solution)/shard_map/ppermute | solution.py:633
  66.4 0.1 stack.2.mine
  66.5 1.3 collective-permute-start.5
  67.7 5.0 %all-to-all-start.2 = ((bf16[8,128,384]{2,1,0:T(8,128)(2,1)}), bf16[8,128,384]{2,1,0:T(8,128)(2,1)S(1)}, u32[]{:S(2)}, u32[]{:S(2)}) async-start(bf16[8,128,384]{2,1,0:T(8,128)(2,1)} %get-tuple-element.50.delta.refs_4_), calls=%async_computation.2 | async-start | bytes 1572864 | tf_op jit(solution)/shard_map/all_to_all | solution.py:638
  72.7 5.6 %back.1 = (bf16[128,1024]{1,0:T(8,128)(2,1)}, s32[1]{0:T(128)}) custom-call(s32[1]{0:T(128)} %bitcast.4.tag.side, bf16[8,128,384]{2,1,0:T(8,128)(2,1)} %get-tuple-element.50.delta.refs_4_, bf16[1024,1024]{1,0:T(8,128)(2,1)} %wq.3, bf16[1024,1024]{1,0:T(8,128)(2,1)} %wk.5, bf16[1024,1024]{1,0:T(8,128)(2,1)} %wv.5), custom_call_target="tpu_custom_call" | custom-call | flops 805306368 | bytes 7340032 | tf_op jit(solution)/shard_map/back/pallas_call | solution.py:425
  78.3 6.6 %all-to-all-done.2.delta = bf16[8,128,384]{2,1,0:T(8,128)(2,1)S(1)} async-done(((bf16[8,128,384]{2,1,0:T(8,128)(2,1)}), bf16[8,128,384]{2,1,0:T(8,128)(2,1)S(1)}, u32[]{:S(2)}, u32[]{:S(2)}) %all-to-all-start.2) | async-done | bytes 786464 | tf_op jit(solution)/shard_map/all_to_all | solution.py:638
  84.9 1.9 %outer.1 = bf16[1024,384]{1,0:T(8,128)(2,1)S(1)} custom-call(s32[1]{0:T(128)} %get-tuple-element.52.core, s32[1]{0:T(128)} %bitcast.5.at_x, bf16[4,1024,128]{2,1,0:T(8,128)(2,1)S(1)} %stack.2.mine, bf16[4,1024,128]{2,1,0:T(8,128)(2,1)S(1)} %collective-permute-done.5.theirs, bf16[8,128,384]{2,1,0:T(8,128)(2,1)S(1)} %all-to-all-done.2.delta), custom_call_target="tpu_custom_call" | custom-call | flops 805306368 | bytes 2883584 | tf_op jit(solution)/shard_map/outer/pallas_call | solution.py:460
  86.8 16.6 %all_to_all.25 = bf16[16,64,384]{2,1,0:T(8,128)(2,1)S(1)} all-to-all(bf16[16,64,384]{2,1,0:T(8,128)(2,1)S(1)} %bitcast.17), channel_id=1, replica_groups=mesh['yl'=2,'c'=2,'x'=4,'z'=4,'yh'=2] {'yl','z','yh'}, dimensions={0} | all-to-all | bytes 1572864 | tf_op jit(solution)/shard_map/all_to_all | solution.py:643
  103.4 0.1 convert_reduce_fusion
  103.5 0.1 broadcast_in_dim.2
  103.6 13.6 %all_to_all.26 = bf16[16,64,384]{2,1,0:T(8,128)(2,1)S(1)} all-to-all(bf16[16,64,384]{2,1,0:T(8,128)(2,1)S(1)} %broadcast_in_dim.2), channel_id=1, replica_groups={{0,1,2,3,4,5,6,7,64,65,66,67,68,69,70,71},{8,9,10,11,12,13,14,15,72,73,..., dimensions={0} | all-to-all | bytes 1572864 | tf_op jit(solution)/shard_map/all_to_all | solution.py:598
  117.2 4.1 %collective-permute-start.8 = (bf16[8,128,384]{2,1,0:T(8,128)(2,1)S(1)}, bf16[8,128,384]{2,1,0:T(8,128)(2,1)S(1)}, u32[]{:S(2)}, u32[]{:S(2)}) collective-permute-start(bf16[8,128,384]{2,1,0:T(8,128)(2,1)S(1)} %bitcast.13), channel_id=1, source_target_pairs={{0,32},{32,0},{1,33},{33,1},{2,34},{34,2},{3,35},{35,3},{4,36},{36... | collective-permute-start | bytes 2359304 | tf_op jit(solution)/shard_map/ppermute | solution.py:595
  121.2 0.4 collective-permute-start.6
  121.7 2.2 %collective-permute-start.7 = (bf16[8,128,384]{2,1,0:T(8,128)(2,1)S(1)}, bf16[8,128,384]{2,1,0:T(8,128)(2,1)S(1)}, u32[]{:S(2)}, u32[]{:S(2)}) collective-permute-start(bf16[8,128,384]{2,1,0:T(8,128)(2,1)S(1)} %bitcast.15), channel_id=1, source_target_pairs={{0,24},{32,38},{1,25},{33,39},{2,26},{34,32},{3,27},{35,33},{4,28}... | collective-permute-start | bytes 2359304 | tf_op jit(solution)/shard_map/ppermute | solution.py:504
  123.9 1.6 %place.4 = (bf16[8,128,1024]{2,1,0:T(8,128)(2,1)}, bf16[8,128,1024]{2,1,0:T(8,128)(2,1)}, bf16[8,128,1024]{2,1,0:T(8,128)(2,1)}, f32[8,128]{1,0:T(8,128)S(1)}) custom-call(s32[1]{0:T(128)} %bitcast.4.tag.side, s32[1]{0:T(128)} %bitcast.5.at_x, s32[1]{0:T(128)} %bitcast.6.at_z, bf16[8,128,384]{2,1,0:T(8,128)(2,1)S(1)} %bitcast.16, ...), custom_call_target="tpu_custom_call" | custom-call | bytes 3145728 | tf_op jit(solution)/shard_map/place/pallas_call | solution.py:554
  125.5 8.1 %collective-permute-done.6.behind = bf16[8,128,384]{2,1,0:T(8,128)(2,1)S(1)} collective-permute-done((bf16[8,128,384]{2,1,0:T(8,128)(2,1)S(1)}, bf16[8,128,384]{2,1,0:T(8,128)(2,1)S(1)}, u32[]{:S(2)}, u32[]{:S(2)}) %collective-permute-start.6) | collective-permute-done | bytes 786464 | tf_op jit(solution)/shard_map/ppermute | solution.py:504
  133.6 0.2 halves.1
  133.8 0.9 collective-permute-start.11
  134.7 2.1 %collective-permute-start.10 = (bf16[4,128,384]{2,1,0:T(8,128)(2,1)S(1)}, bf16[4,128,384]{2,1,0:T(8,128)(2,1)S(1)}, u32[]{:S(2)}, u32[]{:S(2)}) collective-permute-start(bf16[4,128,384]{2,1,0:T(8,128)(2,1)S(1)} %get-tuple-element.56), channel_id=1, source_target_pairs={{0,24},{32,38},{1,25},{33,39},{2,26},{34,32},{3,27},{35,33},{4,28}... | collective-permute-start | bytes 1179656 | tf_op jit(solution)/shard_map/ppermute | solution.py:504
  136.8 0.9 collective-permute-done.11.refs_1_
  137.8 2.5 %place.5 = (bf16[8,128,1024]{2,1,0:T(8,128)(2,1)}, bf16[8,128,1024]{2,1,0:T(8,128)(2,1)}, bf16[8,128,1024]{2,1,0:T(8,128)(2,1)}, f32[8,128]{1,0:T(8,128)S(1)}) custom-call(s32[1]{0:T(128)} %bitcast.4.tag.side, s32[1]{0:T(128)} %bitcast.5.at_x, s32[1]{0:T(128)} %bitcast.6.at_z, ...), custom_call_target="tpu_custom_call", output_to_operand_aliasing={{0}: (5, {}), {1}: (6, {}), {2}: (7, {})} | custom-call | bytes 6291456 | tf_op jit(solution)/shard_map/place/pallas_call | solution.py:554
  140.3 1.4 collective-permute-done.10.refs_1_
  141.7 3.3 %collective-permute-done.9.refs_0_ = bf16[4,128,384]{2,1,0:T(8,128)(2,1)S(1)} collective-permute-done((bf16[4,128,384]{2,1,0:T(8,128)(2,1)S(1)}, bf16[4,128,384]{2,1,0:T(8,128)(2,1)S(1)}, u32[]{:S(2)}, u32[]{:S(2)}) %collective-permute-start.9) | collective-permute-done | bytes 393248 | tf_op jit(solution)/shard_map/ppermute | solution.py:504
  145.0 0.1 stack.3
  145.0 2.1 %collective-permute-start.12 = (bf16[8,128,384]{2,1,0:T(8,128)(2,1)S(1)}, bf16[8,128,384]{2,1,0:T(8,128)(2,1)S(1)}, u32[]{:S(2)}, u32[]{:S(2)}) collective-permute-start(bf16[8,128,384]{2,1,0:T(8,128)(2,1)S(1)} %bitcast.18), channel_id=1, source_target_pairs={{0,32},{32,0},{1,33},{33,1},{2,34},{34,2},{3,35},{35,3},{4,36},{36... | collective-permute-start | bytes 2359304 | tf_op jit(solution)/shard_map/ppermute | solution.py:595
  147.2 1.7 %place.6 = (bf16[8,128,1024]{2,1,0:T(8,128)(2,1)}, bf16[8,128,1024]{2,1,0:T(8,128)(2,1)}, bf16[8,128,1024]{2,1,0:T(8,128)(2,1)}, f32[8,128]{1,0:T(8,128)}) custom-call(s32[1]{0:T(128)} %bitcast.4.tag.side, s32[1]{0:T(128)} %bitcast.5.at_x, s32[1]{0:T(128)} %bitcast.6.at_z, ...), custom_call_target="tpu_custom_call", output_to_operand_aliasing={{0}: (4, {}), {1}: (5, {}), {2}: (6, {})} | custom-call | bytes 1572864 | tf_op jit(solution)/shard_map/place/pallas_call | solution.py:554
  148.8 0.2 collective-permute-done.12.refs_0_
  149.1 1.7 %place.7 = (bf16[8,128,1024]{2,1,0:T(8,128)(2,1)}, bf16[8,128,1024]{2,1,0:T(8,128)(2,1)}, bf16[8,128,1024]{2,1,0:T(8,128)(2,1)}, f32[8,128]{1,0:T(8,128)}) custom-call(s32[1]{0:T(128)S(6)} %sub.3.side, s32[1]{0:T(128)} %bitcast.5.at_x, s32[1]{0:T(128)} %bitcast.6.at_z, ...), custom_call_target="tpu_custom_call", output_to_operand_aliasing={{0}: (4, {}), {1}: (5, {}), {2}: (6, {})} | custom-call | bytes 1572864 | tf_op jit(solution)/shard_map/place/pallas_call | solution.py:554
  (11 shorter events, 0.0 us)
Async XLA Ops:
  6.2 18.1 %collective-permute-start = (bf16[128,1024]{1,0:T(8,128)(2,1)}, bf16[128,1024]{1,0:T(8,128)(2,1)S(1)}, u32[]{:S(2)}, u32[]{:S(2)}) collective-permute-start(bf16[128,1024]{1,0:T(8,128)(2,1)} %get-tuple-element.40.tok), channel_id=1, source_target_pairs={{0,1},{1,2},{2,3},{3,4},{4,5},{5,6},{6,7},{7,8},{8,9},{9,10},{10,1... | collective-permute-start | bytes 786440 | tf_op jit(solution)/shard_map/ppermute | solution.py:625
  11.9 28.5 %all-to-all-start = ((bf16[128,16,128]{2,1,0:T(8,128)(2,1)}), bf16[128,16,128]{2,1,0:T(8,128)(2,1)S(1)}, u32[]{:S(2)}, u32[]{:S(2)}) async-start(bf16[128,16,128]{2,1,0:T(8,128)(2,1)} %bitcast.24), calls=%async_computation | async-start | bytes 1048576 | tf_op jit(solution)/shard_map/all_to_all | solution.py:626
  24.3 0.7 copy-start.3
  25.0 20.9 %copy-start = (bf16[128,1024]{1,0:T(8,128)(2,1)S(1)}, bf16[128,1024]{1,0:T(8,128)(2,1)}, u32[]{:S(2)}) copy-start(bf16[128,1024]{1,0:T(8,128)(2,1)} %get-tuple-element.40.tok) | copy-start | bytes 786436
  33.0 23.2 %collective-permute-start.1 = (bf16[2,128,1024]{2,1,0:T(8,128)(2,1)}, bf16[2,128,1024]{2,1,0:T(8,128)(2,1)S(1)}, u32[]{:S(2)}, u32[]{:S(2)}) collective-permute-start(bf16[2,128,1024]{2,1,0:T(8,128)(2,1)} %get-tuple-element.46), channel_id=1, source_target_pairs={{1,0},{2,1},{3,2},{4,3},{5,4},{6,5},{7,6},{8,7},{9,8},{10,9},{11,1... | collective-permute-start | bytes 1572872 | tf_op jit(solution)/shard_map/ppermute | solution.py:630
  42.3 13.8 %all-to-all-start.1 = ((bf16[128,8,128]{2,1,0:T(8,128)(2,1)}), bf16[128,8,128]{2,1,0:T(8,128)(2,1)S(1)}, u32[]{:S(2)}, u32[]{:S(2)}) async-start(bf16[128,8,128]{2,1,0:T(8,128)(2,1)} %bitcast.2), calls=%async_computation.1 | async-start | bytes 524288 | tf_op jit(solution)/shard_map/all_to_all | solution.py:634
  47.1 13.2 %collective-permute-start.2 = (bf16[1024,128]{1,0:T(8,128)(2,1)S(1)}, bf16[1024,128]{1,0:T(8,128)(2,1)S(1)}, u32[]{:S(2)}, u32[]{:S(2)}) collective-permute-start(bf16[1024,128]{1,0:T(8,128)(2,1)S(1)} %get-tuple-element.53.refs_0_), channel_id=1, source_target_pairs={{0,8},{8,16},{16,24},{24,0},{1,9},{9,17},{17,25},{25,1},{2,10},{10... | collective-permute-start | bytes 786440 | tf_op jit(solution)/shard_map/ppermute | solution.py:633
  47.7 14.1 %collective-permute-start.3 = (bf16[1024,128]{1,0:T(8,128)(2,1)S(1)}, bf16[1024,128]{1,0:T(8,128)(2,1)S(1)}, u32[]{:S(2)}, u32[]{:S(2)}) collective-permute-start(bf16[1024,128]{1,0:T(8,128)(2,1)S(1)} %get-tuple-element.53.refs_0_), channel_id=1, source_target_pairs={{0,16},{8,24},{16,0},{24,8},{1,17},{9,25},{17,1},{25,9},{2,18},{10... | collective-permute-start | bytes 786440 | tf_op jit(solution)/shard_map/ppermute | solution.py:633
  50.1 16.3 %collective-permute-start.4 = (bf16[1024,128]{1,0:T(8,128)(2,1)S(1)}, bf16[1024,128]{1,0:T(8,128)(2,1)S(1)}, u32[]{:S(2)}, u32[]{:S(2)}) collective-permute-start(bf16[1024,128]{1,0:T(8,128)(2,1)S(1)} %get-tuple-element.53.refs_0_), channel_id=1, source_target_pairs={{0,24},{8,0},{16,8},{24,16},{1,25},{9,1},{17,9},{25,17},{2,26},{10... | collective-permute-start | bytes 786440 | tf_op jit(solution)/shard_map/ppermute | solution.py:633
  56.2 0.7 copy-start.1
  56.2 0.9 copy-start.2
  66.5 18.5 %collective-permute-start.5 = (bf16[4,1024,128]{2,1,0:T(8,128)(2,1)S(1)}, bf16[4,1024,128]{2,1,0:T(8,128)(2,1)S(1)}, u32[]{:S(2)}, u32[]{:S(2)}) collective-permute-start(bf16[4,1024,128]{2,1,0:T(8,128)(2,1)S(1)} %stack.2.mine), channel_id=1, source_target_pairs={{0,32},{32,0},{1,33},{33,1},{2,34},{34,2},{3,35},{35,3},{4,36},{36... | collective-permute-start | bytes 3145736 | tf_op jit(solution)/shard_map/ppermute | solution.py:640
  67.7 17.2 %all-to-all-start.2 = ((bf16[8,128,384]{2,1,0:T(8,128)(2,1)}), bf16[8,128,384]{2,1,0:T(8,128)(2,1)S(1)}, u32[]{:S(2)}, u32[]{:S(2)}) async-start(bf16[8,128,384]{2,1,0:T(8,128)(2,1)} %get-tuple-element.50.delta.refs_4_), calls=%async_computation.2 | async-start | bytes 1572864 | tf_op jit(solution)/shard_map/all_to_all | solution.py:638
  117.2 6.8 %collective-permute-start.8 = (bf16[8,128,384]{2,1,0:T(8,128)(2,1)S(1)}, bf16[8,128,384]{2,1,0:T(8,128)(2,1)S(1)}, u32[]{:S(2)}, u32[]{:S(2)}) collective-permute-start(bf16[8,128,384]{2,1,0:T(8,128)(2,1)S(1)} %bitcast.13), channel_id=1, source_target_pairs={{0,32},{32,0},{1,33},{33,1},{2,34},{34,2},{3,35},{35,3},{4,36},{36... | collective-permute-start | bytes 2359304 | tf_op jit(solution)/shard_map/ppermute | solution.py:595
  121.2 12.3 %collective-permute-start.6 = (bf16[8,128,384]{2,1,0:T(8,128)(2,1)S(1)}, bf16[8,128,384]{2,1,0:T(8,128)(2,1)S(1)}, u32[]{:S(2)}, u32[]{:S(2)}) collective-permute-start(bf16[8,128,384]{2,1,0:T(8,128)(2,1)S(1)} %bitcast.14), channel_id=1, source_target_pairs={{0,8},{32,34},{1,9},{33,35},{2,10},{34,36},{3,11},{35,37},{4,12},{... | collective-permute-start | bytes 2359304 | tf_op jit(solution)/shard_map/ppermute | solution.py:504
  121.7 11.9 %collective-permute-start.7 = (bf16[8,128,384]{2,1,0:T(8,128)(2,1)S(1)}, bf16[8,128,384]{2,1,0:T(8,128)(2,1)S(1)}, u32[]{:S(2)}, u32[]{:S(2)}) collective-permute-start(bf16[8,128,384]{2,1,0:T(8,128)(2,1)S(1)} %bitcast.15), channel_id=1, source_target_pairs={{0,24},{32,38},{1,25},{33,39},{2,26},{34,32},{3,27},{35,33},{4,28}... | collective-permute-start | bytes 2359304 | tf_op jit(solution)/shard_map/ppermute | solution.py:504
  133.8 4.0 %collective-permute-start.11 = (bf16[16,128,384]{2,1,0:T(8,128)(2,1)S(1)}, bf16[16,128,384]{2,1,0:T(8,128)(2,1)S(1)}, u32[]{:S(2)}, u32[]{:S(2)}) collective-permute-start(bf16[16,128,384]{2,1,0:T(8,128)(2,1)S(1)} %get-tuple-element.57.refs_0_), channel_id=1, source_target_pairs={{0,32},{32,0},{1,33},{33,1},{2,34},{34,2},{3,35},{35,3},{4,36},{36... | collective-permute-start | bytes 4718600 | tf_op jit(solution)/shard_map/ppermute | solution.py:595
  134.7 6.9 %collective-permute-start.10 = (bf16[4,128,384]{2,1,0:T(8,128)(2,1)S(1)}, bf16[4,128,384]{2,1,0:T(8,128)(2,1)S(1)}, u32[]{:S(2)}, u32[]{:S(2)}) collective-permute-start(bf16[4,128,384]{2,1,0:T(8,128)(2,1)S(1)} %get-tuple-element.56), channel_id=1, source_target_pairs={{0,24},{32,38},{1,25},{33,39},{2,26},{34,32},{3,27},{35,33},{4,28}... | collective-permute-start | bytes 1179656 | tf_op jit(solution)/shard_map/ppermute | solution.py:504
  136.8 8.1 %collective-permute-start.9 = (bf16[4,128,384]{2,1,0:T(8,128)(2,1)S(1)}, bf16[4,128,384]{2,1,0:T(8,128)(2,1)S(1)}, u32[]{:S(2)}, u32[]{:S(2)}) collective-permute-start(bf16[4,128,384]{2,1,0:T(8,128)(2,1)S(1)} %get-tuple-element.55), channel_id=1, source_target_pairs={{0,8},{32,34},{1,9},{33,35},{2,10},{34,36},{3,11},{35,37},{4,12},{... | collective-permute-start | bytes 1179656 | tf_op jit(solution)/shard_map/ppermute | solution.py:504
  145.0 4.1 %collective-permute-start.12 = (bf16[8,128,384]{2,1,0:T(8,128)(2,1)S(1)}, bf16[8,128,384]{2,1,0:T(8,128)(2,1)S(1)}, u32[]{:S(2)}, u32[]{:S(2)}) collective-permute-start(bf16[8,128,384]{2,1,0:T(8,128)(2,1)S(1)} %bitcast.18), channel_id=1, source_target_pairs={{0,32},{32,0},{1,33},{33,1},{2,34},{34,2},{3,35},{35,3},{4,36},{36... | collective-permute-start | bytes 2359304 | tf_op jit(solution)/shard_map/ppermute | solution.py:595
